TPU v7x, 128 devices: a whole 4x4x4 slice. The times are simulated.
128 devices in a mesh: seq: 16 (over z, y), head: 8 (over x, core).
Axes of the slice: x: 4, y: 4, z: 4, core: 2. Of those that a mesh axis runs over, the one named last changes fastest.
Arguments:
- hidden_in: bfloat16 [8192, 768], P('seq'), may hold values from -6 to 6
- cotangent: bfloat16 [8192, 768], P('seq'), may hold values from -6 to 6
- doc_starts: int32 [8192], P('seq'), may hold values from 0 to 1, as said below
- proj_weight: float32 [768, 24, 128], P('seq', 'head'), may hold values from -0.21875 to 0.21875
- step_weight: float32 [768, 24], P('seq', 'head'), may hold values from -0.109375 to 0.109375
- out_weight: float32 [24, 64, 768], P('head', None, 'seq'), may hold values from -0.15625 to 0.15625
- shared_weight: float32 [768, 256], P(('seq', 'head')), may hold values from -0.21875 to 0.21875
- pre_gain: float32 [768], P(('seq', 'head')), may hold values from 0.5 to 1.5
- channel_params: float32 [6, 24, 64], P(None, 'head'), may hold values from -0.5 to 1.5
- head_params: float32 [3, 24], P(None, 'head'), may hold values from -7 to 1.5
- shared_conv: float32 [256, 5], P(('seq', 'head')), may hold values from -0.5 to 0.5
- proj_first: float32 [768, 24, 128], P('seq', 'head'), may hold values from -28 to 28
- proj_second: float32 [768, 24, 128], P('seq', 'head'), may hold values from 1.6384 to 32.768
- step_first: float32 [768, 24], P('seq', 'head'), may hold values from -28 to 28
- step_second: float32 [768, 24], P('seq', 'head'), may hold values from 1.6384 to 32.768
- out_first: float32 [24, 64, 768], P('head', None, 'seq'), may hold values from -28 to 28
- out_second: float32 [24, 64, 768], P('head', None, 'seq'), may hold values from 1.6384 to 32.768
- shared_first: float32 [768, 256], P(('seq', 'head')), may hold values from -28 to 28
- shared_second: float32 [768, 256], P(('seq', 'head')), may hold values from 1.6384 to 32.768
- gain_first: float32 [768], P(('seq', 'head')), may hold values from -28 to 28
- gain_second: float32 [768], P(('seq', 'head')), may hold values from 1.6384 to 32.768
- channel_first: float32 [6, 24, 64], P(None, 'head'), may hold values from -28 to 28
- channel_second: float32 [6, 24, 64], P(None, 'head'), may hold values from 1.6384 to 32.768
- head_first: float32 [3, 24], P(None, 'head'), may hold values from -28 to 28
- head_second: float32 [3, 24], P(None, 'head'), may hold values from 1.6384 to 32.768
- conv_first: float32 [256, 5], P(('seq', 'head')), may hold values from -28 to 28
- conv_second: float32 [256, 5], P(('seq', 'head')), may hold values from 1.6384 to 32.768
Outputs:
- block_out: bfloat16 [8192, 768], P('seq')
- input_grad: float32 [8192, 768], P('seq')
- proj_first_new: float32 [768, 24, 128], P('seq', 'head')
- proj_second_new: float32 [768, 24, 128], P('seq', 'head')
- proj_weight_new: float32 [768, 24, 128], P('seq', 'head')
- step_first_new: float32 [768, 24], P('seq', 'head')
- step_second_new: float32 [768, 24], P('seq', 'head')
- step_weight_new: float32 [768, 24], P('seq', 'head')
- out_first_new: float32 [24, 64, 768], P('head', None, 'seq')
- out_second_new: float32 [24, 64, 768], P('head', None, 'seq')
- out_weight_new: float32 [24, 64, 768], P('head', None, 'seq')
- shared_first_new: float32 [768, 256], P(('seq', 'head'))
- shared_second_new: float32 [768, 256], P(('seq', 'head'))
- shared_weight_new: float32 [768, 256], P(('seq', 'head'))
- gain_first_new: float32 [768], P(('seq', 'head'))
- gain_second_new: float32 [768], P(('seq', 'head'))
- pre_gain_new: float32 [768], P(('seq', 'head'))
- channel_first_new: float32 [6, 24, 64], P(None, 'head')
- channel_second_new: float32 [6, 24, 64], P(None, 'head')
- channel_params_new: float32 [6, 24, 64], P(None, 'head')
- head_first_new: float32 [3, 24], P(None, 'head')
- head_second_new: float32 [3, 24], P(None, 'head')
- head_params_new: float32 [3, 24], P(None, 'head')
- conv_first_new: float32 [256, 5], P(('seq', 'head'))
- conv_second_new: float32 [256, 5], P(('seq', 'head'))
- shared_conv_new: float32 [256, 5], P(('seq', 'head'))
Inputs may be any that keep to these rules, and one draw needn't show every extreme that they name: `doc_starts`: 1 marks a document's first position; position 0 starts one, and documents start only at positions that are multiples of 4.
All inputs are finite; a program needn't handle non-finite values.
Results may differ from a plain program's by a relative error of at most 0.012.
Values may be sent and summed in bfloat16 or wider, within the bound.
No kernel may reach another device: no remote copies, remote signals or barrier semaphores. Data moves between devices by JAX's collectives and lax.ppermute only.
A program may use at most 128 MiB of HBM per device.

v0:
```python
from functools import partial
import functools

import jax
import jax.numpy as jnp
from jax import lax
from jax.sharding import Mesh
from jax.sharding import PartitionSpec as P

D = 768
DI = 1536
Q = 256
STEP = 10
SEQ = ("seq_0", "seq_1")
SEQ_HEAD = ("seq_0", "seq_1", "head_0", "head_1")
HEAD = ("head_0", "head_1")


highest = lax.Precision.HIGHEST
norm_eps = 1e-05
beta_one = 0.9
beta_two = 0.999
adam_eps = 1e-08
decay_rate = 0.01


def rows_first(arrays, axis, dims):
    turned = [jnp.moveaxis(a, dim, 0) for a, dim in zip(arrays, dims)]
    widths = [t[0].size for t in turned]
    both = jnp.concatenate([t.reshape(-1, w) for t, w in zip(turned, widths)], axis=1)
    filled = lax.all_gather(both, axis, axis=0, tiled=True)
    tiles = jnp.split(filled, [sum(widths[:k]) for k in range(1, len(widths))], axis=1)
    return tuple(
        (
            jnp.moveaxis(b.reshape(-1, *t.shape[1:]), 0, dim)
            for b, t, dim in zip(tiles, turned, dims)
        )
    )


def side_by_side(arrays, axis, dim, along):
    columns = [a.reshape(*a.shape[:along], -1) for a in arrays]
    both = jnp.concatenate(columns, axis=along)
    filled, at, finished = (lax.all_gather(both, axis, axis=dim, tiled=True), 0, [])
    for a, column in zip(arrays, columns):
        piece = filled[..., at : at + column.shape[along]]
        finished.append(piece.reshape(*piece.shape[:along], *a.shape[along:]))
        at += column.shape[along]
    return tuple(finished)


def from_behind(array, axis, by):
    peers = lax.axis_size(axis)
    pairs = [(i, i + by) for i in range(peers) if 0 <= i + by < peers]
    return lax.ppermute(array, axis, pairs)


def copy_for_each(array, axis):
    copies = jnp.broadcast_to(array, (lax.axis_size(axis), *array.shape))
    return lax.all_to_all(copies, axis, split_axis=0, concat_axis=0, tiled=True)


def joined_by_halves(pieces, combine):
    while len(jax.tree.leaves(pieces)[0]) > 1:
        pieces = jax.vmap(combine)(
            *(jax.tree.map(lambda part: part[side::2], pieces) for side in (0, 1))
        )
    return jax.tree.map(lambda part: part[0], pieces)


def entering(array, axis, combine, identity, reverse):
    peers, here = (lax.axis_size(axis), lax.axis_index(axis))
    passed = jnp.arange(peers) > here if reverse else jnp.arange(peers) < here

    def kept(part, zero, own):
        part = jnp.where(
            passed.reshape(-1, *(1 for _ in own.shape)), part, jnp.asarray(zero, own.dtype)
        )
        return part[::-1] if reverse else part

    pieces = jax.tree.map(lambda part: copy_for_each(part, axis), array)
    return joined_by_halves(jax.tree.map(kept, pieces, identity, array), combine)


def over_copies(array, axis):
    everything = copy_for_each(array, axis)
    return jnp.sum(everything, axis=0)


def split_up(array, dim, peers):
    before, after = (array.shape[:dim], array.shape[dim + 1 :])
    return jnp.moveaxis(array.reshape(*before, peers, -1, *after), dim, 0)


def sum_at_owner(array, axis, dim):
    peers = lax.axis_size(axis)
    tiles = lax.all_to_all(split_up(array, dim, peers), axis, 0, 0, tiled=True)
    return jnp.sum(tiles, axis=0)


def in_order(tiles, dim):
    dims = list(tiles.shape[1:])
    dims[dim] *= tiles.shape[0]
    return jnp.moveaxis(tiles, 0, dim).reshape(dims)


def gather_directly(array, axis, dim):
    tiles = copy_for_each(array, axis)
    return in_order(tiles, dim)


def padded_to(lines, peers):
    spare = -len(lines) % peers
    return jnp.pad(lines, [(0, spare)] + [(0, 0)] * (lines.ndim - 1))


def sum_in_two_steps(array, axis):
    lines = array.reshape(-1, *array.shape[1:][-1:])
    padded = padded_to(lines, lax.axis_size(axis))
    own = lax.psum_scatter(padded, axis, scatter_dimension=0, tiled=True)
    whole = lax.all_gather(own, axis, axis=0, tiled=True)
    return whole[: len(lines)].reshape(array.shape)


def sum_packed(arrays, axis, dims):
    peers = lax.axis_size(axis)
    tiles = [split_up(a, dim, peers) for a, dim in zip(arrays, dims)]
    lines = jnp.concatenate([b.reshape(peers, -1) for b in tiles], axis=1)
    width = max(16, -(-lines.shape[1] // 1024) * 8)
    lines = jnp.pad(lines, ((0, 0), (0, width * 128 - lines.shape[1]))).reshape(-1, 128)
    line, at, finished = (lax.psum_scatter(lines, axis, tiled=True).reshape(-1), 0, [])
    for b in tiles:
        part = b[0]
        finished.append(line[at : at + part.size].reshape(part.shape))
        at += part.size
    return tuple(finished)


def sum_by_axis(array, axes, dim):
    far, near = axes
    own = sum_at_owner(split_up(array, dim, lax.axis_size(far)), near, dim + 1)
    return jnp.sum(lax.all_to_all(own, far, 0, 0, tiled=True), axis=0)


def in_one_piece(arrays, axis, dim, along):
    columns = [a.reshape(*a.shape[:along], -1) for a in arrays]
    both = jnp.concatenate(columns, axis=along)
    filled, at, finished = (sum_by_axis(both, axis, dim), 0, [])
    for a, column in zip(arrays, columns):
        piece = filled[..., at : at + column.shape[along]]
        finished.append(piece.reshape(*piece.shape[:along], *a.shape[along:]))
        at += column.shape[along]
    return tuple(finished)


def one_axis_at_a_time(array, axes):
    return functools.reduce(lax.psum, axes, array)


def combine(earlier, later):
    return (earlier[0] * later[0], later[0][:, None, None] * earlier[1] + later[1])


def conv_masks(starts, conv_width):
    length_all = starts.shape[0]
    phase = jnp.arange(length_all) % conv_width
    first_mark = jnp.repeat(
        starts.reshape(length_all // conv_width, conv_width)[:, 0], conv_width
    ).astype(jnp.float32)
    return [
        1.0 - first_mark * (phase < lagging).astype(jnp.float32) for lagging in range(conv_width)
    ]


def group_pass(carried, pieces):
    state_now, passed = carried
    x_conv, b_mat, c_mat, delta, log_decay, marks = pieces
    segment = jnp.cumsum(marks)
    cum_log = jnp.cumsum(log_decay, axis=0)
    size_q = marks.shape[0]
    lower_tri = jnp.arange(size_q)[:, None] >= jnp.arange(size_q)[None, :]
    joined_mask = (lower_tri & (segment[:, None] == segment[None, :]))[:, :, None]
    differ = cum_log[:, None, :] - cum_log[None, :, :]
    decay_mat = jnp.where(joined_mask, jnp.exp(jnp.where(joined_mask, differ, 0.0)), 0.0)
    scores = jnp.dot(c_mat, b_mat.T, precision=highest)
    mixing = decay_mat * scores[:, :, None] * delta[None, :, :]
    output = jnp.einsum("ijh,jhp->ihp", mixing, x_conv, precision=highest)
    keeper = jnp.exp(cum_log) * (segment == 0).astype(jnp.float32)[:, None]
    output = output + keeper[:, :, None] * jnp.einsum(
        "in,hpn->ihp", c_mat, state_now, precision=highest
    )
    last_log = cum_log[-1]
    ending = (
        jnp.exp(last_log[None, :] - cum_log) * (segment == segment[-1]).astype(jnp.float32)[:, None]
    )
    summed = jnp.einsum("jh,jhp,jn->hpn", ending * delta, x_conv, b_mat, precision=highest)
    through = jnp.exp(last_log) * (segment[-1] == 0).astype(jnp.float32)
    new_state = through[:, None, None] * state_now + summed
    return ((new_state, passed * through), (output, keeper * passed[None, :]))


def local_mixer(x_raw, shared_raw, edge_rows, delta_raw, channel, head_vals, conv_vals, starts):
    tokens_dev, heads_dev, head_dim = x_raw.shape
    conv_width = channel.shape[0] - 2
    inner_dim = heads_dev * head_dim
    state_dim = shared_raw.shape[1] // 2
    values = jnp.concatenate([x_raw.reshape(tokens_dev, inner_dim), shared_raw], axis=1)
    padded = jnp.concatenate([edge_rows, values], axis=0)
    conv_taps = jnp.concatenate(
        [channel[:conv_width].reshape(conv_width, inner_dim), conv_vals[:, :conv_width].T], axis=1
    )
    biases = jnp.concatenate([channel[conv_width].reshape(inner_dim), conv_vals[:, conv_width]])
    tap_masks = conv_masks(starts, conv_width)
    conv_out = biases[None, :] + conv_taps[conv_width - 1][None, :] * values
    for lagging in range(1, conv_width):
        begin = conv_width - 1 - lagging
        conv_out = (
            conv_out
            + conv_taps[begin][None, :]
            * padded[begin : begin + tokens_dev]
            * tap_masks[lagging][:, None]
        )
    active = jax.nn.silu(conv_out)
    x_conv = active[:, :inner_dim].reshape(tokens_dev, heads_dev, head_dim)
    b_mat = active[:, inner_dim : inner_dim + state_dim]
    c_mat = active[:, inner_dim + state_dim :]
    delta = jax.nn.softplus(delta_raw + head_vals[0][None, :])
    log_decay = -jnp.exp(head_vals[1])[None, :] * delta
    blocks = tokens_dev // Q

    def to_blocks(array_in):
        return array_in.reshape((blocks, Q) + array_in.shape[1:])

    pieces = (
        to_blocks(x_conv),
        to_blocks(b_mat),
        to_blocks(c_mat),
        to_blocks(delta),
        to_blocks(log_decay),
        to_blocks(starts),
    )
    start_carry = (
        jnp.zeros((heads_dev, head_dim, state_dim), jnp.float32),
        jnp.ones((heads_dev,), jnp.float32),
    )
    ends, outs_all = lax.scan(group_pass, start_carry, pieces)
    y_zero = (
        outs_all[0].reshape(tokens_dev, heads_dev, head_dim) + head_vals[2][None, :, None] * x_conv
    )
    keepers = outs_all[1].reshape(tokens_dev, heads_dev)
    return (y_zero, ends[0], ends[1], keepers, c_mat)


def adam_step(weight, grad_sum, first, second, rate):
    first_new = beta_one * first + (1.0 - beta_one) * grad_sum
    second_new = beta_two * second + (1.0 - beta_two) * grad_sum * grad_sum
    first_hat = first_new / (1.0 - beta_one**STEP)
    second_hat = second_new / (1.0 - beta_two**STEP)
    weight_new = weight - rate * (
        first_hat / (jnp.sqrt(second_hat) + adam_eps) + decay_rate * weight
    )
    return (first_new, second_new, weight_new)


def body(
    hidden_in,
    cotangent,
    doc_starts,
    proj_weight,
    step_weight,
    out_weight,
    shared_weight,
    pre_gain,
    channel_params,
    head_params,
    shared_conv,
    proj_first,
    proj_second,
    step_first,
    step_second,
    out_first,
    out_second,
    shared_first,
    shared_second,
    gain_first,
    gain_second,
    channel_first,
    channel_second,
    head_first,
    head_second,
    conv_first,
    conv_second,
):
    proj_low, step_low, out_low = rows_first(
        (
            proj_weight.astype(jnp.bfloat16),
            step_weight.astype(jnp.bfloat16),
            out_weight.astype(jnp.bfloat16),
        ),
        SEQ,
        (0, 0, 2),
    )
    shared_full, gain_full, conv_full = (
        *side_by_side((shared_weight, pre_gain), SEQ_HEAD, 0, 1),
        lax.all_gather(shared_conv, SEQ_HEAD, axis=0, tiled=True),
    )
    shared_low = shared_full.astype(jnp.bfloat16)
    shared_wide = shared_low.astype(jnp.float32)
    tokens_dev, model_dim = hidden_in.shape
    heads_dev = proj_low.shape[1]
    head_dim = proj_low.shape[2] // 2
    inner_dim = heads_dev * head_dim
    conv_width = channel_params.shape[0] - 2
    resid = hidden_in.astype(jnp.float32)
    inv_rms = lax.rsqrt(jnp.mean(resid * resid, axis=1) + norm_eps)
    normalized = resid * inv_rms[:, None]
    normed_low = (normalized * gain_full[None, :]).astype(jnp.bfloat16)
    proj_flat = proj_low.reshape(model_dim, heads_dev * 2 * head_dim)
    zx_out = jnp.dot(normed_low, proj_flat, preferred_element_type=jnp.float32).reshape(
        tokens_dev, heads_dev, 2 * head_dim
    )
    gate_raw = zx_out[:, :, :head_dim]
    x_raw = zx_out[:, :, head_dim:]
    delta_raw = jnp.dot(normed_low, step_low, preferred_element_type=jnp.float32)
    shared_raw = jnp.dot(normed_low, shared_low, preferred_element_type=jnp.float32)
    values = jnp.concatenate([x_raw.reshape(tokens_dev, inner_dim), shared_raw], axis=1)
    tail_start = tokens_dev - conv_width + 1
    edge_rows = from_behind(values[tail_start:], SEQ, 1)
    mixer = partial(local_mixer, starts=doc_starts)
    mixed, pullback = jax.vjp(
        mixer, x_raw, shared_raw, edge_rows, delta_raw, channel_params, head_params, conv_full
    )
    y_zero, state_end, passed_end, keepers, c_mat = mixed
    unit_pair = (jnp.ones_like(passed_end), jnp.zeros_like(state_end))
    prefix_decay, state_in = entering((passed_end, state_end), SEQ, combine, unit_pair, False)
    carried_in = jnp.einsum("tn,hpn->thp", c_mat, state_in, precision=highest)
    y_full = y_zero + keepers[:, :, None] * carried_in
    gate_act = jax.nn.silu(gate_raw)
    gated = y_full * gate_act
    total_sq = over_copies(jnp.sum(gated * gated, axis=(1, 2)), HEAD)
    gate_rms = lax.rsqrt(total_sq / DI + norm_eps)
    out_gain = channel_params[conv_width + 1]
    scaled = gated * gate_rms[:, None, None]
    normed_out = (scaled * out_gain[None]).astype(jnp.bfloat16)
    normed_flat = normed_out.reshape(tokens_dev, inner_dim)
    out_flat = out_low.reshape(inner_dim, model_dim)
    partial_out = jnp.dot(normed_flat, out_flat, preferred_element_type=jnp.float32)
    share_cols = sum_at_owner(partial_out, HEAD, 1)
    col_count = share_cols.shape[1]
    own_cols = lax.dynamic_slice_in_dim(resid, lax.axis_index(HEAD) * col_count, col_count, 1)
    block_out = gather_directly((own_cols + share_cols).astype(jnp.bfloat16), HEAD, 1)
    rows_back = (((1,), (1,)), ((), ()))
    over_rows = (((0,), (0,)), ((), ()))
    d_normed = lax.dot_general(
        cotangent, out_flat, rows_back, preferred_element_type=jnp.float32
    ).reshape(tokens_dev, heads_dev, head_dim)
    grad_out = lax.dot_general(
        normed_flat, cotangent, over_rows, preferred_element_type=jnp.float32
    ).reshape(heads_dev, head_dim, model_dim)
    grad_gain_out = jnp.sum(d_normed * scaled, axis=0)
    total_dot = over_copies(jnp.sum(d_normed * out_gain[None] * gated, axis=(1, 2)), HEAD)
    d_gated = (
        gate_rms[:, None, None] * out_gain[None] * d_normed
        - gated * (gate_rms**3 * total_dot / DI)[:, None, None]
    )
    d_y = d_gated * gate_act
    sigmoid_gate = jax.nn.sigmoid(gate_raw)
    d_gate_raw = d_gated * y_full * sigmoid_gate * (1.0 + gate_raw * (1.0 - sigmoid_gate))
    local_adj = jnp.einsum("thp,th,tn->hpn", d_y, keepers, c_mat, precision=highest)
    decay_back, adj_out = entering((passed_end, local_adj), SEQ, combine, unit_pair, True)
    d_passed = jnp.sum(adj_out * state_in, axis=(1, 2))
    d_keepers = jnp.sum(d_y * carried_in, axis=2)
    d_c_extra = jnp.einsum("thp,th,hpn->tn", d_y, keepers, state_in, precision=highest)
    d_x_raw, d_shared_raw, d_edge, d_delta_raw, d_channel, d_head, d_conv = pullback(
        (d_y, adj_out, d_passed, d_keepers, d_c_extra)
    )
    edge_grad = from_behind(d_edge, SEQ, -1)
    d_values = jnp.concatenate([d_x_raw.reshape(tokens_dev, inner_dim), d_shared_raw], axis=1)
    d_values = d_values.at[tail_start:].add(edge_grad)
    d_x_full = d_values[:, :inner_dim].reshape(tokens_dev, heads_dev, head_dim)
    d_shared_full = d_values[:, inner_dim:]
    d_zx_low = (
        jnp.concatenate([d_gate_raw, d_x_full], axis=2)
        .astype(jnp.bfloat16)
        .reshape(tokens_dev, heads_dev * 2 * head_dim)
    )
    d_delta_low = d_delta_raw.astype(jnp.bfloat16)
    grad_proj = lax.dot_general(
        normed_low, d_zx_low, over_rows, preferred_element_type=jnp.float32
    ).reshape(model_dim, heads_dev, 2 * head_dim)
    grad_step = lax.dot_general(
        normed_low, d_delta_low, over_rows, preferred_element_type=jnp.float32
    )
    grad_shared = lax.dot_general(
        normed_low.astype(jnp.float32), d_shared_full, over_rows, precision=highest
    )
    d_normed_in = lax.dot_general(
        d_zx_low, proj_flat, rows_back, preferred_element_type=jnp.float32
    )
    d_normed_in = d_normed_in + lax.dot_general(
        d_delta_low, step_low, rows_back, preferred_element_type=jnp.float32
    )
    d_normed_in = d_normed_in + lax.dot_general(
        d_shared_full, shared_wide, rows_back, precision=highest
    )
    grad_gain_pre = jnp.sum(d_normed_in * normalized, axis=0)
    d_normed_all = sum_in_two_steps(d_normed_in, HEAD)
    d_scaled = d_normed_all * gain_full[None, :]
    input_grad = (
        resid * 0.0
        + cotangent.astype(jnp.float32)
        + inv_rms[:, None] * d_scaled
        - resid * (inv_rms**3 * jnp.sum(d_scaled * resid, axis=1) / model_dim)[:, None]
    )
    grad_channel = d_channel.at[conv_width + 1].add(grad_gain_out)
    proj_sum, step_sum, out_total = sum_packed((grad_proj, grad_step, grad_out), SEQ, (0, 0, 2))
    shared_sum, gain_sum, conv_sum = (
        *in_one_piece((grad_shared, grad_gain_pre), (("seq_0", "seq_1", "head_0"), "head_1"), 0, 1),
        sum_by_axis(d_conv, (("seq_0", "seq_1", "head_0"), "head_1"), 0),
    )
    channel_sum, head_sum = (one_axis_at_a_time(grad_channel, SEQ), one_axis_at_a_time(d_head, SEQ))
    matrix_rate = 1.4 * D ** (-0.5)
    proj_new = adam_step(proj_weight, proj_sum, proj_first, proj_second, matrix_rate)
    step_new = adam_step(step_weight, step_sum, step_first, step_second, matrix_rate)
    out_new = adam_step(out_weight, out_total, out_first, out_second, 1.4 * DI ** (-0.5))
    shared_new = adam_step(shared_weight, shared_sum, shared_first, shared_second, matrix_rate)
    gain_new = adam_step(pre_gain, gain_sum, gain_first, gain_second, 0.5)
    channel_new = adam_step(channel_params, channel_sum, channel_first, channel_second, 0.5)
    head_new = adam_step(head_params, head_sum, head_first, head_second, 1.0)
    conv_new = adam_step(shared_conv, conv_sum, conv_first, conv_second, 0.5)
    return (
        block_out,
        input_grad,
        proj_new[0],
        proj_new[1],
        proj_new[2],
        step_new[0],
        step_new[1],
        step_new[2],
        out_new[0],
        out_new[1],
        out_new[2],
        shared_new[0],
        shared_new[1],
        shared_new[2],
        gain_new[0],
        gain_new[1],
        gain_new[2],
        channel_new[0],
        channel_new[1],
        channel_new[2],
        head_new[0],
        head_new[1],
        head_new[2],
        conv_new[0],
        conv_new[1],
        conv_new[2],
    )


def solution(mesh):
    finer = Mesh(mesh.devices.reshape(4, 4, 4, 2), ("seq_0", "seq_1", "head_0", "head_1"))
    placed = (
        P(SEQ, None),
        P(SEQ, None),
        P(SEQ),
        P(SEQ, HEAD, None),
        P(SEQ, HEAD),
        P(HEAD, None, SEQ),
        P(SEQ_HEAD, None),
        P(SEQ_HEAD),
        P(None, HEAD, None),
        P(None, HEAD),
        P(SEQ_HEAD, None),
        P(SEQ, HEAD, None),
        P(SEQ, HEAD, None),
        P(SEQ, HEAD),
        P(SEQ, HEAD),
        P(HEAD, None, SEQ),
        P(HEAD, None, SEQ),
        P(SEQ_HEAD, None),
        P(SEQ_HEAD, None),
        P(SEQ_HEAD),
        P(SEQ_HEAD),
        P(None, HEAD, None),
        P(None, HEAD, None),
        P(None, HEAD),
        P(None, HEAD),
        P(SEQ_HEAD, None),
        P(SEQ_HEAD, None),
    )
    return jax.shard_map(
        body,
        mesh=finer,
        in_specs=placed,
        out_specs=(
            P(SEQ, None),
            P(SEQ, None),
            P(SEQ, HEAD, None),
            P(SEQ, HEAD, None),
            P(SEQ, HEAD, None),
            P(SEQ, HEAD),
            P(SEQ, HEAD),
            P(SEQ, HEAD),
            P(HEAD, None, SEQ),
            P(HEAD, None, SEQ),
            P(HEAD, None, SEQ),
            P(SEQ_HEAD, None),
            P(SEQ_HEAD, None),
            P(SEQ_HEAD, None),
            P(SEQ_HEAD),
            P(SEQ_HEAD),
            P(SEQ_HEAD),
            P(None, HEAD, None),
            P(None, HEAD, None),
            P(None, HEAD, None),
            P(None, HEAD),
            P(None, HEAD),
            P(None, HEAD),
            P(SEQ_HEAD, None),
            P(SEQ_HEAD, None),
            P(SEQ_HEAD, None),
        ),
        check_vma=False,
    )
```

profile of v0, /device:TPU:1, one launch (start us, length us, event | category | flops | bytes accessed | tf_op | source)
XLA Modules:
  0.0 584.7 jit_solution(6501978728864324967)
XLA Ops:
  9.4 39.9 %all-gather = f32[128,6,257]{2,1,0:T(8,128)S(1)} all-gather(f32[1,6,257]{2,1,0:T(8,128)S(1)} %maximum_bitcast_fusion.1), channel_id=1, replica_groups=mesh['seq_0'=4,'seq_1'=4,'head_0'=4,'head_1'=2] {'seq_0','seq_1','head_0..., dimensions={0}, use_global_device_ids=true | all-gather | bytes 795672 | tf_op jit(solution)/shard_map/all_gather | solution.py:44
  52.2 19.8 %all_gather.13 = bf16[768,579]{1,0:T(8,128)(2,1)S(1)} all-gather(bf16[48,579]{1,0:T(8,128)(2,1)S(1)} %pad_maximum_fusion.2), channel_id=1, replica_groups=mesh['seq_0'=4,'seq_1'=4,'head_0'=4,'head_1'=2] {'seq_0','seq_1'}, dimensions={0}, use_global_device_ids=true | all-gather | bytes 944928 | tf_op jit(solution)/shard_map/all_gather | solution.py:31
  77.8 39.5 %all-gather.1 = f32[128,2,5]{2,1,0:T(2,128)S(1)} all-gather(f32[1,2,5]{2,1,0:T(2,128)S(1)} %bitcast.683), channel_id=1, replica_groups=mesh['seq_0'=4,'seq_1'=4,'head_0'=4,'head_1'=2] {'seq_0','seq_1','head_0..., dimensions={0}, use_global_device_ids=true | all-gather | bytes 5160 | tf_op jit(solution)/shard_map/all_gather | solution.py:305
  130.0 78.4 %while.101 = (s32[]{:T(128)}, f32[3,64,128]{2,1,0:T(8,128)}, f32[3]{0:T(128)}, f32[2,256,3,64]{1,0,3,2:T(2,128)}, f32[2,256,3]{2,1,0:T(8,128)}, /*index=5*/pred[...) while((s32[]{:T(128)}, f32[3,64,128]{2,1,0:T(8,128)}, ...), condition=%wide.region_6.7_spmd.clone, body=%wide.region_1.6_spmd.clone.sunk | while | flops 405272608 | bytes 9833744 | solution.py:246
  145.0 5.1 dynamic_update_slice.356
  184.3 5.1 dynamic_update_slice.356
  209.1 10.0 %all_to_all.62 = f32[16,1,3]{2,1,0:T(1,128)S(1)} all-to-all(f32[16,1,3]{2,1,0:T(1,128)S(1)} %broadcast_in_dim.392), channel_id=1, replica_groups=mesh['seq_0'=4,'seq_1'=4,'head_0'=4,'head_1'=2] {'seq_0','seq_1'}, dimensions={0} | all-to-all | bytes 384 | tf_op jit(solution)/shard_map/all_to_all | solution.py:60
  221.3 4.4 all-to-all-start.1
  231.2 15.5 %all-to-all-done.1 = f32[16,3,64,128]{3,2,1,0:T(8,128)} async-done(((f32[16,3,64,128]{3,2,1,0:T(8,128)}), f32[16,3,64,128]{3,2,1,0:T(8,128)}, u32[]{:S(2)}, u32[]{:S(2)}) %all-to-all-start.1) | async-done | bytes 1572896 | tf_op jit(solution)/shard_map/all_to_all | solution.py:60
  253.0 7.1 %all-to-all-start.2 = ((f32[8,1,512]{2,1,0:T(1,128)}), f32[8,1,512]{2,1,0:T(1,128)S(1)}, u32[]{:S(2)}, u32[]{:S(2)}) async-start(f32[8,1,512]{2,1,0:T(1,128)} %broadcast_in_dim.397), calls=%async_computation.2 | async-start | bytes 32768 | tf_op jit(solution)/shard_map/all_to_all | solution.py:60
  266.5 7.7 %all_to_all.65 = f32[8,1,512]{2,1,0:T(1,128)S(1)} all-to-all(f32[8,1,512]{2,1,0:T(1,128)S(1)} %broadcast_in_dim.399), channel_id=1, replica_groups=mesh['seq_0'=4,'seq_1'=4,'head_0'=4,'head_1'=2] {'head_0','head_1'}, dimensions={0} | all-to-all | bytes 32768 | tf_op jit(solution)/shard_map/all_to_all | solution.py:60
  274.3 3.2 multiply_reduce_fusion.4
  280.4 4.5 all-to-all-start.6
  287.5 21.3 %all-to-all-done.6 = f32[16,3,64,128]{3,2,1,0:T(8,128)} async-done(((f32[16,3,64,128]{3,2,1,0:T(8,128)}), f32[16,3,64,128]{3,2,1,0:T(8,128)}, u32[]{:S(2)}, u32[]{:S(2)}) %all-to-all-start.6) | async-done | bytes 1572896 | tf_op jit(solution)/shard_map/all_to_all | solution.py:60
  313.6 63.0 %while.100 = (s32[]{:T(128)}, f32[3,64,128]{2,1,0:T(8,128)S(1)}, f32[3]{0:T(128)S(1)}, f32[2,256,3,64]{1,0,3,2:T(2,128)}, f32[2,256,128]{2,1,0:T(8,128)}, /*inde...) while((s32[]{:T(128)}, f32[3,64,128]{2,1,0:T(8,128)S(1)}, ...), condition=%wide.region_25.26_spmd, body=%wide.region_14.25_spmd.sunk | while | flops 808068864 | bytes 11378261 | solution.py:246
  325.8 3.8 reduce-window.67
  336.8 5.1 dynamic_update_slice.339
  357.3 3.8 reduce-window.67
  368.3 5.1 dynamic_update_slice.339
  412.5 3.4 reshape.783
  431.6 7.1 %all-to-all-start.3 = ((f32[8,512,96]{1,2,0:T(8,128)}), f32[8,512,96]{1,2,0:T(8,128)}, u32[]{:S(2)}, u32[]{:S(2)}) async-start(f32[8,512,96]{1,2,0:T(8,128)} %convolution_bitcast_fusion.5), calls=%async_computation.3 | async-start | bytes 3145728 | tf_op jit(solution)/shard_map/all_to_all | solution.py:97
  440.8 18.7 %all-to-all-done.3 = f32[8,512,96]{1,2,0:T(8,128)} async-done(((f32[8,512,96]{1,2,0:T(8,128)}), f32[8,512,96]{1,2,0:T(8,128)}, u32[]{:S(2)}, u32[]{:S(2)}) %all-to-all-start.3) | async-done | bytes 1572896 | tf_op jit(solution)/shard_map/all_to_all | solution.py:97
  462.6 4.3 all_to_all.63
  468.9 5.7 all-to-all-start.10
  474.8 13.7 %all-reduce.20 = (f32[6,3,64]{2,1,0:T(4,128)S(1)}, f32[3,3]{1,0:T(4,128)S(1)}) all-reduce(f32[6,3,64]{2,1,0:T(4,128)S(1)} %fusion.193, f32[3,3]{1,0:T(4,128)S(1)} %pad_add_fusion.5), channel_id=1, replica_groups=mesh['seq_0'=4,'seq_1'=4,'head_0'=4,'head_1'=2] {'seq_0'}, use_global_device_ids=true, to_apply=%region_38.39 | all-reduce | flops 1161 | bytes 9288 | tf_op jit(solution)/shard_map/psum | solution.py:157
  488.5 13.3 %all-reduce.19 = (f32[6,3,64]{2,1,0:T(4,128)S(1)}, f32[3,3]{1,0:T(4,128)S(1)}) all-reduce(f32[6,3,64]{2,1,0:T(4,128)S(1)} %get-tuple-element.2791, f32[3,3]{1,0:T(4,128)S(1)} %get-tuple-element.2792), channel_id=1, replica_groups=mesh['seq_0'=4,'seq_1'=4,'head_0'=4,'head_1'=2] {'seq_1'}, use_global_device_ids=true, to_apply=%region_39.40 | all-reduce | flops 1161 | bytes 9288 | tf_op jit(solution)/shard_map/psum | solution.py:157
  503.4 12.2 %all-to-all-start.4 = ((bf16[8,512,96]{1,2,0:T(8,128)(2,1)}), bf16[8,512,96]{1,2,0:T(8,128)(2,1)}, u32[]{:S(2)}, u32[]{:S(2)}) async-start(bf16[8,512,96]{1,2,0:T(8,128)(2,1)} %broadcast_in_dim.398), calls=%async_computation.4 | async-start | bytes 1572864 | tf_op jit(solution)/shard_map/all_to_all | solution.py:60
  523.4 5.1 all-to-all-done.4
  546.5 4.6 all_to_all.64
  552.4 8.0 %all-to-all-start.8 = ((f32[64,6,257]{2,1,0:T(8,128)}), f32[64,6,257]{2,1,0:T(8,128)}, u32[]{:S(2)}, u32[]{:S(2)}) async-start(f32[64,6,257]{2,1,0:T(8,128)} %copy.1053), calls=%async_computation.9 | async-start | bytes 1572864 | tf_op jit(solution)/shard_map/all_to_all | solution.py:142
  563.3 3.1 copy.1063
  566.4 9.1 %all-to-all-done.8 = f32[64,6,257]{2,1,0:T(8,128)} async-done(((f32[64,6,257]{2,1,0:T(8,128)}), f32[64,6,257]{2,1,0:T(8,128)}, u32[]{:S(2)}, u32[]{:S(2)}) %all-to-all-start.8) | async-done | bytes 394784 | tf_op jit(solution)/shard_map/all_to_all | solution.py:142
  (675 shorter events, 258.7 us)
Async XLA Ops:
  8.9 110.1 %copy-start.54 = (f32[512]{0:T(512)}, f32[512]{0:T(512)S(1)}, u32[]{:S(2)}) copy-start(f32[512]{0:T(512)S(1)} %add_rsqrt_fusion.1) | copy-start | bytes 6148
  72.0 47.0 %copy-start.17 = (bf16[768,579]{1,0:T(8,128)(2,1)}, bf16[768,579]{1,0:T(8,128)(2,1)S(1)}, u32[]{:S(2)}) copy-start(bf16[768,579]{1,0:T(8,128)(2,1)S(1)} %all_gather.13) | copy-start | bytes 2668036
  74.0 47.9 %copy-start.9 = (f32[512,256]{0,1:T(8,128)}, f32[512,256]{0,1:T(8,128)S(1)}, u32[]{:S(2)}) copy-start(f32[512,256]{0,1:T(8,128)S(1)} %fusion.168) | copy-start | bytes 1572868
  74.7 42.8 %slice-start = ((f32[6,3,64]{2,1,0:T(4,128)}), f32[4,3,64]{2,1,0:T(4,128)S(1)}, s32[]{:S(2)}) async-start(f32[6,3,64]{2,1,0:T(4,128)} %param.43), calls=%async_computation.16 | async-start | bytes 16384 | tf_op jit(solution)/shard_map/jvp()/slice | solution.py:210
  74.7 42.9 %copy-start.82 = (s32[512]{0:T(512)S(1)}, s32[512]{0:T(512)}, u32[]{:S(2)}) copy-start(s32[512]{0:T(512)} %param.37) | copy-start | bytes 6148
  74.7 43.5 %copy-start.87 = (f32[3,3]{1,0:T(4,128)S(1)}, f32[3,3]{1,0:T(4,128)}, u32[]{:S(2)}) copy-start(f32[3,3]{1,0:T(4,128)} %param.44) | copy-start | bytes 112
  75.6 46.4 %copy-start.7 = (f32[512,3,64]{0,2,1:T(8,128)}, f32[512,3,64]{0,2,1:T(8,128)S(1)}, u32[]{:S(2)}) copy-start(f32[512,3,64]{0,2,1:T(8,128)S(1)} %slice.389) | copy-start | bytes 1179652
  75.7 45.9 %collective-permute-start = (f32[3,448]{0,1:T(8,128)S(1)}, f32[3,448]{0,1:T(8,128)S(1)}, u32[]{:S(2)}, u32[]{:S(2)}) collective-permute-start(f32[3,448]{0,1:T(8,128)S(1)} %fusion.161), channel_id=1, source_target_pairs={{0,8},{8,16},{16,24},{24,32},{32,40},{40,48},{48,56},{56,64},{64,7... | collective-permute-start | bytes 16136 | tf_op jit(solution)/shard_map/ppermute | solution.py:55
  221.3 25.4 %all-to-all-start.1 = ((f32[16,3,64,128]{3,2,1,0:T(8,128)}), f32[16,3,64,128]{3,2,1,0:T(8,128)}, u32[]{:S(2)}, u32[]{:S(2)}) async-start(f32[16,3,64,128]{3,2,1,0:T(8,128)} %broadcast_in_dim.395), calls=%async_computation.1 | async-start | bytes 3145728 | tf_op jit(solution)/shard_map/all_to_all | solution.py:60
  227.0 21.4 %copy-start.21 = (bf16[768,192]{1,0:T(8,128)(2,1)}, bf16[768,192]{1,0:T(8,128)(2,1)S(1)}, u32[]{:S(2)}) copy-start(bf16[768,192]{1,0:T(8,128)(2,1)S(1)} %split.40) | copy-start | bytes 884740
  231.2 79.8 %copy-start.86 = (f32[3]{0:T(128)}, f32[3]{0:T(128)S(1)}, u32[]{:S(2)}) copy-start(f32[3]{0:T(128)S(1)} %slice_reduce_fusion.4) | copy-start | bytes 40
  248.7 62.3 %copy-start.24 = (f32[2,3,64,128]{3,2,1,0:T(8,128)}, f32[2,3,64,128]{3,2,1,0:T(8,128)S(1)}, u32[]{:S(2)}) copy-start(f32[2,3,64,128]{3,2,1,0:T(8,128)S(1)} %slice_add_fusion.6) | copy-start | bytes 589828
  253.0 11.7 %all-to-all-start.2 = ((f32[8,1,512]{2,1,0:T(1,128)}), f32[8,1,512]{2,1,0:T(1,128)S(1)}, u32[]{:S(2)}, u32[]{:S(2)}) async-start(f32[8,1,512]{2,1,0:T(1,128)} %broadcast_in_dim.397), calls=%async_computation.2 | async-start | bytes 32768 | tf_op jit(solution)/shard_map/all_to_all | solution.py:60
  280.4 28.3 %copy-start.103 = (pred[16]{0:T(512)(128)(4,1)S(1)}, pred[16]{0:T(512)(128)(4,1)}, u32[]{:S(2)}) copy-start(pred[16]{0:T(512)(128)(4,1)} %copy-done.102) | copy-start | bytes 52
  280.4 28.3 %all-to-all-start.6 = ((f32[16,3,64,128]{3,2,1,0:T(8,128)}), f32[16,3,64,128]{3,2,1,0:T(8,128)}, u32[]{:S(2)}, u32[]{:S(2)}) async-start(f32[16,3,64,128]{3,2,1,0:T(8,128)} %broadcast_in_dim.402), calls=%async_computation.6 | async-start | bytes 3145728 | tf_op jit(solution)/shard_map/all_to_all | solution.py:60
  285.0 177.1 %reduce-scatter.7.cloned.1.call-start = ((), (), s32[]{:S(2)}) async-start(), calls=%async_computation.15 | async-start | bytes 1769472 | tf_op jit(solution)/shard_map/reduce_scatter | solution.py:120
  389.7 7.3 %collective-permute-start.1 = (f32[3,448]{0,1:T(8,128)S(1)}, f32[3,448]{0,1:T(8,128)S(1)}, u32[]{:S(2)}, u32[]{:S(2)}) collective-permute-start(f32[3,448]{0,1:T(8,128)S(1)} %pad_add_fusion.1), channel_id=1, source_target_pairs={{8,0},{16,8},{24,16},{32,24},{40,32},{48,40},{56,48},{64,56},{72,6... | collective-permute-start | bytes 16136 | tf_op jit(solution)/shard_map/ppermute | solution.py:55
  404.3 126.6 %reduce-scatter.5.cloned.1.call-start = ((), (), s32[]{:S(2)}) async-start(), calls=%async_computation.14 | async-start | bytes 1949696 | tf_op jit(solution)/shard_map/reduce_scatter | solution.py:131
  431.6 27.9 %all-to-all-start.3 = ((f32[8,512,96]{1,2,0:T(8,128)}), f32[8,512,96]{1,2,0:T(8,128)}, u32[]{:S(2)}, u32[]{:S(2)}) async-start(f32[8,512,96]{1,2,0:T(8,128)} %convolution_bitcast_fusion.5), calls=%async_computation.3 | async-start | bytes 3145728 | tf_op jit(solution)/shard_map/all_to_all | solution.py:97
  438.7 100.7 %all-gather.4.cloned.1.call-start = ((), (), s32[]{:S(2)}) async-start(), calls=%async_computation.13 | async-start | bytes 1769472 | tf_op jit(solution)/shard_map/all_gather | solution.py:121
  440.7 34.0 %copy-start.88 = (f32[3,3]{1,0:T(4,128)S(1)}, f32[3,3]{1,0:T(4,128)}, u32[]{:S(2)}) copy-start(f32[3,3]{1,0:T(4,128)} %param.44) | copy-start | bytes 112
  440.7 34.0 %copy-start.106 = (f32[3]{0:T(128)S(1)}, f32[3]{0:T(128)}, u32[]{:S(2)}) copy-start(f32[3]{0:T(128)} %get-tuple-element.2877) | copy-start | bytes 40
  440.7 34.0 %copy-start.93 = (f32[3]{0:T(128)S(1)}, f32[3]{0:T(128)}, u32[]{:S(2)}) copy-start(f32[3]{0:T(128)} %get-tuple-element.2637) | copy-start | bytes 40
  440.8 34.1 %copy-start.79 = (f32[3,64]{1,0:T(4,128)S(1)}, f32[3,64]{1,0:T(4,128)}, u32[]{:S(2)}) copy-start(f32[3,64]{1,0:T(4,128)} %get-tuple-element.2633) | copy-start | bytes 2308
  440.8 61.0 %copy-start.57 = (f32[6,3,64]{2,1,0:T(4,128)S(1)}, f32[6,3,64]{2,1,0:T(4,128)}, u32[]{:S(2)}) copy-start(f32[6,3,64]{2,1,0:T(4,128)} %param.43) | copy-start | bytes 13828
  440.8 61.0 %copy-start.77 = (f32[6,3,64]{2,1,0:T(4,128)S(1)}, f32[6,3,64]{2,1,0:T(4,128)}, u32[]{:S(2)}) copy-start(f32[6,3,64]{2,1,0:T(4,128)} %param.57) | copy-start | bytes 13828
  440.8 61.0 %copy-start.78 = (f32[6,3,64]{2,1,0:T(4,128)S(1)}, f32[6,3,64]{2,1,0:T(4,128)}, u32[]{:S(2)}) copy-start(f32[6,3,64]{2,1,0:T(4,128)} %param.56) | copy-start | bytes 13828
  462.3 53.4 %copy-start.96 = (f32[3,3]{1,0:T(4,128)S(1)}, f32[3,3]{1,0:T(4,128)}, u32[]{:S(2)}) copy-start(f32[3,3]{1,0:T(4,128)} %param.59) | copy-start | bytes 112
  462.3 53.4 %copy-start.97 = (f32[3,3]{1,0:T(4,128)S(1)}, f32[3,3]{1,0:T(4,128)}, u32[]{:S(2)}) copy-start(f32[3,3]{1,0:T(4,128)} %param.58) | copy-start | bytes 112
  468.9 33.6 %all-to-all-start.10 = ((f32[64,2,5]{2,1,0:T(2,128)}), f32[64,2,5]{2,1,0:T(2,128)S(1)}, u32[]{:S(2)}, u32[]{:S(2)}) async-start(f32[64,2,5]{2,1,0:T(2,128)} %copy.1057), calls=%async_computation.11 | async-start | bytes 131072 | tf_op jit(solution)/shard_map/all_to_all | solution.py:142
  503.4 25.1 %all-to-all-start.4 = ((bf16[8,512,96]{1,2,0:T(8,128)(2,1)}), bf16[8,512,96]{1,2,0:T(8,128)(2,1)}, u32[]{:S(2)}, u32[]{:S(2)}) async-start(bf16[8,512,96]{1,2,0:T(8,128)(2,1)} %broadcast_in_dim.398), calls=%async_computation.4 | async-start | bytes 1572864 | tf_op jit(solution)/shard_map/all_to_all | solution.py:60
  552.4 23.1 %all-to-all-start.8 = ((f32[64,6,257]{2,1,0:T(8,128)}), f32[64,6,257]{2,1,0:T(8,128)}, u32[]{:S(2)}, u32[]{:S(2)}) async-start(f32[64,6,257]{2,1,0:T(8,128)} %copy.1053), calls=%async_computation.9 | async-start | bytes 1572864 | tf_op jit(solution)/shard_map/all_to_all | solution.py:142
  (102 other events, 563.6 us)
Sparse Core Ops, SparseCore 0:
  404.5 28.7 reduce-scatter.6
  436.6 74.2 reduce-scatter.4
  512.5 26.8 all-gather.3
where the time goes:
time: 595 us; the launch traced here: 585 us
  blocking collectives  153 us (26%)
  local copies, waits for them, and re-layouts  149 us (25%)
  waiting for transfers between devices  77.7 us (13%)
  other arithmetic  75.4 us (13%)
  matrix products  59.8 us (10%)
  starting transfers between devices  52.6 us (9%)
  between operations  15.6 us (3%)
    dynamic_update_slice x46, local copies, waits for them, and re-layouts, local_mixer(): ends, outs_all = lax.scan(group_pass, start_carry, pieces)  44.9 us
    all_to_all x4, waiting for transfers between devices, copy_for_each(): return lax.all_to_all(copies, axis, split_axis=0, concat_axis=0, tiled=True)  44.9 us
    all_gather x1, blocking collectives, side_by_side(): lax.all_gather(both, axis, axis=dim, tiled=True)  39.9 us
    all_gather x1, blocking collectives, body(): lax.all_gather(shared_conv, SEQ_HEAD, axis=0, tiled=True)  39.5 us
    all_to_all x4, starting transfers between devices, copy_for_each(): return lax.all_to_all(copies, axis, split_axis=0, concat_axis=0, tiled=True)  28.2 us
    psum x2, blocking collectives, one_axis_at_a_time(): return functools.reduce(lax.psum, axes, array)  27 us
    unnamed x225, local copies, waits for them, and re-layouts  25.2 us
    all_gather x1, blocking collectives, rows_first(): filled = lax.all_gather(both, axis, axis=0, tiled=True)  19.8 us
  transfers between devices with their start and end apart: 12, of which 8 were waited for; matrix products, arithmetic and copies ran while one was open for 13% of the time, Pallas kernels for 0%

commit v1 on v0

v1 whole, which is shorter than its diff:
```python
import functools

import jax
import jax.numpy as jnp
from jax import lax
from jax.experimental import pallas as pl
from jax.experimental.pallas import tpu as pltpu
from jax.sharding import Mesh
from jax.sharding import PartitionSpec as P

D = 768
DI = 1536
STEP = 10
SEQ = ("seq_0", "seq_1")
HEAD = ("head_0", "head_1")
SEQ_HEAD = SEQ + HEAD
N_SEQ = 16
N_HEAD = 8

T = 512
HALO = 16
NV = 640
NW = 896
MISC = 64
SROWS = 208

f32 = jnp.float32
bf16 = jnp.bfloat16
norm_eps = 1e-05
beta_one = 0.9
beta_two = 0.999
adam_eps = 1e-08
decay_rate = 0.01
LOW = -1e30

PARAMS = pltpu.CompilerParams(vmem_limit_bytes=56 * 1024 * 1024)
VM = pl.BlockSpec(memory_space=pltpu.VMEM)
SM = pl.BlockSpec(memory_space=pltpu.SMEM)


def call(kernel, outs, *args, smem=(), scratch=(), name=None):
    return pl.pallas_call(
        kernel,
        out_shape=[jax.ShapeDtypeStruct(s, d) for s, d in outs],
        in_specs=[SM if i in smem else VM for i in range(len(args))],
        out_specs=[VM] * len(outs),
        scratch_shapes=list(scratch),
        compiler_params=PARAMS,
        name=name,
    )(*args)


def dot(a, b, ca=1, cb=0):
    return lax.dot_general(a, b, (((ca,), (cb,)), ((), ())), preferred_element_type=f32)


def lanes(rows):
    return lax.broadcasted_iota(jnp.int32, (rows, 128), 1)


def half(v):
    return pltpu.roll(v, 64, 1)


def rolled(v, by):
    return pltpu.roll(v, by % 128, 1)


def sig(v):
    return 1.0 / (1.0 + jnp.exp(-v))


def silu(v):
    return v * sig(v)


def dsilu(v):
    s = sig(v)
    return s * (1.0 + v * (1.0 - s))


def gate_pair(t0, t1, t2):
    lo = lanes(t0.shape[0]) < 64
    return jnp.where(lo, t0, half(t1)), jnp.where(lo, t2, 0.0)


def x_pair(t0, t1, t2):
    lo = lanes(t0.shape[0]) < 64
    return jnp.where(lo, half(t0), t1), jnp.where(lo, half(t2), 0.0)


def head_tiles(gate, x):
    lo = lanes(gate[0].shape[0]) < 64
    return (
        jnp.where(lo, gate[0], half(x[0])),
        jnp.where(lo, half(gate[0]), x[0]),
        jnp.where(lo, gate[1], half(x[1])),
    )


def spread(a, at):
    lo = lanes(a.shape[0]) < 64
    return (
        jnp.where(lo, a[:, at : at + 1], a[:, at + 1 : at + 2]),
        jnp.where(lo, a[:, at + 2 : at + 3], 0.0),
    )


def head_sums(pair):
    a, b = pair
    lane = lanes(a.shape[0])
    s0 = jnp.sum(jnp.where(lane < 64, a, 0.0), axis=1, keepdims=True)
    s1 = jnp.sum(jnp.where(lane < 64, 0.0, a), axis=1, keepdims=True)
    s2 = jnp.sum(b, axis=1, keepdims=True)
    return jnp.where(lane == 0, s0, jnp.where(lane == 1, s1, jnp.where(lane == 2, s2, 0.0)))


def pair_of(ref):
    return ref[:, 0:128], ref[:, 128:256]


def head_row(hp_ref, k, rows=1):
    lane = lanes(rows)
    return jnp.where(
        lane == 0,
        hp_ref[k, 0],
        jnp.where(lane == 1, hp_ref[k, 1], jnp.where(lane == 2, hp_ref[k, 2], 0.0)),
    )


def skip_pair(hp_ref):
    lane = lanes(1)
    return (
        jnp.where(lane < 64, hp_ref[2, 0], hp_ref[2, 1]),
        jnp.where(lane < 64, hp_ref[2, 2], 0.0),
    )


def three_parts(v):
    hi = v.astype(bf16).astype(f32)
    rest = v - hi
    mid = rest.astype(bf16).astype(f32)
    return hi + rolled(mid, 3) + rolled(rest - mid, 6)


def joined(v):
    total = v + rolled(v, -3) + rolled(v, -6)
    return jnp.where(lanes(v.shape[0]) < 3, total, 0.0)


def aux_parts(aux):
    return aux


def act_tiles(c_ref):
    return [silu(c_ref[:, 128 * k : 128 * (k + 1)]) for k in range(5)]


def valid_masks(starts_col):
    row = lax.broadcasted_iota(jnp.int32, starts_col.shape, 0)
    one = jnp.where(row < 1, 0.0, pltpu.roll(starts_col, 1, 0))
    two = jnp.where(row < 2, 0.0, pltpu.roll(starts_col, 2, 0))
    first = 1.0 - starts_col
    return first, first - one, first - one - two


def column_of(row_ref):
    return jnp.broadcast_to(row_ref[0:1, :], (128, T)).T


def selector():
    r = lax.broadcasted_iota(jnp.int32, (D, 256), 0)
    k = lax.broadcasted_iota(jnp.int32, (D, 256), 1)
    return jnp.where(r == k + 32 * jnp.right_shift(k, 4), 1.0, 0.0).astype(bf16)


def first_kernel(
    hid_ref, halo_ref, st_ref, w_ref, tap_ref, hp_ref,
    normed_ref, v_ref, c_ref, aux_ref, send_ref, row_ref,
):
    misc_t = w_ref[:, 512:640].astype(f32).T
    gain = misc_t[MISC + 3 : MISC + 4] + misc_t[MISC + 4 : MISC + 5]
    conv_t = dot(misc_t.astype(bf16), selector())
    conv_taps = conv_t[MISC + 5 : MISC + 10] + conv_t[MISC + 10 : MISC + 15]
    row_ref[0:1, :] = gain
    row_ref[1:8, :] = jnp.zeros((7, D), f32)
    for src, at, rows in ((halo_ref, 0, HALO), (hid_ref, HALO, T)):
        h = src[...].astype(f32)
        inv = lax.rsqrt(jnp.mean(h * h, axis=1, keepdims=True) + norm_eps)
        normed_ref[at : at + rows, :] = (h * inv * gain).astype(bf16)
    normed = normed_ref[...]
    v_ref[:, 0:384] = dot(normed, w_ref[:, 0:384])
    v_ref[:, 384:640] = dot(normed, w_ref[:, 640:896])
    raw = half(dot(normed[HALO:], w_ref[:, 512:640]))

    lane = lanes(T)
    pre = raw + head_row(hp_ref, 0)
    delta = jnp.where(
        lane < 3, jnp.maximum(pre, 0.0) + jnp.log1p(jnp.exp(-jnp.abs(pre))), 0.0
    )
    slope = jnp.where(lane < 3, sig(pre), 0.0)
    log_decay = -jnp.exp(head_row(hp_ref, 1)) * delta
    starts = column_of(st_ref)
    parts = three_parts(log_decay) + jnp.where(lane == 9, starts, 0.0)
    ri = lax.broadcasted_iota(jnp.int32, (T, T), 0)
    ci = lax.broadcasted_iota(jnp.int32, (T, T), 1)
    summed = dot(jnp.where(ri >= ci, 1.0, 0.0).astype(bf16), parts.astype(bf16))
    cum = joined(summed)
    segment = summed[:, 9:10]
    last = cum[T - 1 : T, :]
    last_segment = segment[T - 1 : T, :]
    keeper = jnp.where((lane < 3) & (segment == 0.0), jnp.exp(cum), 0.0)
    ending = jnp.where((lane < 3) & (segment == last_segment), jnp.exp(last - cum), 0.0)
    aux_ref[...] = (
        cum
        + rolled(delta, 3)
        + rolled(slope, 6)
        + jnp.where(lane == 9, segment, 0.0)
        + rolled(keeper, 10)
        + rolled(ending, 13)
    )

    valid = valid_masks(starts)
    for k in range(5):
        at = slice(128 * k, 128 * (k + 1))
        if k < 3:
            taps = tap_ref[0:5, at]
        else:
            taps = conv_taps[:, 128 * (k - 3) : 128 * (k - 2)]
        total = taps[4:5] + taps[3:4] * v_ref[HALO:, at]
        for lag in (1, 2, 3):
            total = total + taps[3 - lag : 4 - lag] * (
                v_ref[pl.ds(HALO - lag, T), at] * valid[lag - 1]
            )
        c_ref[:, at] = total

    act = act_tiles(c_ref)
    x = x_pair(*act[:3])
    weight = spread(ending * delta, 0)
    ended = jnp.concatenate([x[0] * weight[0], x[1] * weight[1]], axis=1).astype(bf16)
    state = dot(ended, act[3].astype(bf16), 0, 0)
    through = jnp.where(last_segment == 0.0, jnp.exp(last), 0.0)
    high = through.astype(bf16).astype(f32)
    lower = through - high
    sub = lax.broadcasted_iota(jnp.int32, (16, 128), 0)
    tail = jnp.zeros((16, 128), f32)
    for h in range(3):
        tail = jnp.where(sub == h, high[:, h : h + 1], tail)
        tail = jnp.where(sub == 3 + h, lower[:, h : h + 1], tail)
    body = state[0:192].astype(bf16)
    tail = tail.astype(bf16)
    for q in range(N_SEQ):
        send_ref[q, 0:192, :] = body
        send_ref[q, 192:SROWS, :] = tail


def own_kernel(c_ref, aux_ref, cot_ref, w_ref, hp_ref, y_ref, dn_ref, m_ref, mg_ref):
    act = act_tiles(c_ref)
    x = x_pair(*act[:3])
    aux = aux_ref[...]
    aux_t = aux.T
    scores = dot(act[4].astype(bf16), act[3].astype(bf16), 1, 1)
    ri = lax.broadcasted_iota(jnp.int32, (T, T), 0)
    ci = lax.broadcasted_iota(jnp.int32, (T, T), 1)
    allowed = (ri >= ci) & (aux[:, 9:10] == aux_t[9:10, :])
    mask = jnp.where(allowed, 0.0, LOW)
    delta = spread(aux, 3)
    fed = x[0] * delta[0], x[1] * delta[1]
    lo = lanes(T) < 64
    fed_h = (
        jnp.where(lo, fed[0], 0.0).astype(bf16),
        jnp.where(lo, 0.0, fed[0]).astype(bf16),
        fed[1].astype(bf16),
    )
    skip = skip_pair(hp_ref)
    y = [x[0] * skip[0], x[1] * skip[1]]
    for h in range(3):
        decay = jnp.exp(aux[:, h : h + 1] - aux_t[h : h + 1, :] + mask)
        m_ref[h] = decay.astype(bf16)
        mixing = (decay * scores).astype(bf16)
        mg_ref[h] = mixing
        y[h // 2] = y[h // 2] + dot(mixing, fed_h[h])
    y_ref[:, 0:128] = y[0]
    y_ref[:, 128:256] = y[1]
    back = dot(cot_ref[...], w_ref[:, 384:640])
    dn_ref[:, 0:128] = back[:, 0:128]
    dn_ref[:, 128:256] = jnp.where(lo, back[:, 128:256], 0.0)


def decay_rows(tail, shape=(192, 128)):
    both = tail[0:3] + tail[3:6]
    return jnp.concatenate(
        [jnp.broadcast_to(both[h : h + 1], (64, 128)) for h in range(3)], axis=0
    )


def enter_kernel(
    at_ref, got_ref, y0_ref, dn_ref, c_ref, aux_ref, tap_ref, y_ref, state_ref, stat_ref
):
    here = at_ref[0]
    state = jnp.zeros((192, 128), f32)
    for q in range(N_SEQ - 1):
        through = decay_rows(got_ref[q, 192:SROWS, :].astype(f32))
        merged = through * state + got_ref[q, 0:192, :].astype(f32)
        state = jnp.where(q < here, merged, state)
    state_ref[0:192] = state
    state_ref[192:256] = jnp.zeros((64, 128), f32)
    c_mat = silu(c_ref[:, 512:640]).astype(bf16)
    carried = dot(c_mat, state_ref[...].astype(bf16), 1, 1)
    aux = aux_ref[...]
    keeper = spread(aux, 10)
    gate = gate_pair(*[silu(c_ref[:, 128 * k : 128 * (k + 1)]) for k in range(3)])
    squares = jnp.zeros((T, 1), f32)
    inner = jnp.zeros((T, 1), f32)
    for k in range(2):
        at = slice(128 * k, 128 * (k + 1))
        y = y0_ref[:, at] + keeper[k] * carried[:, at]
        y_ref[:, at] = y
        gated = y * gate[k]
        squares = squares + jnp.sum(gated * gated, axis=1, keepdims=True)
        inner = inner + jnp.sum(
            gated * dn_ref[:, at] * tap_ref[0:1, 384 + 128 * k : 512 + 128 * k],
            axis=1, keepdims=True,
        )
    lane = lanes(T)
    both = jnp.where(lane == 0, squares, jnp.where(lane == 1, inner, 0.0)).T
    for q in range(N_HEAD):
        stat_ref[q] = both[0:8]


def gated_kernel(
    got_ref, y_ref, dn_ref, c_ref, aux_ref, tap_ref,
    dy_ref, dgate_ref, nout_ref, send_ref, rows_ref,
):
    total = got_ref[0]
    for q in range(1, N_HEAD):
        total = total + got_ref[q]
    total = jnp.concatenate([total, jnp.zeros((120, T), f32)], axis=0).T
    rms = lax.rsqrt(total[:, 0:1] / DI + norm_eps)
    coef = rms * rms * rms * total[:, 1:2] / DI
    aux = aux_ref[...]
    keeper = spread(aux, 10)
    raw = gate_pair(*[c_ref[:, 128 * k : 128 * (k + 1)] for k in range(3)])
    x = x_pair(*[silu(c_ref[:, 128 * k : 128 * (k + 1)]) for k in range(3)])
    kept = []
    rows_ref[...] = jnp.zeros_like(rows_ref)
    for k in range(2):
        at = slice(128 * k, 128 * (k + 1))
        gain = tap_ref[0:1, 384 + 128 * k : 512 + 128 * k]
        s = sig(raw[k])
        gate = raw[k] * s
        y = y_ref[:, at]
        gated = y * gate
        dn = dn_ref[:, at]
        scaled = gated * rms
        nout_ref[:, at] = (scaled * gain).astype(bf16)
        d_gated = rms * gain * dn - gated * coef
        dy = d_gated * gate
        dy_ref[:, at] = dy
        dgate_ref[:, at] = d_gated * y * s * (1.0 + raw[k] * (1.0 - s))
        kept.append((dy * keeper[k]).astype(bf16))
        rows_ref[0:1, at] = jnp.sum(dn * scaled, axis=0, keepdims=True)
        rows_ref[1:2, at] = jnp.sum(dy * x[k], axis=0, keepdims=True)
    c_mat = silu(c_ref[:, 512:640]).astype(bf16)
    adj = dot(jnp.concatenate(kept, axis=1), c_mat, 0, 0)[0:192].astype(bf16)
    for q in range(N_SEQ):
        send_ref[q] = adj


def out_kernel(nout_ref, w_ref, out_ref):
    lo = lanes(T) < 64
    a = nout_ref[...]
    del lo
    res = dot(a, w_ref[:, 384:640], 1, 1)
    out_ref[...] = res.astype(bf16)


def own_back_kernel(
    dy_ref, y_ref, y0_ref, c_ref, aux_ref, m_ref, mg_ref, state_ref,
    dx_ref, db_ref, dc_ref, dcum_ref,
):
    aux = aux_ref[...]
    aux_t = aux.T
    act = act_tiles(c_ref)
    x = x_pair(*act[:3])
    b_low, c_low = act[3].astype(bf16), act[4].astype(bf16)
    dy = pair_of(dy_ref)
    lo = lanes(T) < 64
    dy_h = (
        jnp.where(lo, dy[0], 0.0).astype(bf16),
        jnp.where(lo, 0.0, dy[0]).astype(bf16),
        dy[1].astype(bf16),
    )
    x_low = x[0].astype(bf16), x[1].astype(bf16)
    lane = lanes(T)
    dx = [jnp.zeros((T, 128), f32), jnp.zeros((T, 128), f32)]
    spread_sum = jnp.zeros((T, T), f32)
    rows = jnp.zeros((T, 128), f32)
    cols = jnp.zeros((128, T), f32)
    sub = lax.broadcasted_iota(jnp.int32, (128, T), 0)
    for h in range(3):
        pairs = dot(dy_h[h], x_low[h // 2], 1, 1) * aux_t[3 + h : 4 + h, :]
        mixing = mg_ref[h]
        spread_sum = spread_sum + pairs * m_ref[h].astype(f32)
        weights = pairs * mixing.astype(f32)
        rows = jnp.where(lane == h, jnp.sum(weights, axis=1, keepdims=True), rows)
        cols = jnp.where(sub == h, jnp.sum(weights, axis=0, keepdims=True), cols)
        dx[h // 2] = dx[h // 2] + dot(mixing, dy_h[h], 0, 0)
    low = spread_sum.astype(bf16)
    keeper = spread(aux, 10)
    kept = jnp.concatenate([dy[0] * keeper[0], dy[1] * keeper[1]], axis=1).astype(bf16)
    dc_ref[...] = dot(low, b_low) + dot(kept, state_ref[...].astype(bf16))
    db_ref[...] = dot(low, c_low, 0, 0)
    dx_ref[:, 0:128] = dx[0]
    dx_ref[:, 128:256] = dx[1]
    carried = [
        dy[k] * (y_ref[:, 128 * k : 128 * (k + 1)] - y0_ref[:, 128 * k : 128 * (k + 1)])
        for k in range(2)
    ]
    dcum_ref[...] = rows - cols.T + head_sums(carried)


def back_kernel(
    at_ref, got_ref, fwd_ref, state_ref, dx_ref, db_ref, dc_ref, dcum_ref, c_ref, aux_ref,
    v_ref, tap_ref, hp_ref, st_ref, dy_ref, dgate_ref, w_ref, rows_ref, hid_ref, halo_ref,
    dv_ref, dstep_ref, dnorm_ref, edge_ref, chan_ref, conv_ref, gain_ref,
    pad_ref, big_ref,
):
    here = at_ref[0]
    adj = jnp.zeros((192, 128), f32)
    for q in range(N_SEQ - 1, 0, -1):
        through = decay_rows(fwd_ref[q, 192:SROWS, :].astype(f32))
        merged = through * adj + got_ref[q].astype(f32)
        adj = jnp.where(q > here, merged, adj)
    aux = aux_ref[...]
    lane = lanes(T)
    conv = [c_ref[:, 128 * k : 128 * (k + 1)] for k in range(5)]
    sigs = [sig(v) for v in conv]
    x = x_pair(*[conv[k] * sigs[k] for k in range(3)])
    b_low = (conv[3] * sigs[3]).astype(bf16)
    delta, ending = spread(aux, 3), spread(aux, 13)
    adj_low = jnp.concatenate([adj, jnp.zeros((64, 128), f32)], axis=0).astype(bf16)
    through_b = dot(b_low, adj_low, 1, 1)
    skip = skip_pair(hp_ref)
    dy = pair_of(dy_ref)
    ended, extra, full, d_x = [], [], [], []
    for k in range(2):
        at = slice(128 * k, 128 * (k + 1))
        late = ending[k] * through_b[:, at]
        total = dx_ref[:, at] + late
        d_x.append(delta[k] * total + skip[k] * dy[k])
        full.append(x[k] * total)
        extra.append(x[k] * late)
        ended.append(x[k] * delta[k] * ending[k])
    d_b = db_ref[...] + dot(jnp.concatenate(ended, axis=1).astype(bf16), adj_low)
    d_delta = head_sums(full)
    tail = head_sums(extra) * rolled(aux, -3)
    tail = jnp.where(lane < 3, tail, 0.0)
    d_cum = dcum_ref[...] - tail
    ri = lax.broadcasted_iota(jnp.int32, (T, T), 0)
    ci = lax.broadcasted_iota(jnp.int32, (T, T), 1)
    upper = jnp.where(ci >= ri, 1.0, 0.0).astype(bf16)
    d_log = joined(dot(upper, three_parts(d_cum).astype(bf16)))
    own = decay_rows(fwd_ref[here, 192:SROWS, :].astype(f32))
    met = own * adj * state_ref[0:192]
    lane1 = lanes(1)
    meets = jnp.zeros((1, 128), f32)
    for h in range(3):
        meets = jnp.where(lane1 == h, jnp.sum(met[64 * h : 64 * h + 64]), meets)
    d_log = d_log + jnp.sum(tail, axis=0, keepdims=True) + meets
    d_log = jnp.where(lane < 3, d_log, 0.0)
    rate = jnp.exp(head_row(hp_ref, 1))
    d_raw = (d_delta - rate * d_log) * rolled(aux, -6)
    d_raw = jnp.where(lane < 3, d_raw, 0.0)
    delta_cols = jnp.where(lane < 3, rolled(aux, -3), 0.0)
    step_low = half(d_raw).astype(bf16)
    dstep_ref[...] = step_low

    d_gate = pair_of(dgate_ref)
    x_tiles = head_tiles((jnp.zeros_like(d_x[0]),) * 2, d_x)
    gate_tiles = head_tiles(d_gate, (jnp.zeros_like(d_x[0]),) * 2)
    lo = lane < 64
    conv_t = dot(w_ref[:, 512:640].astype(f32).T.astype(bf16), selector())
    conv_taps = conv_t[MISC + 5 : MISC + 10] + conv_t[MISC + 10 : MISC + 15]
    starts = column_of(st_ref)
    valid = valid_masks(starts)
    pad_ref[0:HALO] = jnp.zeros((HALO, 128), f32)
    pad_ref[HALO + T :] = jnp.zeros((HALO, 128), f32)
    tap_rows = []
    for k in range(5):
        at = slice(128 * k, 128 * (k + 1))
        slope = sigs[k] * (1.0 + conv[k] * (1.0 - sigs[k]))
        if k < 3:
            d_conv = jnp.where(lo, gate_tiles[k], x_tiles[k] * slope)
            taps = tap_ref[0:5, at]
        else:
            d_conv = (d_b if k == 3 else dc_ref[...]) * slope
            taps = conv_taps[:, 128 * (k - 3) : 128 * (k - 2)]
        sums = [None, None, None, None, jnp.sum(d_conv, axis=0, keepdims=True)]
        sums[3] = jnp.sum(d_conv * v_ref[HALO:, at], axis=0, keepdims=True)
        pad_ref[HALO : HALO + T] = taps[3:4] * d_conv
        acc = pad_ref[0 : HALO + T]
        for lag in (1, 2, 3):
            masked = d_conv * valid[lag - 1]
            sums[3 - lag] = jnp.sum(
                masked * v_ref[pl.ds(HALO - lag, T), at], axis=0, keepdims=True
            )
            pad_ref[HALO : HALO + T] = taps[3 - lag : 4 - lag] * masked
            acc = acc + pad_ref[pl.ds(lag, HALO + T)]
        dv_ref[:, at] = acc.astype(bf16)
        tap_rows.append(sums)

    chan_ref_rows = []
    for j in range(5):
        pair = x_pair(*[tap_rows[k][j] for k in range(3)])
        chan_ref_rows.append(jnp.concatenate(pair, axis=1))
    chan_ref_rows.append(rows_ref[0:1, :])
    h0 = jnp.sum(d_raw, axis=0, keepdims=True)
    h1 = jnp.sum(d_log * (-rate) * delta_cols, axis=0, keepdims=True)
    h2 = head_sums((rows_ref[1:2, 0:128], rows_ref[1:2, 128:256]))
    zero = jnp.zeros((1, 128), f32)
    for r in (h0, h1, h2):
        chan_ref_rows.append(jnp.concatenate([r, zero], axis=1))
    for j, r in enumerate(chan_ref_rows):
        big_ref[j : j + 1, :] = r
    big_ref[9:16, :] = jnp.zeros((7, 256), f32)
    for q in range(N_SEQ):
        chan_ref[q] = big_ref[...]
    for j in range(5):
        conv_ref[j : j + 1, :] = jnp.concatenate([tap_rows[3][j], tap_rows[4][j]], axis=1)
    conv_ref[5:8, :] = jnp.zeros((3, 256), f32)

    d_norm = dot(dv_ref[:, 0:384], w_ref[:, 0:384], 1, 1)
    d_norm = d_norm + dot(dv_ref[:, 384:640], w_ref[:, 640:896], 1, 1)
    main = d_norm[HALO:] + dot(step_low, w_ref[:, 512:640], 1, 1)
    dnorm_ref[...] = main.astype(bf16)
    edge_ref[...] = d_norm[0:HALO].astype(bf16)
    total = jnp.zeros((1, D), f32)
    for src, val in ((halo_ref, d_norm[0:HALO]), (hid_ref, main)):
        h = src[...].astype(f32)
        inv = lax.rsqrt(jnp.mean(h * h, axis=1, keepdims=True) + norm_eps)
        total = total + jnp.sum(val * (h * inv), axis=0, keepdims=True)
    gain_ref[0:1] = total
    gain_ref[1:8] = jnp.zeros((7, D), f32)


def grad_kernel(normed_ref, dv_ref, dstep_ref, nout_ref, cot_ref, conv_ref, gain_ref, out_ref):
    normed = normed_ref[...]
    out_ref[:, 0:384] = dot(normed, dv_ref[:, 0:384], 0, 0).astype(bf16)
    out_ref[:, 640:896] = dot(normed, dv_ref[:, 384:640], 0, 0).astype(bf16)
    outs = dot(cot_ref[...], nout_ref[...], 0, 0)
    out_ref[:, 384:512] = outs[:, 0:128].astype(bf16)
    tile = outs[:, 128:256] + dot(normed_ref[HALO:, :], dstep_ref[...], 0, 0)
    grads = jnp.concatenate([jnp.zeros((MISC + 5, 256), f32), conv_ref[0:5, :]], axis=0)
    grads = jnp.concatenate([grads, jnp.zeros((128 - MISC - 10, 256), f32)], axis=0)
    high = grads.astype(bf16)
    lower = (grads - high.astype(f32)).astype(bf16)
    sel = selector()
    tile = tile + dot(sel, high, 1, 1) + pltpu.roll(dot(sel, lower, 1, 1), 5, 1)
    gain = gain_ref[0:1]
    gain_high = gain.astype(bf16).astype(f32)
    sub = lax.broadcasted_iota(jnp.int32, (128, D), 0)
    column = jnp.where(
        sub == MISC + 3, gain_high, jnp.where(sub == MISC + 4, gain - gain_high, 0.0)
    ).T
    out_ref[:, 512:640] = (tile + column).astype(bf16)


def sum_kernel(got_ref, out_ref):
    total = got_ref[0].astype(f32)
    for q in range(1, N_HEAD):
        total = total + got_ref[q].astype(f32)
    total = total.astype(bf16)
    for q in range(N_HEAD):
        out_ref[q] = total


def block_sum_kernel(at_ref, got_ref, hid_ref, out_ref):
    start = pl.multiple_of(at_ref[1] * (T // N_HEAD), T // N_HEAD)
    total = hid_ref[pl.ds(start, T // N_HEAD), :].astype(f32)
    for q in range(N_HEAD):
        total = total + got_ref[q].astype(f32)
    total = total.astype(bf16)
    for q in range(N_HEAD):
        out_ref[q] = total


def input_kernel(sum_ref, hid_ref, cot_ref, row_ref, out_ref):
    h = hid_ref[...].astype(f32)
    inv = lax.rsqrt(jnp.mean(h * h, axis=1, keepdims=True) + norm_eps)
    d_scaled = sum_ref[...].astype(f32) * row_ref[0:1, :]
    inner = jnp.sum(d_scaled * h, axis=1, keepdims=True)
    out_ref[...] = (
        cot_ref[...].astype(f32) + inv * d_scaled - h * (inv * inv * inv * inner / D)
    )


def adam(weight, grad, first, second, rate):
    first_new = beta_one * first + (1.0 - beta_one) * grad
    second_new = beta_two * second + (1.0 - beta_two) * grad * grad
    first_hat = first_new / (1.0 - beta_one**STEP)
    second_hat = second_new / (1.0 - beta_two**STEP)
    weight_new = weight - rate * (
        first_hat / (jnp.sqrt(second_hat) + adam_eps) + decay_rate * weight
    )
    return first_new, second_new, weight_new


RATE_D = 1.4 * D ** (-0.5)
RATE_I = 1.4 * DI ** (-0.5)


def put(refs, at, values):
    for ref, value in zip(refs, values):
        ref[at] = value


def update_kernel(*refs):
    (grad_ref, chan_ref), refs = refs[:2], refs[2:]
    proj, step, out, chan, head = (refs[3 * k : 3 * k + 3] for k in range(5))
    outs = refs[15:]
    proj_o, step_o, out_o, chan_o, head_o = (outs[3 * k : 3 * k + 3] for k in range(5))
    rest_ref = outs[15]
    total = grad_ref[0].astype(f32)
    for q in range(1, N_SEQ):
        total = total + grad_ref[q].astype(f32)
    misc = total[:, 512:640]
    rest_ref[...] = jnp.zeros_like(rest_ref)
    for h in range(N_HEAD):
        rest_ref[h, 0:6, 0:256] = total[6 * h : 6 * h + 6, 640:896]
        rest_ref[h, 0:6, 256:384] = misc[6 * h : 6 * h + 6]
        rest_ref[h, 0:2, 384:512] = misc[2 * h : 2 * h + 2]
    for h in range(3):
        at = (slice(None), h, slice(None))
        w, m, v = (r[at] for r in proj)
        put(proj_o, at, adam(w, total[:, 128 * h : 128 * (h + 1)], m, v, RATE_D))
    at = (slice(None), slice(None))
    w, m, v = (r[at] for r in step)
    put(step_o, at, adam(w, half(misc)[:, 0:3], m, v, RATE_D))
    filled = jnp.concatenate([total[:, 384:640], jnp.zeros((80, 256), f32)], axis=0).T
    for h in range(3):
        w, m, v = (r[h] for r in out)
        put(out_o, h, adam(w, filled[64 * h : 64 * h + 64, 0:48], m, v, RATE_I))
    sums = chan_ref[0]
    for q in range(1, N_SEQ):
        sums = sums + chan_ref[q]
    for h in range(3):
        piece = sums[0:6, 128 * (h // 2) : 128 * (h // 2) + 128]
        if h == 1:
            piece = half(piece)
        at = (slice(None), h, slice(None))
        w, m, v = (r[at] for r in chan)
        put(chan_o, at, adam(w, piece[:, 0:64], m, v, 0.5))
    at = (slice(None), slice(None))
    w, m, v = (r[at] for r in head)
    put(head_o, at, adam(w, sums[6:9, 0:3], m, v, 1.0))


def rest_kernel(*refs):
    got_ref, refs = refs[0], refs[1:]
    shared, gain, conv = (refs[3 * k : 3 * k + 3] for k in range(3))
    outs = refs[9:]
    shared_o, gain_o, conv_o = (outs[3 * k : 3 * k + 3] for k in range(3))
    total = got_ref[0]
    for q in range(1, N_HEAD):
        total = total + got_ref[q]
    at = (slice(None), slice(None))
    w, m, v = (r[at] for r in shared)
    put(shared_o, at, adam(w, total[0:6, 0:256], m, v, RATE_D))
    column = total[:, 256 + MISC + 3 : 256 + MISC + 4] + total[:, 256 + MISC + 4 : 256 + MISC + 5]
    sub = lax.broadcasted_iota(jnp.int32, (8, 128), 0)
    row = jnp.sum(jnp.where(sub == lanes(8), column, 0.0), axis=0, keepdims=True)
    w, m, v = (r[at] for r in gain)
    put(gain_o, at, adam(w, row[:, 0:6], m, v, 0.5))
    tile = total[0:2, 384:512]
    both = rolled(tile, -(MISC + 5)) + rolled(tile, -(MISC + 10))
    w, m, v = (r[at] for r in conv)
    put(conv_o, at, adam(w, both[:, 0:5], m, v, 0.5))


def two_parts(a):
    high = lax.reduce_precision(a, 8, 7)
    return high.astype(bf16), (a - high).astype(bf16)


def exchange(blocks, axis):
    return lax.all_to_all(blocks, axis, 0, 0, tiled=True)


def shifted(a, by):
    pairs = [(i, i + by) for i in range(N_SEQ) if 0 <= i + by < N_SEQ]
    return lax.ppermute(a, SEQ, pairs)


def body(
    hidden_in, cotangent, doc_starts, proj_weight, step_weight, out_weight, shared_weight,
    pre_gain, channel_params, head_params, shared_conv, proj_first, proj_second, step_first,
    step_second, out_first, out_second, shared_first, shared_second, gain_first, gain_second,
    channel_first, channel_second, head_first, head_second, conv_first, conv_second,
):
    where = jnp.stack([lax.axis_index(SEQ), lax.axis_index(HEAD)]).astype(jnp.int32)
    halo = shifted(hidden_in[T - HALO :], 1)

    small = jnp.concatenate(
        [*two_parts(pre_gain), *(p.reshape(10) for p in two_parts(shared_conv))]
    )
    small = jnp.concatenate(
        [shared_weight.astype(bf16), jnp.pad(small, (0, 224))[None], jnp.zeros((1, 256), bf16)]
    )
    got = exchange(jnp.broadcast_to(small, (N_HEAD, 8, 256)), HEAD)
    line = got[:, 6]
    gain_cols = [line[:, 0:6].reshape(48, 1), line[:, 6:12].reshape(48, 1)]
    conv_cols = jnp.concatenate(
        [line[:, 12:22].reshape(16, 5), line[:, 22:32].reshape(16, 5)], axis=1
    )
    misc = jnp.concatenate(
        [step_weight.astype(bf16), *gain_cols, jnp.pad(conv_cols, ((0, 32), (0, 0)))], axis=1
    )
    pack = jnp.concatenate(
        [
            proj_weight.astype(bf16).reshape(48, 384),
            out_weight.astype(bf16).reshape(192, 48).T,
            jnp.pad(misc, ((0, 0), (0, 49))),
            got[:, 0:6].reshape(48, 256),
        ],
        axis=1,
    )
    weights = exchange(jnp.broadcast_to(pack, (N_SEQ, 48, NW)), SEQ).reshape(D, NW)

    marks = doc_starts.astype(f32).reshape(1, T)
    fixed = jnp.broadcast_to(
        (jnp.arange(6) == 3).astype(f32)[:, None, None], channel_params.shape
    )
    taps = jnp.concatenate([fixed, channel_params], axis=2).reshape(6, 384)
    gains = jnp.pad(channel_params[5].reshape(1, 192), ((0, 5), (0, 64)))
    taps = jnp.pad(jnp.concatenate([taps, gains], axis=1), ((0, 2), (0, 0)))

    normed, values, conv, aux, sent, row = call(
        first_kernel,
        [
            ((HALO + T, D), bf16), ((HALO + T, NV), f32), ((T, NV), f32), ((T, 128), f32),
            ((N_SEQ, SROWS, 128), bf16), ((8, D), f32),
        ],
        hidden_in, halo, marks, weights, taps, head_params, smem=(5,), name="first",
    )
    states = exchange(sent, SEQ)
    y_own, d_normed, decays, mixing = call(
        own_kernel,
        [((T, 256), f32), ((T, 256), f32), ((3, T, T), bf16), ((3, T, T), bf16)],
        conv, aux, cotangent, weights, head_params, smem=(4,), name="own",
    )
    y_full, state, stat = call(
        enter_kernel,
        [((T, 256), f32), ((256, 128), f32), ((N_HEAD, 8, T), f32)],
        where, states, y_own, d_normed, conv, aux, taps, smem=(0,), name="enter",
    )
    stats = exchange(stat, HEAD)
    d_y, d_gate, normed_out, sent_adj, rows = call(
        gated_kernel,
        [
            ((T, 256), f32), ((T, 256), f32), ((T, 256), bf16),
            ((N_SEQ, 192, 128), bf16), ((8, 256), f32),
        ],
        stats, y_full, d_normed, conv, aux, taps, name="gated",
    )
    adjoints = exchange(sent_adj, SEQ)
    (partial_out,) = call(out_kernel, [((T, D), bf16)], normed_out, weights, name="out")
    own_out = exchange(partial_out.reshape(N_HEAD, T // N_HEAD, D), HEAD)
    d_x, d_b, d_c, d_cum = call(
        own_back_kernel,
        [((T, 256), f32), ((T, 128), f32), ((T, 128), f32), ((T, 128), f32)],
        d_y, y_full, y_own, conv, aux, decays, mixing, state, name="own_back",
    )
    (sums,) = call(
        block_sum_kernel, [((N_HEAD, T // N_HEAD, D), bf16)],
        where, own_out, hidden_in, smem=(0,), name="block_sum",
    )
    block_out = exchange(sums, HEAD).reshape(T, D)
    d_values, d_step, d_norm, edge, chan, d_conv, d_gain = call(
        back_kernel,
        [
            ((HALO + T, NV), bf16), ((T, 128), bf16), ((T, D), bf16), ((HALO, D), bf16),
            ((N_SEQ, 16, 256), f32), ((8, 256), f32), ((8, D), f32),
        ],
        where, adjoints, states, state, d_x, d_b, d_c, d_cum, conv, aux,
        values, taps, head_params, marks, d_y, d_gate, weights, rows, hidden_in, halo,
        smem=(0, 12),
        scratch=[pltpu.VMEM((T + 2 * HALO, 128), f32), pltpu.VMEM((16, 256), f32)],
        name="back",
    )
    edge = shifted(edge, -1)
    chans = exchange(chan, SEQ)
    (grads,) = call(
        grad_kernel, [((D, NW), bf16)],
        normed, d_values, d_step, normed_out, cotangent, d_conv, d_gain, name="grad",
    )
    grads = exchange(grads.reshape(N_SEQ, 48, NW), SEQ)
    d_norm = jnp.concatenate([d_norm[: T - HALO], d_norm[T - HALO :] + edge], axis=0)
    d_norm = exchange(d_norm.reshape(N_HEAD, T // N_HEAD, D), HEAD)
    (sums,) = call(sum_kernel, [((N_HEAD, T // N_HEAD, D), bf16)], d_norm, name="sum")
    d_norm = exchange(sums, HEAD).reshape(T, D)

    proj, step, out = (48, 3, 128), (48, 3), (3, 64, 48)
    shapes = [proj] * 3 + [step] * 3 + [out] * 3 + [(6, 3, 64)] * 3 + [(3, 3)] * 3
    updated = call(
        update_kernel,
        [(s, f32) for s in shapes] + [((N_HEAD, 8, 512), f32)],
        grads, chans, proj_weight, proj_first, proj_second, step_weight, step_first,
        step_second, out_weight, out_first, out_second, channel_params, channel_first,
        channel_second, head_params, head_first, head_second, name="update",
    )
    rest = exchange(updated[15], HEAD)
    (input_grad,) = call(
        input_kernel, [((T, D), f32)], d_norm, hidden_in, cotangent, row, name="input",
    )
    shared = call(
        rest_kernel,
        [(s, f32) for s in [(6, 256)] * 3 + [(1, 6)] * 3 + [(2, 5)] * 3],
        rest, shared_weight, shared_first, shared_second, pre_gain.reshape(1, 6),
        gain_first.reshape(1, 6), gain_second.reshape(1, 6), shared_conv, conv_first,
        conv_second, name="rest",
    )
    gain_new = [g.reshape(6) for g in shared[3:6]]
    return (
        block_out, input_grad, *updated[0:9], *shared[0:3], *gain_new, *updated[9:15],
        *shared[6:9],
    )


def solution(mesh):
    finer = Mesh(mesh.devices.reshape(4, 4, 4, 2), SEQ_HEAD)
    matrix = P(SEQ, HEAD, None)
    step = P(SEQ, HEAD)
    out = P(HEAD, None, SEQ)
    both = P(SEQ_HEAD, None)
    gain = P(SEQ_HEAD)
    channel = P(None, HEAD, None)
    head = P(None, HEAD)
    tokens = P(SEQ, None)
    return jax.shard_map(
        body,
        mesh=finer,
        in_specs=(
            tokens, tokens, P(SEQ), matrix, step, out, both, gain, channel, head, both,
            matrix, matrix, step, step, out, out, both, both, gain, gain, channel, channel,
            head, head, both, both,
        ),
        out_specs=(
            (tokens, tokens)
            + (matrix,) * 3 + (step,) * 3 + (out,) * 3 + (both,) * 3 + (gain,) * 3
            + (channel,) * 3 + (head,) * 3 + (both,) * 3
        ),
        check_vma=False,
    )
```

time: 595 us -> 246 us (0.41); the launches traced: 585 us -> 244 us
  blocking collectives: 153 us -> 11.7 us
  local copies, waits for them, and re-layouts: 149 us -> 28 us
  other arithmetic: 75.4 us -> 7.11 us
  matrix products: 59.8 us -> 0 us
  Pallas kernels: 0 us -> 57.2 us
  between operations: 15.6 us -> 0.95 us
  starting transfers between devices: 52.6 us -> 60.4 us
    all_gather x3 -> x0, blocking collectives: 99.2 us -> none  [the longest x1 39.9 us: side_by_side(): lax.all_gather(both, axis, axis=dim, tiled=True)]
    dot_general x39 -> x0, matrix products: 59.8 us -> none  [the longest x6 13.3 us: group_pass(): output = jnp.einsum('ijh,jhp->ihp', mixing, x_conv, precision=highest)]
    pallas_call x0 -> x13, Pallas kernels: none -> 57.2 us  [call(): pl.pallas_call(kernel, out_shape=[jax.ShapeDtypeStruct(s, d) for s, d in...]
    dynamic_update_slice x46 -> x0, local copies, waits for them, and re-layouts: 44.9 us -> none  [local_mixer(): ends, outs_all = lax.scan(group_pass, start_carry, pieces)]
    psum x2 -> x0, blocking collectives: 27 us -> none  [one_axis_at_a_time(): return functools.reduce(lax.psum, axes, array)]
    reduce_sum x20 -> x0, other arithmetic: 16 us -> none  [the longest x1 3.22 us: local_mixer(): head_vals[2][None, :, None] * x_conv]
    reshape x19 -> x8, local copies, waits for them, and re-layouts: 16.2 us -> 0.61 us  [the longest x2 0.17 us: body(): gain_cols = [line[:, 0:6].reshape(48, 1), line[:, 6:12].reshape(48, 1)]]
    all_to_all x4 -> x1, blocking collectives: 26.5 us -> 11.7 us  [exchange(): return lax.all_to_all(blocks, axis, 0, 0, tiled=True)]
  transfers between devices with their start and end apart: 12 -> 13, of which waited for: 8 -> 11; matrix products, arithmetic and copies ran while one was open for 13% -> 11% of each run, Pallas kernels for 0% -> 17%
where the time goes in v1:
time: 246 us; the launch traced here: 244 us
  waiting for transfers between devices  78.3 us (32%)
  starting transfers between devices  60.4 us (25%)
  Pallas kernels  57.2 us (23%)
  local copies, waits for them, and re-layouts  28 us (11%)
  blocking collectives  11.7 us (5%)
  other arithmetic  7.11 us (3%)
    all_to_all x11, waiting for transfers between devices, exchange(): return lax.all_to_all(blocks, axis, 0, 0, tiled=True)  65.3 us
    pallas_call x13, Pallas kernels, call(): pl.pallas_call(kernel, out_shape=[jax.ShapeDtypeStruct(s, d) for s, d in...  57.2 us
    all_to_all x11, starting transfers between devices, exchange(): return lax.all_to_all(blocks, axis, 0, 0, tiled=True)  55.8 us
    unnamed x67, local copies, waits for them, and re-layouts  23.6 us
    ppermute x2, waiting for transfers between devices, shifted(): return lax.ppermute(a, SEQ, pairs)  13 us
    all_to_all x1, blocking collectives, exchange(): return lax.all_to_all(blocks, axis, 0, 0, tiled=True)  11.7 us
  transfers between devices with their start and end apart: 13, of which 11 were waited for; matrix products, arithmetic and copies ran while one was open for 11% of the time, Pallas kernels for 17%

profile of v1, /device:TPU:1, one launch (start us, length us, event | category | flops | bytes accessed | tf_op | source)
XLA Modules:
  0.0 243.6 jit_solution(11614818791070280947)
XLA Ops:
  3.7 5.8 %all-to-all-start = ((bf16[8,8,256]{2,1,0:T(8,128)(2,1)}), bf16[8,8,256]{2,1,0:T(8,128)(2,1)S(1)}, u32[]{:S(2)}, u32[]{:S(2)}) async-start(bf16[8,8,256]{2,1,0:T(8,128)(2,1)} %broadcast_in_dim.20), calls=%async_computation | async-start | bytes 65536 | tf_op jit(solution)/shard_map/all_to_all | solution.py:687
  16.2 7.9 %all-to-all-start.1 = ((bf16[16,48,896]{2,1,0:T(8,128)(2,1)}), bf16[16,48,896]{2,1,0:T(8,128)(2,1)S(1)}, u32[]{:S(2)}, u32[]{:S(2)}) async-start(bf16[16,48,896]{2,1,0:T(8,128)(2,1)} %broadcast_in_dim.21), calls=%async_computation.1 | async-start | bytes 2752512 | tf_op jit(solution)/shard_map/all_to_all | solution.py:687
  24.9 3.3 %collective-permute-start = (bf16[16,768]{1,0:T(8,128)(2,1)S(1)}, bf16[16,768]{1,0:T(8,128)(2,1)S(1)}, u32[]{:S(2)}, u32[]{:S(2)}) collective-permute-start(bf16[16,768]{1,0:T(8,128)(2,1)S(1)} %slice.30), channel_id=1, source_target_pairs={{0,8},{8,16},{16,24},{24,32},{32,40},{40,48},{48,56},{56,64},{64,7... | collective-permute-start | bytes 73736 | tf_op jit(solution)/shard_map/ppermute | solution.py:692
  29.6 9.5 %collective-permute-done.halo_ref = bf16[16,768]{1,0:T(8,128)(2,1)S(1)} collective-permute-done((bf16[16,768]{1,0:T(8,128)(2,1)S(1)}, bf16[16,768]{1,0:T(8,128)(2,1)S(1)}, u32[]{:S(2)}, u32[]{:S(2)}) %collective-permute-start) | collective-permute-done | bytes 24608 | tf_op jit(solution)/shard_map/ppermute | solution.py:692
  39.1 4.5 %all-to-all-done.1 = bf16[16,48,896]{2,1,0:T(8,128)(2,1)S(1)} async-done(((bf16[16,48,896]{2,1,0:T(8,128)(2,1)}), bf16[16,48,896]{2,1,0:T(8,128)(2,1)S(1)}, u32[]{:S(2)}, u32[]{:S(2)}) %all-to-all-start.1) | async-done | bytes 1376288 | tf_op jit(solution)/shard_map/all_to_all | solution.py:687
  44.7 6.3 %first.1 = (bf16[528,768]{1,0:T(8,128)(2,1)}, f32[528,640]{1,0:T(8,128)}, f32[512,640]{1,0:T(8,128)}, f32[512,128]{1,0:T(8,128)}, bf16[16,208,128]{2,1,0:T(8,128)(2,1)}, /*index=5*/f32[8,768]{1,0:T(8,128)}) custom-call(bf16[512,768]{1,0:T(8,128)(2,1)} %hid_ref.7, bf16[16,768]{1,0:T(8,128)(2,1)} %copy-done.12, f32[1,512]{1,0:T(1,128)} %bitcast.46, ...), custom_call_target="tpu_custom_call" | custom-call | tf_op jit(solution)/shard_map/first/pallas_call | solution.py:42
  51.0 5.6 %all-to-all-start.2 = ((bf16[16,208,128]{2,1,0:T(8,128)(2,1)}), bf16[16,208,128]{2,1,0:T(8,128)(2,1)S(1)}, u32[]{:S(2)}, u32[]{:S(2)}) async-start(bf16[16,208,128]{2,1,0:T(8,128)(2,1)} %get-tuple-element.80), calls=%async_computation.2 | async-start | bytes 1703936 | tf_op jit(solution)/shard_map/all_to_all | solution.py:687
  57.2 5.7 %own.1 = (f32[512,256]{1,0:T(8,128)}, f32[512,256]{1,0:T(8,128)}, bf16[3,512,512]{2,1,0:T(8,128)(2,1)}, bf16[3,512,512]{2,1,0:T(8,128)(2,1)}) custom-call(f32[512,640]{1,0:T(8,128)} %get-tuple-element.81.c_ref, f32[512,128]{1,0:T(8,128)} %get-tuple-element.82.aux_ref, bf16[512,768]{1,0:T(8,128)(2,1)} %cot_ref.5, bf16[768,896]{1,0:T(8,128)(2,1)} %bitcast.34, ...), custom_call_target="tpu_custom_call" | custom-call | tf_op jit(solution)/shard_map/own/pallas_call | solution.py:42
  62.9 7.4 %all-to-all-done.2.got_ref.fwd_ref = bf16[16,208,128]{2,1,0:T(8,128)(2,1)S(1)} async-done(((bf16[16,208,128]{2,1,0:T(8,128)(2,1)}), bf16[16,208,128]{2,1,0:T(8,128)(2,1)S(1)}, u32[]{:S(2)}, u32[]{:S(2)}) %all-to-all-start.2) | async-done | bytes 852000 | tf_op jit(solution)/shard_map/all_to_all | solution.py:687
  71.2 3.5 %enter.1 = (f32[512,256]{1,0:T(8,128)}, f32[256,128]{1,0:T(8,128)}, f32[8,8,512]{2,1,0:T(8,128)}) custom-call(s32[2]{0:T(128)} %pad_add_fusion.at_ref, bf16[16,208,128]{2,1,0:T(8,128)(2,1)} %copy-done.1, f32[512,256]{1,0:T(8,128)} %get-tuple-element.83.y0_ref, f32[512,256]{1,0:T(8,128)} %get-tuple-element.84.dn_ref, f32[512,640]{1,0:T(8,128)} %get-tuple-element.81.c_ref, ...), custom_call_target="tpu_custom_call" | custom-call | tf_op jit(solution)/shard_map/enter/pallas_call | solution.py:42
  74.7 11.7 %all_to_all.60.got_ref = f32[8,8,512]{2,1,0:T(8,128)} all-to-all(f32[8,8,512]{2,1,0:T(8,128)} %get-tuple-element.85), channel_id=1, replica_groups=mesh['seq_0'=4,'seq_1'=4,'head_0'=4,'head_1'=2] {'head_0','head_1'}, dimensions={0} | all-to-all | bytes 262144 | tf_op jit(solution)/shard_map/all_to_all | solution.py:687
  86.4 4.1 %gated.1 = (f32[512,256]{1,0:T(8,128)}, f32[512,256]{1,0:T(8,128)}, bf16[512,256]{1,0:T(8,128)(2,1)}, bf16[16,192,128]{2,1,0:T(8,128)(2,1)}, f32[8,256]{1,0:T(8,128)}) custom-call(f32[8,8,512]{2,1,0:T(8,128)} %all_to_all.60.got_ref, f32[512,256]{1,0:T(8,128)} %get-tuple-element.86.y_ref, f32[512,256]{1,0:T(8,128)} %get-tuple-element.84.dn_ref, ...), custom_call_target="tpu_custom_call" | custom-call | tf_op jit(solution)/shard_map/gated/pallas_call | solution.py:42
  90.5 3.6 %all-to-all-start.6 = ((bf16[16,192,128]{2,1,0:T(8,128)(2,1)}), bf16[16,192,128]{2,1,0:T(8,128)(2,1)S(1)}, u32[]{:S(2)}, u32[]{:S(2)}) async-start(bf16[16,192,128]{2,1,0:T(8,128)(2,1)} %get-tuple-element.88), calls=%async_computation.6 | async-start | bytes 1572864 | tf_op jit(solution)/shard_map/all_to_all | solution.py:687
  96.9 10.5 %all-to-all-done.6.got_ref = bf16[16,192,128]{2,1,0:T(8,128)(2,1)S(1)} async-done(((bf16[16,192,128]{2,1,0:T(8,128)(2,1)}), bf16[16,192,128]{2,1,0:T(8,128)(2,1)S(1)}, u32[]{:S(2)}, u32[]{:S(2)}) %all-to-all-start.6) | async-done | bytes 786464 | tf_op jit(solution)/shard_map/all_to_all | solution.py:687
  107.4 5.6 %all-to-all-start.4 = ((bf16[8,64,768]{2,1,0:T(8,128)(2,1)}), bf16[8,64,768]{2,1,0:T(8,128)(2,1)S(1)}, u32[]{:S(2)}, u32[]{:S(2)}) async-start(bf16[8,64,768]{2,1,0:T(8,128)(2,1)} %bitcast.39), calls=%async_computation.4 | async-start | bytes 1572864 | tf_op jit(solution)/shard_map/all_to_all | solution.py:687
  113.0 6.0 %own_back.1 = (f32[512,256]{1,0:T(8,128)}, f32[512,128]{1,0:T(8,128)}, f32[512,128]{1,0:T(8,128)}, f32[512,128]{1,0:T(8,128)}) custom-call(f32[512,256]{1,0:T(8,128)} %get-tuple-element.90.dy_ref, f32[512,256]{1,0:T(8,128)} %get-tuple-element.86.y_ref, f32[512,256]{1,0:T(8,128)} %get-tuple-element.83.y0_ref, f32[512,640]{1,0:T(8,128)} %get-tuple-element.81.c_ref, ...), custom_call_target="tpu_custom_call" | custom-call | tf_op jit(solution)/shard_map/own_back/pallas_call | solution.py:42
  119.0 11.3 %back.1 = (bf16[528,640]{1,0:T(8,128)(2,1)}, bf16[512,128]{1,0:T(8,128)(2,1)}, bf16[512,768]{1,0:T(8,128)(2,1)}, bf16[16,768]{1,0:T(8,128)(2,1)}, f32[16,16,256]...) custom-call(s32[2]{0:T(128)} %pad_add_fusion.at_ref, bf16[16,192,128]{2,1,0:T(8,128)(2,1)} %copy-done.4, ...), custom_call_target="tpu_custom_call" | custom-call | tf_op jit(solution)/shard_map/back/pallas_call | solution.py:42
  130.3 3.5 %all-to-all-start.10 = ((f32[16,16,256]{2,1,0:T(8,128)}), f32[16,16,256]{2,1,0:T(8,128)S(1)}, u32[]{:S(2)}, u32[]{:S(2)}) async-start(f32[16,16,256]{2,1,0:T(8,128)} %get-tuple-element.108), calls=%async_computation.10 | async-start | bytes 524288 | tf_op jit(solution)/shard_map/all_to_all | solution.py:687
  136.4 6.0 %all-to-all-done.10.refs_1_ = f32[16,16,256]{2,1,0:T(8,128)S(1)} async-done(((f32[16,16,256]{2,1,0:T(8,128)}), f32[16,16,256]{2,1,0:T(8,128)S(1)}, u32[]{:S(2)}, u32[]{:S(2)}) %all-to-all-start.10) | async-done | bytes 262176 | tf_op jit(solution)/shard_map/all_to_all | solution.py:687
  142.4 5.6 %all-to-all-start.5 = ((bf16[8,64,768]{2,1,0:T(8,128)(2,1)}), bf16[8,64,768]{2,1,0:T(8,128)(2,1)S(1)}, u32[]{:S(2)}, u32[]{:S(2)}) async-start(bf16[8,64,768]{2,1,0:T(8,128)(2,1)} %block_sum.1), calls=%async_computation.5 | async-start | bytes 1572864 | tf_op jit(solution)/shard_map/all_to_all | solution.py:687
  149.3 3.5 %collective-permute-done.1 = bf16[16,768]{1,0:T(8,128)(2,1)S(1)} collective-permute-done((bf16[16,768]{1,0:T(8,128)(2,1)S(1)}, bf16[16,768]{1,0:T(8,128)(2,1)S(1)}, u32[]{:S(2)}, u32[]{:S(2)}) %collective-permute-start.1) | collective-permute-done | bytes 24608 | tf_op jit(solution)/shard_map/ppermute | solution.py:692
  153.8 6.5 %all-to-all-done.5 = bf16[8,64,768]{2,1,0:T(8,128)(2,1)S(1)} async-done(((bf16[8,64,768]{2,1,0:T(8,128)(2,1)}), bf16[8,64,768]{2,1,0:T(8,128)(2,1)S(1)}, u32[]{:S(2)}, u32[]{:S(2)}) %all-to-all-start.5) | async-done | bytes 786464 | tf_op jit(solution)/shard_map/all_to_all | solution.py:687
  160.2 4.3 %all-to-all-start.7 = ((bf16[8,64,768]{2,1,0:T(8,128)(2,1)}), bf16[8,64,768]{2,1,0:T(8,128)(2,1)S(1)}, u32[]{:S(2)}, u32[]{:S(2)}) async-start(bf16[8,64,768]{2,1,0:T(8,128)(2,1)} %bitcast.8), calls=%async_computation.7 | async-start | bytes 1572864 | tf_op jit(solution)/shard_map/all_to_all | solution.py:687
  164.6 4.6 %grad.1 = bf16[768,896]{1,0:T(8,128)(2,1)} custom-call(bf16[528,768]{1,0:T(8,128)(2,1)} %get-tuple-element.103.normed_ref, bf16[528,640]{1,0:T(8,128)(2,1)} %get-tuple-element.104.dv_ref, bf16[512,128]{1,0:T(8,128)(2,1)} %get-tuple-element.105.dstep_ref, bf16[512,256]{1,0:T(8,128)(2,1)} %get-tuple-element.87.nout_ref, bf16[512,768]{1,0:T(8,128)(2,1)} %cot_ref.5, ...), custom_call_target="tpu_custom_call" | custom-call | tf_op jit(solution)/shard_map/grad/pallas_call | solution.py:42
  169.2 7.7 %all-to-all-done.7.got_ref = bf16[8,64,768]{2,1,0:T(8,128)(2,1)S(1)} async-done(((bf16[8,64,768]{2,1,0:T(8,128)(2,1)}), bf16[8,64,768]{2,1,0:T(8,128)(2,1)S(1)}, u32[]{:S(2)}, u32[]{:S(2)}) %all-to-all-start.7) | async-done | bytes 786464 | tf_op jit(solution)/shard_map/all_to_all | solution.py:687
  176.9 3.7 %all-to-all-start.9 = ((bf16[16,48,896]{2,1,0:T(8,128)(2,1)}), bf16[16,48,896]{2,1,0:T(8,128)(2,1)S(1)}, u32[]{:S(2)}, u32[]{:S(2)}) async-start(bf16[16,48,896]{2,1,0:T(8,128)(2,1)} %bitcast.37), calls=%async_computation.9 | async-start | bytes 2752512 | tf_op jit(solution)/shard_map/all_to_all | solution.py:687
  182.9 17.9 %all-to-all-done.9.refs_0_ = bf16[16,48,896]{2,1,0:T(8,128)(2,1)S(1)} async-done(((bf16[16,48,896]{2,1,0:T(8,128)(2,1)}), bf16[16,48,896]{2,1,0:T(8,128)(2,1)S(1)}, u32[]{:S(2)}, u32[]{:S(2)}) %all-to-all-start.9) | async-done | bytes 1376288 | tf_op jit(solution)/shard_map/all_to_all | solution.py:687
  200.8 6.1 %all-to-all-start.8 = ((bf16[8,64,768]{2,1,0:T(8,128)(2,1)}), bf16[8,64,768]{2,1,0:T(8,128)(2,1)S(1)}, u32[]{:S(2)}, u32[]{:S(2)}) async-start(bf16[8,64,768]{2,1,0:T(8,128)(2,1)} %sum.1), calls=%async_computation.8 | async-start | bytes 1572864 | tf_op jit(solution)/shard_map/all_to_all | solution.py:687
  213.2 3.1 %update.1 = (f32[48,3,128]{2,1,0:T(4,128)}, f32[48,3,128]{2,1,0:T(4,128)}, f32[48,3,128]{2,1,0:T(4,128)}, f32[48,3]{1,0:T(8,128)}, f32[48,3]{1,0:T(8,128)}, /*in...) custom-call(bf16[16,48,896]{2,1,0:T(8,128)(2,1)} %copy-done.2, ...), custom_call_target="tpu_custom_call" | custom-call | tf_op jit(solution)/shard_map/update/pallas_call | solution.py:42
  216.4 2.8 %all-to-all-done.8 = bf16[8,64,768]{2,1,0:T(8,128)(2,1)S(1)} async-done(((bf16[8,64,768]{2,1,0:T(8,128)(2,1)}), bf16[8,64,768]{2,1,0:T(8,128)(2,1)S(1)}, u32[]{:S(2)}, u32[]{:S(2)}) %all-to-all-start.8) | async-done | bytes 786464 | tf_op jit(solution)/shard_map/all_to_all | solution.py:687
  219.2 4.1 %all-to-all-start.11 = ((f32[8,8,512]{2,1,0:T(8,128)}), f32[8,8,512]{2,1,0:T(8,128)S(1)}, u32[]{:S(2)}, u32[]{:S(2)}) async-start(f32[8,8,512]{2,1,0:T(8,128)} %get-tuple-element.118), calls=%async_computation.11 | async-start | bytes 262144 | tf_op jit(solution)/shard_map/all_to_all | solution.py:687
  236.9 3.4 %input.1 = f32[512,768]{1,0:T(8,128)} custom-call(bf16[512,768]{1,0:T(8,128)(2,1)} %bitcast.40, bf16[512,768]{1,0:T(8,128)(2,1)} %hid_ref.7, bf16[512,768]{1,0:T(8,128)(2,1)} %cot_ref.5, f32[8,768]{1,0:T(8,128)} %get-tuple-element.102.row_ref), custom_call_target="tpu_custom_call" | custom-call | tf_op jit(solution)/shard_map/input/pallas_call | solution.py:42
  (117 shorter events, 47.6 us)
Async XLA Ops:
  3.7 10.5 %all-to-all-start = ((bf16[8,8,256]{2,1,0:T(8,128)(2,1)}), bf16[8,8,256]{2,1,0:T(8,128)(2,1)S(1)}, u32[]{:S(2)}, u32[]{:S(2)}) async-start(bf16[8,8,256]{2,1,0:T(8,128)(2,1)} %broadcast_in_dim.20), calls=%async_computation | async-start | bytes 65536 | tf_op jit(solution)/shard_map/all_to_all | solution.py:687
  16.2 12.0 %copy-start.17 = (f32[6,3,64]{2,1,0:T(4,128)S(1)}, f32[6,3,64]{2,1,0:T(4,128)}, u32[]{:S(2)}) copy-start(f32[6,3,64]{2,1,0:T(4,128)} %refs_11_.1) | copy-start | bytes 13828
  16.2 12.1 %slice-start = ((f32[6,3,64]{2,1,0:T(4,128)}), f32[1,3,64]{2,1,0:T(4,128)S(1)}, s32[]{:S(2)}) async-start(f32[6,3,64]{2,1,0:T(4,128)} %refs_11_.1), calls=%async_computation.12 | async-start | bytes 4096 | tf_op jit(solution)/shard_map/slice | solution.py:735
  16.2 12.2 %copy-start.19 = (s32[512]{0:T(512)S(1)}, s32[512]{0:T(512)}, u32[]{:S(2)}) copy-start(s32[512]{0:T(512)} %param.29) | copy-start | bytes 6148
  16.2 27.4 %all-to-all-start.1 = ((bf16[16,48,896]{2,1,0:T(8,128)(2,1)}), bf16[16,48,896]{2,1,0:T(8,128)(2,1)S(1)}, u32[]{:S(2)}, u32[]{:S(2)}) async-start(bf16[16,48,896]{2,1,0:T(8,128)(2,1)} %broadcast_in_dim.21), calls=%async_computation.1 | async-start | bytes 2752512 | tf_op jit(solution)/shard_map/all_to_all | solution.py:687
  24.9 14.2 %collective-permute-start = (bf16[16,768]{1,0:T(8,128)(2,1)S(1)}, bf16[16,768]{1,0:T(8,128)(2,1)S(1)}, u32[]{:S(2)}, u32[]{:S(2)}) collective-permute-start(bf16[16,768]{1,0:T(8,128)(2,1)S(1)} %slice.30), channel_id=1, source_target_pairs={{0,8},{8,16},{16,24},{24,32},{32,40},{40,48},{48,56},{56,64},{64,7... | collective-permute-start | bytes 73736 | tf_op jit(solution)/shard_map/ppermute | solution.py:692
  39.1 4.5 %copy-start.12 = (bf16[16,768]{1,0:T(8,128)(2,1)}, bf16[16,768]{1,0:T(8,128)(2,1)S(1)}, u32[]{:S(2)}) copy-start(bf16[16,768]{1,0:T(8,128)(2,1)S(1)} %collective-permute-done.halo_ref) | copy-start | bytes 73732
  51.0 19.3 %all-to-all-start.2 = ((bf16[16,208,128]{2,1,0:T(8,128)(2,1)}), bf16[16,208,128]{2,1,0:T(8,128)(2,1)S(1)}, u32[]{:S(2)}, u32[]{:S(2)}) async-start(bf16[16,208,128]{2,1,0:T(8,128)(2,1)} %get-tuple-element.80), calls=%async_computation.2 | async-start | bytes 1703936 | tf_op jit(solution)/shard_map/all_to_all | solution.py:687
  90.5 16.9 %all-to-all-start.6 = ((bf16[16,192,128]{2,1,0:T(8,128)(2,1)}), bf16[16,192,128]{2,1,0:T(8,128)(2,1)S(1)}, u32[]{:S(2)}, u32[]{:S(2)}) async-start(bf16[16,192,128]{2,1,0:T(8,128)(2,1)} %get-tuple-element.88), calls=%async_computation.6 | async-start | bytes 1572864 | tf_op jit(solution)/shard_map/all_to_all | solution.py:687
  107.4 11.6 %copy-start.4 = (bf16[16,192,128]{2,1,0:T(8,128)(2,1)}, bf16[16,192,128]{2,1,0:T(8,128)(2,1)S(1)}, u32[]{:S(2)}) copy-start(bf16[16,192,128]{2,1,0:T(8,128)(2,1)S(1)} %all-to-all-done.6.got_ref) | copy-start | bytes 2359300
  107.4 23.0 %all-to-all-start.4 = ((bf16[8,64,768]{2,1,0:T(8,128)(2,1)}), bf16[8,64,768]{2,1,0:T(8,128)(2,1)S(1)}, u32[]{:S(2)}, u32[]{:S(2)}) async-start(bf16[8,64,768]{2,1,0:T(8,128)(2,1)} %bitcast.39), calls=%async_computation.4 | async-start | bytes 1572864 | tf_op jit(solution)/shard_map/all_to_all | solution.py:687
  130.3 12.0 %all-to-all-start.10 = ((f32[16,16,256]{2,1,0:T(8,128)}), f32[16,16,256]{2,1,0:T(8,128)S(1)}, u32[]{:S(2)}, u32[]{:S(2)}) async-start(f32[16,16,256]{2,1,0:T(8,128)} %get-tuple-element.108), calls=%async_computation.10 | async-start | bytes 524288 | tf_op jit(solution)/shard_map/all_to_all | solution.py:687
  133.9 14.1 %copy-start.22 = (bf16[16,768]{1,0:T(8,128)(2,1)S(1)}, bf16[16,768]{1,0:T(8,128)(2,1)}, u32[]{:S(2)}) copy-start(bf16[16,768]{1,0:T(8,128)(2,1)} %get-tuple-element.101) | copy-start | bytes 73732
  133.9 15.3 %copy-start.8 = (bf16[512,768]{1,0:T(8,128)(2,1)S(1)}, bf16[512,768]{1,0:T(8,128)(2,1)}, u32[]{:S(2)}) copy-start(bf16[512,768]{1,0:T(8,128)(2,1)} %get-tuple-element.100) | copy-start | bytes 2359300
  142.4 10.4 %copy-start.7 = (f32[16,16,256]{2,1,0:T(8,128)}, f32[16,16,256]{2,1,0:T(8,128)S(1)}, u32[]{:S(2)}) copy-start(f32[16,16,256]{2,1,0:T(8,128)S(1)} %all-to-all-done.10.refs_1_) | copy-start | bytes 786436
  142.4 17.9 %all-to-all-start.5 = ((bf16[8,64,768]{2,1,0:T(8,128)(2,1)}), bf16[8,64,768]{2,1,0:T(8,128)(2,1)S(1)}, u32[]{:S(2)}, u32[]{:S(2)}) async-start(bf16[8,64,768]{2,1,0:T(8,128)(2,1)} %block_sum.1), calls=%async_computation.5 | async-start | bytes 1572864 | tf_op jit(solution)/shard_map/all_to_all | solution.py:687
  148.0 4.9 %collective-permute-start.1 = (bf16[16,768]{1,0:T(8,128)(2,1)S(1)}, bf16[16,768]{1,0:T(8,128)(2,1)S(1)}, u32[]{:S(2)}, u32[]{:S(2)}) collective-permute-start(bf16[16,768]{1,0:T(8,128)(2,1)S(1)} %copy-done.22), channel_id=1, source_target_pairs={{8,0},{16,8},{24,16},{32,24},{40,32},{48,40},{56,48},{64,56},{72,6... | collective-permute-start | bytes 73736 | tf_op jit(solution)/shard_map/ppermute | solution.py:692
  160.2 16.6 %all-to-all-start.7 = ((bf16[8,64,768]{2,1,0:T(8,128)(2,1)}), bf16[8,64,768]{2,1,0:T(8,128)(2,1)S(1)}, u32[]{:S(2)}, u32[]{:S(2)}) async-start(bf16[8,64,768]{2,1,0:T(8,128)(2,1)} %bitcast.8), calls=%async_computation.7 | async-start | bytes 1572864 | tf_op jit(solution)/shard_map/all_to_all | solution.py:687
  176.9 23.9 %all-to-all-start.9 = ((bf16[16,48,896]{2,1,0:T(8,128)(2,1)}), bf16[16,48,896]{2,1,0:T(8,128)(2,1)S(1)}, u32[]{:S(2)}, u32[]{:S(2)}) async-start(bf16[16,48,896]{2,1,0:T(8,128)(2,1)} %bitcast.37), calls=%async_computation.9 | async-start | bytes 2752512 | tf_op jit(solution)/shard_map/all_to_all | solution.py:687
  180.6 26.3 %copy-start.10 = (f32[48,3,128]{2,0,1:T(8,128)S(1)}, f32[48,3,128]{2,0,1:T(8,128)}, u32[]{:S(2)}) copy-start(f32[48,3,128]{2,0,1:T(8,128)} %param.30) | copy-start | bytes 221188
  180.6 26.9 %copy-start.11 = (f32[3,64,48]{1,2,0:T(8,128)S(1)}, f32[3,64,48]{1,2,0:T(8,128)}, u32[]{:S(2)}) copy-start(f32[3,64,48]{1,2,0:T(8,128)} %param.32) | copy-start | bytes 110596
  180.6 27.7 %copy-start.18 = (f32[48,3]{0,1:T(4,128)S(1)}, f32[48,3]{0,1:T(4,128)}, u32[]{:S(2)}) copy-start(f32[48,3]{0,1:T(4,128)} %param.31) | copy-start | bytes 1732
  180.6 28.3 %copy-start.13 = (f32[48,3,128]{2,0,1:T(8,128)S(1)}, f32[48,3,128]{2,0,1:T(8,128)}, u32[]{:S(2)}) copy-start(f32[48,3,128]{2,0,1:T(8,128)} %param.38) | copy-start | bytes 221188
  180.7 29.0 %copy-start.14 = (f32[48,3,128]{2,0,1:T(8,128)S(1)}, f32[48,3,128]{2,0,1:T(8,128)}, u32[]{:S(2)}) copy-start(f32[48,3,128]{2,0,1:T(8,128)} %param.39) | copy-start | bytes 221188
  180.7 29.7 %copy-start.15 = (f32[3,64,48]{1,2,0:T(8,128)S(1)}, f32[3,64,48]{1,2,0:T(8,128)}, u32[]{:S(2)}) copy-start(f32[3,64,48]{1,2,0:T(8,128)} %param.42) | copy-start | bytes 110596
  182.9 28.2 %copy-start.16 = (f32[3,64,48]{1,2,0:T(8,128)S(1)}, f32[3,64,48]{1,2,0:T(8,128)}, u32[]{:S(2)}) copy-start(f32[3,64,48]{1,2,0:T(8,128)} %param.43) | copy-start | bytes 110596
  182.9 28.9 %copy-start.20 = (f32[48,3]{0,1:T(4,128)S(1)}, f32[48,3]{0,1:T(4,128)}, u32[]{:S(2)}) copy-start(f32[48,3]{0,1:T(4,128)} %param.40) | copy-start | bytes 1732
  182.9 29.6 %copy-start.21 = (f32[48,3]{0,1:T(4,128)S(1)}, f32[48,3]{0,1:T(4,128)}, u32[]{:S(2)}) copy-start(f32[48,3]{0,1:T(4,128)} %param.41) | copy-start | bytes 1732
  200.8 12.4 %copy-start.2 = (bf16[16,48,896]{2,1,0:T(8,128)(2,1)}, bf16[16,48,896]{2,1,0:T(8,128)(2,1)S(1)}, u32[]{:S(2)}) copy-start(bf16[16,48,896]{2,1,0:T(8,128)(2,1)S(1)} %all-to-all-done.9.refs_0_) | copy-start | bytes 4128772
  200.8 18.4 %all-to-all-start.8 = ((bf16[8,64,768]{2,1,0:T(8,128)(2,1)}), bf16[8,64,768]{2,1,0:T(8,128)(2,1)S(1)}, u32[]{:S(2)}, u32[]{:S(2)}) async-start(bf16[8,64,768]{2,1,0:T(8,128)(2,1)} %sum.1), calls=%async_computation.8 | async-start | bytes 1572864 | tf_op jit(solution)/shard_map/all_to_all | solution.py:687
  219.2 17.8 %copy-start.6 = (bf16[8,64,768]{2,1,0:T(8,128)(2,1)}, bf16[8,64,768]{2,1,0:T(8,128)(2,1)S(1)}, u32[]{:S(2)}) copy-start(bf16[8,64,768]{2,1,0:T(8,128)(2,1)S(1)} %all-to-all-done.8) | copy-start | bytes 2359300
  219.2 21.2 %all-to-all-start.11 = ((f32[8,8,512]{2,1,0:T(8,128)}), f32[8,8,512]{2,1,0:T(8,128)S(1)}, u32[]{:S(2)}, u32[]{:S(2)}) async-start(f32[8,8,512]{2,1,0:T(8,128)} %get-tuple-element.118), calls=%async_computation.11 | async-start | bytes 262144 | tf_op jit(solution)/shard_map/all_to_all | solution.py:687
  (5 other events, 10.0 us)

commit v2 on v1

--- a/solution.py
+++ b/solution.py
@@ -172,6 +172,56 @@
     r = lax.broadcasted_iota(jnp.int32, (D, 256), 0)
     k = lax.broadcasted_iota(jnp.int32, (D, 256), 1)
     return jnp.where(r == k + 32 * jnp.right_shift(k, 4), 1.0, 0.0).astype(bf16)
+
+
+def small_kernel(shared_ref, gain_ref, conv_ref, out_ref, rows_ref):
+    rows_ref[...] = jnp.zeros_like(rows_ref)
+    rows_ref[0:6, :] = shared_ref[...]
+    gain = gain_ref[...]
+    high = gain.astype(bf16).astype(f32)
+    rows_ref[6:7, 0:6] = high
+    rows_ref[6:7, 128:134] = gain - high
+    conv = conv_ref[...]
+    high = conv.astype(bf16).astype(f32)
+    rows_ref[8:10, MISC + 5 : MISC + 10] = high
+    rows_ref[8:10, MISC + 10 : MISC + 15] = conv - high
+    low = rows_ref[...].astype(bf16)
+    for q in range(N_HEAD):
+        out_ref[q] = low
+
+
+def pack_kernel(
+    got_ref, proj_ref, outw_ref, step_ref, pack_ref, shared_ref, misc_ref, wide_ref
+):
+    misc_ref[...] = jnp.zeros_like(misc_ref)
+    misc_ref[0:3, 0:48] = step_ref[...]
+    misc = half(misc_ref[...].T)[0:48]
+    misc_ref[0:48, :] = misc
+    sub = lax.broadcasted_iota(jnp.int32, (6, 128), 0)
+    lane = lanes(6)
+    for q in range(N_HEAD):
+        rows = got_ref[q].astype(f32)
+        shared_ref[6 * q : 6 * q + 6, :] = rows[0:6]
+        part = jnp.zeros((6, 128), f32)
+        for k in range(2):
+            line = rows[6:7, 128 * k : 128 * (k + 1)]
+            column = jnp.sum(jnp.where(sub == lane, line, 0.0), axis=1, keepdims=True)
+            part = part + jnp.where(lane == MISC + 3 + k, column, 0.0)
+        misc_ref[6 * q : 6 * q + 6, :] += part
+        misc_ref[2 * q : 2 * q + 2, :] += rows[8:10, 0:128]
+    misc = misc_ref[0:48, :]
+    lo = lanes(48) < 64
+    tiles = [proj_ref[h] for h in range(3)]
+    wide = []
+    for h in range(3):
+        wide_ref[:, 0:64] = outw_ref[h]
+        wide.append(wide_ref[...])
+    tiles += [jnp.where(lo, wide[0], half(wide[1])), jnp.where(lo, wide[2], misc)]
+    tiles += [shared_ref[:, 0:128], shared_ref[:, 128:256]]
+    for k, tile in enumerate(tiles):
+        low = tile.astype(bf16)
+        for q in range(N_SEQ):
+            pack_ref[q, :, 128 * k : 128 * (k + 1)] = low
 
 
 def first_kernel(
@@ -295,7 +345,8 @@
 
 
 def enter_kernel(
-    at_ref, got_ref, y0_ref, dn_ref, c_ref, aux_ref, tap_ref, y_ref, state_ref, stat_ref
+    at_ref, got_ref, y0_ref, dn_ref, c_ref, aux_ref, tap_ref,
+    y_ref, state_ref, stat_ref, fed_ref,
 ):
     here = at_ref[0]
     state = jnp.zeros((192, 128), f32)
@@ -317,11 +368,10 @@
         y = y0_ref[:, at] + keeper[k] * carried[:, at]
         y_ref[:, at] = y
         gated = y * gate[k]
+        fed = gated * tap_ref[0:1, 384 + 128 * k : 512 + 128 * k]
+        fed_ref[:, at] = fed.astype(bf16)
         squares = squares + jnp.sum(gated * gated, axis=1, keepdims=True)
-        inner = inner + jnp.sum(
-            gated * dn_ref[:, at] * tap_ref[0:1, 384 + 128 * k : 512 + 128 * k],
-            axis=1, keepdims=True,
-        )
+        inner = inner + jnp.sum(fed * dn_ref[:, at], axis=1, keepdims=True)
     lane = lanes(T)
     both = jnp.where(lane == 0, squares, jnp.where(lane == 1, inner, 0.0)).T
     for q in range(N_HEAD):
@@ -330,7 +380,7 @@
 
 def gated_kernel(
     got_ref, y_ref, dn_ref, c_ref, aux_ref, tap_ref,
-    dy_ref, dgate_ref, nout_ref, send_ref, rows_ref,
+    dy_ref, dgate_ref, nout_ref, send_ref, rows_ref, rms_ref,
 ):
     total = got_ref[0]
     for q in range(1, N_HEAD):
@@ -338,6 +388,7 @@
     total = jnp.concatenate([total, jnp.zeros((120, T), f32)], axis=0).T
     rms = lax.rsqrt(total[:, 0:1] / DI + norm_eps)
     coef = rms * rms * rms * total[:, 1:2] / DI
+    rms_ref[...] = jnp.broadcast_to(rms, (T, 128))
     aux = aux_ref[...]
     keeper = spread(aux, 10)
     raw = gate_pair(*[c_ref[:, 128 * k : 128 * (k + 1)] for k in range(3)])
@@ -367,12 +418,13 @@
         send_ref[q] = adj
 
 
-def out_kernel(nout_ref, w_ref, out_ref):
-    lo = lanes(T) < 64
-    a = nout_ref[...]
-    del lo
-    res = dot(a, w_ref[:, 384:640], 1, 1)
-    out_ref[...] = res.astype(bf16)
+def out_kernel(fed_ref, w_ref, out_ref):
+    out_ref[...] = dot(fed_ref[...], w_ref[:, 384:640], 1, 1).astype(bf16)
+
+
+def block_kernel(sum_ref, rms_ref, hid_ref, out_ref):
+    rms = rms_ref[:, 0:1]
+    out_ref[...] = (hid_ref[...].astype(f32) + rms * sum_ref[...].astype(f32)).astype(bf16)
 
 
 def own_back_kernel(
@@ -423,8 +475,8 @@
 def back_kernel(
     at_ref, got_ref, fwd_ref, state_ref, dx_ref, db_ref, dc_ref, dcum_ref, c_ref, aux_ref,
     v_ref, tap_ref, hp_ref, st_ref, dy_ref, dgate_ref, w_ref, rows_ref, hid_ref, halo_ref,
-    dv_ref, dstep_ref, dnorm_ref, edge_ref, chan_ref, conv_ref, gain_ref,
-    pad_ref, big_ref,
+    dv_ref, dstep_ref, keep_ref, give_ref, edge_ref, chan_ref, conv_ref, gain_ref,
+    pad_ref, norm_ref,
 ):
     here = at_ref[0]
     adj = jnp.zeros((192, 128), f32)
@@ -522,10 +574,8 @@
     for r in (h0, h1, h2):
         chan_ref_rows.append(jnp.concatenate([r, zero], axis=1))
     for j, r in enumerate(chan_ref_rows):
-        big_ref[j : j + 1, :] = r
-    big_ref[9:16, :] = jnp.zeros((7, 256), f32)
-    for q in range(N_SEQ):
-        chan_ref[q] = big_ref[...]
+        chan_ref[j : j + 1, :] = r
+    chan_ref[9:16, :] = jnp.zeros((7, 256), f32)
     for j in range(5):
         conv_ref[j : j + 1, :] = jnp.concatenate([tap_rows[3][j], tap_rows[4][j]], axis=1)
     conv_ref[5:8, :] = jnp.zeros((3, 256), f32)
@@ -533,7 +583,10 @@
     d_norm = dot(dv_ref[:, 0:384], w_ref[:, 0:384], 1, 1)
     d_norm = d_norm + dot(dv_ref[:, 384:640], w_ref[:, 640:896], 1, 1)
     main = d_norm[HALO:] + dot(step_low, w_ref[:, 512:640], 1, 1)
-    dnorm_ref[...] = main.astype(bf16)
+    norm_ref[...] = main
+    core = at_ref[2]
+    keep_ref[...] = norm_ref[pl.ds(pl.multiple_of(core * 256, 256), 256), :].astype(bf16)
+    give_ref[...] = norm_ref[pl.ds(pl.multiple_of(256 - core * 256, 256), 256), :].astype(bf16)
     edge_ref[...] = d_norm[0:HALO].astype(bf16)
     total = jnp.zeros((1, D), f32)
     for src, val in ((halo_ref, d_norm[0:HALO]), (hid_ref, main)):
@@ -544,7 +597,9 @@
     gain_ref[1:8] = jnp.zeros((7, D), f32)
 
 
-def grad_kernel(normed_ref, dv_ref, dstep_ref, nout_ref, cot_ref, conv_ref, gain_ref, out_ref):
+def grad_kernel(
+    normed_ref, dv_ref, dstep_ref, nout_ref, cot_ref, conv_ref, gain_ref, chan_ref, out_ref
+):
     normed = normed_ref[...]
     out_ref[:, 0:384] = dot(normed, dv_ref[:, 0:384], 0, 0).astype(bf16)
     out_ref[:, 640:896] = dot(normed, dv_ref[:, 384:640], 0, 0).astype(bf16)
@@ -563,36 +618,45 @@
     column = jnp.where(
         sub == MISC + 3, gain_high, jnp.where(sub == MISC + 4, gain - gain_high, 0.0)
     ).T
-    out_ref[:, 512:640] = (tile + column).astype(bf16)
-
-
-def sum_kernel(got_ref, out_ref):
-    total = got_ref[0].astype(f32)
-    for q in range(1, N_HEAD):
-        total = total + got_ref[q].astype(f32)
-    total = total.astype(bf16)
-    for q in range(N_HEAD):
-        out_ref[q] = total
-
-
-def block_sum_kernel(at_ref, got_ref, hid_ref, out_ref):
-    start = pl.multiple_of(at_ref[1] * (T // N_HEAD), T // N_HEAD)
-    total = hid_ref[pl.ds(start, T // N_HEAD), :].astype(f32)
-    for q in range(N_HEAD):
-        total = total + got_ref[q].astype(f32)
-    total = total.astype(bf16)
-    for q in range(N_HEAD):
-        out_ref[q] = total
-
-
-def input_kernel(sum_ref, hid_ref, cot_ref, row_ref, out_ref):
-    h = hid_ref[...].astype(f32)
-    inv = lax.rsqrt(jnp.mean(h * h, axis=1, keepdims=True) + norm_eps)
-    d_scaled = sum_ref[...].astype(f32) * row_ref[0:1, :]
-    inner = jnp.sum(d_scaled * h, axis=1, keepdims=True)
-    out_ref[...] = (
-        cot_ref[...].astype(f32) + inv * d_scaled - h * (inv * inv * inv * inner / D)
-    )
+    turned = jnp.concatenate([chan_ref[...], jnp.zeros((112, 256), f32)], axis=0).T
+    turned = jnp.where(lanes(256) < 9, turned, 0.0)
+    shared = jnp.zeros((48, 128), f32)
+    for g in range(4):
+        shared = shared + rolled(turned[48 * g : 48 * g + 48], MISC + 16 + 9 * g)
+    tile = tile + column + jnp.concatenate([shared] * N_SEQ, axis=0)
+    out_ref[:, 512:640] = tile.astype(bf16)
+
+
+def pair_kernel(at_ref, keep_ref, got_ref, edge0_ref, edge1_ref, own_ref, s1, s2, s3, sum_ref):
+    sum_ref[...] = keep_ref[...].astype(f32) + got_ref[...].astype(f32)
+    sum_ref[256 - HALO :, :] += edge0_ref[...].astype(f32) + edge1_ref[...].astype(f32)
+    for by, ref in enumerate((own_ref, s1, s2, s3)):
+        start = pl.multiple_of(lax.rem(at_ref[1] + by, 4) * 64, 64)
+        ref[...] = sum_ref[pl.ds(start, 64), :].astype(bf16)
+
+
+def four_kernel(a_ref, b_ref, c_ref, d_ref, out_ref):
+    total = a_ref[...].astype(f32) + b_ref[...].astype(f32)
+    out_ref[...] = (total + c_ref[...].astype(f32) + d_ref[...].astype(f32)).astype(bf16)
+
+
+def input_kernel(*refs):
+    at_ref, refs = refs[0], refs[1:]
+    hid_ref, cot_ref, row_ref, out_ref = refs[8:]
+    for side in range(2):
+        core = at_ref[2] if side == 0 else 1 - at_ref[2]
+        for by in range(4):
+            block = core * 4 + lax.rem(at_ref[1] + 4 - by, 4)
+            rows = pl.ds(pl.multiple_of(block * 64, 64), 64)
+            h = hid_ref[rows, :].astype(f32)
+            inv = lax.rsqrt(jnp.mean(h * h, axis=1, keepdims=True) + norm_eps)
+            d_scaled = refs[4 * side + by][...].astype(f32) * row_ref[0:1, :]
+            inner = jnp.sum(d_scaled * h, axis=1, keepdims=True)
+            out_ref[rows, :] = (
+                cot_ref[rows, :].astype(f32)
+                + inv * d_scaled
+                - h * (inv * inv * inv * inner / D)
+            )
 
 
 def adam(weight, grad, first, second, rate):
@@ -616,7 +680,7 @@
 
 
 def update_kernel(*refs):
-    (grad_ref, chan_ref), refs = refs[:2], refs[2:]
+    grad_ref, refs = refs[0], refs[1:]
     proj, step, out, chan, head = (refs[3 * k : 3 * k + 3] for k in range(5))
     outs = refs[15:]
     proj_o, step_o, out_o, chan_o, head_o = (outs[3 * k : 3 * k + 3] for k in range(5))
@@ -631,29 +695,32 @@
         rest_ref[h, 0:6, 256:384] = misc[6 * h : 6 * h + 6]
         rest_ref[h, 0:2, 384:512] = misc[2 * h : 2 * h + 2]
     for h in range(3):
-        at = (slice(None), h, slice(None))
-        w, m, v = (r[at] for r in proj)
-        put(proj_o, at, adam(w, total[:, 128 * h : 128 * (h + 1)], m, v, RATE_D))
+        w, m, v = (r[h] for r in proj)
+        put(proj_o, h, adam(w, total[:, 128 * h : 128 * (h + 1)], m, v, RATE_D))
+        tile = total[:, 384 + 128 * (h // 2) : 512 + 128 * (h // 2)]
+        tile = half(tile) if h == 1 else tile
+        w, m, v = (r[h] for r in out)
+        put(out_o, h, adam(w, tile[:, 0:64], m, v, RATE_I))
+    turned = jnp.concatenate([misc, jnp.zeros((80, 128), f32)], axis=0).T
     at = (slice(None), slice(None))
     w, m, v = (r[at] for r in step)
-    put(step_o, at, adam(w, half(misc)[:, 0:3], m, v, RATE_D))
-    filled = jnp.concatenate([total[:, 384:640], jnp.zeros((80, 256), f32)], axis=0).T
+    put(step_o, at, adam(w, turned[MISC : MISC + 3, 0:48], m, v, RATE_D))
+    first = MISC + 16
+    p = [turned[first + 9 * g : first + 9 * g + 9] for g in range(4)]
+    lane = lanes(9)
+    wrapped = rolled(p[2], 96)
+    pair = (
+        p[0] + rolled(p[1], 48) + jnp.where(lane >= 96, wrapped, 0.0),
+        jnp.where(lane < 16, wrapped, 0.0) + rolled(p[3], 16),
+    )
     for h in range(3):
-        w, m, v = (r[h] for r in out)
-        put(out_o, h, adam(w, filled[64 * h : 64 * h + 64, 0:48], m, v, RATE_I))
-    sums = chan_ref[0]
-    for q in range(1, N_SEQ):
-        sums = sums + chan_ref[q]
-    for h in range(3):
-        piece = sums[0:6, 128 * (h // 2) : 128 * (h // 2) + 128]
-        if h == 1:
-            piece = half(piece)
+        piece = half(pair[0]) if h == 1 else pair[h // 2]
         at = (slice(None), h, slice(None))
         w, m, v = (r[at] for r in chan)
-        put(chan_o, at, adam(w, piece[:, 0:64], m, v, 0.5))
+        put(chan_o, at, adam(w, piece[0:6, 0:64], m, v, 0.5))
     at = (slice(None), slice(None))
     w, m, v = (r[at] for r in head)
-    put(head_o, at, adam(w, sums[6:9, 0:3], m, v, 1.0))
+    put(head_o, at, adam(w, pair[0][6:9, 0:3], m, v, 1.0))
 
 
 def rest_kernel(*refs):
@@ -678,18 +745,22 @@
     put(conv_o, at, adam(w, both[:, 0:5], m, v, 0.5))
 
 
-def two_parts(a):
-    high = lax.reduce_precision(a, 8, 7)
-    return high.astype(bf16), (a - high).astype(bf16)
-
-
 def exchange(blocks, axis):
     return lax.all_to_all(blocks, axis, 0, 0, tiled=True)
 
 
-def shifted(a, by):
-    pairs = [(i, i + by) for i in range(N_SEQ) if 0 <= i + by < N_SEQ]
-    return lax.ppermute(a, SEQ, pairs)
+def around(a, axis, by):
+    peers = lax.axis_size(axis)
+    return lax.ppermute(a, axis, [(i, (i + by) % peers) for i in range(peers)])
+
+
+def to_next(a):
+    return lax.ppermute(a, SEQ, [(i, i + 1) for i in range(N_SEQ - 1)])
+
+
+def to_previous(a, core):
+    pairs = [(2 * i + 2 + core, 2 * i + 1) for i in range(N_SEQ - 1)]
+    return lax.ppermute(a, SEQ + ("head_1",), pairs)
 
 
 def body(
@@ -698,34 +769,29 @@
     step_second, out_first, out_second, shared_first, shared_second, gain_first, gain_second,
     channel_first, channel_second, head_first, head_second, conv_first, conv_second,
 ):
-    where = jnp.stack([lax.axis_index(SEQ), lax.axis_index(HEAD)]).astype(jnp.int32)
-    halo = shifted(hidden_in[T - HALO :], 1)
-
-    small = jnp.concatenate(
-        [*two_parts(pre_gain), *(p.reshape(10) for p in two_parts(shared_conv))]
-    )
-    small = jnp.concatenate(
-        [shared_weight.astype(bf16), jnp.pad(small, (0, 224))[None], jnp.zeros((1, 256), bf16)]
-    )
-    got = exchange(jnp.broadcast_to(small, (N_HEAD, 8, 256)), HEAD)
-    line = got[:, 6]
-    gain_cols = [line[:, 0:6].reshape(48, 1), line[:, 6:12].reshape(48, 1)]
-    conv_cols = jnp.concatenate(
-        [line[:, 12:22].reshape(16, 5), line[:, 22:32].reshape(16, 5)], axis=1
-    )
-    misc = jnp.concatenate(
-        [step_weight.astype(bf16), *gain_cols, jnp.pad(conv_cols, ((0, 32), (0, 0)))], axis=1
-    )
-    pack = jnp.concatenate(
-        [
-            proj_weight.astype(bf16).reshape(48, 384),
-            out_weight.astype(bf16).reshape(192, 48).T,
-            jnp.pad(misc, ((0, 0), (0, 49))),
-            got[:, 0:6].reshape(48, 256),
+    where = jnp.stack(
+        [lax.axis_index(SEQ), lax.axis_index("head_0"), lax.axis_index("head_1")]
+    ).astype(jnp.int32)
+    halo = to_next(hidden_in[T - HALO :])
+    matrices = [jnp.transpose(a, (1, 0, 2)) for a in (proj_weight, proj_first, proj_second)]
+    steps = [a.T for a in (step_weight, step_first, step_second)]
+    out_weights = [jnp.transpose(a, (0, 2, 1)) for a in (out_weight, out_first, out_second)]
+    gains_in = [a.reshape(1, 6) for a in (pre_gain, gain_first, gain_second)]
+
+    (small,) = call(
+        small_kernel, [((N_HEAD, 16, 256), bf16)], shared_weight, gains_in[0], shared_conv,
+        scratch=[pltpu.VMEM((16, 256), f32)], name="small",
+    )
+    small = exchange(small, HEAD)
+    small, halo = lax.optimization_barrier((small, halo))
+    (pack,) = call(
+        pack_kernel, [((N_SEQ, 48, NW), bf16)], small, matrices[0], out_weights[0], steps[0],
+        scratch=[
+            pltpu.VMEM((48, 256), f32), pltpu.VMEM((128, 128), f32), pltpu.VMEM((48, 128), f32)
         ],
-        axis=1,
-    )
-    weights = exchange(jnp.broadcast_to(pack, (N_SEQ, 48, NW)), SEQ).reshape(D, NW)
+        name="pack",
+    )
+    weights = exchange(pack, SEQ).reshape(D, NW)
 
     marks = doc_starts.astype(f32).reshape(1, T)
     fixed = jnp.broadcast_to(
@@ -749,80 +815,88 @@
         [((T, 256), f32), ((T, 256), f32), ((3, T, T), bf16), ((3, T, T), bf16)],
         conv, aux, cotangent, weights, head_params, smem=(4,), name="own",
     )
-    y_full, state, stat = call(
+    y_full, state, stat, fed = call(
         enter_kernel,
-        [((T, 256), f32), ((256, 128), f32), ((N_HEAD, 8, T), f32)],
+        [((T, 256), f32), ((256, 128), f32), ((N_HEAD, 8, T), f32), ((T, 256), bf16)],
         where, states, y_own, d_normed, conv, aux, taps, smem=(0,), name="enter",
     )
     stats = exchange(stat, HEAD)
-    d_y, d_gate, normed_out, sent_adj, rows = call(
+    (partial_out,) = call(out_kernel, [((T, D), bf16)], fed, weights, name="out")
+    block_sum = lax.psum(partial_out, HEAD)
+    d_y, d_gate, normed_out, sent_adj, rows, rms = call(
         gated_kernel,
         [
             ((T, 256), f32), ((T, 256), f32), ((T, 256), bf16),
-            ((N_SEQ, 192, 128), bf16), ((8, 256), f32),
+            ((N_SEQ, 192, 128), bf16), ((8, 256), f32), ((T, 128), f32),
         ],
         stats, y_full, d_normed, conv, aux, taps, name="gated",
     )
     adjoints = exchange(sent_adj, SEQ)
-    (partial_out,) = call(out_kernel, [((T, D), bf16)], normed_out, weights, name="out")
-    own_out = exchange(partial_out.reshape(N_HEAD, T // N_HEAD, D), HEAD)
     d_x, d_b, d_c, d_cum = call(
         own_back_kernel,
         [((T, 256), f32), ((T, 128), f32), ((T, 128), f32), ((T, 128), f32)],
         d_y, y_full, y_own, conv, aux, decays, mixing, state, name="own_back",
     )
-    (sums,) = call(
-        block_sum_kernel, [((N_HEAD, T // N_HEAD, D), bf16)],
-        where, own_out, hidden_in, smem=(0,), name="block_sum",
-    )
-    block_out = exchange(sums, HEAD).reshape(T, D)
-    d_values, d_step, d_norm, edge, chan, d_conv, d_gain = call(
+    d_values, d_step, keep, give, edge, chan, d_conv, d_gain = call(
         back_kernel,
         [
-            ((HALO + T, NV), bf16), ((T, 128), bf16), ((T, D), bf16), ((HALO, D), bf16),
-            ((N_SEQ, 16, 256), f32), ((8, 256), f32), ((8, D), f32),
+            ((HALO + T, NV), bf16), ((T, 128), bf16), ((T // 2, D), bf16), ((T // 2, D), bf16),
+            ((HALO, D), bf16), ((16, 256), f32), ((8, 256), f32), ((8, D), f32),
         ],
         where, adjoints, states, state, d_x, d_b, d_c, d_cum, conv, aux,
         values, taps, head_params, marks, d_y, d_gate, weights, rows, hidden_in, halo,
         smem=(0, 12),
-        scratch=[pltpu.VMEM((T + 2 * HALO, 128), f32), pltpu.VMEM((16, 256), f32)],
+        scratch=[pltpu.VMEM((T + 2 * HALO, 128), f32), pltpu.VMEM((T, D), f32)],
         name="back",
     )
-    edge = shifted(edge, -1)
-    chans = exchange(chan, SEQ)
+    taken = around(give, "head_1", 1)
+    edges = [to_previous(edge, core) for core in range(2)]
     (grads,) = call(
         grad_kernel, [((D, NW), bf16)],
-        normed, d_values, d_step, normed_out, cotangent, d_conv, d_gain, name="grad",
+        normed, d_values, d_step, normed_out, cotangent, d_conv, d_gain, chan, name="grad",
     )
     grads = exchange(grads.reshape(N_SEQ, 48, NW), SEQ)
-    d_norm = jnp.concatenate([d_norm[: T - HALO], d_norm[T - HALO :] + edge], axis=0)
-    d_norm = exchange(d_norm.reshape(N_HEAD, T // N_HEAD, D), HEAD)
-    (sums,) = call(sum_kernel, [((N_HEAD, T // N_HEAD, D), bf16)], d_norm, name="sum")
-    d_norm = exchange(sums, HEAD).reshape(T, D)
-
-    proj, step, out = (48, 3, 128), (48, 3), (3, 64, 48)
+
+    piece = ((T // N_HEAD, D), bf16)
+    pieces = call(
+        pair_kernel, [piece] * 4, where, keep, taken, *edges, smem=(0,),
+        scratch=[pltpu.VMEM((T // 2, D), f32)], name="pair",
+    )
+    parts = [pieces[0]] + [around(pieces[by], "head_0", by) for by in (1, 2, 3)]
+    (own,) = call(four_kernel, [piece], *parts, name="four")
+    near = [own] + [around(own, "head_0", by) for by in (1, 2, 3)]
+    far = [around(a, "head_1", 1) for a in near]
+    (input_grad,) = call(
+        input_kernel, [((T, D), f32)], where, *near, *far, hidden_in, cotangent, row,
+        smem=(0,), name="input",
+    )
+
+    proj, step, out = (3, 48, 128), (3, 48), (3, 48, 64)
     shapes = [proj] * 3 + [step] * 3 + [out] * 3 + [(6, 3, 64)] * 3 + [(3, 3)] * 3
     updated = call(
         update_kernel,
         [(s, f32) for s in shapes] + [((N_HEAD, 8, 512), f32)],
-        grads, chans, proj_weight, proj_first, proj_second, step_weight, step_first,
-        step_second, out_weight, out_first, out_second, channel_params, channel_first,
+        grads, *matrices, *steps, *out_weights, channel_params, channel_first,
         channel_second, head_params, head_first, head_second, name="update",
     )
     rest = exchange(updated[15], HEAD)
-    (input_grad,) = call(
-        input_kernel, [((T, D), f32)], d_norm, hidden_in, cotangent, row, name="input",
+    (block_out,) = call(
+        block_kernel, [((T, D), bf16)], block_sum, rms, hidden_in, name="block"
     )
     shared = call(
         rest_kernel,
         [(s, f32) for s in [(6, 256)] * 3 + [(1, 6)] * 3 + [(2, 5)] * 3],
-        rest, shared_weight, shared_first, shared_second, pre_gain.reshape(1, 6),
-        gain_first.reshape(1, 6), gain_second.reshape(1, 6), shared_conv, conv_first,
+        rest, shared_weight, shared_first, shared_second, *gains_in, shared_conv, conv_first,
         conv_second, name="rest",
     )
-    gain_new = [g.reshape(6) for g in shared[3:6]]
     return (
-        block_out, input_grad, *updated[0:9], *shared[0:3], *gain_new, *updated[9:15],
+        block_out, input_grad,
+        *(jnp.transpose(a, (1, 0, 2)) for a in updated[0:3]),
+        *(a.T for a in updated[3:6]),
+        *(jnp.transpose(a, (0, 2, 1)) for a in updated[6:9]),
+        *shared[0:3],
+        *(g.reshape(6) for g in shared[3:6]),
+        *updated[9:15],
         *shared[6:9],
     )
 

time: 246 us -> 220 us (0.89)
  local copies, waits for them, and re-layouts: 28 us -> 8.85 us
  starting transfers between devices: 60.4 us -> 45.9 us
  between operations: 0.95 us -> 14.3 us
  other arithmetic: 7.11 us -> 1.26 us
  waiting for transfers between devices: 78.3 us -> 72.9 us
  Pallas kernels: 57.2 us -> 62.2 us
    all_to_all x11 -> x6, waiting for transfers between devices: 65.3 us -> 31.7 us  [exchange(): return lax.all_to_all(blocks, axis, 0, 0, tiled=True)]
    all_to_all x11 -> x6, starting transfers between devices: 55.8 us -> 31 us  [exchange(): return lax.all_to_all(blocks, axis, 0, 0, tiled=True)]
    psum x0 -> x1, waiting for transfers between devices: none -> 22.7 us  [body(): block_sum = lax.psum(partial_out, HEAD)]
    unnamed x67 -> x51, local copies, waits for them, and re-layouts: 23.6 us -> 7.34 us
    ppermute x2 -> x14, starting transfers between devices: 4.54 us -> 14.9 us  [the longest x11 9.08 us: around(): return lax.ppermute(a, axis, [(i, (i + by) % peers) for i in range(peers)])]
    ppermute x2 -> x14, waiting for transfers between devices: 13 us -> 18.5 us  [the longest x2 10.5 us: to_previous(): return lax.ppermute(a, SEQ + ('head_1',), pairs)]
    pallas_call x13 -> x16, Pallas kernels: 57.2 us -> 62.2 us  [call(): pl.pallas_call(kernel, out_shape=[jax.ShapeDtypeStruct(s, d) for s, d in...]
    convert_element_type x5 -> x0, other arithmetic: 3.62 us -> none  [the longest x2 1.35 us: two_parts(): return (high.astype(bf16), (a - high).astype(bf16))]
  transfers between devices with their start and end apart: 13 -> 21, of which waited for: 11 -> 9; matrix products, arithmetic and copies ran while one was open for 11% -> 1% of each run, Pallas kernels for 17% -> 12%
where the time goes in v2:
time: 220 us; the launch traced here: 217 us
  waiting for transfers between devices  72.9 us (33%)
  Pallas kernels  62.2 us (28%)
  starting transfers between devices  45.9 us (21%)
  between operations  14.3 us (6%)
  blocking collectives  11.9 us (5%)
  local copies, waits for them, and re-layouts  8.85 us (4%)
    pallas_call x16, Pallas kernels, call(): pl.pallas_call(kernel, out_shape=[jax.ShapeDtypeStruct(s, d) for s, d in...  62.2 us
    all_to_all x6, waiting for transfers between devices, exchange(): return lax.all_to_all(blocks, axis, 0, 0, tiled=True)  31.7 us
    all_to_all x6, starting transfers between devices, exchange(): return lax.all_to_all(blocks, axis, 0, 0, tiled=True)  31 us
    psum x1, waiting for transfers between devices, body(): block_sum = lax.psum(partial_out, HEAD)  22.7 us
    all_to_all x1, blocking collectives, exchange(): return lax.all_to_all(blocks, axis, 0, 0, tiled=True)  11.9 us
    ppermute x2, waiting for transfers between devices, to_previous(): return lax.ppermute(a, SEQ + ('head_1',), pairs)  10.5 us
    ppermute x11, starting transfers between devices, around(): return lax.ppermute(a, axis, [(i, (i + by) % peers) for i in range(peers)])  9.08 us
    unnamed x51, local copies, waits for them, and re-layouts  7.34 us
  transfers between devices with their start and end apart: 21, of which 9 were waited for; matrix products, arithmetic and copies ran while one was open for 1% of the time, Pallas kernels for 12%

profile of v2, /device:TPU:1, one launch (start us, length us, event | category | flops | bytes accessed | tf_op | source)
XLA Modules:
  0.0 217.4 jit_solution(4049524287652173939)
XLA Ops:
  8.6 5.8 %all-to-all-start = ((bf16[8,16,256]{2,1,0:T(8,128)(2,1)}), bf16[8,16,256]{2,1,0:T(8,128)(2,1)S(1)}, u32[]{:S(2)}, u32[]{:S(2)}) async-start(bf16[8,16,256]{2,1,0:T(8,128)(2,1)} %small.1), calls=%async_computation | async-start | bytes 131072 | tf_op jit(solution)/shard_map/all_to_all | solution.py:749
  15.2 3.2 %collective-permute-start = (bf16[16,768]{1,0:T(8,128)(2,1)S(1)}, bf16[16,768]{1,0:T(8,128)(2,1)S(1)}, u32[]{:S(2)}, u32[]{:S(2)}) collective-permute-start(bf16[16,768]{1,0:T(8,128)(2,1)S(1)} %slice.6), channel_id=1, source_target_pairs={{0,8},{8,16},{16,24},{24,32},{32,40},{40,48},{48,56},{56,64},{64,7... | collective-permute-start | bytes 73736 | tf_op jit(solution)/shard_map/ppermute | solution.py:758
  19.9 2.3 %pack.1 = bf16[16,48,896]{2,1,0:T(8,128)(2,1)} custom-call(bf16[8,16,256]{2,1,0:T(8,128)(2,1)} %copy-done.7, f32[3,48,128]{2,1,0:T(8,128)} %bitcast.40, f32[3,48,64]{2,1,0:T(8,128)} %bitcast.42, f32[3,48]{1,0:T(4,128)} %bitcast.51), custom_call_target="tpu_custom_call" | custom-call | tf_op jit(solution)/shard_map/pack/pallas_call | solution.py:42
  22.2 8.3 %all-to-all-start.1 = ((bf16[16,48,896]{2,1,0:T(8,128)(2,1)}), bf16[16,48,896]{2,1,0:T(8,128)(2,1)S(1)}, u32[]{:S(2)}, u32[]{:S(2)}) async-start(bf16[16,48,896]{2,1,0:T(8,128)(2,1)} %pack.1), calls=%async_computation.1 | async-start | bytes 2752512 | tf_op jit(solution)/shard_map/all_to_all | solution.py:749
  32.0 17.5 %all-to-all-done.1 = bf16[16,48,896]{2,1,0:T(8,128)(2,1)S(1)} async-done(((bf16[16,48,896]{2,1,0:T(8,128)(2,1)}), bf16[16,48,896]{2,1,0:T(8,128)(2,1)S(1)}, u32[]{:S(2)}, u32[]{:S(2)}) %all-to-all-start.1) | async-done | bytes 1376288 | tf_op jit(solution)/shard_map/all_to_all | solution.py:749
  50.7 6.2 %first.1 = (bf16[528,768]{1,0:T(8,128)(2,1)}, f32[528,640]{1,0:T(8,128)}, f32[512,640]{1,0:T(8,128)}, f32[512,128]{1,0:T(8,128)}, bf16[16,208,128]{2,1,0:T(8,128)(2,1)}, /*index=5*/f32[8,768]{1,0:T(8,128)}) custom-call(bf16[512,768]{1,0:T(8,128)(2,1)} %refs_9_.2, bf16[16,768]{1,0:T(8,128)(2,1)} %copy-done.8, f32[1,512]{1,0:T(1,128)} %bitcast.49, ...), custom_call_target="tpu_custom_call" | custom-call | tf_op jit(solution)/shard_map/first/pallas_call | solution.py:42
  56.9 5.6 %all-to-all-start.2 = ((bf16[16,208,128]{2,1,0:T(8,128)(2,1)}), bf16[16,208,128]{2,1,0:T(8,128)(2,1)S(1)}, u32[]{:S(2)}, u32[]{:S(2)}) async-start(bf16[16,208,128]{2,1,0:T(8,128)(2,1)} %get-tuple-element.91), calls=%async_computation.2 | async-start | bytes 1703936 | tf_op jit(solution)/shard_map/all_to_all | solution.py:749
  63.1 5.7 %own.1 = (f32[512,256]{1,0:T(8,128)}, f32[512,256]{1,0:T(8,128)}, bf16[3,512,512]{2,1,0:T(8,128)(2,1)}, bf16[3,512,512]{2,1,0:T(8,128)(2,1)}) custom-call(f32[512,640]{1,0:T(8,128)} %get-tuple-element.92.c_ref, f32[512,128]{1,0:T(8,128)} %get-tuple-element.93.aux_ref, bf16[512,768]{1,0:T(8,128)(2,1)} %cot_ref.3, bf16[768,896]{1,0:T(8,128)(2,1)} %bitcast.36, ...), custom_call_target="tpu_custom_call" | custom-call | tf_op jit(solution)/shard_map/own/pallas_call | solution.py:42
  68.8 7.1 %all-to-all-done.2.got_ref.fwd_ref = bf16[16,208,128]{2,1,0:T(8,128)(2,1)S(1)} async-done(((bf16[16,208,128]{2,1,0:T(8,128)(2,1)}), bf16[16,208,128]{2,1,0:T(8,128)(2,1)S(1)}, u32[]{:S(2)}, u32[]{:S(2)}) %all-to-all-start.2) | async-done | bytes 852000 | tf_op jit(solution)/shard_map/all_to_all | solution.py:749
  76.8 3.5 %enter.1 = (f32[512,256]{1,0:T(8,128)}, f32[256,128]{1,0:T(8,128)}, f32[8,8,512]{2,1,0:T(8,128)}, bf16[512,256]{1,0:T(8,128)(2,1)}) custom-call(s32[3]{0:T(128)} %pad_add_fusion.at_ref.refs_0_, bf16[16,208,128]{2,1,0:T(8,128)(2,1)} %copy-done.1, f32[512,256]{1,0:T(8,128)} %get-tuple-element.94.y0_ref, f32[512,256]{1,0:T(8,128)} %get-tuple-element.95.dn_ref, ...), custom_call_target="tpu_custom_call" | custom-call | tf_op jit(solution)/shard_map/enter/pallas_call | solution.py:42
  80.3 11.9 %all_to_all.35.got_ref = f32[8,8,512]{2,1,0:T(8,128)} all-to-all(f32[8,8,512]{2,1,0:T(8,128)} %get-tuple-element.97), channel_id=1, replica_groups=mesh['seq_0'=4,'seq_1'=4,'head_0'=4,'head_1'=2] {'head_0','head_1'}, dimensions={0} | all-to-all | bytes 262144 | tf_op jit(solution)/shard_map/all_to_all | solution.py:749
  92.2 4.2 %gated.1 = (f32[512,256]{1,0:T(8,128)}, f32[512,256]{1,0:T(8,128)}, bf16[512,256]{1,0:T(8,128)(2,1)}, bf16[16,192,128]{2,1,0:T(8,128)(2,1)}, f32[8,256]{1,0:T(8,128)}, /*index=5*/f32[512,128]{1,0:T(8,128)}) custom-call(f32[8,8,512]{2,1,0:T(8,128)} %all_to_all.35.got_ref, f32[512,256]{1,0:T(8,128)} %get-tuple-element.98.y_ref, ...), custom_call_target="tpu_custom_call" | custom-call | tf_op jit(solution)/shard_map/gated/pallas_call | solution.py:42
  96.4 3.8 %all-to-all-start.4 = ((bf16[16,192,128]{2,1,0:T(8,128)(2,1)}), bf16[16,192,128]{2,1,0:T(8,128)(2,1)S(1)}, u32[]{:S(2)}, u32[]{:S(2)}) async-start(bf16[16,192,128]{2,1,0:T(8,128)(2,1)} %get-tuple-element.100), calls=%async_computation.4 | async-start | bytes 1572864 | tf_op jit(solution)/shard_map/all_to_all | solution.py:749
  100.2 6.0 %own_back.1 = (f32[512,256]{1,0:T(8,128)}, f32[512,128]{1,0:T(8,128)}, f32[512,128]{1,0:T(8,128)}, f32[512,128]{1,0:T(8,128)}) custom-call(f32[512,256]{1,0:T(8,128)} %get-tuple-element.102.dy_ref, f32[512,256]{1,0:T(8,128)} %get-tuple-element.98.y_ref, f32[512,256]{1,0:T(8,128)} %get-tuple-element.94.y0_ref, f32[512,640]{1,0:T(8,128)} %get-tuple-element.92.c_ref, ...), custom_call_target="tpu_custom_call" | custom-call | tf_op jit(solution)/shard_map/own_back/pallas_call | solution.py:42
  106.2 7.1 %all-to-all-done.4.got_ref = bf16[16,192,128]{2,1,0:T(8,128)(2,1)S(1)} async-done(((bf16[16,192,128]{2,1,0:T(8,128)(2,1)}), bf16[16,192,128]{2,1,0:T(8,128)(2,1)S(1)}, u32[]{:S(2)}, u32[]{:S(2)}) %all-to-all-start.4) | async-done | bytes 786464 | tf_op jit(solution)/shard_map/all_to_all | solution.py:749
  114.2 11.3 %back.1 = (bf16[528,640]{1,0:T(8,128)(2,1)}, bf16[512,128]{1,0:T(8,128)(2,1)}, bf16[256,768]{1,0:T(8,128)(2,1)}, bf16[256,768]{1,0:T(8,128)(2,1)}, bf16[16,768]{...) custom-call(s32[3]{0:T(128)} %pad_add_fusion.at_ref.refs_0_, ...), custom_call_target="tpu_custom_call" | custom-call | tf_op jit(solution)/shard_map/back/pallas_call | solution.py:42
  125.5 4.6 %grad.1 = bf16[768,896]{1,0:T(8,128)(2,1)} custom-call(bf16[528,768]{1,0:T(8,128)(2,1)} %get-tuple-element.120.normed_ref, bf16[528,640]{1,0:T(8,128)(2,1)} %get-tuple-element.121.dv_ref, bf16[512,128]{1,0:T(8,128)(2,1)} %get-tuple-element.122.dstep_ref, bf16[512,256]{1,0:T(8,128)(2,1)} %get-tuple-element.123.nout_ref, bf16[512,768]{1,0:T(8,128)(2,1)} %cot_ref.3, ...), custom_call_target="tpu_custom_call" | custom-call | tf_op jit(solution)/shard_map/grad/pallas_call | solution.py:42
  130.0 3.8 %all-to-all-start.5 = ((bf16[16,48,896]{2,1,0:T(8,128)(2,1)}), bf16[16,48,896]{2,1,0:T(8,128)(2,1)S(1)}, u32[]{:S(2)}, u32[]{:S(2)}) async-start(bf16[16,48,896]{2,1,0:T(8,128)(2,1)} %bitcast.39), calls=%async_computation.5 | async-start | bytes 2752512 | tf_op jit(solution)/shard_map/all_to_all | solution.py:749
  133.9 2.2 %collective-permute-start.1 = (bf16[256,768]{1,0:T(8,128)(2,1)S(1)}, bf16[256,768]{1,0:T(8,128)(2,1)S(1)}, u32[]{:S(2)}, u32[]{:S(2)}) collective-permute-start(bf16[256,768]{1,0:T(8,128)(2,1)S(1)} %copy-done.23), channel_id=1, source_target_pairs={{0,1},{1,0},{2,3},{3,2},{4,5},{5,4},{6,7},{7,6},{8,9},{9,8},{10,11... | collective-permute-start | bytes 1179656 | tf_op jit(solution)/shard_map/ppermute | solution.py:754
  136.2 2.7 %out.1 = bf16[512,768]{1,0:T(8,128)(2,1)} custom-call(bf16[512,256]{1,0:T(8,128)(2,1)} %get-tuple-element.96.fed_ref, bf16[768,896]{1,0:T(8,128)(2,1)} %bitcast.38), custom_call_target="tpu_custom_call" | custom-call | tf_op jit(solution)/shard_map/out/pallas_call | solution.py:42
  141.5 10.5 %collective-permute-done.2.edge0_ref = bf16[16,768]{1,0:T(8,128)(2,1)S(1)} collective-permute-done((bf16[16,768]{1,0:T(8,128)(2,1)S(1)}, bf16[16,768]{1,0:T(8,128)(2,1)S(1)}, u32[]{:S(2)}, u32[]{:S(2)}) %collective-permute-start.2) | collective-permute-done | bytes 24608 | tf_op jit(solution)/shard_map/ppermute | solution.py:763
  152.8 2.0 pair.1
  155.0 1.8 collective-permute-start.5
  157.6 3.6 %collective-permute-done.4.b_ref = bf16[64,768]{1,0:T(8,128)(2,1)S(1)} collective-permute-done((bf16[64,768]{1,0:T(8,128)(2,1)}, bf16[64,768]{1,0:T(8,128)(2,1)S(1)}, u32[]{:S(2)}, u32[]{:S(2)}) %collective-permute-start.4) | collective-permute-done | bytes 98336 | tf_op jit(solution)/shard_map/ppermute | solution.py:754
  161.2 1.8 collective-permute-done.5.c_ref
  167.2 2.9 %collective-permute-start.8 = (bf16[64,768]{1,0:T(8,128)(2,1)}, bf16[64,768]{1,0:T(8,128)(2,1)S(1)}, u32[]{:S(2)}, u32[]{:S(2)}) collective-permute-start(bf16[64,768]{1,0:T(8,128)(2,1)} %four.1.refs_1_), channel_id=1, source_target_pairs={{0,4},{2,6},{4,0},{6,2},{1,5},{3,7},{5,1},{7,3},{8,12},{10,14},{12... | collective-permute-start | bytes 294920 | tf_op jit(solution)/shard_map/ppermute | solution.py:754
  171.2 2.7 %update.1 = (f32[3,48,128]{2,1,0:T(8,128)}, f32[3,48,128]{2,1,0:T(8,128)}, f32[3,48,128]{2,1,0:T(8,128)}, f32[3,48]{1,0:T(4,128)}, f32[3,48]{1,0:T(4,128)}, /*in...) custom-call(bf16[16,48,896]{2,1,0:T(8,128)(2,1)} %copy-done.2, ...), custom_call_target="tpu_custom_call" | custom-call | tf_op jit(solution)/shard_map/update/pallas_call | solution.py:42
  173.9 3.7 %all-to-all-start.6 = ((f32[8,8,512]{2,1,0:T(8,128)}), f32[8,8,512]{2,1,0:T(8,128)S(1)}, u32[]{:S(2)}, u32[]{:S(2)}) async-start(f32[8,8,512]{2,1,0:T(8,128)} %get-tuple-element.136), calls=%async_computation.6 | async-start | bytes 262144 | tf_op jit(solution)/shard_map/all_to_all | solution.py:749
  178.6 22.7 %all-reduce.4.cloned.1.call-done.sum_ref = bf16[512,768]{1,0:T(8,128)(2,1)} async-done(((bf16[512,768]{1,0:T(8,128)(2,1)}), bf16[512,768]{1,0:T(8,128)(2,1)}) %all-reduce.4.cloned.1.call-update) | async-done | bytes 786448 | tf_op jit(solution)/shard_map/psum | solution.py:825
  201.3 2.6 %block.1 = bf16[512,768]{1,0:T(8,128)(2,1)} custom-call(bf16[512,768]{1,0:T(8,128)(2,1)} %all-reduce.4.cloned.1.call-done.sum_ref, f32[512,128]{1,0:T(8,128)} %get-tuple-element.99.rms_ref, bf16[512,768]{1,0:T(8,128)(2,1)} %refs_9_.2), custom_call_target="tpu_custom_call" | custom-call | tf_op jit(solution)/shard_map/block/pallas_call | solution.py:42
  204.6 3.5 %input.1 = f32[512,768]{1,0:T(8,128)} custom-call(s32[3]{0:T(128)} %pad_add_fusion.at_ref.refs_0_, bf16[64,768]{1,0:T(8,128)(2,1)} %four.1.refs_1_, bf16[64,768]{1,0:T(8,128)(2,1)} %copy-done.12, bf16[64,768]{1,0:T(8,128)(2,1)} %copy-done.13, bf16[64,768]{1,0:T(8,128)(2,1)} %copy-done.14, bf16[64,768]{1,0:T(8,128)(2,1)} %copy-done.15, ...), custom_call_target="tpu_custom_call" | custom-call | tf_op jit(solution)/shard_map/input/pallas_call | solution.py:42
  208.8 1.7 rest.1
  (90 shorter events, 20.7 us)
Async XLA Ops:
  8.6 10.7 %all-to-all-start = ((bf16[8,16,256]{2,1,0:T(8,128)(2,1)}), bf16[8,16,256]{2,1,0:T(8,128)(2,1)S(1)}, u32[]{:S(2)}, u32[]{:S(2)}) async-start(bf16[8,16,256]{2,1,0:T(8,128)(2,1)} %small.1), calls=%async_computation | async-start | bytes 131072 | tf_op jit(solution)/shard_map/all_to_all | solution.py:749
  15.2 4.1 %collective-permute-start = (bf16[16,768]{1,0:T(8,128)(2,1)S(1)}, bf16[16,768]{1,0:T(8,128)(2,1)S(1)}, u32[]{:S(2)}, u32[]{:S(2)}) collective-permute-start(bf16[16,768]{1,0:T(8,128)(2,1)S(1)} %slice.6), channel_id=1, source_target_pairs={{0,8},{8,16},{16,24},{24,32},{32,40},{40,48},{48,56},{56,64},{64,7... | collective-permute-start | bytes 73736 | tf_op jit(solution)/shard_map/ppermute | solution.py:758
  19.3 30.3 %copy-start.8 = (bf16[16,768]{1,0:T(8,128)(2,1)}, bf16[16,768]{1,0:T(8,128)(2,1)S(1)}, u32[]{:S(2)}) copy-start(bf16[16,768]{1,0:T(8,128)(2,1)S(1)} %collective-permute-done.halo_ref) | copy-start | bytes 73732
  22.2 8.4 %copy-start.19 = (f32[6,3,64]{2,1,0:T(4,128)S(1)}, f32[6,3,64]{2,1,0:T(4,128)}, u32[]{:S(2)}) copy-start(f32[6,3,64]{2,1,0:T(4,128)} %refs_10_.3) | copy-start | bytes 13828
  22.2 8.5 %slice-start = ((f32[6,3,64]{2,1,0:T(4,128)}), f32[1,3,64]{2,1,0:T(4,128)S(1)}, s32[]{:S(2)}) async-start(f32[6,3,64]{2,1,0:T(4,128)} %refs_10_.3), calls=%async_computation.8 | async-start | bytes 4096 | tf_op jit(solution)/shard_map/slice | solution.py:801
  22.2 8.6 %copy-start.22 = (s32[512]{0:T(512)S(1)}, s32[512]{0:T(512)}, u32[]{:S(2)}) copy-start(s32[512]{0:T(512)} %param.29) | copy-start | bytes 6148
  22.2 27.4 %all-to-all-start.1 = ((bf16[16,48,896]{2,1,0:T(8,128)(2,1)}), bf16[16,48,896]{2,1,0:T(8,128)(2,1)S(1)}, u32[]{:S(2)}, u32[]{:S(2)}) async-start(bf16[16,48,896]{2,1,0:T(8,128)(2,1)} %pack.1), calls=%async_computation.1 | async-start | bytes 2752512 | tf_op jit(solution)/shard_map/all_to_all | solution.py:749
  56.9 19.0 %all-to-all-start.2 = ((bf16[16,208,128]{2,1,0:T(8,128)(2,1)}), bf16[16,208,128]{2,1,0:T(8,128)(2,1)S(1)}, u32[]{:S(2)}, u32[]{:S(2)}) async-start(bf16[16,208,128]{2,1,0:T(8,128)(2,1)} %get-tuple-element.91), calls=%async_computation.2 | async-start | bytes 1703936 | tf_op jit(solution)/shard_map/all_to_all | solution.py:749
  96.4 16.9 %all-to-all-start.4 = ((bf16[16,192,128]{2,1,0:T(8,128)(2,1)}), bf16[16,192,128]{2,1,0:T(8,128)(2,1)S(1)}, u32[]{:S(2)}, u32[]{:S(2)}) async-start(bf16[16,192,128]{2,1,0:T(8,128)(2,1)} %get-tuple-element.100), calls=%async_computation.4 | async-start | bytes 1572864 | tf_op jit(solution)/shard_map/all_to_all | solution.py:749
  130.0 3.9 %copy-start.23 = (bf16[256,768]{1,0:T(8,128)(2,1)S(1)}, bf16[256,768]{1,0:T(8,128)(2,1)}, u32[]{:S(2)}) copy-start(bf16[256,768]{1,0:T(8,128)(2,1)} %get-tuple-element.113) | copy-start | bytes 1179652
  130.0 40.1 %all-to-all-start.5 = ((bf16[16,48,896]{2,1,0:T(8,128)(2,1)}), bf16[16,48,896]{2,1,0:T(8,128)(2,1)S(1)}, u32[]{:S(2)}, u32[]{:S(2)}) async-start(bf16[16,48,896]{2,1,0:T(8,128)(2,1)} %bitcast.39), calls=%async_computation.5 | async-start | bytes 2752512 | tf_op jit(solution)/shard_map/all_to_all | solution.py:749
  133.9 67.4 %all-reduce.4.cloned.1.call-start = ((), (), s32[]{:S(2)}) async-start(), calls=%async_computation.7 | async-start | bytes 1572864 | tf_op jit(solution)/shard_map/psum | solution.py:825
  133.9 18.1 %collective-permute-start.1 = (bf16[256,768]{1,0:T(8,128)(2,1)S(1)}, bf16[256,768]{1,0:T(8,128)(2,1)S(1)}, u32[]{:S(2)}, u32[]{:S(2)}) collective-permute-start(bf16[256,768]{1,0:T(8,128)(2,1)S(1)} %copy-done.23), channel_id=1, source_target_pairs={{0,1},{1,0},{2,3},{3,2},{4,5},{5,4},{6,7},{7,6},{8,9},{9,8},{10,11... | collective-permute-start | bytes 1179656 | tf_op jit(solution)/shard_map/ppermute | solution.py:754
  136.2 2.8 %copy-start.24 = (bf16[16,768]{1,0:T(8,128)(2,1)S(1)}, bf16[16,768]{1,0:T(8,128)(2,1)}, u32[]{:S(2)}) copy-start(bf16[16,768]{1,0:T(8,128)(2,1)} %get-tuple-element.114) | copy-start | bytes 73732
  138.9 13.1 %collective-permute-start.2 = (bf16[16,768]{1,0:T(8,128)(2,1)S(1)}, bf16[16,768]{1,0:T(8,128)(2,1)S(1)}, u32[]{:S(2)}, u32[]{:S(2)}) collective-permute-start(bf16[16,768]{1,0:T(8,128)(2,1)S(1)} %copy-done.24), channel_id=1, source_target_pairs={{8,1},{16,9},{24,17},{32,25},{40,33},{48,41},{56,49},{64,57},{72,6... | collective-permute-start | bytes 73736 | tf_op jit(solution)/shard_map/ppermute | solution.py:763
  140.2 11.8 %collective-permute-start.3 = (bf16[16,768]{1,0:T(8,128)(2,1)S(1)}, bf16[16,768]{1,0:T(8,128)(2,1)S(1)}, u32[]{:S(2)}, u32[]{:S(2)}) collective-permute-start(bf16[16,768]{1,0:T(8,128)(2,1)S(1)} %copy-done.24), channel_id=1, source_target_pairs={{9,1},{17,9},{25,17},{33,25},{41,33},{49,41},{57,49},{65,57},{73,6... | collective-permute-start | bytes 73736 | tf_op jit(solution)/shard_map/ppermute | solution.py:763
  154.8 6.3 %collective-permute-start.4 = (bf16[64,768]{1,0:T(8,128)(2,1)}, bf16[64,768]{1,0:T(8,128)(2,1)S(1)}, u32[]{:S(2)}, u32[]{:S(2)}) collective-permute-start(bf16[64,768]{1,0:T(8,128)(2,1)} %get-tuple-element.116), channel_id=1, source_target_pairs={{0,2},{2,4},{4,6},{6,0},{1,3},{3,5},{5,7},{7,1},{8,10},{10,12},{12... | collective-permute-start | bytes 294920 | tf_op jit(solution)/shard_map/ppermute | solution.py:754
  155.0 7.9 %collective-permute-start.5 = (bf16[64,768]{1,0:T(8,128)(2,1)}, bf16[64,768]{1,0:T(8,128)(2,1)S(1)}, u32[]{:S(2)}, u32[]{:S(2)}) collective-permute-start(bf16[64,768]{1,0:T(8,128)(2,1)} %get-tuple-element.117), channel_id=1, source_target_pairs={{0,4},{2,6},{4,0},{6,2},{1,5},{3,7},{5,1},{7,3},{8,12},{10,14},{12... | collective-permute-start | bytes 294920 | tf_op jit(solution)/shard_map/ppermute | solution.py:754
  156.8 7.9 %collective-permute-start.6 = (bf16[64,768]{1,0:T(8,128)(2,1)}, bf16[64,768]{1,0:T(8,128)(2,1)S(1)}, u32[]{:S(2)}, u32[]{:S(2)}) collective-permute-start(bf16[64,768]{1,0:T(8,128)(2,1)} %get-tuple-element.118), channel_id=1, source_target_pairs={{0,6},{2,0},{4,2},{6,4},{1,7},{3,1},{5,3},{7,5},{8,14},{10,8},{12,... | collective-permute-start | bytes 294920 | tf_op jit(solution)/shard_map/ppermute | solution.py:754
  161.2 3.5 %copy-start.9 = (bf16[64,768]{1,0:T(8,128)(2,1)}, bf16[64,768]{1,0:T(8,128)(2,1)S(1)}, u32[]{:S(2)}) copy-start(bf16[64,768]{1,0:T(8,128)(2,1)S(1)} %collective-permute-done.4.b_ref) | copy-start | bytes 294916
  167.1 10.5 %copy-start.6 = (bf16[64,768]{1,0:T(8,128)(2,1)S(1)}, bf16[64,768]{1,0:T(8,128)(2,1)}, u32[]{:S(2)}) copy-start(bf16[64,768]{1,0:T(8,128)(2,1)} %four.1.refs_1_) | copy-start | bytes 294916
  167.1 10.6 %collective-permute-start.7 = (bf16[64,768]{1,0:T(8,128)(2,1)}, bf16[64,768]{1,0:T(8,128)(2,1)S(1)}, u32[]{:S(2)}, u32[]{:S(2)}) collective-permute-start(bf16[64,768]{1,0:T(8,128)(2,1)} %four.1.refs_1_), channel_id=1, source_target_pairs={{0,2},{2,4},{4,6},{6,0},{1,3},{3,5},{5,7},{7,1},{8,10},{10,12},{12... | collective-permute-start | bytes 294920 | tf_op jit(solution)/shard_map/ppermute | solution.py:754
  167.2 10.9 %collective-permute-start.8 = (bf16[64,768]{1,0:T(8,128)(2,1)}, bf16[64,768]{1,0:T(8,128)(2,1)S(1)}, u32[]{:S(2)}, u32[]{:S(2)}) collective-permute-start(bf16[64,768]{1,0:T(8,128)(2,1)} %four.1.refs_1_), channel_id=1, source_target_pairs={{0,4},{2,6},{4,0},{6,2},{1,5},{3,7},{5,1},{7,3},{8,12},{10,14},{12... | collective-permute-start | bytes 294920 | tf_op jit(solution)/shard_map/ppermute | solution.py:754
  170.1 8.1 %collective-permute-start.9 = (bf16[64,768]{1,0:T(8,128)(2,1)}, bf16[64,768]{1,0:T(8,128)(2,1)S(1)}, u32[]{:S(2)}, u32[]{:S(2)}) collective-permute-start(bf16[64,768]{1,0:T(8,128)(2,1)} %four.1.refs_1_), channel_id=1, source_target_pairs={{0,6},{2,0},{4,2},{6,4},{1,7},{3,1},{5,3},{7,5},{8,14},{10,8},{12,... | collective-permute-start | bytes 294920 | tf_op jit(solution)/shard_map/ppermute | solution.py:754
  173.9 34.3 %all-to-all-start.6 = ((f32[8,8,512]{2,1,0:T(8,128)}), f32[8,8,512]{2,1,0:T(8,128)S(1)}, u32[]{:S(2)}, u32[]{:S(2)}) async-start(f32[8,8,512]{2,1,0:T(8,128)} %get-tuple-element.136), calls=%async_computation.6 | async-start | bytes 262144 | tf_op jit(solution)/shard_map/all_to_all | solution.py:749
  177.6 26.3 %collective-permute-start.10 = (bf16[64,768]{1,0:T(8,128)(2,1)S(1)}, bf16[64,768]{1,0:T(8,128)(2,1)S(1)}, u32[]{:S(2)}, u32[]{:S(2)}) collective-permute-start(bf16[64,768]{1,0:T(8,128)(2,1)S(1)} %copy-done.6), channel_id=1, source_target_pairs={{0,1},{1,0},{2,3},{3,2},{4,5},{5,4},{6,7},{7,6},{8,9},{9,8},{10,11... | collective-permute-start | bytes 294920 | tf_op jit(solution)/shard_map/ppermute | solution.py:754
  177.7 26.3 %copy-start.12 = (bf16[64,768]{1,0:T(8,128)(2,1)}, bf16[64,768]{1,0:T(8,128)(2,1)S(1)}, u32[]{:S(2)}) copy-start(bf16[64,768]{1,0:T(8,128)(2,1)S(1)} %collective-permute-done.7.refs_2_) | copy-start | bytes 294916
  177.7 26.2 %collective-permute-start.11 = (bf16[64,768]{1,0:T(8,128)(2,1)S(1)}, bf16[64,768]{1,0:T(8,128)(2,1)S(1)}, u32[]{:S(2)}, u32[]{:S(2)}) collective-permute-start(bf16[64,768]{1,0:T(8,128)(2,1)S(1)} %collective-permute-done.7.refs_2_), channel_id=1, source_target_pairs={{0,1},{1,0},{2,3},{3,2},{4,5},{5,4},{6,7},{7,6},{8,9},{9,8},{10,11... | collective-permute-start | bytes 294920 | tf_op jit(solution)/shard_map/ppermute | solution.py:754
  178.1 25.9 %copy-start.13 = (bf16[64,768]{1,0:T(8,128)(2,1)}, bf16[64,768]{1,0:T(8,128)(2,1)S(1)}, u32[]{:S(2)}) copy-start(bf16[64,768]{1,0:T(8,128)(2,1)S(1)} %collective-permute-done.8.refs_3_) | copy-start | bytes 294916
  178.1 25.8 %collective-permute-start.12 = (bf16[64,768]{1,0:T(8,128)(2,1)S(1)}, bf16[64,768]{1,0:T(8,128)(2,1)S(1)}, u32[]{:S(2)}, u32[]{:S(2)}) collective-permute-start(bf16[64,768]{1,0:T(8,128)(2,1)S(1)} %collective-permute-done.8.refs_3_), channel_id=1, source_target_pairs={{0,1},{1,0},{2,3},{3,2},{4,5},{5,4},{6,7},{7,6},{8,9},{9,8},{10,11... | collective-permute-start | bytes 294920 | tf_op jit(solution)/shard_map/ppermute | solution.py:754
  178.2 25.8 %copy-start.14 = (bf16[64,768]{1,0:T(8,128)(2,1)}, bf16[64,768]{1,0:T(8,128)(2,1)S(1)}, u32[]{:S(2)}) copy-start(bf16[64,768]{1,0:T(8,128)(2,1)S(1)} %collective-permute-done.9.refs_4_) | copy-start | bytes 294916
  178.2 25.7 %collective-permute-start.13 = (bf16[64,768]{1,0:T(8,128)(2,1)S(1)}, bf16[64,768]{1,0:T(8,128)(2,1)S(1)}, u32[]{:S(2)}, u32[]{:S(2)}) collective-permute-start(bf16[64,768]{1,0:T(8,128)(2,1)S(1)} %collective-permute-done.9.refs_4_), channel_id=1, source_target_pairs={{0,1},{1,0},{2,3},{3,2},{4,5},{5,4},{6,7},{7,6},{8,9},{9,8},{10,11... | collective-permute-start | bytes 294920 | tf_op jit(solution)/shard_map/ppermute | solution.py:754
  (15 other events, 12.3 us)
Sparse Core Ops, SparseCore 0:
  139.0 62.1 all-reduce.3

commit v3 on v2

--- a/solution.py
+++ b/solution.py
@@ -20,8 +20,10 @@
 T = 512
 HALO = 16
 NV = 640
-NW = 896
+NW = 640
+NG = 896
 MISC = 64
+SLAB = 96
 SROWS = 208
 
 f32 = jnp.float32
@@ -148,10 +150,6 @@
     return jnp.where(lanes(v.shape[0]) < 3, total, 0.0)
 
 
-def aux_parts(aux):
-    return aux
-
-
 def act_tiles(c_ref):
     return [silu(c_ref[:, 128 * k : 128 * (k + 1)]) for k in range(5)]
 
@@ -171,67 +169,91 @@
 def selector():
     r = lax.broadcasted_iota(jnp.int32, (D, 256), 0)
     k = lax.broadcasted_iota(jnp.int32, (D, 256), 1)
-    return jnp.where(r == k + 32 * jnp.right_shift(k, 4), 1.0, 0.0).astype(bf16)
-
-
-def small_kernel(shared_ref, gain_ref, conv_ref, out_ref, rows_ref):
-    rows_ref[...] = jnp.zeros_like(rows_ref)
-    rows_ref[0:6, :] = shared_ref[...]
-    gain = gain_ref[...]
-    high = gain.astype(bf16).astype(f32)
-    rows_ref[6:7, 0:6] = high
-    rows_ref[6:7, 128:134] = gain - high
-    conv = conv_ref[...]
-    high = conv.astype(bf16).astype(f32)
-    rows_ref[8:10, MISC + 5 : MISC + 10] = high
-    rows_ref[8:10, MISC + 10 : MISC + 15] = conv - high
-    low = rows_ref[...].astype(bf16)
-    for q in range(N_HEAD):
-        out_ref[q] = low
+    h = jnp.bitwise_and(jnp.right_shift(k, 1), 7)
+    at = 48 * jnp.right_shift(k, 4) + 6 * h + jnp.bitwise_and(k, 1)
+    return jnp.where(r == at, 1.0, 0.0).astype(bf16)
+
+
+def slab_rows(a):
+    s = jnp.right_shift(a * 43, 8)
+    return 42 * s + a
 
 
 def pack_kernel(
-    got_ref, proj_ref, outw_ref, step_ref, pack_ref, shared_ref, misc_ref, wide_ref
+    proj_ref, outw_ref, step_ref, shared_ref, gain_ref, conv_ref, pack_ref, misc_ref, wide_ref
 ):
     misc_ref[...] = jnp.zeros_like(misc_ref)
     misc_ref[0:3, 0:48] = step_ref[...]
-    misc = half(misc_ref[...].T)[0:48]
-    misc_ref[0:48, :] = misc
+    misc_ref[0:48, :] = half(misc_ref[...].T)[0:48]
+    wide_ref[...] = jnp.zeros_like(wide_ref)
+    wide_ref[0:1, 0:6] = gain_ref[...]
     sub = lax.broadcasted_iota(jnp.int32, (6, 128), 0)
     lane = lanes(6)
-    for q in range(N_HEAD):
-        rows = got_ref[q].astype(f32)
-        shared_ref[6 * q : 6 * q + 6, :] = rows[0:6]
-        part = jnp.zeros((6, 128), f32)
-        for k in range(2):
-            line = rows[6:7, 128 * k : 128 * (k + 1)]
-            column = jnp.sum(jnp.where(sub == lane, line, 0.0), axis=1, keepdims=True)
-            part = part + jnp.where(lane == MISC + 3 + k, column, 0.0)
-        misc_ref[6 * q : 6 * q + 6, :] += part
-        misc_ref[2 * q : 2 * q + 2, :] += rows[8:10, 0:128]
+    column = jnp.sum(jnp.where(sub == lane, wide_ref[0:1, :], 0.0), axis=1, keepdims=True)
+    high = column.astype(bf16).astype(f32)
+    misc_ref[0:6, :] += jnp.where(lane == MISC + 3, high, 0.0) + jnp.where(
+        lane == MISC + 4, column - high, 0.0
+    )
+    conv = conv_ref[...]
+    high = conv.astype(bf16).astype(f32)
+    misc_ref[0:2, MISC + 5 : MISC + 10] = high
+    misc_ref[0:2, MISC + 10 : MISC + 15] = conv - high
+    for j in range(8):
+        tile = rolled(shared_ref[:, 128 * (j // 4) : 128 * (j // 4) + 128], SLAB - 32 * (j % 4))
+        misc_ref[6 * j : 6 * j + 6, :] += jnp.where(lane >= SLAB, tile, 0.0)
     misc = misc_ref[0:48, :]
     lo = lanes(48) < 64
-    tiles = [proj_ref[h] for h in range(3)]
     wide = []
     for h in range(3):
         wide_ref[:, 0:64] = outw_ref[h]
         wide.append(wide_ref[...])
+    tiles = [proj_ref[h] for h in range(3)]
     tiles += [jnp.where(lo, wide[0], half(wide[1])), jnp.where(lo, wide[2], misc)]
-    tiles += [shared_ref[:, 0:128], shared_ref[:, 128:256]]
     for k, tile in enumerate(tiles):
         low = tile.astype(bf16)
         for q in range(N_SEQ):
             pack_ref[q, :, 128 * k : 128 * (k + 1)] = low
 
 
-def first_kernel(
-    hid_ref, halo_ref, st_ref, w_ref, tap_ref, hp_ref,
-    normed_ref, v_ref, c_ref, aux_ref, send_ref, row_ref,
-):
-    misc_t = w_ref[:, 512:640].astype(f32).T
+def slab_kernel(w_ref, slab_ref):
+    misc = w_ref[:, 512:640]
+    a = lax.broadcasted_iota(jnp.int32, (96, D), 0)
+    d = lax.broadcasted_iota(jnp.int32, (96, D), 1)
+    gap = d - slab_rows(a)
+    lane = lanes(96)
+    tiles = [jnp.zeros((96, 128), f32)] * 2
+    for j in range(8):
+        got = dot(jnp.where(gap == 6 * j, 1.0, 0.0).astype(bf16), misc)
+        if j == 0:
+            slab_ref[:, 256:384] = jnp.where(lane < SLAB, got, 0.0).astype(bf16)
+        own = jnp.where(lane >= SLAB, got, 0.0)
+        tiles[j // 4] = tiles[j // 4] + rolled(own, 32 * (j % 4) - SLAB)
+    slab_ref[:, 0:128] = tiles[0].astype(bf16)
+    slab_ref[:, 128:256] = tiles[1].astype(bf16)
+
+
+def first_kernel(*refs):
+    at_ref, slabs, refs = refs[0], refs[1:9], refs[9:]
+    hid_ref, halo_ref, st_ref, w_ref, tap_ref, hp_ref = refs[:6]
+    normed_ref, v_ref, c_ref, aux_ref, send_ref, row_ref, wide_ref, ctap_ref = refs[6:14]
+    all_ref = refs[14]
+    d = lax.broadcasted_iota(jnp.int32, (D, 96), 0)
+    a = lax.broadcasted_iota(jnp.int32, (D, 96), 1)
+    gap = d - slab_rows(a)
+    picks = []
+    for b in range(8):
+        core = at_ref[2] if b < 4 else 1 - at_ref[2]
+        head = 2 * lax.rem(at_ref[1] + 4 - b % 4, 4) + core
+        all_ref[96 * b : 96 * b + 96, :] = slabs[b][...]
+        picks.append(jnp.where(gap == 6 * head, 1.0, 0.0))
+    spread_rows = dot(jnp.concatenate(picks, axis=1).astype(bf16), all_ref[...])
+    wide_ref[...] = spread_rows[:, 0:256].astype(bf16)
+    misc_t = spread_rows[:, 256:384].T
     gain = misc_t[MISC + 3 : MISC + 4] + misc_t[MISC + 4 : MISC + 5]
     conv_t = dot(misc_t.astype(bf16), selector())
     conv_taps = conv_t[MISC + 5 : MISC + 10] + conv_t[MISC + 10 : MISC + 15]
+    ctap_ref[0:5, :] = conv_taps
+    ctap_ref[5:8, :] = jnp.zeros((3, 256), f32)
     row_ref[0:1, :] = gain
     row_ref[1:8, :] = jnp.zeros((7, D), f32)
     for src, at, rows in ((halo_ref, 0, HALO), (hid_ref, HALO, T)):
@@ -240,7 +262,7 @@
         normed_ref[at : at + rows, :] = (h * inv * gain).astype(bf16)
     normed = normed_ref[...]
     v_ref[:, 0:384] = dot(normed, w_ref[:, 0:384])
-    v_ref[:, 384:640] = dot(normed, w_ref[:, 640:896])
+    v_ref[:, 384:640] = dot(normed, wide_ref[...])
     raw = half(dot(normed[HALO:], w_ref[:, 512:640]))
 
     lane = lanes(T)
@@ -346,7 +368,7 @@
 
 def enter_kernel(
     at_ref, got_ref, y0_ref, dn_ref, c_ref, aux_ref, tap_ref,
-    y_ref, state_ref, stat_ref, fed_ref,
+    y_ref, state_ref, stat_ref,
 ):
     here = at_ref[0]
     state = jnp.zeros((192, 128), f32)
@@ -369,26 +391,21 @@
         y_ref[:, at] = y
         gated = y * gate[k]
         fed = gated * tap_ref[0:1, 384 + 128 * k : 512 + 128 * k]
-        fed_ref[:, at] = fed.astype(bf16)
         squares = squares + jnp.sum(gated * gated, axis=1, keepdims=True)
         inner = inner + jnp.sum(fed * dn_ref[:, at], axis=1, keepdims=True)
     lane = lanes(T)
     both = jnp.where(lane == 0, squares, jnp.where(lane == 1, inner, 0.0)).T
-    for q in range(N_HEAD):
-        stat_ref[q] = both[0:8]
+    stat_ref[...] = both[0:8]
 
 
 def gated_kernel(
-    got_ref, y_ref, dn_ref, c_ref, aux_ref, tap_ref,
-    dy_ref, dgate_ref, nout_ref, send_ref, rows_ref, rms_ref,
+    s0_ref, s1_ref, s2_ref, s3_ref, y_ref, dn_ref, c_ref, aux_ref, tap_ref,
+    dy_ref, dgate_ref, nout_ref, send_ref, rows_ref,
 ):
-    total = got_ref[0]
-    for q in range(1, N_HEAD):
-        total = total + got_ref[q]
+    total = s0_ref[...] + s1_ref[...] + s2_ref[...] + s3_ref[...]
     total = jnp.concatenate([total, jnp.zeros((120, T), f32)], axis=0).T
     rms = lax.rsqrt(total[:, 0:1] / DI + norm_eps)
     coef = rms * rms * rms * total[:, 1:2] / DI
-    rms_ref[...] = jnp.broadcast_to(rms, (T, 128))
     aux = aux_ref[...]
     keeper = spread(aux, 10)
     raw = gate_pair(*[c_ref[:, 128 * k : 128 * (k + 1)] for k in range(3)])
@@ -418,23 +435,55 @@
         send_ref[q] = adj
 
 
-def out_kernel(fed_ref, w_ref, out_ref):
-    out_ref[...] = dot(fed_ref[...], w_ref[:, 384:640], 1, 1).astype(bf16)
-
-
-def block_kernel(sum_ref, rms_ref, hid_ref, out_ref):
-    rms = rms_ref[:, 0:1]
-    out_ref[...] = (hid_ref[...].astype(f32) + rms * sum_ref[...].astype(f32)).astype(bf16)
+def halves(ref, core):
+    keep = ref[pl.ds(pl.multiple_of(core * 256, 256), 256), :]
+    give = ref[pl.ds(pl.multiple_of(256 - core * 256, 256), 256), :]
+    return keep.astype(bf16), give.astype(bf16)
+
+
+def clear_edges(pad_ref):
+    pad_ref[0:HALO] = jnp.zeros((HALO, 128), f32)
+    pad_ref[HALO + T :] = jnp.zeros((HALO, 128), f32)
+
+
+def conv_back(d_conv, taps, v_ref, at, valid, pad_ref):
+    sums = [None, None, None, None, jnp.sum(d_conv, axis=0, keepdims=True)]
+    sums[3] = jnp.sum(d_conv * v_ref[HALO:, at], axis=0, keepdims=True)
+    pad_ref[HALO : HALO + T] = taps[3:4] * d_conv
+    acc = pad_ref[0 : HALO + T]
+    for lag in (1, 2, 3):
+        masked = d_conv * valid[lag - 1]
+        sums[3 - lag] = jnp.sum(
+            masked * v_ref[pl.ds(HALO - lag, T), at], axis=0, keepdims=True
+        )
+        pad_ref[HALO : HALO + T] = taps[3 - lag : 4 - lag] * masked
+        acc = acc + pad_ref[pl.ds(lag, HALO + T)]
+    return acc, sums
 
 
 def own_back_kernel(
-    dy_ref, y_ref, y0_ref, c_ref, aux_ref, m_ref, mg_ref, state_ref,
-    dx_ref, db_ref, dc_ref, dcum_ref,
+    at_ref, dy_ref, y_ref, y0_ref, c_ref, aux_ref, m_ref, mg_ref, state_ref, nout_ref, w_ref,
+    v_ref, ctap_ref, st_ref,
+    dx_ref, db_ref, dcum_ref, xs_ref, b_ref, slope_ref, keep_ref, give_ref, dvc_ref, crow_ref,
+    pad_ref, norm_ref,
 ):
+    norm_ref[...] = dot(nout_ref[...], w_ref[:, 384:640], 1, 1)
+    keep_ref[...], give_ref[...] = halves(norm_ref, at_ref[2])
     aux = aux_ref[...]
     aux_t = aux.T
-    act = act_tiles(c_ref)
+    act = []
+    for k in range(5):
+        at = slice(128 * k, 128 * (k + 1))
+        v = c_ref[:, at]
+        s = sig(v)
+        act.append(v * s)
+        slope = s * (1.0 + v * (1.0 - s))
+        if k < 4:
+            slope_ref[:, at] = slope
     x = x_pair(*act[:3])
+    xs_ref[:, 0:128] = x[0]
+    xs_ref[:, 128:256] = x[1]
+    b_ref[...] = act[3].astype(bf16)
     b_low, c_low = act[3].astype(bf16), act[4].astype(bf16)
     dy = pair_of(dy_ref)
     lo = lanes(T) < 64
@@ -461,7 +510,12 @@
     low = spread_sum.astype(bf16)
     keeper = spread(aux, 10)
     kept = jnp.concatenate([dy[0] * keeper[0], dy[1] * keeper[1]], axis=1).astype(bf16)
-    dc_ref[...] = dot(low, b_low) + dot(kept, state_ref[...].astype(bf16))
+    d_c = dot(low, b_low) + dot(kept, state_ref[...].astype(bf16))
+    valid = valid_masks(column_of(st_ref))
+    clear_edges(pad_ref)
+    dv, sums = conv_back(d_c * slope, ctap_ref[0:5, 128:256], v_ref, slice(512, 640), valid, pad_ref)
+    dvc_ref[...] = dv.astype(bf16)
+    crow_ref[...] = jnp.concatenate([*sums, jnp.zeros((3, 128), f32)], axis=0)
     db_ref[...] = dot(low, c_low, 0, 0)
     dx_ref[:, 0:128] = dx[0]
     dx_ref[:, 128:256] = dx[1]
@@ -473,8 +527,9 @@
 
 
 def back_kernel(
-    at_ref, got_ref, fwd_ref, state_ref, dx_ref, db_ref, dc_ref, dcum_ref, c_ref, aux_ref,
-    v_ref, tap_ref, hp_ref, st_ref, dy_ref, dgate_ref, w_ref, rows_ref, hid_ref, halo_ref,
+    at_ref, got_ref, fwd_ref, state_ref, dx_ref, db_ref, dcum_ref, xs_ref, b_ref, slope_ref,
+    dvc_ref, crow_ref, aux_ref, v_ref, tap_ref, ctap_ref, hp_ref, st_ref, dy_ref, dgate_ref,
+    w_ref, wide_ref, rows_ref, hid_ref, halo_ref,
     dv_ref, dstep_ref, keep_ref, give_ref, edge_ref, chan_ref, conv_ref, gain_ref,
     pad_ref, norm_ref,
 ):
@@ -486,10 +541,8 @@
         adj = jnp.where(q > here, merged, adj)
     aux = aux_ref[...]
     lane = lanes(T)
-    conv = [c_ref[:, 128 * k : 128 * (k + 1)] for k in range(5)]
-    sigs = [sig(v) for v in conv]
-    x = x_pair(*[conv[k] * sigs[k] for k in range(3)])
-    b_low = (conv[3] * sigs[3]).astype(bf16)
+    x = pair_of(xs_ref)
+    b_low = b_ref[...]
     delta, ending = spread(aux, 3), spread(aux, 13)
     adj_low = jnp.concatenate([adj, jnp.zeros((64, 128), f32)], axis=0).astype(bf16)
     through_b = dot(b_low, adj_low, 1, 1)
@@ -532,35 +585,23 @@
     x_tiles = head_tiles((jnp.zeros_like(d_x[0]),) * 2, d_x)
     gate_tiles = head_tiles(d_gate, (jnp.zeros_like(d_x[0]),) * 2)
     lo = lane < 64
-    conv_t = dot(w_ref[:, 512:640].astype(f32).T.astype(bf16), selector())
-    conv_taps = conv_t[MISC + 5 : MISC + 10] + conv_t[MISC + 10 : MISC + 15]
-    starts = column_of(st_ref)
-    valid = valid_masks(starts)
-    pad_ref[0:HALO] = jnp.zeros((HALO, 128), f32)
-    pad_ref[HALO + T :] = jnp.zeros((HALO, 128), f32)
+    valid = valid_masks(column_of(st_ref))
+    clear_edges(pad_ref)
     tap_rows = []
-    for k in range(5):
+    for k in range(4):
         at = slice(128 * k, 128 * (k + 1))
-        slope = sigs[k] * (1.0 + conv[k] * (1.0 - sigs[k]))
+        slope = slope_ref[:, at]
         if k < 3:
             d_conv = jnp.where(lo, gate_tiles[k], x_tiles[k] * slope)
             taps = tap_ref[0:5, at]
         else:
-            d_conv = (d_b if k == 3 else dc_ref[...]) * slope
-            taps = conv_taps[:, 128 * (k - 3) : 128 * (k - 2)]
-        sums = [None, None, None, None, jnp.sum(d_conv, axis=0, keepdims=True)]
-        sums[3] = jnp.sum(d_conv * v_ref[HALO:, at], axis=0, keepdims=True)
-        pad_ref[HALO : HALO + T] = taps[3:4] * d_conv
-        acc = pad_ref[0 : HALO + T]
-        for lag in (1, 2, 3):
-            masked = d_conv * valid[lag - 1]
-            sums[3 - lag] = jnp.sum(
-                masked * v_ref[pl.ds(HALO - lag, T), at], axis=0, keepdims=True
-            )
-            pad_ref[HALO : HALO + T] = taps[3 - lag : 4 - lag] * masked
-            acc = acc + pad_ref[pl.ds(lag, HALO + T)]
-        dv_ref[:, at] = acc.astype(bf16)
+            d_conv = d_b * slope
+            taps = ctap_ref[0:5, 0:128]
+        dv, sums = conv_back(d_conv, taps, v_ref, at, valid, pad_ref)
+        dv_ref[:, at] = dv.astype(bf16)
         tap_rows.append(sums)
+    dv_ref[:, 512:640] = dvc_ref[...]
+    tap_rows.append([crow_ref[j : j + 1, :] for j in range(5)])
 
     chan_ref_rows = []
     for j in range(5):
@@ -581,12 +622,10 @@
     conv_ref[5:8, :] = jnp.zeros((3, 256), f32)
 
     d_norm = dot(dv_ref[:, 0:384], w_ref[:, 0:384], 1, 1)
-    d_norm = d_norm + dot(dv_ref[:, 384:640], w_ref[:, 640:896], 1, 1)
+    d_norm = d_norm + dot(dv_ref[:, 384:640], wide_ref[...], 1, 1)
     main = d_norm[HALO:] + dot(step_low, w_ref[:, 512:640], 1, 1)
     norm_ref[...] = main
-    core = at_ref[2]
-    keep_ref[...] = norm_ref[pl.ds(pl.multiple_of(core * 256, 256), 256), :].astype(bf16)
-    give_ref[...] = norm_ref[pl.ds(pl.multiple_of(256 - core * 256, 256), 256), :].astype(bf16)
+    keep_ref[...], give_ref[...] = halves(norm_ref, at_ref[2])
     edge_ref[...] = d_norm[0:HALO].astype(bf16)
     total = jnp.zeros((1, D), f32)
     for src, val in ((halo_ref, d_norm[0:HALO]), (hid_ref, main)):
@@ -627,36 +666,45 @@
     out_ref[:, 512:640] = tile.astype(bf16)
 
 
-def pair_kernel(at_ref, keep_ref, got_ref, edge0_ref, edge1_ref, own_ref, s1, s2, s3, sum_ref):
-    sum_ref[...] = keep_ref[...].astype(f32) + got_ref[...].astype(f32)
-    sum_ref[256 - HALO :, :] += edge0_ref[...].astype(f32) + edge1_ref[...].astype(f32)
+def pair_kernel(
+    at_ref, keep_ref, got_ref, edge0_ref, edge1_ref, out_keep_ref, out_got_ref,
+    own_ref, s1, s2, s3, sum_ref,
+):
+    sum_ref[:, 0:D] = keep_ref[...].astype(f32) + got_ref[...].astype(f32)
+    sum_ref[256 - HALO :, 0:D] += edge0_ref[...].astype(f32) + edge1_ref[...].astype(f32)
+    sum_ref[:, D:] = out_keep_ref[...].astype(f32) + out_got_ref[...].astype(f32)
     for by, ref in enumerate((own_ref, s1, s2, s3)):
         start = pl.multiple_of(lax.rem(at_ref[1] + by, 4) * 64, 64)
         ref[...] = sum_ref[pl.ds(start, 64), :].astype(bf16)
 
 
-def four_kernel(a_ref, b_ref, c_ref, d_ref, out_ref):
+def four_kernel(at_ref, a_ref, b_ref, c_ref, d_ref, hid_ref, out_ref):
     total = a_ref[...].astype(f32) + b_ref[...].astype(f32)
-    out_ref[...] = (total + c_ref[...].astype(f32) + d_ref[...].astype(f32)).astype(bf16)
+    total = total + c_ref[...].astype(f32) + d_ref[...].astype(f32)
+    start = pl.multiple_of((4 * at_ref[2] + at_ref[1]) * 64, 64)
+    out_ref[:, 0:D] = total[:, 0:D].astype(bf16)
+    out_ref[:, D:] = (total[:, D:] + hid_ref[pl.ds(start, 64), :].astype(f32)).astype(bf16)
 
 
 def input_kernel(*refs):
     at_ref, refs = refs[0], refs[1:]
-    hid_ref, cot_ref, row_ref, out_ref = refs[8:]
+    hid_ref, cot_ref, row_ref, out_ref, block_ref = refs[8:]
     for side in range(2):
         core = at_ref[2] if side == 0 else 1 - at_ref[2]
         for by in range(4):
             block = core * 4 + lax.rem(at_ref[1] + 4 - by, 4)
             rows = pl.ds(pl.multiple_of(block * 64, 64), 64)
+            piece = refs[4 * side + by]
             h = hid_ref[rows, :].astype(f32)
             inv = lax.rsqrt(jnp.mean(h * h, axis=1, keepdims=True) + norm_eps)
-            d_scaled = refs[4 * side + by][...].astype(f32) * row_ref[0:1, :]
+            d_scaled = piece[:, 0:D].astype(f32) * row_ref[0:1, :]
             inner = jnp.sum(d_scaled * h, axis=1, keepdims=True)
             out_ref[rows, :] = (
                 cot_ref[rows, :].astype(f32)
                 + inv * d_scaled
                 - h * (inv * inv * inv * inner / D)
             )
+            block_ref[rows, :] = piece[:, D:]
 
 
 def adam(weight, grad, first, second, rate):
@@ -693,7 +741,6 @@
     for h in range(N_HEAD):
         rest_ref[h, 0:6, 0:256] = total[6 * h : 6 * h + 6, 640:896]
         rest_ref[h, 0:6, 256:384] = misc[6 * h : 6 * h + 6]
-        rest_ref[h, 0:2, 384:512] = misc[2 * h : 2 * h + 2]
     for h in range(3):
         w, m, v = (r[h] for r in proj)
         put(proj_o, h, adam(w, total[:, 128 * h : 128 * (h + 1)], m, v, RATE_D))
@@ -739,7 +786,7 @@
     row = jnp.sum(jnp.where(sub == lanes(8), column, 0.0), axis=0, keepdims=True)
     w, m, v = (r[at] for r in gain)
     put(gain_o, at, adam(w, row[:, 0:6], m, v, 0.5))
-    tile = total[0:2, 384:512]
+    tile = total[0:2, 256:384]
     both = rolled(tile, -(MISC + 5)) + rolled(tile, -(MISC + 10))
     w, m, v = (r[at] for r in conv)
     put(conv_o, at, adam(w, both[:, 0:5], m, v, 0.5))
@@ -778,20 +825,15 @@
     out_weights = [jnp.transpose(a, (0, 2, 1)) for a in (out_weight, out_first, out_second)]
     gains_in = [a.reshape(1, 6) for a in (pre_gain, gain_first, gain_second)]
 
-    (small,) = call(
-        small_kernel, [((N_HEAD, 16, 256), bf16)], shared_weight, gains_in[0], shared_conv,
-        scratch=[pltpu.VMEM((16, 256), f32)], name="small",
-    )
-    small = exchange(small, HEAD)
-    small, halo = lax.optimization_barrier((small, halo))
     (pack,) = call(
-        pack_kernel, [((N_SEQ, 48, NW), bf16)], small, matrices[0], out_weights[0], steps[0],
-        scratch=[
-            pltpu.VMEM((48, 256), f32), pltpu.VMEM((128, 128), f32), pltpu.VMEM((48, 128), f32)
-        ],
-        name="pack",
+        pack_kernel, [((N_SEQ, 48, NW), bf16)],
+        matrices[0], out_weights[0], steps[0], shared_weight, gains_in[0], shared_conv,
+        scratch=[pltpu.VMEM((128, 128), f32), pltpu.VMEM((48, 128), f32)], name="pack",
     )
     weights = exchange(pack, SEQ).reshape(D, NW)
+    (slab,) = call(slab_kernel, [((96, 384), bf16)], weights, name="slab")
+    near = [slab] + [around(slab, "head_0", by) for by in (1, 2, 3)]
+    slabs = near + [around(a, "head_1", 1) for a in near]
 
     marks = doc_starts.astype(f32).reshape(1, T)
     fixed = jnp.broadcast_to(
@@ -801,13 +843,14 @@
     gains = jnp.pad(channel_params[5].reshape(1, 192), ((0, 5), (0, 64)))
     taps = jnp.pad(jnp.concatenate([taps, gains], axis=1), ((0, 2), (0, 0)))
 
-    normed, values, conv, aux, sent, row = call(
+    normed, values, conv, aux, sent, row, wide, conv_taps = call(
         first_kernel,
         [
             ((HALO + T, D), bf16), ((HALO + T, NV), f32), ((T, NV), f32), ((T, 128), f32),
-            ((N_SEQ, SROWS, 128), bf16), ((8, D), f32),
+            ((N_SEQ, SROWS, 128), bf16), ((8, D), f32), ((D, 256), bf16), ((8, 256), f32),
         ],
-        hidden_in, halo, marks, weights, taps, head_params, smem=(5,), name="first",
+        where, *slabs, hidden_in, halo, marks, weights, taps, head_params, smem=(0, 14),
+        scratch=[pltpu.VMEM((D, 384), bf16)], name="first",
     )
     states = exchange(sent, SEQ)
     y_own, d_normed, decays, mixing = call(
@@ -815,59 +858,70 @@
         [((T, 256), f32), ((T, 256), f32), ((3, T, T), bf16), ((3, T, T), bf16)],
         conv, aux, cotangent, weights, head_params, smem=(4,), name="own",
     )
-    y_full, state, stat, fed = call(
+    y_full, state, stat = call(
         enter_kernel,
-        [((T, 256), f32), ((256, 128), f32), ((N_HEAD, 8, T), f32), ((T, 256), bf16)],
+        [((T, 256), f32), ((256, 128), f32), ((8, T), f32)],
         where, states, y_own, d_normed, conv, aux, taps, smem=(0,), name="enter",
     )
-    stats = exchange(stat, HEAD)
-    (partial_out,) = call(out_kernel, [((T, D), bf16)], fed, weights, name="out")
-    block_sum = lax.psum(partial_out, HEAD)
-    d_y, d_gate, normed_out, sent_adj, rows, rms = call(
+    stat = stat + around(stat, "head_1", 1)
+    stats = [stat] + [around(stat, "head_0", by) for by in (1, 2, 3)]
+    d_y, d_gate, normed_out, sent_adj, rows = call(
         gated_kernel,
         [
             ((T, 256), f32), ((T, 256), f32), ((T, 256), bf16),
-            ((N_SEQ, 192, 128), bf16), ((8, 256), f32), ((T, 128), f32),
+            ((N_SEQ, 192, 128), bf16), ((8, 256), f32),
         ],
-        stats, y_full, d_normed, conv, aux, taps, name="gated",
+        *stats, y_full, d_normed, conv, aux, taps, name="gated",
     )
     adjoints = exchange(sent_adj, SEQ)
-    d_x, d_b, d_c, d_cum = call(
+    half_rows = ((T // 2, D), bf16)
+    (
+        d_x, d_b, d_cum, x_act, b_act, slopes, out_keep, out_give, d_value_c, c_rows
+    ) = call(
         own_back_kernel,
-        [((T, 256), f32), ((T, 128), f32), ((T, 128), f32), ((T, 128), f32)],
-        d_y, y_full, y_own, conv, aux, decays, mixing, state, name="own_back",
-    )
+        [
+            ((T, 256), f32), ((T, 128), f32), ((T, 128), f32), ((T, 256), f32),
+            ((T, 128), bf16), ((T, 512), f32), half_rows, half_rows,
+            ((HALO + T, 128), bf16), ((8, 128), f32),
+        ],
+        where, d_y, y_full, y_own, conv, aux, decays, mixing, state, normed_out, weights,
+        values, conv_taps, marks, smem=(0,),
+        scratch=[pltpu.VMEM((T + 2 * HALO, 128), f32), pltpu.VMEM((T, D), f32)],
+        name="own_back",
+    )
+    out_taken = around(out_give, "head_1", 1)
     d_values, d_step, keep, give, edge, chan, d_conv, d_gain = call(
         back_kernel,
         [
-            ((HALO + T, NV), bf16), ((T, 128), bf16), ((T // 2, D), bf16), ((T // 2, D), bf16),
+            ((HALO + T, NV), bf16), ((T, 128), bf16), half_rows, half_rows,
             ((HALO, D), bf16), ((16, 256), f32), ((8, 256), f32), ((8, D), f32),
         ],
-        where, adjoints, states, state, d_x, d_b, d_c, d_cum, conv, aux,
-        values, taps, head_params, marks, d_y, d_gate, weights, rows, hidden_in, halo,
-        smem=(0, 12),
+        where, adjoints, states, state, d_x, d_b, d_cum, x_act, b_act, slopes, d_value_c,
+        c_rows, aux, values, taps, conv_taps, head_params, marks, d_y, d_gate, weights, wide,
+        rows, hidden_in, halo,
+        smem=(0, 16),
         scratch=[pltpu.VMEM((T + 2 * HALO, 128), f32), pltpu.VMEM((T, D), f32)],
         name="back",
     )
     taken = around(give, "head_1", 1)
     edges = [to_previous(edge, core) for core in range(2)]
     (grads,) = call(
-        grad_kernel, [((D, NW), bf16)],
+        grad_kernel, [((D, NG), bf16)],
         normed, d_values, d_step, normed_out, cotangent, d_conv, d_gain, chan, name="grad",
     )
-    grads = exchange(grads.reshape(N_SEQ, 48, NW), SEQ)
-
-    piece = ((T // N_HEAD, D), bf16)
+    grads = exchange(grads.reshape(N_SEQ, 48, NG), SEQ)
+
+    piece = ((T // N_HEAD, 2 * D), bf16)
     pieces = call(
-        pair_kernel, [piece] * 4, where, keep, taken, *edges, smem=(0,),
-        scratch=[pltpu.VMEM((T // 2, D), f32)], name="pair",
+        pair_kernel, [piece] * 4, where, keep, taken, *edges, out_keep, out_taken,
+        smem=(0,), scratch=[pltpu.VMEM((T // 2, 2 * D), f32)], name="pair",
     )
     parts = [pieces[0]] + [around(pieces[by], "head_0", by) for by in (1, 2, 3)]
-    (own,) = call(four_kernel, [piece], *parts, name="four")
+    (own,) = call(four_kernel, [piece], where, *parts, hidden_in, smem=(0,), name="four")
     near = [own] + [around(own, "head_0", by) for by in (1, 2, 3)]
     far = [around(a, "head_1", 1) for a in near]
-    (input_grad,) = call(
-        input_kernel, [((T, D), f32)], where, *near, *far, hidden_in, cotangent, row,
+    input_grad, block_out = call(
+        input_kernel, [((T, D), f32), ((T, D), bf16)], where, *near, *far, hidden_in, cotangent, row,
         smem=(0,), name="input",
     )
 
@@ -875,14 +929,11 @@
     shapes = [proj] * 3 + [step] * 3 + [out] * 3 + [(6, 3, 64)] * 3 + [(3, 3)] * 3
     updated = call(
         update_kernel,
-        [(s, f32) for s in shapes] + [((N_HEAD, 8, 512), f32)],
+        [(s, f32) for s in shapes] + [((N_HEAD, 8, 384), f32)],
         grads, *matrices, *steps, *out_weights, channel_params, channel_first,
         channel_second, head_params, head_first, head_second, name="update",
     )
     rest = exchange(updated[15], HEAD)
-    (block_out,) = call(
-        block_kernel, [((T, D), bf16)], block_sum, rms, hidden_in, name="block"
-    )
     shared = call(
         rest_kernel,
         [(s, f32) for s in [(6, 256)] * 3 + [(1, 6)] * 3 + [(2, 5)] * 3],

time: 220 us -> 191 us (0.87)
  the two profiles are of different devices: /device:TPU:1 before, /device:TPU:8 now
where the time goes in v3:
time: 191 us; the launch traced here: 189 us
  waiting for transfers between devices  66.1 us (35%)
  Pallas kernels  60.8 us (32%)
  starting transfers between devices  49.9 us (26%)
  local copies, waits for them, and re-layouts  9.51 us (5%)
  other arithmetic  1.97 us (1%)
    pallas_call x14, Pallas kernels, call(): pl.pallas_call(kernel, out_shape=[jax.ShapeDtypeStruct(s, d) for s, d in...  60.8 us
    ppermute x23, waiting for transfers between devices, around(): return lax.ppermute(a, axis, [(i, (i + by) % peers) for i in range(peers)])  31.8 us
    all_to_all x5, starting transfers between devices, exchange(): return lax.all_to_all(blocks, axis, 0, 0, tiled=True)  27.9 us
    all_to_all x5, waiting for transfers between devices, exchange(): return lax.all_to_all(blocks, axis, 0, 0, tiled=True)  24.9 us
    ppermute x23, starting transfers between devices, around(): return lax.ppermute(a, axis, [(i, (i + by) % peers) for i in range(peers)])  15.3 us
    ppermute x2, waiting for transfers between devices, to_previous(): return lax.ppermute(a, SEQ + ('head_1',), pairs)  9.43 us
    unnamed x73, local copies, waits for them, and re-layouts  8 us
  transfers between devices with their start and end apart: 31, of which 18 were waited for; matrix products, arithmetic and copies ran while one was open for 1% of the time, Pallas kernels for 15%

profile of v3, /device:TPU:8, one launch (start us, length us, event | category | flops | bytes accessed | tf_op | source)
XLA Modules:
  0.0 189.5 jit_solution(17405831760146256944)
XLA Ops:
  0.7 2.1 %pack.1 = bf16[16,48,640]{2,1,0:T(8,128)(2,1)} custom-call(f32[3,48,128]{2,1,0:T(8,128)} %bitcast.41, f32[3,48,64]{2,1,0:T(8,128)} %bitcast.43, f32[3,48]{1,0:T(4,128)} %bitcast.53, f32[6,256]{1,0:T(8,128)} %refs_1_.1, f32[1,6]{1,0:T(1,128)} %bitcast.55, f32[2,5]{1,0:T(2,128)} %refs_7_.1), custom_call_target="tpu_custom_call" | custom-call | tf_op jit(solution)/shard_map/pack/pallas_call | solution.py:44
  2.8 8.5 %all-to-all-start = ((bf16[16,48,640]{2,1,0:T(8,128)(2,1)}), bf16[16,48,640]{2,1,0:T(8,128)(2,1)S(1)}, u32[]{:S(2)}, u32[]{:S(2)}) async-start(bf16[16,48,640]{2,1,0:T(8,128)(2,1)} %pack.1), calls=%async_computation | async-start | bytes 1966080 | tf_op jit(solution)/shard_map/all_to_all | solution.py:796
  12.1 3.4 %collective-permute-start.7 = (bf16[16,768]{1,0:T(8,128)(2,1)S(1)}, bf16[16,768]{1,0:T(8,128)(2,1)S(1)}, u32[]{:S(2)}, u32[]{:S(2)}) collective-permute-start(bf16[16,768]{1,0:T(8,128)(2,1)S(1)} %slice.6), channel_id=1, source_target_pairs={{0,8},{8,16},{16,24},{24,32},{32,40},{40,48},{48,56},{56,64},{64,7... | collective-permute-start | bytes 73736 | tf_op jit(solution)/shard_map/ppermute | solution.py:805
  15.7 10.7 %all-to-all-done = bf16[16,48,640]{2,1,0:T(8,128)(2,1)S(1)} async-done(((bf16[16,48,640]{2,1,0:T(8,128)(2,1)}), bf16[16,48,640]{2,1,0:T(8,128)(2,1)S(1)}, u32[]{:S(2)}, u32[]{:S(2)}) %all-to-all-start) | async-done | bytes 983072 | tf_op jit(solution)/shard_map/all_to_all | solution.py:796
  27.4 2.3 %slab.1.refs_1_ = bf16[96,384]{1,0:T(8,128)(2,1)} custom-call(bf16[768,640]{1,0:T(8,128)(2,1)} %bitcast.35), custom_call_target="tpu_custom_call" | custom-call | tf_op jit(solution)/shard_map/slab/pallas_call | solution.py:44
  29.7 2.8 %collective-permute-start.2 = (bf16[96,384]{1,0:T(8,128)(2,1)}, bf16[96,384]{1,0:T(8,128)(2,1)S(1)}, u32[]{:S(2)}, u32[]{:S(2)}) collective-permute-start(bf16[96,384]{1,0:T(8,128)(2,1)} %slab.1.refs_1_), channel_id=1, source_target_pairs={{0,6},{2,0},{4,2},{6,4},{1,7},{3,1},{5,3},{7,5},{8,14},{10,8},{12,... | collective-permute-start | bytes 221192 | tf_op jit(solution)/shard_map/ppermute | solution.py:801
  34.8 3.8 %collective-permute-done.1.refs_3_ = bf16[96,384]{1,0:T(8,128)(2,1)S(1)} collective-permute-done((bf16[96,384]{1,0:T(8,128)(2,1)}, bf16[96,384]{1,0:T(8,128)(2,1)S(1)}, u32[]{:S(2)}, u32[]{:S(2)}) %collective-permute-start.1) | collective-permute-done | bytes 73760 | tf_op jit(solution)/shard_map/ppermute | solution.py:801
  41.9 7.1 %first.1 = (bf16[528,768]{1,0:T(8,128)(2,1)}, f32[528,640]{1,0:T(8,128)}, f32[512,640]{1,0:T(8,128)}, f32[512,128]{1,0:T(8,128)}, bf16[16,208,128]{2,1,0:T(8,128...) custom-call(s32[3]{0:T(128)} %pad_add_fusion.refs_0_.at_ref, bf16[96,384]{1,0:T(8,128)(2,1)} %slab.1.refs_1_, ...), custom_call_target="tpu_custom_call" | custom-call | tf_op jit(solution)/shard_map/first/pallas_call | solution.py:44
  48.9 5.3 %all-to-all-start.1 = ((bf16[16,208,128]{2,1,0:T(8,128)(2,1)}), bf16[16,208,128]{2,1,0:T(8,128)(2,1)S(1)}, u32[]{:S(2)}, u32[]{:S(2)}) async-start(bf16[16,208,128]{2,1,0:T(8,128)(2,1)} %get-tuple-element.95), calls=%async_computation.1 | async-start | bytes 1703936 | tf_op jit(solution)/shard_map/all_to_all | solution.py:796
  54.2 5.5 %own.1 = (f32[512,256]{1,0:T(8,128)}, f32[512,256]{1,0:T(8,128)}, bf16[3,512,512]{2,1,0:T(8,128)(2,1)}, bf16[3,512,512]{2,1,0:T(8,128)(2,1)}) custom-call(f32[512,640]{1,0:T(8,128)} %get-tuple-element.96.c_ref, f32[512,128]{1,0:T(8,128)} %get-tuple-element.97.aux_ref, bf16[512,768]{1,0:T(8,128)(2,1)} %cot_ref.3, bf16[768,640]{1,0:T(8,128)(2,1)} %bitcast.37, ...), custom_call_target="tpu_custom_call" | custom-call | tf_op jit(solution)/shard_map/own/pallas_call | solution.py:44
  59.7 9.3 %all-to-all-done.1.got_ref.fwd_ref = bf16[16,208,128]{2,1,0:T(8,128)(2,1)S(1)} async-done(((bf16[16,208,128]{2,1,0:T(8,128)(2,1)}), bf16[16,208,128]{2,1,0:T(8,128)(2,1)S(1)}, u32[]{:S(2)}, u32[]{:S(2)}) %all-to-all-start.1) | async-done | bytes 852000 | tf_op jit(solution)/shard_map/all_to_all | solution.py:796
  69.9 3.4 %enter.1 = (f32[512,256]{1,0:T(8,128)}, f32[256,128]{1,0:T(8,128)}, f32[8,512]{1,0:T(8,128)}) custom-call(s32[3]{0:T(128)} %pad_add_fusion.refs_0_.at_ref, bf16[16,208,128]{2,1,0:T(8,128)(2,1)} %copy-done.1, f32[512,256]{1,0:T(8,128)} %get-tuple-element.98.y0_ref, f32[512,256]{1,0:T(8,128)} %get-tuple-element.99.dn_ref, f32[512,640]{1,0:T(8,128)} %get-tuple-element.96.c_ref, ...), custom_call_target="tpu_custom_call" | custom-call | tf_op jit(solution)/shard_map/enter/pallas_call | solution.py:44
  82.5 4.2 %gated.1 = (f32[512,256]{1,0:T(8,128)}, f32[512,256]{1,0:T(8,128)}, bf16[512,256]{1,0:T(8,128)(2,1)}, bf16[16,192,128]{2,1,0:T(8,128)(2,1)}, f32[8,256]{1,0:T(8,128)}) custom-call(f32[8,512]{1,0:T(8,128)} %copy-done.25, f32[8,512]{1,0:T(8,128)} %copy-done.31, f32[8,512]{1,0:T(8,128)} %copy-done.30, f32[8,512]{1,0:T(8,128)} %copy-done.29, ...), custom_call_target="tpu_custom_call" | custom-call | tf_op jit(solution)/shard_map/gated/pallas_call | solution.py:44
  86.7 5.6 %all-to-all-start.2 = ((bf16[16,192,128]{2,1,0:T(8,128)(2,1)}), bf16[16,192,128]{2,1,0:T(8,128)(2,1)S(1)}, u32[]{:S(2)}, u32[]{:S(2)}) async-start(bf16[16,192,128]{2,1,0:T(8,128)(2,1)} %get-tuple-element.102), calls=%async_computation.2 | async-start | bytes 1572864 | tf_op jit(solution)/shard_map/all_to_all | solution.py:796
  92.2 8.4 %own_back.1 = (f32[512,256]{1,0:T(8,128)}, f32[512,128]{1,0:T(8,128)}, f32[512,128]{1,0:T(8,128)}, f32[512,256]{1,0:T(8,128)}, bf16[512,128]{1,0:T(8,128)(2,1)},...) custom-call(s32[3]{0:T(128)} %pad_add_fusion.refs_0_.at_ref, ...), custom_call_target="tpu_custom_call" | custom-call | tf_op jit(solution)/shard_map/own_back/pallas_call | solution.py:44
  100.6 3.9 %all-to-all-done.2.got_ref = bf16[16,192,128]{2,1,0:T(8,128)(2,1)S(1)} async-done(((bf16[16,192,128]{2,1,0:T(8,128)(2,1)}), bf16[16,192,128]{2,1,0:T(8,128)(2,1)S(1)}, u32[]{:S(2)}, u32[]{:S(2)}) %all-to-all-start.2) | async-done | bytes 786464 | tf_op jit(solution)/shard_map/all_to_all | solution.py:796
  105.4 10.2 %back.1 = (bf16[528,640]{1,0:T(8,128)(2,1)}, bf16[512,128]{1,0:T(8,128)(2,1)}, bf16[256,768]{1,0:T(8,128)(2,1)}, bf16[256,768]{1,0:T(8,128)(2,1)}, bf16[16,768]{...) custom-call(s32[3]{0:T(128)} %pad_add_fusion.refs_0_.at_ref, ...), custom_call_target="tpu_custom_call" | custom-call | tf_op jit(solution)/shard_map/back/pallas_call | solution.py:44
  115.6 4.6 %grad.1 = bf16[768,896]{1,0:T(8,128)(2,1)} custom-call(bf16[528,768]{1,0:T(8,128)(2,1)} %get-tuple-element.133.normed_ref, bf16[528,640]{1,0:T(8,128)(2,1)} %get-tuple-element.134.dv_ref, bf16[512,128]{1,0:T(8,128)(2,1)} %get-tuple-element.135.dstep_ref, bf16[512,256]{1,0:T(8,128)(2,1)} %get-tuple-element.107.nout_ref, bf16[512,768]{1,0:T(8,128)(2,1)} %cot_ref.3, ...), custom_call_target="tpu_custom_call" | custom-call | tf_op jit(solution)/shard_map/grad/pallas_call | solution.py:44
  120.1 5.1 %all-to-all-start.3 = ((bf16[16,48,896]{2,1,0:T(8,128)(2,1)}), bf16[16,48,896]{2,1,0:T(8,128)(2,1)S(1)}, u32[]{:S(2)}, u32[]{:S(2)}) async-start(bf16[16,48,896]{2,1,0:T(8,128)(2,1)} %bitcast.40), calls=%async_computation.3 | async-start | bytes 2752512 | tf_op jit(solution)/shard_map/all_to_all | solution.py:796
  126.5 2.7 %collective-permute-start.13 = (bf16[16,768]{1,0:T(8,128)(2,1)S(1)}, bf16[16,768]{1,0:T(8,128)(2,1)S(1)}, u32[]{:S(2)}, u32[]{:S(2)}) collective-permute-start(bf16[16,768]{1,0:T(8,128)(2,1)S(1)} %copy-done.35), channel_id=1, source_target_pairs={{8,1},{16,9},{24,17},{32,25},{40,33},{48,41},{56,49},{64,57},{72,6... | collective-permute-start | bytes 73736 | tf_op jit(solution)/shard_map/ppermute | solution.py:810
  129.2 9.4 %collective-permute-done.13.edge0_ref = bf16[16,768]{1,0:T(8,128)(2,1)S(1)} collective-permute-done((bf16[16,768]{1,0:T(8,128)(2,1)S(1)}, bf16[16,768]{1,0:T(8,128)(2,1)S(1)}, u32[]{:S(2)}, u32[]{:S(2)}) %collective-permute-start.13) | collective-permute-done | bytes 24608 | tf_op jit(solution)/shard_map/ppermute | solution.py:810
  139.4 2.5 %pair.1 = (bf16[64,1536]{1,0:T(8,128)(2,1)}, bf16[64,1536]{1,0:T(8,128)(2,1)}, bf16[64,1536]{1,0:T(8,128)(2,1)}, bf16[64,1536]{1,0:T(8,128)(2,1)}) custom-call(s32[3]{0:T(128)} %pad_add_fusion.refs_0_.at_ref, bf16[256,768]{1,0:T(8,128)(2,1)} %get-tuple-element.121.keep_ref, bf16[256,768]{1,0:T(8,128)(2,1)} %copy-done.6, bf16[16,768]{1,0:T(8,128)(2,1)} %copy-done.28, ...), custom_call_target="tpu_custom_call" | custom-call | tf_op jit(solution)/shard_map/pair/pallas_call | solution.py:44
  142.8 2.6 %collective-permute-start.17 = (bf16[64,1536]{1,0:T(8,128)(2,1)}, bf16[64,1536]{1,0:T(8,128)(2,1)S(1)}, u32[]{:S(2)}, u32[]{:S(2)}) collective-permute-start(bf16[64,1536]{1,0:T(8,128)(2,1)} %get-tuple-element.128), channel_id=1, source_target_pairs={{0,4},{2,6},{4,0},{6,2},{1,5},{3,7},{5,1},{7,3},{8,12},{10,14},{12... | collective-permute-start | bytes 589832 | tf_op jit(solution)/shard_map/ppermute | solution.py:801
  146.1 4.9 %collective-permute-done.16.b_ref = bf16[64,1536]{1,0:T(8,128)(2,1)S(1)} collective-permute-done((bf16[64,1536]{1,0:T(8,128)(2,1)}, bf16[64,1536]{1,0:T(8,128)(2,1)S(1)}, u32[]{:S(2)}, u32[]{:S(2)}) %collective-permute-start.16) | collective-permute-done | bytes 196640 | tf_op jit(solution)/shard_map/ppermute | solution.py:801
  151.0 4.4 %collective-permute-done.17.c_ref = bf16[64,1536]{1,0:T(8,128)(2,1)S(1)} collective-permute-done((bf16[64,1536]{1,0:T(8,128)(2,1)}, bf16[64,1536]{1,0:T(8,128)(2,1)S(1)}, u32[]{:S(2)}, u32[]{:S(2)}) %collective-permute-start.17) | collective-permute-done | bytes 196640 | tf_op jit(solution)/shard_map/ppermute | solution.py:801
  156.8 2.3 %four.1.refs_1_ = bf16[64,1536]{1,0:T(8,128)(2,1)} custom-call(s32[3]{0:T(128)} %pad_add_fusion.refs_0_.at_ref, bf16[64,1536]{1,0:T(8,128)(2,1)} %get-tuple-element.126.a_ref, bf16[64,1536]{1,0:T(8,128)(2,1)} %copy-done.7, bf16[64,1536]{1,0:T(8,128)(2,1)} %copy-done.8, bf16[64,1536]{1,0:T(8,128)(2,1)} %copy-done.9, bf16[512,768]{1,0:T(8,128)(2,1)} %refs_9_.4), custom_call_target="tpu_custom_call" | custom-call | tf_op jit(solution)/shard_map/four/pallas_call | solution.py:44
  159.1 2.6 %collective-permute-start.21 = (bf16[64,1536]{1,0:T(8,128)(2,1)}, bf16[64,1536]{1,0:T(8,128)(2,1)S(1)}, u32[]{:S(2)}, u32[]{:S(2)}) collective-permute-start(bf16[64,1536]{1,0:T(8,128)(2,1)} %four.1.refs_1_), channel_id=1, source_target_pairs={{0,6},{2,0},{4,2},{6,4},{1,7},{3,1},{5,3},{7,5},{8,14},{10,8},{12,... | collective-permute-start | bytes 589832 | tf_op jit(solution)/shard_map/ppermute | solution.py:801
  162.6 8.1 %collective-permute-done.21.refs_4_ = bf16[64,1536]{1,0:T(8,128)(2,1)S(1)} collective-permute-done((bf16[64,1536]{1,0:T(8,128)(2,1)}, bf16[64,1536]{1,0:T(8,128)(2,1)S(1)}, u32[]{:S(2)}, u32[]{:S(2)}) %collective-permute-start.21) | collective-permute-done | bytes 196640 | tf_op jit(solution)/shard_map/ppermute | solution.py:801
  171.3 2.7 %collective-permute-done.19.refs_2_ = bf16[64,1536]{1,0:T(8,128)(2,1)S(1)} collective-permute-done((bf16[64,1536]{1,0:T(8,128)(2,1)}, bf16[64,1536]{1,0:T(8,128)(2,1)S(1)}, u32[]{:S(2)}, u32[]{:S(2)}) %collective-permute-start.19) | collective-permute-done | bytes 196640 | tf_op jit(solution)/shard_map/ppermute | solution.py:801
  175.2 2.7 %update.1 = (f32[3,48,128]{2,1,0:T(8,128)}, f32[3,48,128]{2,1,0:T(8,128)}, f32[3,48,128]{2,1,0:T(8,128)}, f32[3,48]{1,0:T(4,128)}, f32[3,48]{1,0:T(4,128)}, /*in...) custom-call(bf16[16,48,896]{2,1,0:T(8,128)(2,1)} %copy-done.2, ...), custom_call_target="tpu_custom_call" | custom-call | tf_op jit(solution)/shard_map/update/pallas_call | solution.py:44
  177.8 3.4 %all-to-all-start.4 = ((f32[8,8,384]{2,1,0:T(8,128)}), f32[8,8,384]{2,1,0:T(8,128)S(1)}, u32[]{:S(2)}, u32[]{:S(2)}) async-start(f32[8,8,384]{2,1,0:T(8,128)} %get-tuple-element.148), calls=%async_computation.4 | async-start | bytes 196608 | tf_op jit(solution)/shard_map/all_to_all | solution.py:796
  182.1 3.8 %input.1 = (f32[512,768]{1,0:T(8,128)}, bf16[512,768]{1,0:T(8,128)(2,1)}) custom-call(s32[3]{0:T(128)} %pad_add_fusion.refs_0_.at_ref, bf16[64,1536]{1,0:T(8,128)(2,1)} %four.1.refs_1_, bf16[64,1536]{1,0:T(8,128)(2,1)} %copy-done.12, bf16[64,1536]{1,0:T(8,128)(2,1)} %copy-done.11, bf16[64,1536]{1,0:T(8,128)(2,1)} %copy-done.10, bf16[64,1536]{1,0:T(8,128)(2,1)} %copy-done.13, ...), custom_call_target="tpu_custom_call" | custom-call | tf_op jit(solution)/shard_map/input/pallas_call | solution.py:44
  (129 shorter events, 30.0 us)
Async XLA Ops:
  2.8 37.1 %copy-start.32 = (s32[512]{0:T(512)S(1)}, s32[512]{0:T(512)}, u32[]{:S(2)}) copy-start(s32[512]{0:T(512)} %param.29) | copy-start | bytes 6148
  2.8 23.6 %all-to-all-start = ((bf16[16,48,640]{2,1,0:T(8,128)(2,1)}), bf16[16,48,640]{2,1,0:T(8,128)(2,1)S(1)}, u32[]{:S(2)}, u32[]{:S(2)}) async-start(bf16[16,48,640]{2,1,0:T(8,128)(2,1)} %pack.1), calls=%async_computation | async-start | bytes 1966080 | tf_op jit(solution)/shard_map/all_to_all | solution.py:796
  12.1 29.1 %collective-permute-start.7 = (bf16[16,768]{1,0:T(8,128)(2,1)S(1)}, bf16[16,768]{1,0:T(8,128)(2,1)S(1)}, u32[]{:S(2)}, u32[]{:S(2)}) collective-permute-start(bf16[16,768]{1,0:T(8,128)(2,1)S(1)} %slice.6), channel_id=1, source_target_pairs={{0,8},{8,16},{16,24},{24,32},{32,40},{40,48},{48,56},{56,64},{64,7... | collective-permute-start | bytes 73736 | tf_op jit(solution)/shard_map/ppermute | solution.py:805
  29.7 5.1 %collective-permute-start.2 = (bf16[96,384]{1,0:T(8,128)(2,1)}, bf16[96,384]{1,0:T(8,128)(2,1)S(1)}, u32[]{:S(2)}, u32[]{:S(2)}) collective-permute-start(bf16[96,384]{1,0:T(8,128)(2,1)} %slab.1.refs_1_), channel_id=1, source_target_pairs={{0,6},{2,0},{4,2},{6,4},{1,7},{3,1},{5,3},{7,5},{8,14},{10,8},{12,... | collective-permute-start | bytes 221192 | tf_op jit(solution)/shard_map/ppermute | solution.py:801
  32.5 6.1 %collective-permute-start.1 = (bf16[96,384]{1,0:T(8,128)(2,1)}, bf16[96,384]{1,0:T(8,128)(2,1)S(1)}, u32[]{:S(2)}, u32[]{:S(2)}) collective-permute-start(bf16[96,384]{1,0:T(8,128)(2,1)} %slab.1.refs_1_), channel_id=1, source_target_pairs={{0,4},{2,6},{4,0},{6,2},{1,5},{3,7},{5,1},{7,3},{8,12},{10,14},{12... | collective-permute-start | bytes 221192 | tf_op jit(solution)/shard_map/ppermute | solution.py:801
  33.3 6.0 %collective-permute-start = (bf16[96,384]{1,0:T(8,128)(2,1)}, bf16[96,384]{1,0:T(8,128)(2,1)S(1)}, u32[]{:S(2)}, u32[]{:S(2)}) collective-permute-start(bf16[96,384]{1,0:T(8,128)(2,1)} %slab.1.refs_1_), channel_id=1, source_target_pairs={{0,2},{2,4},{4,6},{6,0},{1,3},{3,5},{5,7},{7,1},{8,10},{10,12},{12... | collective-permute-start | bytes 221192 | tf_op jit(solution)/shard_map/ppermute | solution.py:801
  34.2 6.9 %collective-permute-start.3 = (bf16[96,384]{1,0:T(8,128)(2,1)}, bf16[96,384]{1,0:T(8,128)(2,1)S(1)}, u32[]{:S(2)}, u32[]{:S(2)}) collective-permute-start(bf16[96,384]{1,0:T(8,128)(2,1)} %slab.1.refs_1_), channel_id=1, source_target_pairs={{0,1},{1,0},{2,3},{3,2},{4,5},{5,4},{6,7},{7,6},{8,9},{9,8},{10,11... | collective-permute-start | bytes 221192 | tf_op jit(solution)/shard_map/ppermute | solution.py:801
  34.8 6.4 %collective-permute-start.6 = (bf16[96,384]{1,0:T(8,128)(2,1)S(1)}, bf16[96,384]{1,0:T(8,128)(2,1)S(1)}, u32[]{:S(2)}, u32[]{:S(2)}) collective-permute-start(bf16[96,384]{1,0:T(8,128)(2,1)S(1)} %collective-permute-done.2.refs_4_), channel_id=1, source_target_pairs={{0,1},{1,0},{2,3},{3,2},{4,5},{5,4},{6,7},{7,6},{8,9},{9,8},{10,11... | collective-permute-start | bytes 221192 | tf_op jit(solution)/shard_map/ppermute | solution.py:801
  38.6 2.6 %collective-permute-start.5 = (bf16[96,384]{1,0:T(8,128)(2,1)S(1)}, bf16[96,384]{1,0:T(8,128)(2,1)S(1)}, u32[]{:S(2)}, u32[]{:S(2)}) collective-permute-start(bf16[96,384]{1,0:T(8,128)(2,1)S(1)} %collective-permute-done.1.refs_3_), channel_id=1, source_target_pairs={{0,1},{1,0},{2,3},{3,2},{4,5},{5,4},{6,7},{7,6},{8,9},{9,8},{10,11... | collective-permute-start | bytes 221192 | tf_op jit(solution)/shard_map/ppermute | solution.py:801
  39.4 1.8 collective-permute-start.4
  48.9 20.1 %all-to-all-start.1 = ((bf16[16,208,128]{2,1,0:T(8,128)(2,1)}), bf16[16,208,128]{2,1,0:T(8,128)(2,1)S(1)}, u32[]{:S(2)}, u32[]{:S(2)}) async-start(bf16[16,208,128]{2,1,0:T(8,128)(2,1)} %get-tuple-element.95), calls=%async_computation.1 | async-start | bytes 1703936 | tf_op jit(solution)/shard_map/all_to_all | solution.py:796
  73.4 1.4 collective-permute-start.8
  75.5 3.7 %collective-permute-start.11 = (f32[8,512]{1,0:T(8,128)S(1)}, f32[8,512]{1,0:T(8,128)S(1)}, u32[]{:S(2)}, u32[]{:S(2)}) collective-permute-start(f32[8,512]{1,0:T(8,128)S(1)} %add.11.s0_ref), channel_id=1, source_target_pairs={{0,6},{2,0},{4,2},{6,4},{1,7},{3,1},{5,3},{7,5},{8,14},{10,8},{12,... | collective-permute-start | bytes 49160 | tf_op jit(solution)/shard_map/ppermute | solution.py:801
  76.0 5.2 %collective-permute-start.10 = (f32[8,512]{1,0:T(8,128)S(1)}, f32[8,512]{1,0:T(8,128)S(1)}, u32[]{:S(2)}, u32[]{:S(2)}) collective-permute-start(f32[8,512]{1,0:T(8,128)S(1)} %add.11.s0_ref), channel_id=1, source_target_pairs={{0,4},{2,6},{4,0},{6,2},{1,5},{3,7},{5,1},{7,3},{8,12},{10,14},{12... | collective-permute-start | bytes 49160 | tf_op jit(solution)/shard_map/ppermute | solution.py:801
  76.9 5.0 %collective-permute-start.9 = (f32[8,512]{1,0:T(8,128)S(1)}, f32[8,512]{1,0:T(8,128)S(1)}, u32[]{:S(2)}, u32[]{:S(2)}) collective-permute-start(f32[8,512]{1,0:T(8,128)S(1)} %add.11.s0_ref), channel_id=1, source_target_pairs={{0,2},{2,4},{4,6},{6,0},{1,3},{3,5},{5,7},{7,1},{8,10},{10,12},{12... | collective-permute-start | bytes 49160 | tf_op jit(solution)/shard_map/ppermute | solution.py:801
  86.7 17.8 %all-to-all-start.2 = ((bf16[16,192,128]{2,1,0:T(8,128)(2,1)}), bf16[16,192,128]{2,1,0:T(8,128)(2,1)S(1)}, u32[]{:S(2)}, u32[]{:S(2)}) async-start(bf16[16,192,128]{2,1,0:T(8,128)(2,1)} %get-tuple-element.102), calls=%async_computation.2 | async-start | bytes 1572864 | tf_op jit(solution)/shard_map/all_to_all | solution.py:796
  120.1 53.9 %all-to-all-start.3 = ((bf16[16,48,896]{2,1,0:T(8,128)(2,1)}), bf16[16,48,896]{2,1,0:T(8,128)(2,1)S(1)}, u32[]{:S(2)}, u32[]{:S(2)}) async-start(bf16[16,48,896]{2,1,0:T(8,128)(2,1)} %bitcast.40), calls=%async_computation.3 | async-start | bytes 2752512 | tf_op jit(solution)/shard_map/all_to_all | solution.py:796
  125.2 3.9 %collective-permute-start.15 = (bf16[256,768]{1,0:T(8,128)(2,1)S(1)}, bf16[256,768]{1,0:T(8,128)(2,1)S(1)}, u32[]{:S(2)}, u32[]{:S(2)}) collective-permute-start(bf16[256,768]{1,0:T(8,128)(2,1)S(1)} %copy-done.33), channel_id=1, source_target_pairs={{0,1},{1,0},{2,3},{3,2},{4,5},{5,4},{6,7},{7,6},{8,9},{9,8},{10,11... | collective-permute-start | bytes 1179656 | tf_op jit(solution)/shard_map/ppermute | solution.py:801
  125.3 13.3 %collective-permute-start.12 = (bf16[256,768]{1,0:T(8,128)(2,1)S(1)}, bf16[256,768]{1,0:T(8,128)(2,1)S(1)}, u32[]{:S(2)}, u32[]{:S(2)}) collective-permute-start(bf16[256,768]{1,0:T(8,128)(2,1)S(1)} %copy-done.34), channel_id=1, source_target_pairs={{0,1},{1,0},{2,3},{3,2},{4,5},{5,4},{6,7},{7,6},{8,9},{9,8},{10,11... | collective-permute-start | bytes 1179656 | tf_op jit(solution)/shard_map/ppermute | solution.py:801
  125.8 3.4 %collective-permute-start.14 = (bf16[16,768]{1,0:T(8,128)(2,1)S(1)}, bf16[16,768]{1,0:T(8,128)(2,1)S(1)}, u32[]{:S(2)}, u32[]{:S(2)}) collective-permute-start(bf16[16,768]{1,0:T(8,128)(2,1)S(1)} %copy-done.35), channel_id=1, source_target_pairs={{9,1},{17,9},{25,17},{33,25},{41,33},{49,41},{57,49},{65,57},{73,6... | collective-permute-start | bytes 73736 | tf_op jit(solution)/shard_map/ppermute | solution.py:810
  126.5 12.2 %collective-permute-start.13 = (bf16[16,768]{1,0:T(8,128)(2,1)S(1)}, bf16[16,768]{1,0:T(8,128)(2,1)S(1)}, u32[]{:S(2)}, u32[]{:S(2)}) collective-permute-start(bf16[16,768]{1,0:T(8,128)(2,1)S(1)} %copy-done.35), channel_id=1, source_target_pairs={{8,1},{16,9},{24,17},{32,25},{40,33},{48,41},{56,49},{64,57},{72,6... | collective-permute-start | bytes 73736 | tf_op jit(solution)/shard_map/ppermute | solution.py:810
  142.0 9.0 %collective-permute-start.16 = (bf16[64,1536]{1,0:T(8,128)(2,1)}, bf16[64,1536]{1,0:T(8,128)(2,1)S(1)}, u32[]{:S(2)}, u32[]{:S(2)}) collective-permute-start(bf16[64,1536]{1,0:T(8,128)(2,1)} %get-tuple-element.127), channel_id=1, source_target_pairs={{0,2},{2,4},{4,6},{6,0},{1,3},{3,5},{5,7},{7,1},{8,10},{10,12},{12... | collective-permute-start | bytes 589832 | tf_op jit(solution)/shard_map/ppermute | solution.py:801
  142.8 12.6 %collective-permute-start.17 = (bf16[64,1536]{1,0:T(8,128)(2,1)}, bf16[64,1536]{1,0:T(8,128)(2,1)S(1)}, u32[]{:S(2)}, u32[]{:S(2)}) collective-permute-start(bf16[64,1536]{1,0:T(8,128)(2,1)} %get-tuple-element.128), channel_id=1, source_target_pairs={{0,4},{2,6},{4,0},{6,2},{1,5},{3,7},{5,1},{7,3},{8,12},{10,14},{12... | collective-permute-start | bytes 589832 | tf_op jit(solution)/shard_map/ppermute | solution.py:801
  145.4 10.7 %collective-permute-start.18 = (bf16[64,1536]{1,0:T(8,128)(2,1)}, bf16[64,1536]{1,0:T(8,128)(2,1)S(1)}, u32[]{:S(2)}, u32[]{:S(2)}) collective-permute-start(bf16[64,1536]{1,0:T(8,128)(2,1)} %get-tuple-element.129), channel_id=1, source_target_pairs={{0,6},{2,0},{4,2},{6,4},{1,7},{3,1},{5,3},{7,5},{8,14},{10,8},{12,... | collective-permute-start | bytes 589832 | tf_op jit(solution)/shard_map/ppermute | solution.py:801
  159.1 11.6 %collective-permute-start.21 = (bf16[64,1536]{1,0:T(8,128)(2,1)}, bf16[64,1536]{1,0:T(8,128)(2,1)S(1)}, u32[]{:S(2)}, u32[]{:S(2)}) collective-permute-start(bf16[64,1536]{1,0:T(8,128)(2,1)} %four.1.refs_1_), channel_id=1, source_target_pairs={{0,6},{2,0},{4,2},{6,4},{1,7},{3,1},{5,3},{7,5},{8,14},{10,8},{12,... | collective-permute-start | bytes 589832 | tf_op jit(solution)/shard_map/ppermute | solution.py:801
  161.8 9.5 %collective-permute-start.20 = (bf16[64,1536]{1,0:T(8,128)(2,1)}, bf16[64,1536]{1,0:T(8,128)(2,1)S(1)}, u32[]{:S(2)}, u32[]{:S(2)}) collective-permute-start(bf16[64,1536]{1,0:T(8,128)(2,1)} %four.1.refs_1_), channel_id=1, source_target_pairs={{0,4},{2,6},{4,0},{6,2},{1,5},{3,7},{5,1},{7,3},{8,12},{10,14},{12... | collective-permute-start | bytes 589832 | tf_op jit(solution)/shard_map/ppermute | solution.py:801
  162.1 12.0 %collective-permute-start.19 = (bf16[64,1536]{1,0:T(8,128)(2,1)}, bf16[64,1536]{1,0:T(8,128)(2,1)S(1)}, u32[]{:S(2)}, u32[]{:S(2)}) collective-permute-start(bf16[64,1536]{1,0:T(8,128)(2,1)} %four.1.refs_1_), channel_id=1, source_target_pairs={{0,2},{2,4},{4,6},{6,0},{1,3},{3,5},{5,7},{7,1},{8,10},{10,12},{12... | collective-permute-start | bytes 589832 | tf_op jit(solution)/shard_map/ppermute | solution.py:801
  162.6 18.6 %collective-permute-start.22 = (bf16[64,1536]{1,0:T(8,128)(2,1)}, bf16[64,1536]{1,0:T(8,128)(2,1)S(1)}, u32[]{:S(2)}, u32[]{:S(2)}) collective-permute-start(bf16[64,1536]{1,0:T(8,128)(2,1)} %four.1.refs_1_), channel_id=1, source_target_pairs={{0,1},{1,0},{2,3},{3,2},{4,5},{5,4},{6,7},{7,6},{8,9},{9,8},{10,11... | collective-permute-start | bytes 589832 | tf_op jit(solution)/shard_map/ppermute | solution.py:801
  170.7 10.5 %collective-permute-start.25 = (bf16[64,1536]{1,0:T(8,128)(2,1)S(1)}, bf16[64,1536]{1,0:T(8,128)(2,1)S(1)}, u32[]{:S(2)}, u32[]{:S(2)}) collective-permute-start(bf16[64,1536]{1,0:T(8,128)(2,1)S(1)} %collective-permute-done.21.refs_4_), channel_id=1, source_target_pairs={{0,1},{1,0},{2,3},{3,2},{4,5},{5,4},{6,7},{7,6},{8,9},{9,8},{10,11... | collective-permute-start | bytes 589832 | tf_op jit(solution)/shard_map/ppermute | solution.py:801
  171.3 10.0 %collective-permute-start.24 = (bf16[64,1536]{1,0:T(8,128)(2,1)S(1)}, bf16[64,1536]{1,0:T(8,128)(2,1)S(1)}, u32[]{:S(2)}, u32[]{:S(2)}) collective-permute-start(bf16[64,1536]{1,0:T(8,128)(2,1)S(1)} %collective-permute-done.20.refs_3_), channel_id=1, source_target_pairs={{0,1},{1,0},{2,3},{3,2},{4,5},{5,4},{6,7},{7,6},{8,9},{9,8},{10,11... | collective-permute-start | bytes 589832 | tf_op jit(solution)/shard_map/ppermute | solution.py:801
  174.0 7.2 %collective-permute-start.23 = (bf16[64,1536]{1,0:T(8,128)(2,1)S(1)}, bf16[64,1536]{1,0:T(8,128)(2,1)S(1)}, u32[]{:S(2)}, u32[]{:S(2)}) collective-permute-start(bf16[64,1536]{1,0:T(8,128)(2,1)S(1)} %collective-permute-done.19.refs_2_), channel_id=1, source_target_pairs={{0,1},{1,0},{2,3},{3,2},{4,5},{5,4},{6,7},{7,6},{8,9},{9,8},{10,11... | collective-permute-start | bytes 589832 | tf_op jit(solution)/shard_map/ppermute | solution.py:801
  177.8 9.1 %all-to-all-start.4 = ((f32[8,8,384]{2,1,0:T(8,128)}), f32[8,8,384]{2,1,0:T(8,128)S(1)}, u32[]{:S(2)}, u32[]{:S(2)}) async-start(f32[8,8,384]{2,1,0:T(8,128)} %get-tuple-element.148), calls=%async_computation.4 | async-start | bytes 196608 | tf_op jit(solution)/shard_map/all_to_all | solution.py:796
  (36 other events, 132.6 us)

commit v4 on v3

--- a/solution.py
+++ b/solution.py
@@ -35,7 +35,7 @@
 decay_rate = 0.01
 LOW = -1e30
 
-PARAMS = pltpu.CompilerParams(vmem_limit_bytes=56 * 1024 * 1024)
+PARAMS = pltpu.CompilerParams(vmem_limit_bytes=32 * 1024 * 1024)
 VM = pl.BlockSpec(memory_space=pltpu.VMEM)
 SM = pl.BlockSpec(memory_space=pltpu.SMEM)
 
@@ -319,11 +319,8 @@
     for h in range(3):
         tail = jnp.where(sub == h, high[:, h : h + 1], tail)
         tail = jnp.where(sub == 3 + h, lower[:, h : h + 1], tail)
-    body = state[0:192].astype(bf16)
-    tail = tail.astype(bf16)
-    for q in range(N_SEQ):
-        send_ref[q, 0:192, :] = body
-        send_ref[q, 192:SROWS, :] = tail
+    send_ref[0:192, :] = state[0:192].astype(bf16)
+    send_ref[192:SROWS, :] = tail.astype(bf16)
 
 
 def own_kernel(c_ref, aux_ref, cot_ref, w_ref, hp_ref, y_ref, dn_ref, m_ref, mg_ref):
@@ -359,23 +356,81 @@
     dn_ref[:, 128:256] = jnp.where(lo, back[:, 128:256], 0.0)
 
 
-def decay_rows(tail, shape=(192, 128)):
+def decay_rows(tail):
     both = tail[0:3] + tail[3:6]
     return jnp.concatenate(
         [jnp.broadcast_to(both[h : h + 1], (64, 128)) for h in range(3)], axis=0
     )
 
 
+def in_place(here, refs, rows):
+    pieces = [r[rows, :].astype(f32) for r in refs]
+    placed = []
+    for p in range(4):
+        by = lax.rem(here + 4 - p, 4)
+        piece = pieces[0]
+        for k in (1, 2, 3):
+            piece = jnp.where(by == k, pieces[k], piece)
+        placed.append(piece)
+    return placed
+
+
+def fold(here, states, tails, reverse):
+    total = entering = jnp.zeros((192, 128), f32)
+    passed = whole = jnp.ones((192, 128), f32)
+    for p in reversed(range(4)) if reverse else range(4):
+        decay = decay_rows(tails[p])
+        before = (p > here) if reverse else (p < here)
+        total = decay * total + states[p]
+        entering = jnp.where(before, total, entering)
+        passed = jnp.where(before, passed * decay, passed)
+        whole = whole * decay
+    return total, entering, passed, whole
+
+
+def group_kernel(at_ref, a_ref, b_ref, c_ref, d_ref, send_ref, own_ref, passed_ref, tail_ref):
+    here = lax.rem(at_ref[0], 4)
+    refs = (a_ref, b_ref, c_ref, d_ref)
+    states = in_place(here, refs, slice(0, 192))
+    tails = in_place(here, refs, slice(192, SROWS))
+    total, entering, passed, whole = fold(here, states, tails, False)
+    own_ref[...] = entering
+    passed_ref[...] = passed
+    send_ref[0:192, :] = total.astype(bf16)
+    sub = lax.broadcasted_iota(jnp.int32, (16, 128), 0)
+    tail = jnp.zeros((16, 128), f32)
+    for h in range(3):
+        row = whole[64 * h : 64 * h + 1]
+        high = row.astype(bf16).astype(f32)
+        tail = jnp.where(sub == h, high, tail)
+        tail = jnp.where(sub == 3 + h, row - high, tail)
+    send_ref[192:SROWS, :] = tail.astype(bf16)
+    for p in range(4):
+        tail_ref[16 * p : 16 * p + 16, :] = tails[p]
+
+
+def group_back_kernel(at_ref, a_ref, b_ref, c_ref, d_ref, tail_ref, send_ref, own_ref, passed_ref):
+    here = lax.rem(at_ref[0], 4)
+    states = in_place(here, (a_ref, b_ref, c_ref, d_ref), slice(0, 192))
+    tails = [tail_ref[16 * p : 16 * p + 16, :] for p in range(4)]
+    total, entering, passed, _ = fold(here, states, tails, True)
+    own_ref[...] = entering
+    passed_ref[...] = passed
+    send_ref[...] = total.astype(bf16)
+
+
 def enter_kernel(
-    at_ref, got_ref, y0_ref, dn_ref, c_ref, aux_ref, tap_ref,
-    y_ref, state_ref, stat_ref,
+    at_ref, s0_ref, s1_ref, s2_ref, s3_ref, own_ref, passed_ref, y0_ref, dn_ref, c_ref,
+    aux_ref, tap_ref, y_ref, state_ref, stat_ref, tail_ref,
 ):
-    here = at_ref[0]
-    state = jnp.zeros((192, 128), f32)
-    for q in range(N_SEQ - 1):
-        through = decay_rows(got_ref[q, 192:SROWS, :].astype(f32))
-        merged = through * state + got_ref[q, 0:192, :].astype(f32)
-        state = jnp.where(q < here, merged, state)
+    here = jnp.right_shift(at_ref[0], 2)
+    refs = (s0_ref, s1_ref, s2_ref, s3_ref)
+    states = in_place(here, refs, slice(0, 192))
+    tails = in_place(here, refs, slice(192, SROWS))
+    for p in range(4):
+        tail_ref[16 * p : 16 * p + 16, :] = tails[p]
+    _, entering, _, _ = fold(here, states, tails, False)
+    state = passed_ref[...] * entering + own_ref[...]
     state_ref[0:192] = state
     state_ref[192:256] = jnp.zeros((64, 128), f32)
     c_mat = silu(c_ref[:, 512:640]).astype(bf16)
@@ -430,9 +485,7 @@
         rows_ref[0:1, at] = jnp.sum(dn * scaled, axis=0, keepdims=True)
         rows_ref[1:2, at] = jnp.sum(dy * x[k], axis=0, keepdims=True)
     c_mat = silu(c_ref[:, 512:640]).astype(bf16)
-    adj = dot(jnp.concatenate(kept, axis=1), c_mat, 0, 0)[0:192].astype(bf16)
-    for q in range(N_SEQ):
-        send_ref[q] = adj
+    send_ref[...] = dot(jnp.concatenate(kept, axis=1), c_mat, 0, 0)[0:192].astype(bf16)
 
 
 def halves(ref, core):
@@ -527,18 +580,18 @@
 
 
 def back_kernel(
-    at_ref, got_ref, fwd_ref, state_ref, dx_ref, db_ref, dcum_ref, xs_ref, b_ref, slope_ref,
+    at_ref, a0_ref, a1_ref, a2_ref, a3_ref, own_ref, passed_ref, tails_ref, mine_ref,
+    state_ref, dx_ref, db_ref, dcum_ref, xs_ref, b_ref, slope_ref,
     dvc_ref, crow_ref, aux_ref, v_ref, tap_ref, ctap_ref, hp_ref, st_ref, dy_ref, dgate_ref,
     w_ref, wide_ref, rows_ref, hid_ref, halo_ref,
     dv_ref, dstep_ref, keep_ref, give_ref, edge_ref, chan_ref, conv_ref, gain_ref,
     pad_ref, norm_ref,
 ):
-    here = at_ref[0]
-    adj = jnp.zeros((192, 128), f32)
-    for q in range(N_SEQ - 1, 0, -1):
-        through = decay_rows(fwd_ref[q, 192:SROWS, :].astype(f32))
-        merged = through * adj + got_ref[q].astype(f32)
-        adj = jnp.where(q > here, merged, adj)
+    here = jnp.right_shift(at_ref[0], 2)
+    states = in_place(here, (a0_ref, a1_ref, a2_ref, a3_ref), slice(0, 192))
+    tails = [tails_ref[16 * p : 16 * p + 16, :] for p in range(4)]
+    _, entering, _, _ = fold(here, states, tails, True)
+    adj = passed_ref[...] * entering + own_ref[...]
     aux = aux_ref[...]
     lane = lanes(T)
     x = pair_of(xs_ref)
@@ -566,7 +619,7 @@
     ci = lax.broadcasted_iota(jnp.int32, (T, T), 1)
     upper = jnp.where(ci >= ri, 1.0, 0.0).astype(bf16)
     d_log = joined(dot(upper, three_parts(d_cum).astype(bf16)))
-    own = decay_rows(fwd_ref[here, 192:SROWS, :].astype(f32))
+    own = decay_rows(mine_ref[192:SROWS, :].astype(f32))
     met = own * adj * state_ref[0:192]
     lane1 = lanes(1)
     meets = jnp.zeros((1, 128), f32)
@@ -847,21 +900,27 @@
         first_kernel,
         [
             ((HALO + T, D), bf16), ((HALO + T, NV), f32), ((T, NV), f32), ((T, 128), f32),
-            ((N_SEQ, SROWS, 128), bf16), ((8, D), f32), ((D, 256), bf16), ((8, 256), f32),
+            ((SROWS, 128), bf16), ((8, D), f32), ((D, 256), bf16), ((8, 256), f32),
         ],
         where, *slabs, hidden_in, halo, marks, weights, taps, head_params, smem=(0, 14),
         scratch=[pltpu.VMEM((D, 384), bf16)], name="first",
     )
-    states = exchange(sent, SEQ)
+    states = [sent] + [around(sent, "seq_1", by) for by in (1, 2, 3)]
+    group, group_in, group_passed, group_tails = call(
+        group_kernel,
+        [((SROWS, 128), bf16), ((192, 128), f32), ((192, 128), f32), ((64, 128), f32)],
+        where, *states, smem=(0,), name="group",
+    )
+    groups = [group] + [around(group, "seq_0", by) for by in (1, 2, 3)]
     y_own, d_normed, decays, mixing = call(
         own_kernel,
         [((T, 256), f32), ((T, 256), f32), ((3, T, T), bf16), ((3, T, T), bf16)],
         conv, aux, cotangent, weights, head_params, smem=(4,), name="own",
     )
-    y_full, state, stat = call(
+    y_full, state, stat, all_tails = call(
         enter_kernel,
-        [((T, 256), f32), ((256, 128), f32), ((8, T), f32)],
-        where, states, y_own, d_normed, conv, aux, taps, smem=(0,), name="enter",
+        [((T, 256), f32), ((256, 128), f32), ((8, T), f32), ((64, 128), f32)],
+        where, *groups, group_in, group_passed, y_own, d_normed, conv, aux, taps, smem=(0,), name="enter",
     )
     stat = stat + around(stat, "head_1", 1)
     stats = [stat] + [around(stat, "head_0", by) for by in (1, 2, 3)]
@@ -869,11 +928,17 @@
         gated_kernel,
         [
             ((T, 256), f32), ((T, 256), f32), ((T, 256), bf16),
-            ((N_SEQ, 192, 128), bf16), ((8, 256), f32),
+            ((192, 128), bf16), ((8, 256), f32),
         ],
         *stats, y_full, d_normed, conv, aux, taps, name="gated",
     )
-    adjoints = exchange(sent_adj, SEQ)
+    adjoints = [sent_adj] + [around(sent_adj, "seq_1", by) for by in (1, 2, 3)]
+    group, adj_in, adj_passed = call(
+        group_back_kernel,
+        [((192, 128), bf16), ((192, 128), f32), ((192, 128), f32)],
+        where, *adjoints, group_tails, smem=(0,), name="group_back",
+    )
+    groups = [group] + [around(group, "seq_0", by) for by in (1, 2, 3)]
     half_rows = ((T // 2, D), bf16)
     (
         d_x, d_b, d_cum, x_act, b_act, slopes, out_keep, out_give, d_value_c, c_rows
@@ -896,10 +961,10 @@
             ((HALO + T, NV), bf16), ((T, 128), bf16), half_rows, half_rows,
             ((HALO, D), bf16), ((16, 256), f32), ((8, 256), f32), ((8, D), f32),
         ],
-        where, adjoints, states, state, d_x, d_b, d_cum, x_act, b_act, slopes, d_value_c,
+        where, *groups, adj_in, adj_passed, all_tails, sent, state, d_x, d_b, d_cum, x_act, b_act, slopes, d_value_c,
         c_rows, aux, values, taps, conv_taps, head_params, marks, d_y, d_gate, weights, wide,
         rows, hidden_in, halo,
-        smem=(0, 16),
+        smem=(0, 22),
         scratch=[pltpu.VMEM((T + 2 * HALO, 128), f32), pltpu.VMEM((T, D), f32)],
         name="back",
     )
@@ -908,6 +973,9 @@
     (grads,) = call(
         grad_kernel, [((D, NG), bf16)],
         normed, d_values, d_step, normed_out, cotangent, d_conv, d_gain, chan, name="grad",
+    )
+    grads, taken, out_taken, edges = lax.optimization_barrier(
+        (grads, taken, out_taken, edges)
     )
     grads = exchange(grads.reshape(N_SEQ, 48, NG), SEQ)
 

time: 191 us -> 160 us (0.84)
  the two profiles are of different devices: /device:TPU:8 before, /device:TPU:1 now
where the time goes in v4:
time: 160 us; the launch traced here: 159 us
  starting transfers between devices  66.5 us (42%)
  waiting for transfers between devices  46.4 us (29%)
  Pallas kernels  32.6 us (20%)
  local copies, waits for them, and re-layouts  12.1 us (8%)
    ppermute x35, starting transfers between devices, around(): return lax.ppermute(a, axis, [(i, (i + by) % peers) for i in range(peers)])  41.1 us
    pallas_call x16, Pallas kernels, call(): pl.pallas_call(kernel, out_shape=[jax.ShapeDtypeStruct(s, d) for s, d in...  32.6 us
    ppermute x35, waiting for transfers between devices, around(): return lax.ppermute(a, axis, [(i, (i + by) % peers) for i in range(peers)])  31.9 us
    all_to_all x3, starting transfers between devices, exchange(): return lax.all_to_all(blocks, axis, 0, 0, tiled=True)  19.5 us
    all_to_all x3, waiting for transfers between devices, exchange(): return lax.all_to_all(blocks, axis, 0, 0, tiled=True)  13.5 us
    unnamed x81, local copies, waits for them, and re-layouts  12 us
    ppermute x1, starting transfers between devices, to_next(): return lax.ppermute(a, SEQ, [(i, i + 1) for i in range(N_SEQ - 1)])  3.27 us
  transfers between devices with their start and end apart: 41, of which 20 were waited for; matrix products, arithmetic and copies ran while one was open for 0% of the time, Pallas kernels for 14%

profile of v4, /device:TPU:1, one launch (start us, length us, event | category | flops | bytes accessed | tf_op | source)
XLA Modules:
  0.0 158.9 jit_solution(839080891496519368)
XLA Ops:
  6.3 8.7 %all-to-all-start = ((bf16[16,48,640]{2,1,0:T(8,128)(2,1)}), bf16[16,48,640]{2,1,0:T(8,128)(2,1)S(1)}, u32[]{:S(2)}, u32[]{:S(2)}) async-start(bf16[16,48,640]{2,1,0:T(8,128)(2,1)} %pack.1), calls=%async_computation | async-start | bytes 1966080 | tf_op jit(solution)/shard_map/all_to_all | solution.py:849
  15.1 3.3 %collective-permute-start.7 = (bf16[16,768]{1,0:T(8,128)(2,1)S(1)}, bf16[16,768]{1,0:T(8,128)(2,1)S(1)}, u32[]{:S(2)}, u32[]{:S(2)}) collective-permute-start(bf16[16,768]{1,0:T(8,128)(2,1)S(1)} %slice.6), channel_id=1, source_target_pairs={{0,8},{8,16},{16,24},{24,32},{32,40},{40,48},{48,56},{56,64},{64,7... | collective-permute-start | bytes 73736 | tf_op jit(solution)/shard_map/ppermute | solution.py:858
  18.6 11.7 %all-to-all-done = bf16[16,48,640]{2,1,0:T(8,128)(2,1)S(1)} async-done(((bf16[16,48,640]{2,1,0:T(8,128)(2,1)}), bf16[16,48,640]{2,1,0:T(8,128)(2,1)S(1)}, u32[]{:S(2)}, u32[]{:S(2)}) %all-to-all-start) | async-done | bytes 983072 | tf_op jit(solution)/shard_map/all_to_all | solution.py:849
  30.9 2.5 %collective-permute-start.2 = (bf16[96,384]{1,0:T(8,128)(2,1)S(1)}, bf16[96,384]{1,0:T(8,128)(2,1)S(1)}, u32[]{:S(2)}, u32[]{:S(2)}) collective-permute-start(bf16[96,384]{1,0:T(8,128)(2,1)S(1)} %slab.1.refs_1_), channel_id=1, source_target_pairs={{0,6},{2,0},{4,2},{6,4},{1,7},{3,1},{5,3},{7,5},{8,14},{10,8},{12,... | collective-permute-start | bytes 221192 | tf_op jit(solution)/shard_map/ppermute | solution.py:854
  34.6 3.4 %collective-permute-start.3 = (bf16[96,384]{1,0:T(8,128)(2,1)S(1)}, bf16[96,384]{1,0:T(8,128)(2,1)S(1)}, u32[]{:S(2)}, u32[]{:S(2)}) collective-permute-start(bf16[96,384]{1,0:T(8,128)(2,1)S(1)} %slab.1.refs_1_), channel_id=1, source_target_pairs={{0,1},{1,0},{2,3},{3,2},{4,5},{5,4},{6,7},{7,6},{8,9},{9,8},{10,11... | collective-permute-start | bytes 221192 | tf_op jit(solution)/shard_map/ppermute | solution.py:854
  38.2 3.9 %collective-permute-start.5 = (bf16[96,384]{1,0:T(8,128)(2,1)S(1)}, bf16[96,384]{1,0:T(8,128)(2,1)S(1)}, u32[]{:S(2)}, u32[]{:S(2)}) collective-permute-start(bf16[96,384]{1,0:T(8,128)(2,1)S(1)} %collective-permute-done.1.refs_3_), channel_id=1, source_target_pairs={{0,1},{1,0},{2,3},{3,2},{4,5},{5,4},{6,7},{7,6},{8,9},{9,8},{10,11... | collective-permute-start | bytes 221192 | tf_op jit(solution)/shard_map/ppermute | solution.py:854
  43.8 4.7 %first.1 = (bf16[528,768]{1,0:T(8,128)(2,1)S(1)}, f32[528,640]{1,0:T(8,128)S(1)}, f32[512,640]{1,0:T(8,128)S(1)}, f32[512,128]{1,0:T(8,128)S(1)}, bf16[208,128]{...) custom-call(s32[3]{0:T(128)S(1)} %pad_add_fusion.refs_0_.at_ref, ...), custom_call_target="tpu_custom_call" | custom-call | tf_op jit(solution)/shard_map/first/pallas_call | solution.py:44
  48.5 1.7 %collective-permute-start.9 = (bf16[208,128]{1,0:T(8,128)(2,1)S(1)}, bf16[208,128]{1,0:T(8,128)(2,1)S(1)}, u32[]{:S(2)}, u32[]{:S(2)}) collective-permute-start(bf16[208,128]{1,0:T(8,128)(2,1)S(1)} %get-tuple-element.108.a_ref.mine_ref), channel_id=1, source_target_pairs={{0,16},{8,24},{16,0},{24,8},{1,17},{9,25},{17,1},{25,9},{2,18},{10... | collective-permute-start | bytes 159752 | tf_op jit(solution)/shard_map/ppermute | solution.py:854
  51.5 1.6 %collective-permute-done.9.c_ref = bf16[208,128]{1,0:T(8,128)(2,1)S(1)} collective-permute-done((bf16[208,128]{1,0:T(8,128)(2,1)S(1)}, bf16[208,128]{1,0:T(8,128)(2,1)S(1)}, u32[]{:S(2)}, u32[]{:S(2)}) %collective-permute-start.9) | collective-permute-done | bytes 53280 | tf_op jit(solution)/shard_map/ppermute | solution.py:854
  53.1 1.4 collective-permute-done.8.b_ref
  57.4 2.3 %own.1 = (f32[512,256]{1,0:T(8,128)S(1)}, f32[512,256]{1,0:T(8,128)S(1)}, bf16[3,512,512]{2,1,0:T(8,128)(2,1)S(1)}, bf16[3,512,512]{2,1,0:T(8,128)(2,1)S(1)}) custom-call(f32[512,640]{1,0:T(8,128)S(1)} %get-tuple-element.112.c_ref, f32[512,128]{1,0:T(8,128)S(1)} %get-tuple-element.113.aux_ref, bf16[512,768]{1,0:T(8,128)(2,1)S(1)} %copy-done.1, ...), custom_call_target="tpu_custom_call" | custom-call | tf_op jit(solution)/shard_map/own/pallas_call | solution.py:44
  62.6 3.0 %collective-permute-start.14 = (f32[8,512]{1,0:T(8,128)S(1)}, f32[8,512]{1,0:T(8,128)S(1)}, u32[]{:S(2)}, u32[]{:S(2)}) collective-permute-start(f32[8,512]{1,0:T(8,128)S(1)} %get-tuple-element.116), channel_id=1, source_target_pairs={{0,1},{1,0},{2,3},{3,2},{4,5},{5,4},{6,7},{7,6},{8,9},{9,8},{10,11... | collective-permute-start | bytes 49160 | tf_op jit(solution)/shard_map/ppermute | solution.py:854
  69.1 1.8 %collective-permute-done.16.s2_ref = f32[8,512]{1,0:T(8,128)S(1)} collective-permute-done((f32[8,512]{1,0:T(8,128)S(1)}, f32[8,512]{1,0:T(8,128)S(1)}, u32[]{:S(2)}, u32[]{:S(2)}) %collective-permute-start.16) | collective-permute-done | bytes 16416 | tf_op jit(solution)/shard_map/ppermute | solution.py:854
  71.5 1.5 gated.1
  76.0 2.3 %collective-permute-done.19.c_ref = bf16[192,128]{1,0:T(8,128)(2,1)S(1)} collective-permute-done((bf16[192,128]{1,0:T(8,128)(2,1)S(1)}, bf16[192,128]{1,0:T(8,128)(2,1)S(1)}, u32[]{:S(2)}, u32[]{:S(2)}) %collective-permute-start.19) | collective-permute-done | bytes 49184 | tf_op jit(solution)/shard_map/ppermute | solution.py:854
  79.5 1.7 %collective-permute-start.23 = (bf16[192,128]{1,0:T(8,128)(2,1)S(1)}, bf16[192,128]{1,0:T(8,128)(2,1)S(1)}, u32[]{:S(2)}, u32[]{:S(2)}) collective-permute-start(bf16[192,128]{1,0:T(8,128)(2,1)S(1)} %get-tuple-element.120.a0_ref), channel_id=1, source_target_pairs={{0,96},{32,0},{64,32},{96,64},{1,97},{33,1},{65,33},{97,65},{2,98}... | collective-permute-start | bytes 147464 | tf_op jit(solution)/shard_map/ppermute | solution.py:854
  81.8 4.0 %own_back.1 = (f32[512,256]{1,0:T(8,128)S(1)}, f32[512,128]{1,0:T(8,128)S(1)}, f32[512,128]{1,0:T(8,128)S(1)}, f32[512,256]{1,0:T(8,128)S(1)}, bf16[512,128]{1,0...) custom-call(s32[3]{0:T(128)S(1)} %pad_add_fusion.refs_0_.at_ref, ...), custom_call_target="tpu_custom_call" | custom-call | tf_op jit(solution)/shard_map/own_back/pallas_call | solution.py:44
  85.9 4.3 %collective-permute-start.25 = (bf16[256,768]{1,0:T(8,128)(2,1)S(1)}, bf16[256,768]{1,0:T(8,128)(2,1)S(1)}, u32[]{:S(2)}, u32[]{:S(2)}) collective-permute-start(bf16[256,768]{1,0:T(8,128)(2,1)S(1)} %get-tuple-element.150), channel_id=1, source_target_pairs={{0,1},{1,0},{2,3},{3,2},{4,5},{5,4},{6,7},{7,6},{8,9},{9,8},{10,11... | collective-permute-start | bytes 1179656 | tf_op jit(solution)/shard_map/ppermute | solution.py:854
  90.2 6.2 %back.1 = (bf16[528,640]{1,0:T(8,128)(2,1)S(1)}, bf16[512,128]{1,0:T(8,128)(2,1)S(1)}, bf16[256,768]{1,0:T(8,128)(2,1)S(1)}, bf16[256,768]{1,0:T(8,128)(2,1)S(1)...) custom-call(s32[3]{0:T(128)S(1)} %pad_add_fusion.refs_0_.at_ref, ...), custom_call_target="tpu_custom_call" | custom-call | tf_op jit(solution)/shard_map/back/pallas_call | solution.py:44
  99.8 1.8 %grad.1 = bf16[768,896]{1,0:T(8,128)(2,1)S(1)} custom-call(bf16[528,768]{1,0:T(8,128)(2,1)S(1)} %get-tuple-element.143.normed_ref, bf16[528,640]{1,0:T(8,128)(2,1)S(1)} %get-tuple-element.144.dv_ref, bf16[512,128]{1,0:T(8,128)(2,1)S(1)} %get-tuple-element.145.dstep_ref, bf16[512,256]{1,0:T(8,128)(2,1)S(1)} %get-tuple-element.128.nout_ref, ...), custom_call_target="tpu_custom_call" | custom-call | tf_op jit(solution)/shard_map/grad/pallas_call | solution.py:44
  104.3 7.5 %all-to-all-start.1 = ((bf16[16,48,896]{2,1,0:T(8,128)(2,1)}), bf16[16,48,896]{2,1,0:T(8,128)(2,1)}, u32[]{:S(2)}, u32[]{:S(2)}) async-start(bf16[16,48,896]{2,1,0:T(8,128)(2,1)} %bitcast.40), calls=%async_computation.1 | async-start | bytes 2752512 | tf_op jit(solution)/shard_map/all_to_all | solution.py:849
  114.8 2.4 %collective-permute-start.29 = (bf16[64,1536]{1,0:T(8,128)(2,1)S(1)}, bf16[64,1536]{1,0:T(8,128)(2,1)S(1)}, u32[]{:S(2)}, u32[]{:S(2)}) collective-permute-start(bf16[64,1536]{1,0:T(8,128)(2,1)S(1)} %get-tuple-element.159), channel_id=1, source_target_pairs={{0,4},{2,6},{4,0},{6,2},{1,5},{3,7},{5,1},{7,3},{8,12},{10,14},{12... | collective-permute-start | bytes 589832 | tf_op jit(solution)/shard_map/ppermute | solution.py:854
  117.5 4.6 %collective-permute-done.28.b_ref = bf16[64,1536]{1,0:T(8,128)(2,1)S(1)} collective-permute-done((bf16[64,1536]{1,0:T(8,128)(2,1)S(1)}, bf16[64,1536]{1,0:T(8,128)(2,1)S(1)}, u32[]{:S(2)}, u32[]{:S(2)}) %collective-permute-start.28) | collective-permute-done | bytes 196640 | tf_op jit(solution)/shard_map/ppermute | solution.py:854
  122.0 4.5 %collective-permute-done.29.c_ref = bf16[64,1536]{1,0:T(8,128)(2,1)S(1)} collective-permute-done((bf16[64,1536]{1,0:T(8,128)(2,1)S(1)}, bf16[64,1536]{1,0:T(8,128)(2,1)S(1)}, u32[]{:S(2)}, u32[]{:S(2)}) %collective-permute-start.29) | collective-permute-done | bytes 196640 | tf_op jit(solution)/shard_map/ppermute | solution.py:854
  127.2 3.1 %collective-permute-start.33 = (bf16[64,1536]{1,0:T(8,128)(2,1)S(1)}, bf16[64,1536]{1,0:T(8,128)(2,1)S(1)}, u32[]{:S(2)}, u32[]{:S(2)}) collective-permute-start(bf16[64,1536]{1,0:T(8,128)(2,1)S(1)} %four.1.refs_1_), channel_id=1, source_target_pairs={{0,6},{2,0},{4,2},{6,4},{1,7},{3,1},{5,3},{7,5},{8,14},{10,8},{12,... | collective-permute-start | bytes 589832 | tf_op jit(solution)/shard_map/ppermute | solution.py:854
  131.9 6.4 %collective-permute-done.33.refs_4_ = bf16[64,1536]{1,0:T(8,128)(2,1)S(1)} collective-permute-done((bf16[64,1536]{1,0:T(8,128)(2,1)S(1)}, bf16[64,1536]{1,0:T(8,128)(2,1)S(1)}, u32[]{:S(2)}, u32[]{:S(2)}) %collective-permute-start.33) | collective-permute-done | bytes 196640 | tf_op jit(solution)/shard_map/ppermute | solution.py:854
  138.3 1.3 collective-permute-start.37
  140.3 2.0 %collective-permute-done.31.refs_2_ = bf16[64,1536]{1,0:T(8,128)(2,1)S(1)} collective-permute-done((bf16[64,1536]{1,0:T(8,128)(2,1)S(1)}, bf16[64,1536]{1,0:T(8,128)(2,1)S(1)}, u32[]{:S(2)}, u32[]{:S(2)}) %collective-permute-start.31) | collective-permute-done | bytes 196640 | tf_op jit(solution)/shard_map/ppermute | solution.py:854
  147.4 2.5 %update.1 = (f32[3,48,128]{2,1,0:T(8,128)}, f32[3,48,128]{2,1,0:T(8,128)}, f32[3,48,128]{2,1,0:T(8,128)}, f32[3,48]{1,0:T(4,128)}, f32[3,48]{1,0:T(4,128)}, /*in...) custom-call(bf16[16,48,896]{2,1,0:T(8,128)(2,1)} %all-to-all-done.1., ...), custom_call_target="tpu_custom_call" | custom-call | tf_op jit(solution)/shard_map/update/pallas_call | solution.py:44
  149.8 3.3 %all-to-all-start.2 = ((f32[8,8,384]{2,1,0:T(8,128)}), f32[8,8,384]{2,1,0:T(8,128)S(1)}, u32[]{:S(2)}, u32[]{:S(2)}) async-start(f32[8,8,384]{2,1,0:T(8,128)} %get-tuple-element.174), calls=%async_computation.2 | async-start | bytes 196608 | tf_op jit(solution)/shard_map/all_to_all | solution.py:849
  153.3 3.0 %input.1 = (f32[512,768]{1,0:T(8,128)}, bf16[512,768]{1,0:T(8,128)(2,1)}) custom-call(s32[3]{0:T(128)S(1)} %pad_add_fusion.refs_0_.at_ref, bf16[64,1536]{1,0:T(8,128)(2,1)S(1)} %four.1.refs_1_, bf16[64,1536]{1,0:T(8,128)(2,1)S(1)} %collective-permute-done.31.refs_2_, bf16[64,1536]{1,0:T(8,128)(2,1)S(1)} %collective-permute-done.32.refs_3_, ...), custom_call_target="tpu_custom_call" | custom-call | tf_op jit(solution)/shard_map/input/pallas_call | solution.py:44
  156.3 1.8 %all-to-all-done.2.refs_0_ = f32[8,8,384]{2,1,0:T(8,128)S(1)} async-done(((f32[8,8,384]{2,1,0:T(8,128)}), f32[8,8,384]{2,1,0:T(8,128)S(1)}, u32[]{:S(2)}, u32[]{:S(2)}) %all-to-all-start.2) | async-done | bytes 98336 | tf_op jit(solution)/shard_map/all_to_all | solution.py:849
  (159 shorter events, 43.6 us)
Async XLA Ops:
  6.3 24.0 %all-to-all-start = ((bf16[16,48,640]{2,1,0:T(8,128)(2,1)}), bf16[16,48,640]{2,1,0:T(8,128)(2,1)S(1)}, u32[]{:S(2)}, u32[]{:S(2)}) async-start(bf16[16,48,640]{2,1,0:T(8,128)(2,1)} %pack.1), calls=%async_computation | async-start | bytes 1966080 | tf_op jit(solution)/shard_map/all_to_all | solution.py:849
  15.1 27.9 %collective-permute-start.7 = (bf16[16,768]{1,0:T(8,128)(2,1)S(1)}, bf16[16,768]{1,0:T(8,128)(2,1)S(1)}, u32[]{:S(2)}, u32[]{:S(2)}) collective-permute-start(bf16[16,768]{1,0:T(8,128)(2,1)S(1)} %slice.6), channel_id=1, source_target_pairs={{0,8},{8,16},{16,24},{24,32},{32,40},{40,48},{48,56},{56,64},{64,7... | collective-permute-start | bytes 73736 | tf_op jit(solution)/shard_map/ppermute | solution.py:858
  30.9 7.1 %collective-permute-start.2 = (bf16[96,384]{1,0:T(8,128)(2,1)S(1)}, bf16[96,384]{1,0:T(8,128)(2,1)S(1)}, u32[]{:S(2)}, u32[]{:S(2)}) collective-permute-start(bf16[96,384]{1,0:T(8,128)(2,1)S(1)} %slab.1.refs_1_), channel_id=1, source_target_pairs={{0,6},{2,0},{4,2},{6,4},{1,7},{3,1},{5,3},{7,5},{8,14},{10,8},{12,... | collective-permute-start | bytes 221192 | tf_op jit(solution)/shard_map/ppermute | solution.py:854
  33.4 4.8 %collective-permute-start.1 = (bf16[96,384]{1,0:T(8,128)(2,1)S(1)}, bf16[96,384]{1,0:T(8,128)(2,1)S(1)}, u32[]{:S(2)}, u32[]{:S(2)}) collective-permute-start(bf16[96,384]{1,0:T(8,128)(2,1)S(1)} %slab.1.refs_1_), channel_id=1, source_target_pairs={{0,4},{2,6},{4,0},{6,2},{1,5},{3,7},{5,1},{7,3},{8,12},{10,14},{12... | collective-permute-start | bytes 221192 | tf_op jit(solution)/shard_map/ppermute | solution.py:854
  33.9 8.2 %collective-permute-start = (bf16[96,384]{1,0:T(8,128)(2,1)S(1)}, bf16[96,384]{1,0:T(8,128)(2,1)S(1)}, u32[]{:S(2)}, u32[]{:S(2)}) collective-permute-start(bf16[96,384]{1,0:T(8,128)(2,1)S(1)} %slab.1.refs_1_), channel_id=1, source_target_pairs={{0,2},{2,4},{4,6},{6,0},{1,3},{3,5},{5,7},{7,1},{8,10},{10,12},{12... | collective-permute-start | bytes 221192 | tf_op jit(solution)/shard_map/ppermute | solution.py:854
  34.6 8.4 %collective-permute-start.3 = (bf16[96,384]{1,0:T(8,128)(2,1)S(1)}, bf16[96,384]{1,0:T(8,128)(2,1)S(1)}, u32[]{:S(2)}, u32[]{:S(2)}) collective-permute-start(bf16[96,384]{1,0:T(8,128)(2,1)S(1)} %slab.1.refs_1_), channel_id=1, source_target_pairs={{0,1},{1,0},{2,3},{3,2},{4,5},{5,4},{6,7},{7,6},{8,9},{9,8},{10,11... | collective-permute-start | bytes 221192 | tf_op jit(solution)/shard_map/ppermute | solution.py:854
  37.9 5.1 %collective-permute-start.6 = (bf16[96,384]{1,0:T(8,128)(2,1)S(1)}, bf16[96,384]{1,0:T(8,128)(2,1)S(1)}, u32[]{:S(2)}, u32[]{:S(2)}) collective-permute-start(bf16[96,384]{1,0:T(8,128)(2,1)S(1)} %collective-permute-done.2.refs_4_), channel_id=1, source_target_pairs={{0,1},{1,0},{2,3},{3,2},{4,5},{5,4},{6,7},{7,6},{8,9},{9,8},{10,11... | collective-permute-start | bytes 221192 | tf_op jit(solution)/shard_map/ppermute | solution.py:854
  38.2 4.8 %collective-permute-start.5 = (bf16[96,384]{1,0:T(8,128)(2,1)S(1)}, bf16[96,384]{1,0:T(8,128)(2,1)S(1)}, u32[]{:S(2)}, u32[]{:S(2)}) collective-permute-start(bf16[96,384]{1,0:T(8,128)(2,1)S(1)} %collective-permute-done.1.refs_3_), channel_id=1, source_target_pairs={{0,1},{1,0},{2,3},{3,2},{4,5},{5,4},{6,7},{7,6},{8,9},{9,8},{10,11... | collective-permute-start | bytes 221192 | tf_op jit(solution)/shard_map/ppermute | solution.py:854
  48.5 4.6 %collective-permute-start.9 = (bf16[208,128]{1,0:T(8,128)(2,1)S(1)}, bf16[208,128]{1,0:T(8,128)(2,1)S(1)}, u32[]{:S(2)}, u32[]{:S(2)}) collective-permute-start(bf16[208,128]{1,0:T(8,128)(2,1)S(1)} %get-tuple-element.108.a_ref.mine_ref), channel_id=1, source_target_pairs={{0,16},{8,24},{16,0},{24,8},{1,17},{9,25},{17,1},{25,9},{2,18},{10... | collective-permute-start | bytes 159752 | tf_op jit(solution)/shard_map/ppermute | solution.py:854
  55.2 4.5 %collective-permute-start.13 = (bf16[208,128]{1,0:T(8,128)(2,1)S(1)}, bf16[208,128]{1,0:T(8,128)(2,1)S(1)}, u32[]{:S(2)}, u32[]{:S(2)}) collective-permute-start(bf16[208,128]{1,0:T(8,128)(2,1)S(1)} %get-tuple-element.109.s0_ref), channel_id=1, source_target_pairs={{0,96},{32,0},{64,32},{96,64},{1,97},{33,1},{65,33},{97,65},{2,98}... | collective-permute-start | bytes 159752 | tf_op jit(solution)/shard_map/ppermute | solution.py:854
  56.2 4.5 %collective-permute-start.12 = (bf16[208,128]{1,0:T(8,128)(2,1)S(1)}, bf16[208,128]{1,0:T(8,128)(2,1)S(1)}, u32[]{:S(2)}, u32[]{:S(2)}) collective-permute-start(bf16[208,128]{1,0:T(8,128)(2,1)S(1)} %get-tuple-element.109.s0_ref), channel_id=1, source_target_pairs={{0,64},{32,96},{64,0},{96,32},{1,65},{33,97},{65,1},{97,33},{2,66}... | collective-permute-start | bytes 159752 | tf_op jit(solution)/shard_map/ppermute | solution.py:854
  56.9 4.4 %collective-permute-start.11 = (bf16[208,128]{1,0:T(8,128)(2,1)S(1)}, bf16[208,128]{1,0:T(8,128)(2,1)S(1)}, u32[]{:S(2)}, u32[]{:S(2)}) collective-permute-start(bf16[208,128]{1,0:T(8,128)(2,1)S(1)} %get-tuple-element.109.s0_ref), channel_id=1, source_target_pairs={{0,32},{32,64},{64,96},{96,0},{1,33},{33,65},{65,97},{97,1},{2,34}... | collective-permute-start | bytes 159752 | tf_op jit(solution)/shard_map/ppermute | solution.py:854
  73.8 4.5 %collective-permute-start.19 = (bf16[192,128]{1,0:T(8,128)(2,1)S(1)}, bf16[192,128]{1,0:T(8,128)(2,1)S(1)}, u32[]{:S(2)}, u32[]{:S(2)}) collective-permute-start(bf16[192,128]{1,0:T(8,128)(2,1)S(1)} %get-tuple-element.118.a_ref), channel_id=1, source_target_pairs={{0,16},{8,24},{16,0},{24,8},{1,17},{9,25},{17,1},{25,9},{2,18},{10... | collective-permute-start | bytes 147464 | tf_op jit(solution)/shard_map/ppermute | solution.py:854
  79.5 10.7 %collective-permute-start.23 = (bf16[192,128]{1,0:T(8,128)(2,1)S(1)}, bf16[192,128]{1,0:T(8,128)(2,1)S(1)}, u32[]{:S(2)}, u32[]{:S(2)}) collective-permute-start(bf16[192,128]{1,0:T(8,128)(2,1)S(1)} %get-tuple-element.120.a0_ref), channel_id=1, source_target_pairs={{0,96},{32,0},{64,32},{96,64},{1,97},{33,1},{65,33},{97,65},{2,98}... | collective-permute-start | bytes 147464 | tf_op jit(solution)/shard_map/ppermute | solution.py:854
  81.2 9.0 %collective-permute-start.22 = (bf16[192,128]{1,0:T(8,128)(2,1)S(1)}, bf16[192,128]{1,0:T(8,128)(2,1)S(1)}, u32[]{:S(2)}, u32[]{:S(2)}) collective-permute-start(bf16[192,128]{1,0:T(8,128)(2,1)S(1)} %get-tuple-element.120.a0_ref), channel_id=1, source_target_pairs={{0,64},{32,96},{64,0},{96,32},{1,65},{33,97},{65,1},{97,33},{2,66}... | collective-permute-start | bytes 147464 | tf_op jit(solution)/shard_map/ppermute | solution.py:854
  81.8 8.4 %collective-permute-start.21 = (bf16[192,128]{1,0:T(8,128)(2,1)S(1)}, bf16[192,128]{1,0:T(8,128)(2,1)S(1)}, u32[]{:S(2)}, u32[]{:S(2)}) collective-permute-start(bf16[192,128]{1,0:T(8,128)(2,1)S(1)} %get-tuple-element.120.a0_ref), channel_id=1, source_target_pairs={{0,32},{32,64},{64,96},{96,0},{1,33},{33,65},{65,97},{97,1},{2,34}... | collective-permute-start | bytes 147464 | tf_op jit(solution)/shard_map/ppermute | solution.py:854
  85.9 17.8 %collective-permute-start.25 = (bf16[256,768]{1,0:T(8,128)(2,1)S(1)}, bf16[256,768]{1,0:T(8,128)(2,1)S(1)}, u32[]{:S(2)}, u32[]{:S(2)}) collective-permute-start(bf16[256,768]{1,0:T(8,128)(2,1)S(1)} %get-tuple-element.150), channel_id=1, source_target_pairs={{0,1},{1,0},{2,3},{3,2},{4,5},{5,4},{6,7},{7,6},{8,9},{9,8},{10,11... | collective-permute-start | bytes 1179656 | tf_op jit(solution)/shard_map/ppermute | solution.py:854
  96.5 7.2 %collective-permute-start.24 = (bf16[256,768]{1,0:T(8,128)(2,1)S(1)}, bf16[256,768]{1,0:T(8,128)(2,1)S(1)}, u32[]{:S(2)}, u32[]{:S(2)}) collective-permute-start(bf16[256,768]{1,0:T(8,128)(2,1)S(1)} %get-tuple-element.149), channel_id=1, source_target_pairs={{0,1},{1,0},{2,3},{3,2},{4,5},{5,4},{6,7},{7,6},{8,9},{9,8},{10,11... | collective-permute-start | bytes 1179656 | tf_op jit(solution)/shard_map/ppermute | solution.py:854
  97.2 5.5 %collective-permute-start.27 = (bf16[16,768]{1,0:T(8,128)(2,1)S(1)}, bf16[16,768]{1,0:T(8,128)(2,1)S(1)}, u32[]{:S(2)}, u32[]{:S(2)}) collective-permute-start(bf16[16,768]{1,0:T(8,128)(2,1)S(1)} %get-tuple-element.151), channel_id=1, source_target_pairs={{9,1},{17,9},{25,17},{33,25},{41,33},{49,41},{57,49},{65,57},{73,6... | collective-permute-start | bytes 73736 | tf_op jit(solution)/shard_map/ppermute | solution.py:863
  98.5 5.1 %collective-permute-start.26 = (bf16[16,768]{1,0:T(8,128)(2,1)S(1)}, bf16[16,768]{1,0:T(8,128)(2,1)S(1)}, u32[]{:S(2)}, u32[]{:S(2)}) collective-permute-start(bf16[16,768]{1,0:T(8,128)(2,1)S(1)} %get-tuple-element.151), channel_id=1, source_target_pairs={{8,1},{16,9},{24,17},{32,25},{40,33},{48,41},{56,49},{64,57},{72,6... | collective-permute-start | bytes 73736 | tf_op jit(solution)/shard_map/ppermute | solution.py:863
  104.3 38.8 %all-to-all-start.1 = ((bf16[16,48,896]{2,1,0:T(8,128)(2,1)}), bf16[16,48,896]{2,1,0:T(8,128)(2,1)}, u32[]{:S(2)}, u32[]{:S(2)}) async-start(bf16[16,48,896]{2,1,0:T(8,128)(2,1)} %bitcast.40), calls=%async_computation.1 | async-start | bytes 2752512 | tf_op jit(solution)/shard_map/all_to_all | solution.py:849
  114.2 7.9 %collective-permute-start.28 = (bf16[64,1536]{1,0:T(8,128)(2,1)S(1)}, bf16[64,1536]{1,0:T(8,128)(2,1)S(1)}, u32[]{:S(2)}, u32[]{:S(2)}) collective-permute-start(bf16[64,1536]{1,0:T(8,128)(2,1)S(1)} %get-tuple-element.158), channel_id=1, source_target_pairs={{0,2},{2,4},{4,6},{6,0},{1,3},{3,5},{5,7},{7,1},{8,10},{10,12},{12... | collective-permute-start | bytes 589832 | tf_op jit(solution)/shard_map/ppermute | solution.py:854
  114.8 11.7 %collective-permute-start.29 = (bf16[64,1536]{1,0:T(8,128)(2,1)S(1)}, bf16[64,1536]{1,0:T(8,128)(2,1)S(1)}, u32[]{:S(2)}, u32[]{:S(2)}) collective-permute-start(bf16[64,1536]{1,0:T(8,128)(2,1)S(1)} %get-tuple-element.159), channel_id=1, source_target_pairs={{0,4},{2,6},{4,0},{6,2},{1,5},{3,7},{5,1},{7,3},{8,12},{10,14},{12... | collective-permute-start | bytes 589832 | tf_op jit(solution)/shard_map/ppermute | solution.py:854
  117.2 9.4 %collective-permute-start.30 = (bf16[64,1536]{1,0:T(8,128)(2,1)S(1)}, bf16[64,1536]{1,0:T(8,128)(2,1)S(1)}, u32[]{:S(2)}, u32[]{:S(2)}) collective-permute-start(bf16[64,1536]{1,0:T(8,128)(2,1)S(1)} %get-tuple-element.160), channel_id=1, source_target_pairs={{0,6},{2,0},{4,2},{6,4},{1,7},{3,1},{5,3},{7,5},{8,14},{10,8},{12,... | collective-permute-start | bytes 589832 | tf_op jit(solution)/shard_map/ppermute | solution.py:854
  127.2 11.1 %collective-permute-start.33 = (bf16[64,1536]{1,0:T(8,128)(2,1)S(1)}, bf16[64,1536]{1,0:T(8,128)(2,1)S(1)}, u32[]{:S(2)}, u32[]{:S(2)}) collective-permute-start(bf16[64,1536]{1,0:T(8,128)(2,1)S(1)} %four.1.refs_1_), channel_id=1, source_target_pairs={{0,6},{2,0},{4,2},{6,4},{1,7},{3,1},{5,3},{7,5},{8,14},{10,8},{12,... | collective-permute-start | bytes 589832 | tf_op jit(solution)/shard_map/ppermute | solution.py:854
  130.3 9.3 %collective-permute-start.32 = (bf16[64,1536]{1,0:T(8,128)(2,1)S(1)}, bf16[64,1536]{1,0:T(8,128)(2,1)S(1)}, u32[]{:S(2)}, u32[]{:S(2)}) collective-permute-start(bf16[64,1536]{1,0:T(8,128)(2,1)S(1)} %four.1.refs_1_), channel_id=1, source_target_pairs={{0,4},{2,6},{4,0},{6,2},{1,5},{3,7},{5,1},{7,3},{8,12},{10,14},{12... | collective-permute-start | bytes 589832 | tf_op jit(solution)/shard_map/ppermute | solution.py:854
  130.3 11.9 %collective-permute-start.31 = (bf16[64,1536]{1,0:T(8,128)(2,1)S(1)}, bf16[64,1536]{1,0:T(8,128)(2,1)S(1)}, u32[]{:S(2)}, u32[]{:S(2)}) collective-permute-start(bf16[64,1536]{1,0:T(8,128)(2,1)S(1)} %four.1.refs_1_), channel_id=1, source_target_pairs={{0,2},{2,4},{4,6},{6,0},{1,3},{3,5},{5,7},{7,1},{8,10},{10,12},{12... | collective-permute-start | bytes 589832 | tf_op jit(solution)/shard_map/ppermute | solution.py:854
  131.0 22.2 %collective-permute-start.34 = (bf16[64,1536]{1,0:T(8,128)(2,1)S(1)}, bf16[64,1536]{1,0:T(8,128)(2,1)S(1)}, u32[]{:S(2)}, u32[]{:S(2)}) collective-permute-start(bf16[64,1536]{1,0:T(8,128)(2,1)S(1)} %four.1.refs_1_), channel_id=1, source_target_pairs={{0,1},{1,0},{2,3},{3,2},{4,5},{5,4},{6,7},{7,6},{8,9},{9,8},{10,11... | collective-permute-start | bytes 589832 | tf_op jit(solution)/shard_map/ppermute | solution.py:854
  138.3 14.9 %collective-permute-start.37 = (bf16[64,1536]{1,0:T(8,128)(2,1)S(1)}, bf16[64,1536]{1,0:T(8,128)(2,1)}, u32[]{:S(2)}, u32[]{:S(2)}) collective-permute-start(bf16[64,1536]{1,0:T(8,128)(2,1)S(1)} %collective-permute-done.33.refs_4_), channel_id=1, source_target_pairs={{0,1},{1,0},{2,3},{3,2},{4,5},{5,4},{6,7},{7,6},{8,9},{9,8},{10,11... | collective-permute-start | bytes 589832 | tf_op jit(solution)/shard_map/ppermute | solution.py:854
  139.6 13.6 %collective-permute-start.36 = (bf16[64,1536]{1,0:T(8,128)(2,1)S(1)}, bf16[64,1536]{1,0:T(8,128)(2,1)}, u32[]{:S(2)}, u32[]{:S(2)}) collective-permute-start(bf16[64,1536]{1,0:T(8,128)(2,1)S(1)} %collective-permute-done.32.refs_3_), channel_id=1, source_target_pairs={{0,1},{1,0},{2,3},{3,2},{4,5},{5,4},{6,7},{7,6},{8,9},{9,8},{10,11... | collective-permute-start | bytes 589832 | tf_op jit(solution)/shard_map/ppermute | solution.py:854
  142.2 11.0 %collective-permute-start.35 = (bf16[64,1536]{1,0:T(8,128)(2,1)S(1)}, bf16[64,1536]{1,0:T(8,128)(2,1)}, u32[]{:S(2)}, u32[]{:S(2)}) collective-permute-start(bf16[64,1536]{1,0:T(8,128)(2,1)S(1)} %collective-permute-done.31.refs_2_), channel_id=1, source_target_pairs={{0,1},{1,0},{2,3},{3,2},{4,5},{5,4},{6,7},{7,6},{8,9},{9,8},{10,11... | collective-permute-start | bytes 589832 | tf_op jit(solution)/shard_map/ppermute | solution.py:854
  149.8 8.3 %all-to-all-start.2 = ((f32[8,8,384]{2,1,0:T(8,128)}), f32[8,8,384]{2,1,0:T(8,128)S(1)}, u32[]{:S(2)}, u32[]{:S(2)}) async-start(f32[8,8,384]{2,1,0:T(8,128)} %get-tuple-element.174), calls=%async_computation.2 | async-start | bytes 196608 | tf_op jit(solution)/shard_map/all_to_all | solution.py:849
  (50 other events, 474.2 us)

commit v5 on v4

--- a/solution.py
+++ b/solution.py
@@ -21,8 +21,8 @@
 HALO = 16
 NV = 640
 NW = 640
-NG = 896
 MISC = 64
+CHAN = (69, 78, 84, 90)
 SLAB = 96
 SROWS = 208
 
@@ -36,18 +36,22 @@
 LOW = -1e30
 
 PARAMS = pltpu.CompilerParams(vmem_limit_bytes=32 * 1024 * 1024)
+WIDE = pltpu.CompilerParams(vmem_limit_bytes=56 * 1024 * 1024)
 VM = pl.BlockSpec(memory_space=pltpu.VMEM)
 SM = pl.BlockSpec(memory_space=pltpu.SMEM)
-
-
-def call(kernel, outs, *args, smem=(), scratch=(), name=None):
+ANY = pl.BlockSpec(memory_space=pl.ANY)
+
+
+def call(kernel, outs, *args, smem=(), anywhere=(), scratch=(), params=PARAMS, name=None):
     return pl.pallas_call(
         kernel,
         out_shape=[jax.ShapeDtypeStruct(s, d) for s, d in outs],
-        in_specs=[SM if i in smem else VM for i in range(len(args))],
+        in_specs=[
+            SM if i in smem else ANY if i in anywhere else VM for i in range(len(args))
+        ],
         out_specs=[VM] * len(outs),
         scratch_shapes=list(scratch),
-        compiler_params=PARAMS,
+        compiler_params=params,
         name=name,
     )(*args)
 
@@ -409,7 +413,10 @@
         tail_ref[16 * p : 16 * p + 16, :] = tails[p]
 
 
-def group_back_kernel(at_ref, a_ref, b_ref, c_ref, d_ref, tail_ref, send_ref, own_ref, passed_ref):
+def group_back_kernel(
+    at_ref, a_ref, b_ref, c_ref, d_ref, tail_ref, after_ref, send_ref, own_ref, passed_ref
+):
+    del after_ref
     here = lax.rem(at_ref[0], 4)
     states = in_place(here, (a_ref, b_ref, c_ref, d_ref), slice(0, 192))
     tails = [tail_ref[16 * p : 16 * p + 16, :] for p in range(4)]
@@ -494,6 +501,11 @@
     return keep.astype(bf16), give.astype(bf16)
 
 
+def out_kernel(at_ref, nout_ref, w_ref, keep_ref, give_ref, norm_ref):
+    norm_ref[...] = dot(nout_ref[...], w_ref[:, 384:640], 1, 1)
+    keep_ref[...], give_ref[...] = halves(norm_ref, at_ref[2])
+
+
 def clear_edges(pad_ref):
     pad_ref[0:HALO] = jnp.zeros((HALO, 128), f32)
     pad_ref[HALO + T :] = jnp.zeros((HALO, 128), f32)
@@ -515,13 +527,11 @@
 
 
 def own_back_kernel(
-    at_ref, dy_ref, y_ref, y0_ref, c_ref, aux_ref, m_ref, mg_ref, state_ref, nout_ref, w_ref,
+    dy_ref, y_ref, y0_ref, c_ref, aux_ref, m_ref, mg_ref, state_ref,
     v_ref, ctap_ref, st_ref,
-    dx_ref, db_ref, dcum_ref, xs_ref, b_ref, slope_ref, keep_ref, give_ref, dvc_ref, crow_ref,
-    pad_ref, norm_ref,
+    dx_ref, db_ref, dcum_ref, xs_ref, b_ref, slope_ref, dvc_ref, crow_ref,
+    pad_ref,
 ):
-    norm_ref[...] = dot(nout_ref[...], w_ref[:, 384:640], 1, 1)
-    keep_ref[...], give_ref[...] = halves(norm_ref, at_ref[2])
     aux = aux_ref[...]
     aux_t = aux.T
     act = []
@@ -689,54 +699,93 @@
     gain_ref[1:8] = jnp.zeros((7, D), f32)
 
 
+def picked(rows, head):
+    a = lax.broadcasted_iota(jnp.int32, (rows, D), 0)
+    d = lax.broadcasted_iota(jnp.int32, (rows, D), 1)
+    return jnp.where(d - slab_rows(a) == 6 * head, 1.0, 0.0).astype(bf16)
+
+
 def grad_kernel(
-    normed_ref, dv_ref, dstep_ref, nout_ref, cot_ref, conv_ref, gain_ref, chan_ref, out_ref
+    at_ref, normed_ref, dv_ref, dstep_ref, nout_ref, cot_ref, conv_ref, gain_ref, chan_ref,
+    a0, a1, out_ref, keep_ref, give_ref, slab_ref,
 ):
+    del a0, a1
     normed = normed_ref[...]
+    slab_ref[:, 0:256] = dot(normed, dv_ref[:, 384:640], 0, 0).astype(bf16)
+    grads = jnp.concatenate([jnp.zeros((MISC + 5, 256), f32), conv_ref[0:5, :]], axis=0)
+    grads = jnp.concatenate([grads, jnp.zeros((128 - MISC - 10, 256), f32)], axis=0)
+    sub = lax.broadcasted_iota(jnp.int32, (128, D), 0)
+    column = jnp.where(sub == MISC + 3, gain_ref[0:1], 0.0).T
+    slab_ref[:, 256:384] = (dot(selector(), grads.astype(bf16), 1, 1) + column).astype(bf16)
+    slab = slab_ref[...]
+    for x in range(4):
+        rows = slice(96 * x, 96 * x + 96)
+        keep_ref[rows, :] = dot(picked(96, 2 * x + at_ref[2]), slab).astype(bf16)
+        give_ref[rows, :] = dot(picked(96, 2 * x + 1 - at_ref[2]), slab).astype(bf16)
     out_ref[:, 0:384] = dot(normed, dv_ref[:, 0:384], 0, 0).astype(bf16)
-    out_ref[:, 640:896] = dot(normed, dv_ref[:, 384:640], 0, 0).astype(bf16)
     outs = dot(cot_ref[...], nout_ref[...], 0, 0)
     out_ref[:, 384:512] = outs[:, 0:128].astype(bf16)
     tile = outs[:, 128:256] + dot(normed_ref[HALO:, :], dstep_ref[...], 0, 0)
-    grads = jnp.concatenate([jnp.zeros((MISC + 5, 256), f32), conv_ref[0:5, :]], axis=0)
-    grads = jnp.concatenate([grads, jnp.zeros((128 - MISC - 10, 256), f32)], axis=0)
-    high = grads.astype(bf16)
-    lower = (grads - high.astype(f32)).astype(bf16)
-    sel = selector()
-    tile = tile + dot(sel, high, 1, 1) + pltpu.roll(dot(sel, lower, 1, 1), 5, 1)
-    gain = gain_ref[0:1]
-    gain_high = gain.astype(bf16).astype(f32)
-    sub = lax.broadcasted_iota(jnp.int32, (128, D), 0)
-    column = jnp.where(
-        sub == MISC + 3, gain_high, jnp.where(sub == MISC + 4, gain - gain_high, 0.0)
-    ).T
     turned = jnp.concatenate([chan_ref[...], jnp.zeros((112, 256), f32)], axis=0).T
-    turned = jnp.where(lanes(256) < 9, turned, 0.0)
     shared = jnp.zeros((48, 128), f32)
     for g in range(4):
-        shared = shared + rolled(turned[48 * g : 48 * g + 48], MISC + 16 + 9 * g)
-    tile = tile + column + jnp.concatenate([shared] * N_SEQ, axis=0)
-    out_ref[:, 512:640] = tile.astype(bf16)
+        piece = turned[48 * g : 48 * g + 48]
+        piece = jnp.where(lanes(48) < (9 if g == 0 else 6), piece, 0.0)
+        shared = shared + rolled(piece, CHAN[g])
+    out_ref[:, 512:640] = (tile + jnp.concatenate([shared] * N_SEQ, axis=0)).astype(bf16)
+
+
+def slab_pair_kernel(at_ref, keep_ref, got_ref, after_ref, own_ref, s1, s2, s3, sum_ref):
+    del after_ref
+    sum_ref[...] = keep_ref[...].astype(f32) + got_ref[...].astype(f32)
+    for by, ref in enumerate((own_ref, s1, s2, s3)):
+        start = pl.multiple_of(lax.rem(at_ref[1] + by, 4) * 96, 96)
+        ref[...] = sum_ref[pl.ds(start, 96), :].astype(bf16)
+
+
+def merge_kernel(a_ref, b_ref, c_ref, d_ref, pack_ref, out_ref):
+    total = a_ref[...].astype(f32) + b_ref[...].astype(f32)
+    total = total + c_ref[...].astype(f32) + d_ref[...].astype(f32)
+    misc = total[:, 256:384]
+    lane = lanes(96)
+    d = lax.broadcasted_iota(jnp.int32, (D, 96), 0)
+    a = lax.broadcasted_iota(jnp.int32, (D, 96), 1)
+    gap = d - slab_rows(a)
+    places, laid = [], []
+    for j in range(8):
+        tile = rolled(total[:, 128 * (j // 4) : 128 * (j // 4) + 128], SLAB - 32 * (j % 4))
+        one = misc if j == 0 else rolled(misc, -1 - j)
+        laid.append(
+            jnp.where(lane >= SLAB, tile, jnp.where((lane == MISC + 3) & (j < 6), one, 0.0))
+        )
+        places.append(jnp.where(gap == 6 * j, 1.0, 0.0))
+    added = dot(
+        jnp.concatenate(places, axis=1).astype(bf16),
+        jnp.concatenate(laid, axis=0).astype(bf16),
+    )
+    out_ref[:, 0:512] = pack_ref[:, 0:512]
+    out_ref[:, 512:640] = (pack_ref[:, 512:640].astype(f32) + added).astype(bf16)
 
 
 def pair_kernel(
     at_ref, keep_ref, got_ref, edge0_ref, edge1_ref, out_keep_ref, out_got_ref,
     own_ref, s1, s2, s3, sum_ref,
 ):
-    sum_ref[:, 0:D] = keep_ref[...].astype(f32) + got_ref[...].astype(f32)
-    sum_ref[256 - HALO :, 0:D] += edge0_ref[...].astype(f32) + edge1_ref[...].astype(f32)
-    sum_ref[:, D:] = out_keep_ref[...].astype(f32) + out_got_ref[...].astype(f32)
+    sum_ref[0:256] = keep_ref[...].astype(f32) + got_ref[...].astype(f32)
+    sum_ref[256 - HALO : 256] += edge0_ref[...].astype(f32) + edge1_ref[...].astype(f32)
+    sum_ref[256:512] = out_keep_ref[...].astype(f32) + out_got_ref[...].astype(f32)
     for by, ref in enumerate((own_ref, s1, s2, s3)):
         start = pl.multiple_of(lax.rem(at_ref[1] + by, 4) * 64, 64)
-        ref[...] = sum_ref[pl.ds(start, 64), :].astype(bf16)
+        for k in range(2):
+            ref[64 * k : 64 * k + 64] = sum_ref[pl.ds(256 * k + start, 64), :].astype(bf16)
 
 
 def four_kernel(at_ref, a_ref, b_ref, c_ref, d_ref, hid_ref, out_ref):
     total = a_ref[...].astype(f32) + b_ref[...].astype(f32)
     total = total + c_ref[...].astype(f32) + d_ref[...].astype(f32)
     start = pl.multiple_of((4 * at_ref[2] + at_ref[1]) * 64, 64)
-    out_ref[:, 0:D] = total[:, 0:D].astype(bf16)
-    out_ref[:, D:] = (total[:, D:] + hid_ref[pl.ds(start, 64), :].astype(f32)).astype(bf16)
+    out_ref[:, 0:D] = total[0:64].astype(bf16)
+    out_ref[:, D:] = (total[64:128] + hid_ref[pl.ds(start, 64), :].astype(f32)).astype(bf16)
 
 
 def input_kernel(*refs):
@@ -782,18 +831,18 @@
 
 def update_kernel(*refs):
     grad_ref, refs = refs[0], refs[1:]
-    proj, step, out, chan, head = (refs[3 * k : 3 * k + 3] for k in range(5))
-    outs = refs[15:]
-    proj_o, step_o, out_o, chan_o, head_o = (outs[3 * k : 3 * k + 3] for k in range(5))
-    rest_ref = outs[15]
+    proj, step, out, chan, head, shared, gain, conv = (
+        refs[3 * k : 3 * k + 3] for k in range(8)
+    )
+    outs = refs[24:]
+    proj_o, step_o, out_o, chan_o, head_o, shared_o, gain_o, conv_o = (
+        outs[3 * k : 3 * k + 3] for k in range(8)
+    )
+    wide_ref, conv_ref = outs[24:]
     total = grad_ref[0].astype(f32)
     for q in range(1, N_SEQ):
         total = total + grad_ref[q].astype(f32)
     misc = total[:, 512:640]
-    rest_ref[...] = jnp.zeros_like(rest_ref)
-    for h in range(N_HEAD):
-        rest_ref[h, 0:6, 0:256] = total[6 * h : 6 * h + 6, 640:896]
-        rest_ref[h, 0:6, 256:384] = misc[6 * h : 6 * h + 6]
     for h in range(3):
         w, m, v = (r[h] for r in proj)
         put(proj_o, h, adam(w, total[:, 128 * h : 128 * (h + 1)], m, v, RATE_D))
@@ -805,8 +854,7 @@
     at = (slice(None), slice(None))
     w, m, v = (r[at] for r in step)
     put(step_o, at, adam(w, turned[MISC : MISC + 3, 0:48], m, v, RATE_D))
-    first = MISC + 16
-    p = [turned[first + 9 * g : first + 9 * g + 9] for g in range(4)]
+    p = [turned[CHAN[g] : CHAN[g] + 9] for g in range(4)]
     lane = lanes(9)
     wrapped = rolled(p[2], 96)
     pair = (
@@ -815,34 +863,33 @@
     )
     for h in range(3):
         piece = half(pair[0]) if h == 1 else pair[h // 2]
-        at = (slice(None), h, slice(None))
-        w, m, v = (r[at] for r in chan)
-        put(chan_o, at, adam(w, piece[0:6, 0:64], m, v, 0.5))
-    at = (slice(None), slice(None))
+        spot = (slice(None), h, slice(None))
+        w, m, v = (r[spot] for r in chan)
+        put(chan_o, spot, adam(w, piece[0:6, 0:64], m, v, 0.5))
     w, m, v = (r[at] for r in head)
-    put(head_o, at, adam(w, pair[0][6:9, 0:3], m, v, 1.0))
-
-
-def rest_kernel(*refs):
-    got_ref, refs = refs[0], refs[1:]
-    shared, gain, conv = (refs[3 * k : 3 * k + 3] for k in range(3))
-    outs = refs[9:]
-    shared_o, gain_o, conv_o = (outs[3 * k : 3 * k + 3] for k in range(3))
-    total = got_ref[0]
-    for q in range(1, N_HEAD):
-        total = total + got_ref[q]
-    at = (slice(None), slice(None))
+    put(head_o, at, adam(w, p[0][6:9, 0:3], m, v, 1.0))
+    lane = lanes(6)
+    for t in range(2):
+        tile = jnp.zeros((6, 128), f32)
+        for i in range(4):
+            j = 4 * t + i
+            own = jnp.where(lane >= SLAB, misc[6 * j : 6 * j + 6], 0.0)
+            tile = tile + rolled(own, 32 * i - SLAB)
+        wide_ref[:, 128 * t : 128 * t + 128] = tile
     w, m, v = (r[at] for r in shared)
-    put(shared_o, at, adam(w, total[0:6, 0:256], m, v, RATE_D))
-    column = total[:, 256 + MISC + 3 : 256 + MISC + 4] + total[:, 256 + MISC + 4 : 256 + MISC + 5]
-    sub = lax.broadcasted_iota(jnp.int32, (8, 128), 0)
-    row = jnp.sum(jnp.where(sub == lanes(8), column, 0.0), axis=0, keepdims=True)
+    put(shared_o, at, adam(w, wide_ref[...], m, v, RATE_D))
+    column = turned[MISC + 3 : MISC + 4]
     w, m, v = (r[at] for r in gain)
-    put(gain_o, at, adam(w, row[:, 0:6], m, v, 0.5))
-    tile = total[0:2, 256:384]
-    both = rolled(tile, -(MISC + 5)) + rolled(tile, -(MISC + 10))
+    put(gain_o, at, adam(w, column[:, 0:6], m, v, 0.5))
+    lane = lanes(2)
+    taps = jnp.zeros((2, 128), f32)
+    for t in range(5):
+        taps = jnp.where(
+            lane == t, misc[6 + 6 * t : 8 + 6 * t, MISC + 3 : MISC + 4], taps
+        )
+    conv_ref[...] = taps
     w, m, v = (r[at] for r in conv)
-    put(conv_o, at, adam(w, both[:, 0:5], m, v, 0.5))
+    put(conv_o, at, adam(w, conv_ref[:, 0:5], m, v, 0.5))
 
 
 def exchange(blocks, axis):
@@ -933,28 +980,28 @@
         *stats, y_full, d_normed, conv, aux, taps, name="gated",
     )
     adjoints = [sent_adj] + [around(sent_adj, "seq_1", by) for by in (1, 2, 3)]
+    half_rows = ((T // 2, D), bf16)
+    out_keep, out_give = call(
+        out_kernel, [half_rows] * 2, where, normed_out, weights, smem=(0,),
+        scratch=[pltpu.VMEM((T, D), f32)], name="out",
+    )
+    out_taken = around(out_give, "head_1", 1)
     group, adj_in, adj_passed = call(
         group_back_kernel,
         [((192, 128), bf16), ((192, 128), f32), ((192, 128), f32)],
-        where, *adjoints, group_tails, smem=(0,), name="group_back",
+        where, *adjoints, group_tails, out_keep, smem=(0,), anywhere=(6,), name="group_back",
     )
     groups = [group] + [around(group, "seq_0", by) for by in (1, 2, 3)]
-    half_rows = ((T // 2, D), bf16)
-    (
-        d_x, d_b, d_cum, x_act, b_act, slopes, out_keep, out_give, d_value_c, c_rows
-    ) = call(
+    piece = ((T // N_HEAD, D), bf16)
+    d_x, d_b, d_cum, x_act, b_act, slopes, d_value_c, c_rows = call(
         own_back_kernel,
         [
             ((T, 256), f32), ((T, 128), f32), ((T, 128), f32), ((T, 256), f32),
-            ((T, 128), bf16), ((T, 512), f32), half_rows, half_rows,
-            ((HALO + T, 128), bf16), ((8, 128), f32),
+            ((T, 128), bf16), ((T, 512), f32), ((HALO + T, 128), bf16), ((8, 128), f32),
         ],
-        where, d_y, y_full, y_own, conv, aux, decays, mixing, state, normed_out, weights,
-        values, conv_taps, marks, smem=(0,),
-        scratch=[pltpu.VMEM((T + 2 * HALO, 128), f32), pltpu.VMEM((T, D), f32)],
-        name="own_back",
-    )
-    out_taken = around(out_give, "head_1", 1)
+        d_y, y_full, y_own, conv, aux, decays, mixing, state, values, conv_taps, marks,
+        scratch=[pltpu.VMEM((T + 2 * HALO, 128), f32)], name="own_back",
+    )
     d_values, d_step, keep, give, edge, chan, d_conv, d_gain = call(
         back_kernel,
         [
@@ -970,22 +1017,34 @@
     )
     taken = around(give, "head_1", 1)
     edges = [to_previous(edge, core) for core in range(2)]
-    (grads,) = call(
-        grad_kernel, [((D, NG), bf16)],
-        normed, d_values, d_step, normed_out, cotangent, d_conv, d_gain, chan, name="grad",
-    )
-    grads, taken, out_taken, edges = lax.optimization_barrier(
-        (grads, taken, out_taken, edges)
-    )
-    grads = exchange(grads.reshape(N_SEQ, 48, NG), SEQ)
-
-    piece = ((T // N_HEAD, 2 * D), bf16)
+    slab_rows_all = ((384, 384), bf16)
+    grads, slab_keep, slab_give = call(
+        grad_kernel, [((D, NW), bf16), slab_rows_all, slab_rows_all],
+        where, normed, d_values, d_step, normed_out, cotangent, d_conv, d_gain, chan,
+        *edges, smem=(0,), anywhere=(9, 10),
+        scratch=[pltpu.VMEM((D, 384), bf16)], name="grad",
+    )
+    slab_taken = around(slab_give, "head_1", 1)
     pieces = call(
-        pair_kernel, [piece] * 4, where, keep, taken, *edges, out_keep, out_taken,
-        smem=(0,), scratch=[pltpu.VMEM((T // 2, 2 * D), f32)], name="pair",
+        pair_kernel, [((T // 4, D), bf16)] * 4, where, keep, taken, *edges, out_keep,
+        out_taken, smem=(0,), scratch=[pltpu.VMEM((T, D), f32)], name="pair",
     )
     parts = [pieces[0]] + [around(pieces[by], "head_0", by) for by in (1, 2, 3)]
-    (own,) = call(four_kernel, [piece], where, *parts, hidden_in, smem=(0,), name="four")
+    slab_piece = ((96, 384), bf16)
+    slabs = call(
+        slab_pair_kernel, [slab_piece] * 4, where, slab_keep, slab_taken, pieces[0],
+        smem=(0,), anywhere=(3,),
+        scratch=[pltpu.VMEM((384, 384), f32)], name="slab_pair",
+    )
+    slabs = [slabs[0]] + [around(slabs[by], "head_0", by) for by in (1, 2, 3)]
+
+    (grads,) = call(merge_kernel, [((D, NW), bf16)], *slabs, grads, name="merge")
+    grads, parts = lax.optimization_barrier((grads, parts))
+    grads = exchange(grads.reshape(N_SEQ, 48, NW), SEQ)
+    (own,) = call(
+        four_kernel, [((T // N_HEAD, 2 * D), bf16)], where, *parts, hidden_in,
+        smem=(0,), name="four",
+    )
     near = [own] + [around(own, "head_0", by) for by in (1, 2, 3)]
     far = [around(a, "head_1", 1) for a in near]
     input_grad, block_out = call(
@@ -995,28 +1054,24 @@
 
     proj, step, out = (3, 48, 128), (3, 48), (3, 48, 64)
     shapes = [proj] * 3 + [step] * 3 + [out] * 3 + [(6, 3, 64)] * 3 + [(3, 3)] * 3
+    shapes += [(6, 256)] * 3 + [(1, 6)] * 3 + [(2, 5)] * 3
     updated = call(
-        update_kernel,
-        [(s, f32) for s in shapes] + [((N_HEAD, 8, 384), f32)],
+        update_kernel, [(s, f32) for s in shapes],
         grads, *matrices, *steps, *out_weights, channel_params, channel_first,
-        channel_second, head_params, head_first, head_second, name="update",
-    )
-    rest = exchange(updated[15], HEAD)
-    shared = call(
-        rest_kernel,
-        [(s, f32) for s in [(6, 256)] * 3 + [(1, 6)] * 3 + [(2, 5)] * 3],
-        rest, shared_weight, shared_first, shared_second, *gains_in, shared_conv, conv_first,
-        conv_second, name="rest",
+        channel_second, head_params, head_first, head_second, shared_weight, shared_first,
+        shared_second, *gains_in, shared_conv, conv_first, conv_second,
+        scratch=[pltpu.VMEM((6, 256), f32), pltpu.VMEM((2, 128), f32)],
+        params=WIDE, name="update",
     )
     return (
         block_out, input_grad,
         *(jnp.transpose(a, (1, 0, 2)) for a in updated[0:3]),
         *(a.T for a in updated[3:6]),
         *(jnp.transpose(a, (0, 2, 1)) for a in updated[6:9]),
-        *shared[0:3],
-        *(g.reshape(6) for g in shared[3:6]),
+        *updated[15:18],
+        *(g.reshape(6) for g in updated[18:21]),
         *updated[9:15],
-        *shared[6:9],
+        *updated[21:24],
     )
 
 

time: 160 us -> 155 us (0.969)
  local copies, waits for them, and re-layouts: 12.1 us -> 4.74 us
  starting transfers between devices: 66.5 us -> 72.3 us
  waiting for transfers between devices: 46.4 us -> 40.9 us
  Pallas kernels: 32.6 us -> 35.4 us
    ppermute x35 -> x39, starting transfers between devices: 41.1 us -> 51.3 us  [around(): return lax.ppermute(a, axis, [(i, (i + by) % peers) for i in range(peers)])]
    unnamed x81 -> x23, local copies, waits for them, and re-layouts: 12 us -> 4.57 us
    ppermute x35 -> x39, waiting for transfers between devices: 31.9 us -> 25.3 us  [around(): return lax.ppermute(a, axis, [(i, (i + by) % peers) for i in range(peers)])]
    all_to_all x3 -> x2, starting transfers between devices: 19.5 us -> 15.2 us  [exchange(): return lax.all_to_all(blocks, axis, 0, 0, tiled=True)]
    ppermute x2, waiting for transfers between devices: 0.97 us -> 3.85 us  [to_previous(): return lax.ppermute(a, SEQ + ('head_1',), pairs)]
    pallas_call x16 -> x18, Pallas kernels: 32.6 us -> 35.4 us  [call(): pl.pallas_call(kernel, out_shape=[jax.ShapeDtypeStruct(s, d) for s, d in...]
    all_to_all x3 -> x2, waiting for transfers between devices: 13.5 us -> 11.7 us  [exchange(): return lax.all_to_all(blocks, axis, 0, 0, tiled=True)]
  transfers between devices with their start and end apart: 41 -> 44, of which waited for: 20 -> 19; matrix products, arithmetic and copies ran while one was open for 0% -> 0% of each run, Pallas kernels for 14% -> 15%
where the time goes in v5:
time: 155 us
  starting transfers between devices  72.3 us (47%)
  waiting for transfers between devices  40.9 us (26%)
  Pallas kernels  35.4 us (23%)
  local copies, waits for them, and re-layouts  4.74 us (3%)
    ppermute x39, starting transfers between devices, around(): return lax.ppermute(a, axis, [(i, (i + by) % peers) for i in range(peers)])  51.3 us
    pallas_call x18, Pallas kernels, call(): pl.pallas_call(kernel, out_shape=[jax.ShapeDtypeStruct(s, d) for s, d in...  35.4 us
    ppermute x39, waiting for transfers between devices, around(): return lax.ppermute(a, axis, [(i, (i + by) % peers) for i in range(peers)])  25.3 us
    all_to_all x2, starting transfers between devices, exchange(): return lax.all_to_all(blocks, axis, 0, 0, tiled=True)  15.2 us
    all_to_all x2, waiting for transfers between devices, exchange(): return lax.all_to_all(blocks, axis, 0, 0, tiled=True)  11.7 us
    unnamed x23, local copies, waits for them, and re-layouts  4.57 us
    ppermute x2, waiting for transfers between devices, to_previous(): return lax.ppermute(a, SEQ + ('head_1',), pairs)  3.85 us
    ppermute x1, starting transfers between devices, to_next(): return lax.ppermute(a, SEQ, [(i, i + 1) for i in range(N_SEQ - 1)])  3.27 us
  transfers between devices with their start and end apart: 44, of which 19 were waited for; matrix products, arithmetic and copies ran while one was open for 0% of the time, Pallas kernels for 15%

profile of v5, /device:TPU:1, one launch (start us, length us, event | category | flops | bytes accessed | tf_op | source)
XLA Modules:
  0.0 154.7 jit_solution(15840809508297654404)
XLA Ops:
  6.4 8.7 %all-to-all-start = ((bf16[16,48,640]{2,1,0:T(8,128)(2,1)}), bf16[16,48,640]{2,1,0:T(8,128)(2,1)S(1)}, u32[]{:S(2)}, u32[]{:S(2)}) async-start(bf16[16,48,640]{2,1,0:T(8,128)(2,1)} %pack.1), calls=%async_computation | async-start | bytes 1966080 | tf_op jit(solution)/shard_map/all_to_all | solution.py:896
  15.2 3.3 %collective-permute-start.7 = (bf16[16,768]{1,0:T(8,128)(2,1)S(1)}, bf16[16,768]{1,0:T(8,128)(2,1)S(1)}, u32[]{:S(2)}, u32[]{:S(2)}) collective-permute-start(bf16[16,768]{1,0:T(8,128)(2,1)S(1)} %slice.6), channel_id=1, source_target_pairs={{0,8},{8,16},{16,24},{24,32},{32,40},{40,48},{48,56},{56,64},{64,7... | collective-permute-start | bytes 73736 | tf_op jit(solution)/shard_map/ppermute | solution.py:905
  18.7 11.7 %all-to-all-done = bf16[16,48,640]{2,1,0:T(8,128)(2,1)S(1)} async-done(((bf16[16,48,640]{2,1,0:T(8,128)(2,1)}), bf16[16,48,640]{2,1,0:T(8,128)(2,1)S(1)}, u32[]{:S(2)}, u32[]{:S(2)}) %all-to-all-start) | async-done | bytes 983072 | tf_op jit(solution)/shard_map/all_to_all | solution.py:896
  31.0 2.5 %collective-permute-start.2 = (bf16[96,384]{1,0:T(8,128)(2,1)S(1)}, bf16[96,384]{1,0:T(8,128)(2,1)S(1)}, u32[]{:S(2)}, u32[]{:S(2)}) collective-permute-start(bf16[96,384]{1,0:T(8,128)(2,1)S(1)} %slab.1.refs_1_), channel_id=1, source_target_pairs={{0,6},{2,0},{4,2},{6,4},{1,7},{3,1},{5,3},{7,5},{8,14},{10,8},{12,... | collective-permute-start | bytes 221192 | tf_op jit(solution)/shard_map/ppermute | solution.py:901
  34.6 3.4 %collective-permute-start.3 = (bf16[96,384]{1,0:T(8,128)(2,1)S(1)}, bf16[96,384]{1,0:T(8,128)(2,1)S(1)}, u32[]{:S(2)}, u32[]{:S(2)}) collective-permute-start(bf16[96,384]{1,0:T(8,128)(2,1)S(1)} %slab.1.refs_1_), channel_id=1, source_target_pairs={{0,1},{1,0},{2,3},{3,2},{4,5},{5,4},{6,7},{7,6},{8,9},{9,8},{10,11... | collective-permute-start | bytes 221192 | tf_op jit(solution)/shard_map/ppermute | solution.py:901
  38.3 3.9 %collective-permute-start.5 = (bf16[96,384]{1,0:T(8,128)(2,1)S(1)}, bf16[96,384]{1,0:T(8,128)(2,1)S(1)}, u32[]{:S(2)}, u32[]{:S(2)}) collective-permute-start(bf16[96,384]{1,0:T(8,128)(2,1)S(1)} %collective-permute-done.1.refs_3_), channel_id=1, source_target_pairs={{0,1},{1,0},{2,3},{3,2},{4,5},{5,4},{6,7},{7,6},{8,9},{9,8},{10,11... | collective-permute-start | bytes 221192 | tf_op jit(solution)/shard_map/ppermute | solution.py:901
  43.9 4.7 %first.1 = (bf16[528,768]{1,0:T(8,128)(2,1)S(1)}, f32[528,640]{1,0:T(8,128)S(1)}, f32[512,640]{1,0:T(8,128)S(1)}, f32[512,128]{1,0:T(8,128)S(1)}, bf16[208,128]{...) custom-call(s32[3]{0:T(128)S(1)} %pad_add_fusion.refs_0_.at_ref, ...), custom_call_target="tpu_custom_call" | custom-call | tf_op jit(solution)/shard_map/first/pallas_call | solution.py:46
  48.7 1.7 %collective-permute-start.9 = (bf16[208,128]{1,0:T(8,128)(2,1)S(1)}, bf16[208,128]{1,0:T(8,128)(2,1)S(1)}, u32[]{:S(2)}, u32[]{:S(2)}) collective-permute-start(bf16[208,128]{1,0:T(8,128)(2,1)S(1)} %get-tuple-element.115.a_ref.mine_ref), channel_id=1, source_target_pairs={{0,16},{8,24},{16,0},{24,8},{1,17},{9,25},{17,1},{25,9},{2,18},{10... | collective-permute-start | bytes 159752 | tf_op jit(solution)/shard_map/ppermute | solution.py:901
  51.6 1.6 %collective-permute-done.9.c_ref = bf16[208,128]{1,0:T(8,128)(2,1)S(1)} collective-permute-done((bf16[208,128]{1,0:T(8,128)(2,1)S(1)}, bf16[208,128]{1,0:T(8,128)(2,1)S(1)}, u32[]{:S(2)}, u32[]{:S(2)}) %collective-permute-start.9) | collective-permute-done | bytes 53280 | tf_op jit(solution)/shard_map/ppermute | solution.py:901
  57.5 2.4 %own.1 = (f32[512,256]{1,0:T(8,128)S(1)}, f32[512,256]{1,0:T(8,128)S(1)}, bf16[3,512,512]{2,1,0:T(8,128)(2,1)S(1)}, bf16[3,512,512]{2,1,0:T(8,128)(2,1)S(1)}) custom-call(f32[512,640]{1,0:T(8,128)S(1)} %get-tuple-element.119.c_ref, f32[512,128]{1,0:T(8,128)S(1)} %get-tuple-element.120.aux_ref, bf16[512,768]{1,0:T(8,128)(2,1)S(1)} %copy-done.1, ...), custom_call_target="tpu_custom_call" | custom-call | tf_op jit(solution)/shard_map/own/pallas_call | solution.py:46
  62.7 3.1 %collective-permute-start.14 = (f32[8,512]{1,0:T(8,128)S(1)}, f32[8,512]{1,0:T(8,128)S(1)}, u32[]{:S(2)}, u32[]{:S(2)}) collective-permute-start(f32[8,512]{1,0:T(8,128)S(1)} %get-tuple-element.123), channel_id=1, source_target_pairs={{0,1},{1,0},{2,3},{3,2},{4,5},{5,4},{6,7},{7,6},{8,9},{9,8},{10,11... | collective-permute-start | bytes 49160 | tf_op jit(solution)/shard_map/ppermute | solution.py:901
  69.2 1.8 %collective-permute-done.16.s2_ref = f32[8,512]{1,0:T(8,128)S(1)} collective-permute-done((f32[8,512]{1,0:T(8,128)S(1)}, f32[8,512]{1,0:T(8,128)S(1)}, u32[]{:S(2)}, u32[]{:S(2)}) %collective-permute-start.16) | collective-permute-done | bytes 16416 | tf_op jit(solution)/shard_map/ppermute | solution.py:901
  71.6 1.5 gated.1
  76.3 2.2 %collective-permute-done.19.c_ref = bf16[192,128]{1,0:T(8,128)(2,1)S(1)} collective-permute-done((bf16[192,128]{1,0:T(8,128)(2,1)S(1)}, bf16[192,128]{1,0:T(8,128)(2,1)S(1)}, u32[]{:S(2)}, u32[]{:S(2)}) %collective-permute-start.19) | collective-permute-done | bytes 49184 | tf_op jit(solution)/shard_map/ppermute | solution.py:901
  79.7 1.7 %collective-permute-start.23 = (bf16[192,128]{1,0:T(8,128)(2,1)S(1)}, bf16[192,128]{1,0:T(8,128)(2,1)S(1)}, u32[]{:S(2)}, u32[]{:S(2)}) collective-permute-start(bf16[192,128]{1,0:T(8,128)(2,1)S(1)} %get-tuple-element.129.a0_ref), channel_id=1, source_target_pairs={{0,96},{32,0},{64,32},{96,64},{1,97},{33,1},{65,33},{97,65},{2,98}... | collective-permute-start | bytes 147464 | tf_op jit(solution)/shard_map/ppermute | solution.py:901
  82.0 4.0 %collective-permute-start.28 = (bf16[256,768]{1,0:T(8,128)(2,1)S(1)}, bf16[256,768]{1,0:T(8,128)(2,1)S(1)}, u32[]{:S(2)}, u32[]{:S(2)}) collective-permute-start(bf16[256,768]{1,0:T(8,128)(2,1)S(1)} %get-tuple-element.160), channel_id=1, source_target_pairs={{0,1},{1,0},{2,3},{3,2},{4,5},{5,4},{6,7},{7,6},{8,9},{9,8},{10,11... | collective-permute-start | bytes 1179656 | tf_op jit(solution)/shard_map/ppermute | solution.py:901
  86.1 3.0 %own_back.1 = (f32[512,256]{1,0:T(8,128)S(1)}, f32[512,128]{1,0:T(8,128)S(1)}, f32[512,128]{1,0:T(8,128)S(1)}, f32[512,256]{1,0:T(8,128)S(1)}, bf16[512,128]{1,0...) custom-call(f32[512,256]{1,0:T(8,128)S(1)} %get-tuple-element.134.dy_ref, ...), custom_call_target="tpu_custom_call" | custom-call | tf_op jit(solution)/shard_map/own_back/pallas_call | solution.py:46
  89.1 6.3 %back.1 = (bf16[528,640]{1,0:T(8,128)(2,1)S(1)}, bf16[512,128]{1,0:T(8,128)(2,1)S(1)}, bf16[256,768]{1,0:T(8,128)(2,1)S(1)}, bf16[256,768]{1,0:T(8,128)(2,1)S(1)...) custom-call(s32[3]{0:T(128)S(1)} %pad_add_fusion.refs_0_.at_ref, ...), custom_call_target="tpu_custom_call" | custom-call | tf_op jit(solution)/shard_map/back/pallas_call | solution.py:46
  95.4 2.1 %collective-permute-start.27 = (bf16[256,768]{1,0:T(8,128)(2,1)S(1)}, bf16[256,768]{1,0:T(8,128)(2,1)S(1)}, u32[]{:S(2)}, u32[]{:S(2)}) collective-permute-start(bf16[256,768]{1,0:T(8,128)(2,1)S(1)} %get-tuple-element.159), channel_id=1, source_target_pairs={{0,1},{1,0},{2,3},{3,2},{4,5},{5,4},{6,7},{7,6},{8,9},{9,8},{10,11... | collective-permute-start | bytes 1179656 | tf_op jit(solution)/shard_map/ppermute | solution.py:901
  100.1 2.0 %collective-permute-done.25.a1.edge1_ref = bf16[16,768]{1,0:T(8,128)(2,1)S(1)} collective-permute-done((bf16[16,768]{1,0:T(8,128)(2,1)S(1)}, bf16[16,768]{1,0:T(8,128)(2,1)S(1)}, u32[]{:S(2)}, u32[]{:S(2)}) %collective-permute-start.25) | collective-permute-done | bytes 24608 | tf_op jit(solution)/shard_map/ppermute | solution.py:910
  102.1 1.9 %collective-permute-done.24.a0.edge0_ref = bf16[16,768]{1,0:T(8,128)(2,1)S(1)} collective-permute-done((bf16[16,768]{1,0:T(8,128)(2,1)S(1)}, bf16[16,768]{1,0:T(8,128)(2,1)S(1)}, u32[]{:S(2)}, u32[]{:S(2)}) %collective-permute-start.24) | collective-permute-done | bytes 24608 | tf_op jit(solution)/shard_map/ppermute | solution.py:910
  103.9 3.3 %grad.1 = (bf16[768,640]{1,0:T(8,128)(2,1)S(1)}, bf16[384,384]{1,0:T(8,128)(2,1)S(1)}, bf16[384,384]{1,0:T(8,128)(2,1)S(1)}) custom-call(s32[3]{0:T(128)S(1)} %pad_add_fusion.refs_0_.at_ref, bf16[528,768]{1,0:T(8,128)(2,1)S(1)} %get-tuple-element.114.normed_ref, bf16[528,640]{1,0:T(8,128)(2,1)S(1)} %get-tuple-element.150.dv_ref, ...), custom_call_target="tpu_custom_call" | custom-call | tf_op jit(solution)/shard_map/grad/pallas_call | solution.py:46
  108.9 2.3 %collective-permute-start.33 = (bf16[128,768]{1,0:T(8,128)(2,1)S(1)}, bf16[128,768]{1,0:T(8,128)(2,1)S(1)}, u32[]{:S(2)}, u32[]{:S(2)}) collective-permute-start(bf16[128,768]{1,0:T(8,128)(2,1)S(1)} %get-tuple-element.168), channel_id=1, source_target_pairs={{0,4},{2,6},{4,0},{6,2},{1,5},{3,7},{5,1},{7,3},{8,12},{10,14},{12... | collective-permute-start | bytes 589832 | tf_op jit(solution)/shard_map/ppermute | solution.py:901
  114.5 7.6 %collective-permute-done.29.b_ref = bf16[96,384]{1,0:T(8,128)(2,1)S(1)} collective-permute-done((bf16[96,384]{1,0:T(8,128)(2,1)S(1)}, bf16[96,384]{1,0:T(8,128)(2,1)S(1)}, u32[]{:S(2)}, u32[]{:S(2)}) %collective-permute-start.29) | collective-permute-done | bytes 73760 | tf_op jit(solution)/shard_map/ppermute | solution.py:901
  122.9 2.4 %collective-permute-done.31.d_ref = bf16[96,384]{1,0:T(8,128)(2,1)S(1)} collective-permute-done((bf16[96,384]{1,0:T(8,128)(2,1)S(1)}, bf16[96,384]{1,0:T(8,128)(2,1)S(1)}, u32[]{:S(2)}, u32[]{:S(2)}) %collective-permute-start.31) | collective-permute-done | bytes 73760 | tf_op jit(solution)/shard_map/ppermute | solution.py:901
  125.3 1.7 %merge.1 = bf16[768,640]{1,0:T(8,128)(2,1)} custom-call(bf16[96,384]{1,0:T(8,128)(2,1)S(1)} %get-tuple-element.162.a_ref, bf16[96,384]{1,0:T(8,128)(2,1)S(1)} %collective-permute-done.29.b_ref, bf16[96,384]{1,0:T(8,128)(2,1)S(1)} %collective-permute-done.30.c_ref, bf16[96,384]{1,0:T(8,128)(2,1)S(1)} %collective-permute-done.31.d_ref, ...), custom_call_target="tpu_custom_call" | custom-call | tf_op jit(solution)/shard_map/merge/pallas_call | solution.py:46
  127.0 6.4 %all-to-all-start.1 = ((bf16[16,48,640]{2,1,0:T(8,128)(2,1)}), bf16[16,48,640]{2,1,0:T(8,128)(2,1)}, u32[]{:S(2)}, u32[]{:S(2)}) async-start(bf16[16,48,640]{2,1,0:T(8,128)(2,1)} %bitcast.9), calls=%async_computation.1 | async-start | bytes 1966080 | tf_op jit(solution)/shard_map/all_to_all | solution.py:896
  136.1 3.9 %collective-permute-start.38 = (bf16[64,1536]{1,0:T(8,128)(2,1)S(1)}, bf16[64,1536]{1,0:T(8,128)(2,1)S(1)}, u32[]{:S(2)}, u32[]{:S(2)}) collective-permute-start(bf16[64,1536]{1,0:T(8,128)(2,1)S(1)} %four.1.refs_1_), channel_id=1, source_target_pairs={{0,1},{1,0},{2,3},{3,2},{4,5},{5,4},{6,7},{7,6},{8,9},{9,8},{10,11... | collective-permute-start | bytes 589832 | tf_op jit(solution)/shard_map/ppermute | solution.py:901
  140.0 5.1 %collective-permute-start.41 = (bf16[64,1536]{1,0:T(8,128)(2,1)S(1)}, bf16[64,1536]{1,0:T(8,128)(2,1)S(1)}, u32[]{:S(2)}, u32[]{:S(2)}) collective-permute-start(bf16[64,1536]{1,0:T(8,128)(2,1)S(1)} %collective-permute-done.37.refs_4_), channel_id=1, source_target_pairs={{0,1},{1,0},{2,3},{3,2},{4,5},{5,4},{6,7},{7,6},{8,9},{9,8},{10,11... | collective-permute-start | bytes 589832 | tf_op jit(solution)/shard_map/ppermute | solution.py:901
  146.5 1.9 %collective-permute-start.39 = (bf16[64,1536]{1,0:T(8,128)(2,1)S(1)}, bf16[64,1536]{1,0:T(8,128)(2,1)S(1)}, u32[]{:S(2)}, u32[]{:S(2)}) collective-permute-start(bf16[64,1536]{1,0:T(8,128)(2,1)S(1)} %collective-permute-done.35.refs_2_), channel_id=1, source_target_pairs={{0,1},{1,0},{2,3},{3,2},{4,5},{5,4},{6,7},{7,6},{8,9},{9,8},{10,11... | collective-permute-start | bytes 589832 | tf_op jit(solution)/shard_map/ppermute | solution.py:901
  149.5 2.4 %input.1 = (f32[512,768]{1,0:T(8,128)}, bf16[512,768]{1,0:T(8,128)(2,1)}) custom-call(s32[3]{0:T(128)S(1)} %pad_add_fusion.refs_0_.at_ref, bf16[64,1536]{1,0:T(8,128)(2,1)S(1)} %four.1.refs_1_, bf16[64,1536]{1,0:T(8,128)(2,1)S(1)} %collective-permute-done.35.refs_2_, bf16[64,1536]{1,0:T(8,128)(2,1)S(1)} %collective-permute-done.36.refs_3_, ...), custom_call_target="tpu_custom_call" | custom-call | tf_op jit(solution)/shard_map/input/pallas_call | solution.py:46
  151.9 2.6 %update.1 = (f32[3,48,128]{2,1,0:T(8,128)}, f32[3,48,128]{2,1,0:T(8,128)}, f32[3,48,128]{2,1,0:T(8,128)}, f32[3,48]{1,0:T(4,128)}, f32[3,48]{1,0:T(4,128)}, /*in...) custom-call(bf16[16,48,640]{2,1,0:T(8,128)(2,1)} %all-to-all-done.1., ...), custom_call_target="tpu_custom_call" | custom-call | tf_op jit(solution)/shard_map/update/pallas_call | solution.py:46
  (109 shorter events, 40.3 us)
Async XLA Ops:
  6.4 24.0 %all-to-all-start = ((bf16[16,48,640]{2,1,0:T(8,128)(2,1)}), bf16[16,48,640]{2,1,0:T(8,128)(2,1)S(1)}, u32[]{:S(2)}, u32[]{:S(2)}) async-start(bf16[16,48,640]{2,1,0:T(8,128)(2,1)} %pack.1), calls=%async_computation | async-start | bytes 1966080 | tf_op jit(solution)/shard_map/all_to_all | solution.py:896
  15.2 27.9 %collective-permute-start.7 = (bf16[16,768]{1,0:T(8,128)(2,1)S(1)}, bf16[16,768]{1,0:T(8,128)(2,1)S(1)}, u32[]{:S(2)}, u32[]{:S(2)}) collective-permute-start(bf16[16,768]{1,0:T(8,128)(2,1)S(1)} %slice.6), channel_id=1, source_target_pairs={{0,8},{8,16},{16,24},{24,32},{32,40},{40,48},{48,56},{56,64},{64,7... | collective-permute-start | bytes 73736 | tf_op jit(solution)/shard_map/ppermute | solution.py:905
  31.0 7.0 %collective-permute-start.2 = (bf16[96,384]{1,0:T(8,128)(2,1)S(1)}, bf16[96,384]{1,0:T(8,128)(2,1)S(1)}, u32[]{:S(2)}, u32[]{:S(2)}) collective-permute-start(bf16[96,384]{1,0:T(8,128)(2,1)S(1)} %slab.1.refs_1_), channel_id=1, source_target_pairs={{0,6},{2,0},{4,2},{6,4},{1,7},{3,1},{5,3},{7,5},{8,14},{10,8},{12,... | collective-permute-start | bytes 221192 | tf_op jit(solution)/shard_map/ppermute | solution.py:901
  33.5 4.8 %collective-permute-start.1 = (bf16[96,384]{1,0:T(8,128)(2,1)S(1)}, bf16[96,384]{1,0:T(8,128)(2,1)S(1)}, u32[]{:S(2)}, u32[]{:S(2)}) collective-permute-start(bf16[96,384]{1,0:T(8,128)(2,1)S(1)} %slab.1.refs_1_), channel_id=1, source_target_pairs={{0,4},{2,6},{4,0},{6,2},{1,5},{3,7},{5,1},{7,3},{8,12},{10,14},{12... | collective-permute-start | bytes 221192 | tf_op jit(solution)/shard_map/ppermute | solution.py:901
  34.0 8.2 %collective-permute-start = (bf16[96,384]{1,0:T(8,128)(2,1)S(1)}, bf16[96,384]{1,0:T(8,128)(2,1)S(1)}, u32[]{:S(2)}, u32[]{:S(2)}) collective-permute-start(bf16[96,384]{1,0:T(8,128)(2,1)S(1)} %slab.1.refs_1_), channel_id=1, source_target_pairs={{0,2},{2,4},{4,6},{6,0},{1,3},{3,5},{5,7},{7,1},{8,10},{10,12},{12... | collective-permute-start | bytes 221192 | tf_op jit(solution)/shard_map/ppermute | solution.py:901
  34.6 8.4 %collective-permute-start.3 = (bf16[96,384]{1,0:T(8,128)(2,1)S(1)}, bf16[96,384]{1,0:T(8,128)(2,1)S(1)}, u32[]{:S(2)}, u32[]{:S(2)}) collective-permute-start(bf16[96,384]{1,0:T(8,128)(2,1)S(1)} %slab.1.refs_1_), channel_id=1, source_target_pairs={{0,1},{1,0},{2,3},{3,2},{4,5},{5,4},{6,7},{7,6},{8,9},{9,8},{10,11... | collective-permute-start | bytes 221192 | tf_op jit(solution)/shard_map/ppermute | solution.py:901
  38.0 5.1 %collective-permute-start.6 = (bf16[96,384]{1,0:T(8,128)(2,1)S(1)}, bf16[96,384]{1,0:T(8,128)(2,1)S(1)}, u32[]{:S(2)}, u32[]{:S(2)}) collective-permute-start(bf16[96,384]{1,0:T(8,128)(2,1)S(1)} %collective-permute-done.2.refs_4_), channel_id=1, source_target_pairs={{0,1},{1,0},{2,3},{3,2},{4,5},{5,4},{6,7},{7,6},{8,9},{9,8},{10,11... | collective-permute-start | bytes 221192 | tf_op jit(solution)/shard_map/ppermute | solution.py:901
  38.3 4.8 %collective-permute-start.5 = (bf16[96,384]{1,0:T(8,128)(2,1)S(1)}, bf16[96,384]{1,0:T(8,128)(2,1)S(1)}, u32[]{:S(2)}, u32[]{:S(2)}) collective-permute-start(bf16[96,384]{1,0:T(8,128)(2,1)S(1)} %collective-permute-done.1.refs_3_), channel_id=1, source_target_pairs={{0,1},{1,0},{2,3},{3,2},{4,5},{5,4},{6,7},{7,6},{8,9},{9,8},{10,11... | collective-permute-start | bytes 221192 | tf_op jit(solution)/shard_map/ppermute | solution.py:901
  48.7 4.6 %collective-permute-start.9 = (bf16[208,128]{1,0:T(8,128)(2,1)S(1)}, bf16[208,128]{1,0:T(8,128)(2,1)S(1)}, u32[]{:S(2)}, u32[]{:S(2)}) collective-permute-start(bf16[208,128]{1,0:T(8,128)(2,1)S(1)} %get-tuple-element.115.a_ref.mine_ref), channel_id=1, source_target_pairs={{0,16},{8,24},{16,0},{24,8},{1,17},{9,25},{17,1},{25,9},{2,18},{10... | collective-permute-start | bytes 159752 | tf_op jit(solution)/shard_map/ppermute | solution.py:901
  55.3 4.6 %collective-permute-start.13 = (bf16[208,128]{1,0:T(8,128)(2,1)S(1)}, bf16[208,128]{1,0:T(8,128)(2,1)S(1)}, u32[]{:S(2)}, u32[]{:S(2)}) collective-permute-start(bf16[208,128]{1,0:T(8,128)(2,1)S(1)} %get-tuple-element.116.s0_ref), channel_id=1, source_target_pairs={{0,96},{32,0},{64,32},{96,64},{1,97},{33,1},{65,33},{97,65},{2,98}... | collective-permute-start | bytes 159752 | tf_op jit(solution)/shard_map/ppermute | solution.py:901
  56.3 4.5 %collective-permute-start.12 = (bf16[208,128]{1,0:T(8,128)(2,1)S(1)}, bf16[208,128]{1,0:T(8,128)(2,1)S(1)}, u32[]{:S(2)}, u32[]{:S(2)}) collective-permute-start(bf16[208,128]{1,0:T(8,128)(2,1)S(1)} %get-tuple-element.116.s0_ref), channel_id=1, source_target_pairs={{0,64},{32,96},{64,0},{96,32},{1,65},{33,97},{65,1},{97,33},{2,66}... | collective-permute-start | bytes 159752 | tf_op jit(solution)/shard_map/ppermute | solution.py:901
  57.0 4.4 %collective-permute-start.11 = (bf16[208,128]{1,0:T(8,128)(2,1)S(1)}, bf16[208,128]{1,0:T(8,128)(2,1)S(1)}, u32[]{:S(2)}, u32[]{:S(2)}) collective-permute-start(bf16[208,128]{1,0:T(8,128)(2,1)S(1)} %get-tuple-element.116.s0_ref), channel_id=1, source_target_pairs={{0,32},{32,64},{64,96},{96,0},{1,33},{33,65},{65,97},{97,1},{2,34}... | collective-permute-start | bytes 159752 | tf_op jit(solution)/shard_map/ppermute | solution.py:901
  74.1 4.5 %collective-permute-start.19 = (bf16[192,128]{1,0:T(8,128)(2,1)S(1)}, bf16[192,128]{1,0:T(8,128)(2,1)S(1)}, u32[]{:S(2)}, u32[]{:S(2)}) collective-permute-start(bf16[192,128]{1,0:T(8,128)(2,1)S(1)} %get-tuple-element.125.a_ref), channel_id=1, source_target_pairs={{0,16},{8,24},{16,0},{24,8},{1,17},{9,25},{17,1},{25,9},{2,18},{10... | collective-permute-start | bytes 147464 | tf_op jit(solution)/shard_map/ppermute | solution.py:901
  74.7 4.3 %collective-permute-start.18 = (bf16[192,128]{1,0:T(8,128)(2,1)S(1)}, bf16[192,128]{1,0:T(8,128)(2,1)S(1)}, u32[]{:S(2)}, u32[]{:S(2)}) collective-permute-start(bf16[192,128]{1,0:T(8,128)(2,1)S(1)} %get-tuple-element.125.a_ref), channel_id=1, source_target_pairs={{0,8},{8,16},{16,24},{24,0},{1,9},{9,17},{17,25},{25,1},{2,10},{10... | collective-permute-start | bytes 147464 | tf_op jit(solution)/shard_map/ppermute | solution.py:901
  79.7 9.4 %collective-permute-start.23 = (bf16[192,128]{1,0:T(8,128)(2,1)S(1)}, bf16[192,128]{1,0:T(8,128)(2,1)S(1)}, u32[]{:S(2)}, u32[]{:S(2)}) collective-permute-start(bf16[192,128]{1,0:T(8,128)(2,1)S(1)} %get-tuple-element.129.a0_ref), channel_id=1, source_target_pairs={{0,96},{32,0},{64,32},{96,64},{1,97},{33,1},{65,33},{97,65},{2,98}... | collective-permute-start | bytes 147464 | tf_op jit(solution)/shard_map/ppermute | solution.py:901
  81.4 7.7 %collective-permute-start.22 = (bf16[192,128]{1,0:T(8,128)(2,1)S(1)}, bf16[192,128]{1,0:T(8,128)(2,1)S(1)}, u32[]{:S(2)}, u32[]{:S(2)}) collective-permute-start(bf16[192,128]{1,0:T(8,128)(2,1)S(1)} %get-tuple-element.129.a0_ref), channel_id=1, source_target_pairs={{0,64},{32,96},{64,0},{96,32},{1,65},{33,97},{65,1},{97,33},{2,66}... | collective-permute-start | bytes 147464 | tf_op jit(solution)/shard_map/ppermute | solution.py:901
  82.0 7.1 %collective-permute-start.21 = (bf16[192,128]{1,0:T(8,128)(2,1)S(1)}, bf16[192,128]{1,0:T(8,128)(2,1)S(1)}, u32[]{:S(2)}, u32[]{:S(2)}) collective-permute-start(bf16[192,128]{1,0:T(8,128)(2,1)S(1)} %get-tuple-element.129.a0_ref), channel_id=1, source_target_pairs={{0,32},{32,64},{64,96},{96,0},{1,33},{33,65},{65,97},{97,1},{2,34}... | collective-permute-start | bytes 147464 | tf_op jit(solution)/shard_map/ppermute | solution.py:901
  82.0 25.3 %collective-permute-start.28 = (bf16[256,768]{1,0:T(8,128)(2,1)S(1)}, bf16[256,768]{1,0:T(8,128)(2,1)S(1)}, u32[]{:S(2)}, u32[]{:S(2)}) collective-permute-start(bf16[256,768]{1,0:T(8,128)(2,1)S(1)} %get-tuple-element.160), channel_id=1, source_target_pairs={{0,1},{1,0},{2,3},{3,2},{4,5},{5,4},{6,7},{7,6},{8,9},{9,8},{10,11... | collective-permute-start | bytes 1179656 | tf_op jit(solution)/shard_map/ppermute | solution.py:901
  95.4 11.9 %collective-permute-start.27 = (bf16[256,768]{1,0:T(8,128)(2,1)S(1)}, bf16[256,768]{1,0:T(8,128)(2,1)S(1)}, u32[]{:S(2)}, u32[]{:S(2)}) collective-permute-start(bf16[256,768]{1,0:T(8,128)(2,1)S(1)} %get-tuple-element.159), channel_id=1, source_target_pairs={{0,1},{1,0},{2,3},{3,2},{4,5},{5,4},{6,7},{7,6},{8,9},{9,8},{10,11... | collective-permute-start | bytes 1179656 | tf_op jit(solution)/shard_map/ppermute | solution.py:901
  97.5 4.6 %collective-permute-start.25 = (bf16[16,768]{1,0:T(8,128)(2,1)S(1)}, bf16[16,768]{1,0:T(8,128)(2,1)S(1)}, u32[]{:S(2)}, u32[]{:S(2)}) collective-permute-start(bf16[16,768]{1,0:T(8,128)(2,1)S(1)} %get-tuple-element.155), channel_id=1, source_target_pairs={{9,1},{17,9},{25,17},{33,25},{41,33},{49,41},{57,49},{65,57},{73,6... | collective-permute-start | bytes 73736 | tf_op jit(solution)/shard_map/ppermute | solution.py:910
  98.8 5.1 %collective-permute-start.24 = (bf16[16,768]{1,0:T(8,128)(2,1)S(1)}, bf16[16,768]{1,0:T(8,128)(2,1)S(1)}, u32[]{:S(2)}, u32[]{:S(2)}) collective-permute-start(bf16[16,768]{1,0:T(8,128)(2,1)S(1)} %get-tuple-element.155), channel_id=1, source_target_pairs={{8,1},{16,9},{24,17},{32,25},{40,33},{48,41},{56,49},{64,57},{72,6... | collective-permute-start | bytes 73736 | tf_op jit(solution)/shard_map/ppermute | solution.py:910
  108.2 18.8 %collective-permute-start.32 = (bf16[128,768]{1,0:T(8,128)(2,1)S(1)}, bf16[128,768]{1,0:T(8,128)(2,1)S(1)}, u32[]{:S(2)}, u32[]{:S(2)}) collective-permute-start(bf16[128,768]{1,0:T(8,128)(2,1)S(1)} %get-tuple-element.167), channel_id=1, source_target_pairs={{0,2},{2,4},{4,6},{6,0},{1,3},{3,5},{5,7},{7,1},{8,10},{10,12},{12... | collective-permute-start | bytes 589832 | tf_op jit(solution)/shard_map/ppermute | solution.py:901
  108.9 18.1 %collective-permute-start.33 = (bf16[128,768]{1,0:T(8,128)(2,1)S(1)}, bf16[128,768]{1,0:T(8,128)(2,1)S(1)}, u32[]{:S(2)}, u32[]{:S(2)}) collective-permute-start(bf16[128,768]{1,0:T(8,128)(2,1)S(1)} %get-tuple-element.168), channel_id=1, source_target_pairs={{0,4},{2,6},{4,0},{6,2},{1,5},{3,7},{5,1},{7,3},{8,12},{10,14},{12... | collective-permute-start | bytes 589832 | tf_op jit(solution)/shard_map/ppermute | solution.py:901
  111.2 15.8 %collective-permute-start.34 = (bf16[128,768]{1,0:T(8,128)(2,1)S(1)}, bf16[128,768]{1,0:T(8,128)(2,1)S(1)}, u32[]{:S(2)}, u32[]{:S(2)}) collective-permute-start(bf16[128,768]{1,0:T(8,128)(2,1)S(1)} %get-tuple-element.169), channel_id=1, source_target_pairs={{0,6},{2,0},{4,2},{6,4},{1,7},{3,1},{5,3},{7,5},{8,14},{10,8},{12,... | collective-permute-start | bytes 589832 | tf_op jit(solution)/shard_map/ppermute | solution.py:901
  112.2 9.9 %collective-permute-start.29 = (bf16[96,384]{1,0:T(8,128)(2,1)S(1)}, bf16[96,384]{1,0:T(8,128)(2,1)S(1)}, u32[]{:S(2)}, u32[]{:S(2)}) collective-permute-start(bf16[96,384]{1,0:T(8,128)(2,1)S(1)} %get-tuple-element.163), channel_id=1, source_target_pairs={{0,2},{2,4},{4,6},{6,0},{1,3},{3,5},{5,7},{7,1},{8,10},{10,12},{12... | collective-permute-start | bytes 221192 | tf_op jit(solution)/shard_map/ppermute | solution.py:901
  113.4 9.4 %collective-permute-start.30 = (bf16[96,384]{1,0:T(8,128)(2,1)S(1)}, bf16[96,384]{1,0:T(8,128)(2,1)S(1)}, u32[]{:S(2)}, u32[]{:S(2)}) collective-permute-start(bf16[96,384]{1,0:T(8,128)(2,1)S(1)} %get-tuple-element.164), channel_id=1, source_target_pairs={{0,4},{2,6},{4,0},{6,2},{1,5},{3,7},{5,1},{7,3},{8,12},{10,14},{12... | collective-permute-start | bytes 221192 | tf_op jit(solution)/shard_map/ppermute | solution.py:901
  127.0 24.9 %all-to-all-start.1 = ((bf16[16,48,640]{2,1,0:T(8,128)(2,1)}), bf16[16,48,640]{2,1,0:T(8,128)(2,1)}, u32[]{:S(2)}, u32[]{:S(2)}) async-start(bf16[16,48,640]{2,1,0:T(8,128)(2,1)} %bitcast.9), calls=%async_computation.1 | async-start | bytes 1966080 | tf_op jit(solution)/shard_map/all_to_all | solution.py:896
  134.1 5.9 %collective-permute-start.37 = (bf16[64,1536]{1,0:T(8,128)(2,1)S(1)}, bf16[64,1536]{1,0:T(8,128)(2,1)S(1)}, u32[]{:S(2)}, u32[]{:S(2)}) collective-permute-start(bf16[64,1536]{1,0:T(8,128)(2,1)S(1)} %four.1.refs_1_), channel_id=1, source_target_pairs={{0,6},{2,0},{4,2},{6,4},{1,7},{3,1},{5,3},{7,5},{8,14},{10,8},{12,... | collective-permute-start | bytes 589832 | tf_op jit(solution)/shard_map/ppermute | solution.py:901
  135.4 9.7 %collective-permute-start.36 = (bf16[64,1536]{1,0:T(8,128)(2,1)S(1)}, bf16[64,1536]{1,0:T(8,128)(2,1)S(1)}, u32[]{:S(2)}, u32[]{:S(2)}) collective-permute-start(bf16[64,1536]{1,0:T(8,128)(2,1)S(1)} %four.1.refs_1_), channel_id=1, source_target_pairs={{0,4},{2,6},{4,0},{6,2},{1,5},{3,7},{5,1},{7,3},{8,12},{10,14},{12... | collective-permute-start | bytes 589832 | tf_op jit(solution)/shard_map/ppermute | solution.py:901
  135.7 10.8 %collective-permute-start.35 = (bf16[64,1536]{1,0:T(8,128)(2,1)S(1)}, bf16[64,1536]{1,0:T(8,128)(2,1)S(1)}, u32[]{:S(2)}, u32[]{:S(2)}) collective-permute-start(bf16[64,1536]{1,0:T(8,128)(2,1)S(1)} %four.1.refs_1_), channel_id=1, source_target_pairs={{0,2},{2,4},{4,6},{6,0},{1,3},{3,5},{5,7},{7,1},{8,10},{10,12},{12... | collective-permute-start | bytes 589832 | tf_op jit(solution)/shard_map/ppermute | solution.py:901
  136.1 12.3 %collective-permute-start.38 = (bf16[64,1536]{1,0:T(8,128)(2,1)S(1)}, bf16[64,1536]{1,0:T(8,128)(2,1)S(1)}, u32[]{:S(2)}, u32[]{:S(2)}) collective-permute-start(bf16[64,1536]{1,0:T(8,128)(2,1)S(1)} %four.1.refs_1_), channel_id=1, source_target_pairs={{0,1},{1,0},{2,3},{3,2},{4,5},{5,4},{6,7},{7,6},{8,9},{9,8},{10,11... | collective-permute-start | bytes 589832 | tf_op jit(solution)/shard_map/ppermute | solution.py:901
  140.0 8.4 %collective-permute-start.41 = (bf16[64,1536]{1,0:T(8,128)(2,1)S(1)}, bf16[64,1536]{1,0:T(8,128)(2,1)S(1)}, u32[]{:S(2)}, u32[]{:S(2)}) collective-permute-start(bf16[64,1536]{1,0:T(8,128)(2,1)S(1)} %collective-permute-done.37.refs_4_), channel_id=1, source_target_pairs={{0,1},{1,0},{2,3},{3,2},{4,5},{5,4},{6,7},{7,6},{8,9},{9,8},{10,11... | collective-permute-start | bytes 589832 | tf_op jit(solution)/shard_map/ppermute | solution.py:901
  (24 other events, 186.9 us)

commit v6 on v5

--- a/solution.py
+++ b/solution.py
@@ -707,9 +707,10 @@
 
 def grad_kernel(
     at_ref, normed_ref, dv_ref, dstep_ref, nout_ref, cot_ref, conv_ref, gain_ref, chan_ref,
-    a0, a1, out_ref, keep_ref, give_ref, slab_ref,
+    edge_ref, out_ref, keep_ref, give_ref, slab_ref,
 ):
-    del a0, a1
+    give_ref[384:400, :] = edge_ref[:, 0:384]
+    give_ref[400:416, :] = edge_ref[:, 384:768]
     normed = normed_ref[...]
     slab_ref[:, 0:256] = dot(normed, dv_ref[:, 384:640], 0, 0).astype(bf16)
     grads = jnp.concatenate([jnp.zeros((MISC + 5, 256), f32), conv_ref[0:5, :]], axis=0)
@@ -735,17 +736,10 @@
     out_ref[:, 512:640] = (tile + jnp.concatenate([shared] * N_SEQ, axis=0)).astype(bf16)
 
 
-def slab_pair_kernel(at_ref, keep_ref, got_ref, after_ref, own_ref, s1, s2, s3, sum_ref):
-    del after_ref
-    sum_ref[...] = keep_ref[...].astype(f32) + got_ref[...].astype(f32)
-    for by, ref in enumerate((own_ref, s1, s2, s3)):
-        start = pl.multiple_of(lax.rem(at_ref[1] + by, 4) * 96, 96)
-        ref[...] = sum_ref[pl.ds(start, 96), :].astype(bf16)
-
-
 def merge_kernel(a_ref, b_ref, c_ref, d_ref, pack_ref, out_ref):
-    total = a_ref[...].astype(f32) + b_ref[...].astype(f32)
-    total = total + c_ref[...].astype(f32) + d_ref[...].astype(f32)
+    total = a_ref[128:176].astype(f32) + b_ref[128:176].astype(f32)
+    total = total + c_ref[128:176].astype(f32) + d_ref[128:176].astype(f32)
+    total = jnp.concatenate([total[:, 0:384], total[:, 384:768]], axis=0)
     misc = total[:, 256:384]
     lane = lanes(96)
     d = lax.broadcasted_iota(jnp.int32, (D, 96), 0)
@@ -768,21 +762,27 @@
 
 
 def pair_kernel(
-    at_ref, keep_ref, got_ref, edge0_ref, edge1_ref, out_keep_ref, out_got_ref,
-    own_ref, s1, s2, s3, sum_ref,
+    at_ref, keep_ref, got_ref, edge_ref, slab_keep_ref, slab_ref, out_keep_ref, out_got_ref,
+    own_ref, s1, s2, s3, sum_ref, both_ref,
 ):
+    both_ref[...] = slab_keep_ref[...].astype(f32) + slab_ref[0:384].astype(f32)
     sum_ref[0:256] = keep_ref[...].astype(f32) + got_ref[...].astype(f32)
-    sum_ref[256 - HALO : 256] += edge0_ref[...].astype(f32) + edge1_ref[...].astype(f32)
+    sibling = jnp.concatenate([slab_ref[384:400, :], slab_ref[400:416, :]], axis=1)
+    edge = edge_ref[...].astype(f32) + sibling.astype(f32)
+    sum_ref[256 - HALO : 256] += jnp.where(at_ref[2] == 1, edge, 0.0)
     sum_ref[256:512] = out_keep_ref[...].astype(f32) + out_got_ref[...].astype(f32)
     for by, ref in enumerate((own_ref, s1, s2, s3)):
-        start = pl.multiple_of(lax.rem(at_ref[1] + by, 4) * 64, 64)
+        x = lax.rem(at_ref[1] + by, 4)
+        start = pl.multiple_of(x * 64, 64)
         for k in range(2):
+            rows = pl.ds(pl.multiple_of(x * 96 + 48 * k, 48), 48)
+            ref[128:176, 384 * k : 384 * k + 384] = both_ref[rows, :].astype(bf16)
             ref[64 * k : 64 * k + 64] = sum_ref[pl.ds(256 * k + start, 64), :].astype(bf16)
 
 
 def four_kernel(at_ref, a_ref, b_ref, c_ref, d_ref, hid_ref, out_ref):
-    total = a_ref[...].astype(f32) + b_ref[...].astype(f32)
-    total = total + c_ref[...].astype(f32) + d_ref[...].astype(f32)
+    total = a_ref[0:128].astype(f32) + b_ref[0:128].astype(f32)
+    total = total + c_ref[0:128].astype(f32) + d_ref[0:128].astype(f32)
     start = pl.multiple_of((4 * at_ref[2] + at_ref[1]) * 64, 64)
     out_ref[:, 0:D] = total[0:64].astype(bf16)
     out_ref[:, D:] = (total[64:128] + hid_ref[pl.ds(start, 64), :].astype(f32)).astype(bf16)
@@ -905,9 +905,8 @@
     return lax.ppermute(a, SEQ, [(i, i + 1) for i in range(N_SEQ - 1)])
 
 
-def to_previous(a, core):
-    pairs = [(2 * i + 2 + core, 2 * i + 1) for i in range(N_SEQ - 1)]
-    return lax.ppermute(a, SEQ + ("head_1",), pairs)
+def to_previous(a):
+    return lax.ppermute(a, SEQ, [(i + 1, i) for i in range(N_SEQ - 1)])
 
 
 def body(
@@ -1016,30 +1015,20 @@
         name="back",
     )
     taken = around(give, "head_1", 1)
-    edges = [to_previous(edge, core) for core in range(2)]
-    slab_rows_all = ((384, 384), bf16)
+    edge = to_previous(edge)
     grads, slab_keep, slab_give = call(
-        grad_kernel, [((D, NW), bf16), slab_rows_all, slab_rows_all],
+        grad_kernel, [((D, NW), bf16), ((384, 384), bf16), ((416, 384), bf16)],
         where, normed, d_values, d_step, normed_out, cotangent, d_conv, d_gain, chan,
-        *edges, smem=(0,), anywhere=(9, 10),
+        edge, smem=(0,),
         scratch=[pltpu.VMEM((D, 384), bf16)], name="grad",
     )
     slab_taken = around(slab_give, "head_1", 1)
     pieces = call(
-        pair_kernel, [((T // 4, D), bf16)] * 4, where, keep, taken, *edges, out_keep,
-        out_taken, smem=(0,), scratch=[pltpu.VMEM((T, D), f32)], name="pair",
+        pair_kernel, [((176, D), bf16)] * 4, where, keep, taken, edge, slab_keep, slab_taken,
+        out_keep, out_taken, smem=(0,), scratch=[pltpu.VMEM((T, D), f32), pltpu.VMEM((384, 384), f32)], name="pair",
     )
     parts = [pieces[0]] + [around(pieces[by], "head_0", by) for by in (1, 2, 3)]
-    slab_piece = ((96, 384), bf16)
-    slabs = call(
-        slab_pair_kernel, [slab_piece] * 4, where, slab_keep, slab_taken, pieces[0],
-        smem=(0,), anywhere=(3,),
-        scratch=[pltpu.VMEM((384, 384), f32)], name="slab_pair",
-    )
-    slabs = [slabs[0]] + [around(slabs[by], "head_0", by) for by in (1, 2, 3)]
-
-    (grads,) = call(merge_kernel, [((D, NW), bf16)], *slabs, grads, name="merge")
-    grads, parts = lax.optimization_barrier((grads, parts))
+    (grads,) = call(merge_kernel, [((D, NW), bf16)], *parts, grads, name="merge")
     grads = exchange(grads.reshape(N_SEQ, 48, NW), SEQ)
     (own,) = call(
         four_kernel, [((T // N_HEAD, 2 * D), bf16)], where, *parts, hidden_in,

time: 155 us -> 155 us (level)
  waiting for transfers between devices: 40.9 us -> 50 us
  starting transfers between devices: 72.3 us -> 63.6 us
    ppermute x39 -> x36, waiting for transfers between devices: 25.3 us -> 35 us  [around(): return lax.ppermute(a, axis, [(i, (i + by) % peers) for i in range(peers)])]
    ppermute x39 -> x36, starting transfers between devices: 51.3 us -> 44.6 us  [around(): return lax.ppermute(a, axis, [(i, (i + by) % peers) for i in range(peers)])]
    ppermute x2 -> x1, waiting for transfers between devices: 3.85 us -> 3.27 us  [to_previous(): return lax.ppermute(a, SEQ, [(i + 1, i) for i in range(N_SEQ - 1)])]
    pallas_call x18 -> x17, Pallas kernels: 35.4 us -> 34.9 us  [call(): pl.pallas_call(kernel, out_shape=[jax.ShapeDtypeStruct(s, d) for s, d in...]
  transfers between devices with their start and end apart: 44 -> 40, of which waited for: 19 -> 20; matrix products, arithmetic and copies ran while one was open for 0% -> 0% of each run, Pallas kernels for 15% -> 13%
where the time goes in v6:
time: 155 us
  starting transfers between devices  63.6 us (41%)
  waiting for transfers between devices  50 us (32%)
  Pallas kernels  34.9 us (23%)
  local copies, waits for them, and re-layouts  4.74 us (3%)
    ppermute x36, starting transfers between devices, around(): return lax.ppermute(a, axis, [(i, (i + by) % peers) for i in range(peers)])  44.6 us
    ppermute x36, waiting for transfers between devices, around(): return lax.ppermute(a, axis, [(i, (i + by) % peers) for i in range(peers)])  35 us
    pallas_call x17, Pallas kernels, call(): pl.pallas_call(kernel, out_shape=[jax.ShapeDtypeStruct(s, d) for s, d in...  34.9 us
    all_to_all x2, starting transfers between devices, exchange(): return lax.all_to_all(blocks, axis, 0, 0, tiled=True)  14.5 us
    all_to_all x2, waiting for transfers between devices, exchange(): return lax.all_to_all(blocks, axis, 0, 0, tiled=True)  11.7 us
    unnamed x23, local copies, waits for them, and re-layouts  4.57 us
    ppermute x1, waiting for transfers between devices, to_previous(): return lax.ppermute(a, SEQ, [(i + 1, i) for i in range(N_SEQ - 1)])  3.27 us
    ppermute x1, starting transfers between devices, to_next(): return lax.ppermute(a, SEQ, [(i, i + 1) for i in range(N_SEQ - 1)])  3.27 us
  transfers between devices with their start and end apart: 40, of which 20 were waited for; matrix products, arithmetic and copies ran while one was open for 0% of the time, Pallas kernels for 13%

profile of v6, /device:TPU:1, one launch (start us, length us, event | category | flops | bytes accessed | tf_op | source)
XLA Modules:
  0.0 154.6 jit_solution(11442241888989428200)
XLA Ops:
  6.4 8.7 %all-to-all-start = ((bf16[16,48,640]{2,1,0:T(8,128)(2,1)}), bf16[16,48,640]{2,1,0:T(8,128)(2,1)S(1)}, u32[]{:S(2)}, u32[]{:S(2)}) async-start(bf16[16,48,640]{2,1,0:T(8,128)(2,1)} %pack.1), calls=%async_computation | async-start | bytes 1966080 | tf_op jit(solution)/shard_map/all_to_all | solution.py:896
  15.2 3.3 %collective-permute-start.7 = (bf16[16,768]{1,0:T(8,128)(2,1)S(1)}, bf16[16,768]{1,0:T(8,128)(2,1)S(1)}, u32[]{:S(2)}, u32[]{:S(2)}) collective-permute-start(bf16[16,768]{1,0:T(8,128)(2,1)S(1)} %slice.6), channel_id=1, source_target_pairs={{0,8},{8,16},{16,24},{24,32},{32,40},{40,48},{48,56},{56,64},{64,7... | collective-permute-start | bytes 73736 | tf_op jit(solution)/shard_map/ppermute | solution.py:905
  18.7 11.7 %all-to-all-done = bf16[16,48,640]{2,1,0:T(8,128)(2,1)S(1)} async-done(((bf16[16,48,640]{2,1,0:T(8,128)(2,1)}), bf16[16,48,640]{2,1,0:T(8,128)(2,1)S(1)}, u32[]{:S(2)}, u32[]{:S(2)}) %all-to-all-start) | async-done | bytes 983072 | tf_op jit(solution)/shard_map/all_to_all | solution.py:896
  31.0 2.5 %collective-permute-start.2 = (bf16[96,384]{1,0:T(8,128)(2,1)S(1)}, bf16[96,384]{1,0:T(8,128)(2,1)S(1)}, u32[]{:S(2)}, u32[]{:S(2)}) collective-permute-start(bf16[96,384]{1,0:T(8,128)(2,1)S(1)} %slab.1.refs_1_), channel_id=1, source_target_pairs={{0,6},{2,0},{4,2},{6,4},{1,7},{3,1},{5,3},{7,5},{8,14},{10,8},{12,... | collective-permute-start | bytes 221192 | tf_op jit(solution)/shard_map/ppermute | solution.py:901
  34.6 3.4 %collective-permute-start.3 = (bf16[96,384]{1,0:T(8,128)(2,1)S(1)}, bf16[96,384]{1,0:T(8,128)(2,1)S(1)}, u32[]{:S(2)}, u32[]{:S(2)}) collective-permute-start(bf16[96,384]{1,0:T(8,128)(2,1)S(1)} %slab.1.refs_1_), channel_id=1, source_target_pairs={{0,1},{1,0},{2,3},{3,2},{4,5},{5,4},{6,7},{7,6},{8,9},{9,8},{10,11... | collective-permute-start | bytes 221192 | tf_op jit(solution)/shard_map/ppermute | solution.py:901
  38.3 3.9 %collective-permute-start.5 = (bf16[96,384]{1,0:T(8,128)(2,1)S(1)}, bf16[96,384]{1,0:T(8,128)(2,1)S(1)}, u32[]{:S(2)}, u32[]{:S(2)}) collective-permute-start(bf16[96,384]{1,0:T(8,128)(2,1)S(1)} %collective-permute-done.1.refs_3_), channel_id=1, source_target_pairs={{0,1},{1,0},{2,3},{3,2},{4,5},{5,4},{6,7},{7,6},{8,9},{9,8},{10,11... | collective-permute-start | bytes 221192 | tf_op jit(solution)/shard_map/ppermute | solution.py:901
  43.9 4.7 %first.1 = (bf16[528,768]{1,0:T(8,128)(2,1)S(1)}, f32[528,640]{1,0:T(8,128)S(1)}, f32[512,640]{1,0:T(8,128)S(1)}, f32[512,128]{1,0:T(8,128)S(1)}, bf16[208,128]{...) custom-call(s32[3]{0:T(128)S(1)} %pad_add_fusion.refs_0_.at_ref, ...), custom_call_target="tpu_custom_call" | custom-call | tf_op jit(solution)/shard_map/first/pallas_call | solution.py:46
  48.7 1.7 %collective-permute-start.9 = (bf16[208,128]{1,0:T(8,128)(2,1)S(1)}, bf16[208,128]{1,0:T(8,128)(2,1)S(1)}, u32[]{:S(2)}, u32[]{:S(2)}) collective-permute-start(bf16[208,128]{1,0:T(8,128)(2,1)S(1)} %get-tuple-element.105.a_ref.mine_ref), channel_id=1, source_target_pairs={{0,16},{8,24},{16,0},{24,8},{1,17},{9,25},{17,1},{25,9},{2,18},{10... | collective-permute-start | bytes 159752 | tf_op jit(solution)/shard_map/ppermute | solution.py:901
  51.6 1.6 %collective-permute-done.9.c_ref = bf16[208,128]{1,0:T(8,128)(2,1)S(1)} collective-permute-done((bf16[208,128]{1,0:T(8,128)(2,1)S(1)}, bf16[208,128]{1,0:T(8,128)(2,1)S(1)}, u32[]{:S(2)}, u32[]{:S(2)}) %collective-permute-start.9) | collective-permute-done | bytes 53280 | tf_op jit(solution)/shard_map/ppermute | solution.py:901
  53.2 1.4 collective-permute-done.8.b_ref
  57.5 2.4 %own.1 = (f32[512,256]{1,0:T(8,128)S(1)}, f32[512,256]{1,0:T(8,128)S(1)}, bf16[3,512,512]{2,1,0:T(8,128)(2,1)S(1)}, bf16[3,512,512]{2,1,0:T(8,128)(2,1)S(1)}) custom-call(f32[512,640]{1,0:T(8,128)S(1)} %get-tuple-element.109.c_ref, f32[512,128]{1,0:T(8,128)S(1)} %get-tuple-element.110.aux_ref, bf16[512,768]{1,0:T(8,128)(2,1)S(1)} %copy-done.1, ...), custom_call_target="tpu_custom_call" | custom-call | tf_op jit(solution)/shard_map/own/pallas_call | solution.py:46
  62.7 3.1 %collective-permute-start.14 = (f32[8,512]{1,0:T(8,128)S(1)}, f32[8,512]{1,0:T(8,128)S(1)}, u32[]{:S(2)}, u32[]{:S(2)}) collective-permute-start(f32[8,512]{1,0:T(8,128)S(1)} %get-tuple-element.113), channel_id=1, source_target_pairs={{0,1},{1,0},{2,3},{3,2},{4,5},{5,4},{6,7},{7,6},{8,9},{9,8},{10,11... | collective-permute-start | bytes 49160 | tf_op jit(solution)/shard_map/ppermute | solution.py:901
  69.2 1.8 %collective-permute-done.16.s2_ref = f32[8,512]{1,0:T(8,128)S(1)} collective-permute-done((f32[8,512]{1,0:T(8,128)S(1)}, f32[8,512]{1,0:T(8,128)S(1)}, u32[]{:S(2)}, u32[]{:S(2)}) %collective-permute-start.16) | collective-permute-done | bytes 16416 | tf_op jit(solution)/shard_map/ppermute | solution.py:901
  71.6 1.5 gated.1
  76.3 2.2 %collective-permute-done.19.c_ref = bf16[192,128]{1,0:T(8,128)(2,1)S(1)} collective-permute-done((bf16[192,128]{1,0:T(8,128)(2,1)S(1)}, bf16[192,128]{1,0:T(8,128)(2,1)S(1)}, u32[]{:S(2)}, u32[]{:S(2)}) %collective-permute-start.19) | collective-permute-done | bytes 49184 | tf_op jit(solution)/shard_map/ppermute | solution.py:901
  79.7 1.7 %collective-permute-start.23 = (bf16[192,128]{1,0:T(8,128)(2,1)S(1)}, bf16[192,128]{1,0:T(8,128)(2,1)S(1)}, u32[]{:S(2)}, u32[]{:S(2)}) collective-permute-start(bf16[192,128]{1,0:T(8,128)(2,1)S(1)} %get-tuple-element.119.a0_ref), channel_id=1, source_target_pairs={{0,96},{32,0},{64,32},{96,64},{1,97},{33,1},{65,33},{97,65},{2,98}... | collective-permute-start | bytes 147464 | tf_op jit(solution)/shard_map/ppermute | solution.py:901
  82.0 4.0 %collective-permute-start.27 = (bf16[256,768]{1,0:T(8,128)(2,1)S(1)}, bf16[256,768]{1,0:T(8,128)(2,1)S(1)}, u32[]{:S(2)}, u32[]{:S(2)}) collective-permute-start(bf16[256,768]{1,0:T(8,128)(2,1)S(1)} %get-tuple-element.151), channel_id=1, source_target_pairs={{0,1},{1,0},{2,3},{3,2},{4,5},{5,4},{6,7},{7,6},{8,9},{9,8},{10,11... | collective-permute-start | bytes 1179656 | tf_op jit(solution)/shard_map/ppermute | solution.py:901
  86.1 3.0 %own_back.1 = (f32[512,256]{1,0:T(8,128)S(1)}, f32[512,128]{1,0:T(8,128)S(1)}, f32[512,128]{1,0:T(8,128)S(1)}, f32[512,256]{1,0:T(8,128)S(1)}, bf16[512,128]{1,0...) custom-call(f32[512,256]{1,0:T(8,128)S(1)} %get-tuple-element.124.dy_ref, ...), custom_call_target="tpu_custom_call" | custom-call | tf_op jit(solution)/shard_map/own_back/pallas_call | solution.py:46
  89.1 6.3 %back.1 = (bf16[528,640]{1,0:T(8,128)(2,1)S(1)}, bf16[512,128]{1,0:T(8,128)(2,1)S(1)}, bf16[256,768]{1,0:T(8,128)(2,1)S(1)}, bf16[256,768]{1,0:T(8,128)(2,1)S(1)...) custom-call(s32[3]{0:T(128)S(1)} %pad_add_fusion.refs_0_.at_ref, ...), custom_call_target="tpu_custom_call" | custom-call | tf_op jit(solution)/shard_map/back/pallas_call | solution.py:46
  95.4 2.1 %collective-permute-start.24 = (bf16[256,768]{1,0:T(8,128)(2,1)S(1)}, bf16[256,768]{1,0:T(8,128)(2,1)S(1)}, u32[]{:S(2)}, u32[]{:S(2)}) collective-permute-start(bf16[256,768]{1,0:T(8,128)(2,1)S(1)} %get-tuple-element.141), channel_id=1, source_target_pairs={{0,1},{1,0},{2,3},{3,2},{4,5},{5,4},{6,7},{7,6},{8,9},{9,8},{10,11... | collective-permute-start | bytes 1179656 | tf_op jit(solution)/shard_map/ppermute | solution.py:901
  98.8 3.3 %collective-permute-done.25.edge_ref = bf16[16,768]{1,0:T(8,128)(2,1)S(1)} collective-permute-done((bf16[16,768]{1,0:T(8,128)(2,1)S(1)}, bf16[16,768]{1,0:T(8,128)(2,1)S(1)}, u32[]{:S(2)}, u32[]{:S(2)}) %collective-permute-start.25) | collective-permute-done | bytes 24608 | tf_op jit(solution)/shard_map/ppermute | solution.py:909
  102.1 3.3 %grad.1 = (bf16[768,640]{1,0:T(8,128)(2,1)S(1)}, bf16[384,384]{1,0:T(8,128)(2,1)S(1)}, bf16[416,384]{1,0:T(8,128)(2,1)S(1)}) custom-call(s32[3]{0:T(128)S(1)} %pad_add_fusion.refs_0_.at_ref, bf16[528,768]{1,0:T(8,128)(2,1)S(1)} %get-tuple-element.143.normed_ref, bf16[528,640]{1,0:T(8,128)(2,1)S(1)} %get-tuple-element.144.dv_ref, ...), custom_call_target="tpu_custom_call" | custom-call | tf_op jit(solution)/shard_map/grad/pallas_call | solution.py:46
  109.5 2.3 %collective-permute-start.29 = (bf16[176,768]{1,0:T(8,128)(2,1)S(1)}, bf16[176,768]{1,0:T(8,128)(2,1)S(1)}, u32[]{:S(2)}, u32[]{:S(2)}) collective-permute-start(bf16[176,768]{1,0:T(8,128)(2,1)S(1)} %get-tuple-element.154), channel_id=1, source_target_pairs={{0,4},{2,6},{4,0},{6,2},{1,5},{3,7},{5,1},{7,3},{8,12},{10,14},{12... | collective-permute-start | bytes 811016 | tf_op jit(solution)/shard_map/ppermute | solution.py:901
  112.1 5.7 %collective-permute-done.28.b_ref = bf16[176,768]{1,0:T(8,128)(2,1)S(1)} collective-permute-done((bf16[176,768]{1,0:T(8,128)(2,1)S(1)}, bf16[176,768]{1,0:T(8,128)(2,1)S(1)}, u32[]{:S(2)}, u32[]{:S(2)}) %collective-permute-start.28) | collective-permute-done | bytes 270368 | tf_op jit(solution)/shard_map/ppermute | solution.py:901
  117.8 6.0 %collective-permute-done.29.c_ref = bf16[176,768]{1,0:T(8,128)(2,1)S(1)} collective-permute-done((bf16[176,768]{1,0:T(8,128)(2,1)S(1)}, bf16[176,768]{1,0:T(8,128)(2,1)S(1)}, u32[]{:S(2)}, u32[]{:S(2)}) %collective-permute-start.29) | collective-permute-done | bytes 270368 | tf_op jit(solution)/shard_map/ppermute | solution.py:901
  123.9 1.7 %merge.1 = bf16[768,640]{1,0:T(8,128)(2,1)} custom-call(bf16[176,768]{1,0:T(8,128)(2,1)S(1)} %get-tuple-element.152.a_ref, bf16[176,768]{1,0:T(8,128)(2,1)S(1)} %collective-permute-done.28.b_ref, bf16[176,768]{1,0:T(8,128)(2,1)S(1)} %collective-permute-done.29.c_ref, bf16[176,768]{1,0:T(8,128)(2,1)S(1)} %collective-permute-done.30.d_ref, ...), custom_call_target="tpu_custom_call" | custom-call | tf_op jit(solution)/shard_map/merge/pallas_call | solution.py:46
  125.7 5.8 %all-to-all-start.1 = ((bf16[16,48,640]{2,1,0:T(8,128)(2,1)}), bf16[16,48,640]{2,1,0:T(8,128)(2,1)}, u32[]{:S(2)}, u32[]{:S(2)}) async-start(bf16[16,48,640]{2,1,0:T(8,128)(2,1)} %bitcast.9), calls=%async_computation.1 | async-start | bytes 1966080 | tf_op jit(solution)/shard_map/all_to_all | solution.py:896
  132.1 3.4 %collective-permute-start.33 = (bf16[64,1536]{1,0:T(8,128)(2,1)S(1)}, bf16[64,1536]{1,0:T(8,128)(2,1)S(1)}, u32[]{:S(2)}, u32[]{:S(2)}) collective-permute-start(bf16[64,1536]{1,0:T(8,128)(2,1)S(1)} %four.1.refs_1_), channel_id=1, source_target_pairs={{0,6},{2,0},{4,2},{6,4},{1,7},{3,1},{5,3},{7,5},{8,14},{10,8},{12,... | collective-permute-start | bytes 589832 | tf_op jit(solution)/shard_map/ppermute | solution.py:901
  137.6 5.9 %collective-permute-done.33.refs_4_ = bf16[64,1536]{1,0:T(8,128)(2,1)S(1)} collective-permute-done((bf16[64,1536]{1,0:T(8,128)(2,1)S(1)}, bf16[64,1536]{1,0:T(8,128)(2,1)S(1)}, u32[]{:S(2)}, u32[]{:S(2)}) %collective-permute-start.33) | collective-permute-done | bytes 196640 | tf_op jit(solution)/shard_map/ppermute | solution.py:901
  146.0 1.6 %collective-permute-done.31.refs_2_ = bf16[64,1536]{1,0:T(8,128)(2,1)S(1)} collective-permute-done((bf16[64,1536]{1,0:T(8,128)(2,1)S(1)}, bf16[64,1536]{1,0:T(8,128)(2,1)S(1)}, u32[]{:S(2)}, u32[]{:S(2)}) %collective-permute-start.31) | collective-permute-done | bytes 196640 | tf_op jit(solution)/shard_map/ppermute | solution.py:901
  149.4 2.4 %input.1 = (f32[512,768]{1,0:T(8,128)}, bf16[512,768]{1,0:T(8,128)(2,1)}) custom-call(s32[3]{0:T(128)S(1)} %pad_add_fusion.refs_0_.at_ref, bf16[64,1536]{1,0:T(8,128)(2,1)S(1)} %four.1.refs_1_, bf16[64,1536]{1,0:T(8,128)(2,1)S(1)} %collective-permute-done.31.refs_2_, bf16[64,1536]{1,0:T(8,128)(2,1)S(1)} %collective-permute-done.32.refs_3_, ...), custom_call_target="tpu_custom_call" | custom-call | tf_op jit(solution)/shard_map/input/pallas_call | solution.py:46
  151.8 2.6 %update.1 = (f32[3,48,128]{2,1,0:T(8,128)}, f32[3,48,128]{2,1,0:T(8,128)}, f32[3,48,128]{2,1,0:T(8,128)}, f32[3,48]{1,0:T(4,128)}, f32[3,48]{1,0:T(4,128)}, /*in...) custom-call(bf16[16,48,640]{2,1,0:T(8,128)(2,1)} %all-to-all-done.1., ...), custom_call_target="tpu_custom_call" | custom-call | tf_op jit(solution)/shard_map/update/pallas_call | solution.py:46
  (100 shorter events, 38.3 us)
Async XLA Ops:
  6.4 24.0 %all-to-all-start = ((bf16[16,48,640]{2,1,0:T(8,128)(2,1)}), bf16[16,48,640]{2,1,0:T(8,128)(2,1)S(1)}, u32[]{:S(2)}, u32[]{:S(2)}) async-start(bf16[16,48,640]{2,1,0:T(8,128)(2,1)} %pack.1), calls=%async_computation | async-start | bytes 1966080 | tf_op jit(solution)/shard_map/all_to_all | solution.py:896
  15.2 27.9 %collective-permute-start.7 = (bf16[16,768]{1,0:T(8,128)(2,1)S(1)}, bf16[16,768]{1,0:T(8,128)(2,1)S(1)}, u32[]{:S(2)}, u32[]{:S(2)}) collective-permute-start(bf16[16,768]{1,0:T(8,128)(2,1)S(1)} %slice.6), channel_id=1, source_target_pairs={{0,8},{8,16},{16,24},{24,32},{32,40},{40,48},{48,56},{56,64},{64,7... | collective-permute-start | bytes 73736 | tf_op jit(solution)/shard_map/ppermute | solution.py:905
  31.0 7.0 %collective-permute-start.2 = (bf16[96,384]{1,0:T(8,128)(2,1)S(1)}, bf16[96,384]{1,0:T(8,128)(2,1)S(1)}, u32[]{:S(2)}, u32[]{:S(2)}) collective-permute-start(bf16[96,384]{1,0:T(8,128)(2,1)S(1)} %slab.1.refs_1_), channel_id=1, source_target_pairs={{0,6},{2,0},{4,2},{6,4},{1,7},{3,1},{5,3},{7,5},{8,14},{10,8},{12,... | collective-permute-start | bytes 221192 | tf_op jit(solution)/shard_map/ppermute | solution.py:901
  33.5 4.8 %collective-permute-start.1 = (bf16[96,384]{1,0:T(8,128)(2,1)S(1)}, bf16[96,384]{1,0:T(8,128)(2,1)S(1)}, u32[]{:S(2)}, u32[]{:S(2)}) collective-permute-start(bf16[96,384]{1,0:T(8,128)(2,1)S(1)} %slab.1.refs_1_), channel_id=1, source_target_pairs={{0,4},{2,6},{4,0},{6,2},{1,5},{3,7},{5,1},{7,3},{8,12},{10,14},{12... | collective-permute-start | bytes 221192 | tf_op jit(solution)/shard_map/ppermute | solution.py:901
  34.0 8.2 %collective-permute-start = (bf16[96,384]{1,0:T(8,128)(2,1)S(1)}, bf16[96,384]{1,0:T(8,128)(2,1)S(1)}, u32[]{:S(2)}, u32[]{:S(2)}) collective-permute-start(bf16[96,384]{1,0:T(8,128)(2,1)S(1)} %slab.1.refs_1_), channel_id=1, source_target_pairs={{0,2},{2,4},{4,6},{6,0},{1,3},{3,5},{5,7},{7,1},{8,10},{10,12},{12... | collective-permute-start | bytes 221192 | tf_op jit(solution)/shard_map/ppermute | solution.py:901
  34.6 8.4 %collective-permute-start.3 = (bf16[96,384]{1,0:T(8,128)(2,1)S(1)}, bf16[96,384]{1,0:T(8,128)(2,1)S(1)}, u32[]{:S(2)}, u32[]{:S(2)}) collective-permute-start(bf16[96,384]{1,0:T(8,128)(2,1)S(1)} %slab.1.refs_1_), channel_id=1, source_target_pairs={{0,1},{1,0},{2,3},{3,2},{4,5},{5,4},{6,7},{7,6},{8,9},{9,8},{10,11... | collective-permute-start | bytes 221192 | tf_op jit(solution)/shard_map/ppermute | solution.py:901
  38.0 5.1 %collective-permute-start.6 = (bf16[96,384]{1,0:T(8,128)(2,1)S(1)}, bf16[96,384]{1,0:T(8,128)(2,1)S(1)}, u32[]{:S(2)}, u32[]{:S(2)}) collective-permute-start(bf16[96,384]{1,0:T(8,128)(2,1)S(1)} %collective-permute-done.2.refs_4_), channel_id=1, source_target_pairs={{0,1},{1,0},{2,3},{3,2},{4,5},{5,4},{6,7},{7,6},{8,9},{9,8},{10,11... | collective-permute-start | bytes 221192 | tf_op jit(solution)/shard_map/ppermute | solution.py:901
  38.3 4.8 %collective-permute-start.5 = (bf16[96,384]{1,0:T(8,128)(2,1)S(1)}, bf16[96,384]{1,0:T(8,128)(2,1)S(1)}, u32[]{:S(2)}, u32[]{:S(2)}) collective-permute-start(bf16[96,384]{1,0:T(8,128)(2,1)S(1)} %collective-permute-done.1.refs_3_), channel_id=1, source_target_pairs={{0,1},{1,0},{2,3},{3,2},{4,5},{5,4},{6,7},{7,6},{8,9},{9,8},{10,11... | collective-permute-start | bytes 221192 | tf_op jit(solution)/shard_map/ppermute | solution.py:901
  48.7 4.6 %collective-permute-start.9 = (bf16[208,128]{1,0:T(8,128)(2,1)S(1)}, bf16[208,128]{1,0:T(8,128)(2,1)S(1)}, u32[]{:S(2)}, u32[]{:S(2)}) collective-permute-start(bf16[208,128]{1,0:T(8,128)(2,1)S(1)} %get-tuple-element.105.a_ref.mine_ref), channel_id=1, source_target_pairs={{0,16},{8,24},{16,0},{24,8},{1,17},{9,25},{17,1},{25,9},{2,18},{10... | collective-permute-start | bytes 159752 | tf_op jit(solution)/shard_map/ppermute | solution.py:901
  50.3 4.3 %collective-permute-start.8 = (bf16[208,128]{1,0:T(8,128)(2,1)S(1)}, bf16[208,128]{1,0:T(8,128)(2,1)S(1)}, u32[]{:S(2)}, u32[]{:S(2)}) collective-permute-start(bf16[208,128]{1,0:T(8,128)(2,1)S(1)} %get-tuple-element.105.a_ref.mine_ref), channel_id=1, source_target_pairs={{0,8},{8,16},{16,24},{24,0},{1,9},{9,17},{17,25},{25,1},{2,10},{10... | collective-permute-start | bytes 159752 | tf_op jit(solution)/shard_map/ppermute | solution.py:901
  55.3 4.6 %collective-permute-start.13 = (bf16[208,128]{1,0:T(8,128)(2,1)S(1)}, bf16[208,128]{1,0:T(8,128)(2,1)S(1)}, u32[]{:S(2)}, u32[]{:S(2)}) collective-permute-start(bf16[208,128]{1,0:T(8,128)(2,1)S(1)} %get-tuple-element.106.s0_ref), channel_id=1, source_target_pairs={{0,96},{32,0},{64,32},{96,64},{1,97},{33,1},{65,33},{97,65},{2,98}... | collective-permute-start | bytes 159752 | tf_op jit(solution)/shard_map/ppermute | solution.py:901
  56.3 4.5 %collective-permute-start.12 = (bf16[208,128]{1,0:T(8,128)(2,1)S(1)}, bf16[208,128]{1,0:T(8,128)(2,1)S(1)}, u32[]{:S(2)}, u32[]{:S(2)}) collective-permute-start(bf16[208,128]{1,0:T(8,128)(2,1)S(1)} %get-tuple-element.106.s0_ref), channel_id=1, source_target_pairs={{0,64},{32,96},{64,0},{96,32},{1,65},{33,97},{65,1},{97,33},{2,66}... | collective-permute-start | bytes 159752 | tf_op jit(solution)/shard_map/ppermute | solution.py:901
  57.0 4.4 %collective-permute-start.11 = (bf16[208,128]{1,0:T(8,128)(2,1)S(1)}, bf16[208,128]{1,0:T(8,128)(2,1)S(1)}, u32[]{:S(2)}, u32[]{:S(2)}) collective-permute-start(bf16[208,128]{1,0:T(8,128)(2,1)S(1)} %get-tuple-element.106.s0_ref), channel_id=1, source_target_pairs={{0,32},{32,64},{64,96},{96,0},{1,33},{33,65},{65,97},{97,1},{2,34}... | collective-permute-start | bytes 159752 | tf_op jit(solution)/shard_map/ppermute | solution.py:901
  66.9 4.1 %collective-permute-start.16 = (f32[8,512]{1,0:T(8,128)S(1)}, f32[8,512]{1,0:T(8,128)S(1)}, u32[]{:S(2)}, u32[]{:S(2)}) collective-permute-start(f32[8,512]{1,0:T(8,128)S(1)} %add.11.s0_ref), channel_id=1, source_target_pairs={{0,4},{2,6},{4,0},{6,2},{1,5},{3,7},{5,1},{7,3},{8,12},{10,14},{12... | collective-permute-start | bytes 49160 | tf_op jit(solution)/shard_map/ppermute | solution.py:901
  67.6 4.0 %collective-permute-start.15 = (f32[8,512]{1,0:T(8,128)S(1)}, f32[8,512]{1,0:T(8,128)S(1)}, u32[]{:S(2)}, u32[]{:S(2)}) collective-permute-start(f32[8,512]{1,0:T(8,128)S(1)} %add.11.s0_ref), channel_id=1, source_target_pairs={{0,2},{2,4},{4,6},{6,0},{1,3},{3,5},{5,7},{7,1},{8,10},{10,12},{12... | collective-permute-start | bytes 49160 | tf_op jit(solution)/shard_map/ppermute | solution.py:901
  74.1 4.5 %collective-permute-start.19 = (bf16[192,128]{1,0:T(8,128)(2,1)S(1)}, bf16[192,128]{1,0:T(8,128)(2,1)S(1)}, u32[]{:S(2)}, u32[]{:S(2)}) collective-permute-start(bf16[192,128]{1,0:T(8,128)(2,1)S(1)} %get-tuple-element.115.a_ref), channel_id=1, source_target_pairs={{0,16},{8,24},{16,0},{24,8},{1,17},{9,25},{17,1},{25,9},{2,18},{10... | collective-permute-start | bytes 147464 | tf_op jit(solution)/shard_map/ppermute | solution.py:901
  74.7 4.3 %collective-permute-start.18 = (bf16[192,128]{1,0:T(8,128)(2,1)S(1)}, bf16[192,128]{1,0:T(8,128)(2,1)S(1)}, u32[]{:S(2)}, u32[]{:S(2)}) collective-permute-start(bf16[192,128]{1,0:T(8,128)(2,1)S(1)} %get-tuple-element.115.a_ref), channel_id=1, source_target_pairs={{0,8},{8,16},{16,24},{24,0},{1,9},{9,17},{17,25},{25,1},{2,10},{10... | collective-permute-start | bytes 147464 | tf_op jit(solution)/shard_map/ppermute | solution.py:901
  79.7 9.4 %collective-permute-start.23 = (bf16[192,128]{1,0:T(8,128)(2,1)S(1)}, bf16[192,128]{1,0:T(8,128)(2,1)S(1)}, u32[]{:S(2)}, u32[]{:S(2)}) collective-permute-start(bf16[192,128]{1,0:T(8,128)(2,1)S(1)} %get-tuple-element.119.a0_ref), channel_id=1, source_target_pairs={{0,96},{32,0},{64,32},{96,64},{1,97},{33,1},{65,33},{97,65},{2,98}... | collective-permute-start | bytes 147464 | tf_op jit(solution)/shard_map/ppermute | solution.py:901
  81.4 7.7 %collective-permute-start.22 = (bf16[192,128]{1,0:T(8,128)(2,1)S(1)}, bf16[192,128]{1,0:T(8,128)(2,1)S(1)}, u32[]{:S(2)}, u32[]{:S(2)}) collective-permute-start(bf16[192,128]{1,0:T(8,128)(2,1)S(1)} %get-tuple-element.119.a0_ref), channel_id=1, source_target_pairs={{0,64},{32,96},{64,0},{96,32},{1,65},{33,97},{65,1},{97,33},{2,66}... | collective-permute-start | bytes 147464 | tf_op jit(solution)/shard_map/ppermute | solution.py:901
  82.0 7.1 %collective-permute-start.21 = (bf16[192,128]{1,0:T(8,128)(2,1)S(1)}, bf16[192,128]{1,0:T(8,128)(2,1)S(1)}, u32[]{:S(2)}, u32[]{:S(2)}) collective-permute-start(bf16[192,128]{1,0:T(8,128)(2,1)S(1)} %get-tuple-element.119.a0_ref), channel_id=1, source_target_pairs={{0,32},{32,64},{64,96},{96,0},{1,33},{33,65},{65,97},{97,1},{2,34}... | collective-permute-start | bytes 147464 | tf_op jit(solution)/shard_map/ppermute | solution.py:901
  82.0 24.6 %collective-permute-start.27 = (bf16[256,768]{1,0:T(8,128)(2,1)S(1)}, bf16[256,768]{1,0:T(8,128)(2,1)S(1)}, u32[]{:S(2)}, u32[]{:S(2)}) collective-permute-start(bf16[256,768]{1,0:T(8,128)(2,1)S(1)} %get-tuple-element.151), channel_id=1, source_target_pairs={{0,1},{1,0},{2,3},{3,2},{4,5},{5,4},{6,7},{7,6},{8,9},{9,8},{10,11... | collective-permute-start | bytes 1179656 | tf_op jit(solution)/shard_map/ppermute | solution.py:901
  95.4 12.5 %collective-permute-start.24 = (bf16[256,768]{1,0:T(8,128)(2,1)S(1)}, bf16[256,768]{1,0:T(8,128)(2,1)S(1)}, u32[]{:S(2)}, u32[]{:S(2)}) collective-permute-start(bf16[256,768]{1,0:T(8,128)(2,1)S(1)} %get-tuple-element.141), channel_id=1, source_target_pairs={{0,1},{1,0},{2,3},{3,2},{4,5},{5,4},{6,7},{7,6},{8,9},{9,8},{10,11... | collective-permute-start | bytes 1179656 | tf_op jit(solution)/shard_map/ppermute | solution.py:901
  97.5 4.6 %collective-permute-start.25 = (bf16[16,768]{1,0:T(8,128)(2,1)S(1)}, bf16[16,768]{1,0:T(8,128)(2,1)S(1)}, u32[]{:S(2)}, u32[]{:S(2)}) collective-permute-start(bf16[16,768]{1,0:T(8,128)(2,1)S(1)} %get-tuple-element.142), channel_id=1, source_target_pairs={{8,0},{16,8},{24,16},{32,24},{40,32},{48,40},{56,48},{64,56},{72,6... | collective-permute-start | bytes 73736 | tf_op jit(solution)/shard_map/ppermute | solution.py:909
  108.9 9.0 %collective-permute-start.28 = (bf16[176,768]{1,0:T(8,128)(2,1)S(1)}, bf16[176,768]{1,0:T(8,128)(2,1)S(1)}, u32[]{:S(2)}, u32[]{:S(2)}) collective-permute-start(bf16[176,768]{1,0:T(8,128)(2,1)S(1)} %get-tuple-element.153), channel_id=1, source_target_pairs={{0,2},{2,4},{4,6},{6,0},{1,3},{3,5},{5,7},{7,1},{8,10},{10,12},{12... | collective-permute-start | bytes 811016 | tf_op jit(solution)/shard_map/ppermute | solution.py:901
  109.5 14.4 %collective-permute-start.29 = (bf16[176,768]{1,0:T(8,128)(2,1)S(1)}, bf16[176,768]{1,0:T(8,128)(2,1)S(1)}, u32[]{:S(2)}, u32[]{:S(2)}) collective-permute-start(bf16[176,768]{1,0:T(8,128)(2,1)S(1)} %get-tuple-element.154), channel_id=1, source_target_pairs={{0,4},{2,6},{4,0},{6,2},{1,5},{3,7},{5,1},{7,3},{8,12},{10,14},{12... | collective-permute-start | bytes 811016 | tf_op jit(solution)/shard_map/ppermute | solution.py:901
  111.9 12.1 %collective-permute-start.30 = (bf16[176,768]{1,0:T(8,128)(2,1)S(1)}, bf16[176,768]{1,0:T(8,128)(2,1)S(1)}, u32[]{:S(2)}, u32[]{:S(2)}) collective-permute-start(bf16[176,768]{1,0:T(8,128)(2,1)S(1)} %get-tuple-element.155), channel_id=1, source_target_pairs={{0,6},{2,0},{4,2},{6,4},{1,7},{3,1},{5,3},{7,5},{8,14},{10,8},{12,... | collective-permute-start | bytes 811016 | tf_op jit(solution)/shard_map/ppermute | solution.py:901
  125.7 26.1 %all-to-all-start.1 = ((bf16[16,48,640]{2,1,0:T(8,128)(2,1)}), bf16[16,48,640]{2,1,0:T(8,128)(2,1)}, u32[]{:S(2)}, u32[]{:S(2)}) async-start(bf16[16,48,640]{2,1,0:T(8,128)(2,1)} %bitcast.9), calls=%async_computation.1 | async-start | bytes 1966080 | tf_op jit(solution)/shard_map/all_to_all | solution.py:896
  132.1 11.4 %collective-permute-start.33 = (bf16[64,1536]{1,0:T(8,128)(2,1)S(1)}, bf16[64,1536]{1,0:T(8,128)(2,1)S(1)}, u32[]{:S(2)}, u32[]{:S(2)}) collective-permute-start(bf16[64,1536]{1,0:T(8,128)(2,1)S(1)} %four.1.refs_1_), channel_id=1, source_target_pairs={{0,6},{2,0},{4,2},{6,4},{1,7},{3,1},{5,3},{7,5},{8,14},{10,8},{12,... | collective-permute-start | bytes 589832 | tf_op jit(solution)/shard_map/ppermute | solution.py:901
  135.6 9.3 %collective-permute-start.32 = (bf16[64,1536]{1,0:T(8,128)(2,1)S(1)}, bf16[64,1536]{1,0:T(8,128)(2,1)S(1)}, u32[]{:S(2)}, u32[]{:S(2)}) collective-permute-start(bf16[64,1536]{1,0:T(8,128)(2,1)S(1)} %four.1.refs_1_), channel_id=1, source_target_pairs={{0,4},{2,6},{4,0},{6,2},{1,5},{3,7},{5,1},{7,3},{8,12},{10,14},{12... | collective-permute-start | bytes 589832 | tf_op jit(solution)/shard_map/ppermute | solution.py:901
  135.6 12.0 %collective-permute-start.31 = (bf16[64,1536]{1,0:T(8,128)(2,1)S(1)}, bf16[64,1536]{1,0:T(8,128)(2,1)S(1)}, u32[]{:S(2)}, u32[]{:S(2)}) collective-permute-start(bf16[64,1536]{1,0:T(8,128)(2,1)S(1)} %four.1.refs_1_), channel_id=1, source_target_pairs={{0,2},{2,4},{4,6},{6,0},{1,3},{3,5},{5,7},{7,1},{8,10},{10,12},{12... | collective-permute-start | bytes 589832 | tf_op jit(solution)/shard_map/ppermute | solution.py:901
  136.2 12.1 %collective-permute-start.34 = (bf16[64,1536]{1,0:T(8,128)(2,1)S(1)}, bf16[64,1536]{1,0:T(8,128)(2,1)S(1)}, u32[]{:S(2)}, u32[]{:S(2)}) collective-permute-start(bf16[64,1536]{1,0:T(8,128)(2,1)S(1)} %four.1.refs_1_), channel_id=1, source_target_pairs={{0,1},{1,0},{2,3},{3,2},{4,5},{5,4},{6,7},{7,6},{8,9},{9,8},{10,11... | collective-permute-start | bytes 589832 | tf_op jit(solution)/shard_map/ppermute | solution.py:901
  143.5 4.8 %collective-permute-start.37 = (bf16[64,1536]{1,0:T(8,128)(2,1)S(1)}, bf16[64,1536]{1,0:T(8,128)(2,1)S(1)}, u32[]{:S(2)}, u32[]{:S(2)}) collective-permute-start(bf16[64,1536]{1,0:T(8,128)(2,1)S(1)} %collective-permute-done.33.refs_4_), channel_id=1, source_target_pairs={{0,1},{1,0},{2,3},{3,2},{4,5},{5,4},{6,7},{7,6},{8,9},{9,8},{10,11... | collective-permute-start | bytes 589832 | tf_op jit(solution)/shard_map/ppermute | solution.py:901
  (20 other events, 168.4 us)
